TPU v7x, 32 devices: a whole 2x2x4 slice. The times are simulated.
32 devices in a mesh: gx: 8 (over y, x, core), gy: 4 (over z).
Axes of the slice: x: 2, y: 2, z: 4, core: 2. Of those that a mesh axis runs over, the one named last changes fastest.
Arguments:
- log_density: float32 [256, 256, 512], P('gx', 'gy'), may hold values from -3 to 3
- weights: bfloat16 [2048, 32, 32, 128], P(('gx', 'gy')), may hold values from -0.09375 to 0.09375
- observed: float32 [2048, 32], P(('gx', 'gy')), may hold values from -6 to 6
- inverse_var: float32 [2048, 32], P(('gx', 'gy')), may hold values from 0.25 to 4
- star_counts: int32 [2048], P(('gx', 'gy')), may hold values from 1 to 32
- block_ids: int32 [2048, 32], P(('gx', 'gy')), may hold values from 0 to 262143, as said below
Outputs:
- new_log_density: float32 [256, 256, 512], P('gx', 'gy')
- extinction: float32 [2048, 32], P(('gx', 'gy'))
Inputs may be any that keep to these rules, and one draw needn't show every extreme that they name: `block_ids`: among the 2048 ids of one device's rows (rows d * 64 to (d + 1) * 64 - 1), at most 128 name blocks of any one tile (blocks t * 8192 to (t + 1) * 8192 - 1), and exactly 128 name blocks of tile d.
All inputs are finite; a program needn't handle non-finite values.
Results may differ from a plain program's by a relative error of at most 0.0029.
Values may be sent and summed in bfloat16 or wider, within the bound.
No kernel may reach another device: no remote copies, remote signals or barrier semaphores. Data moves between devices by JAX's collectives and lax.ppermute only.
A program may use at most 128 MiB of HBM per device.

v0:
```python
import jax
import jax.numpy as jnp
from jax import lax
from jax.sharding import PartitionSpec as P

shift_kappa = 0.5
prior_weight = 0.05
step_rate = 2.0


def extended(x, sides, width):
    for axis, dim in sides:
        peers, length = (lax.axis_size(axis), x.shape[dim])
        up = [(i, (i + 1) % peers) for i in range(peers - 1)]
        down = [(j, i) for i, j in up]
        last = lax.slice_in_dim(x, length - width, length, axis=dim)
        first = lax.slice_in_dim(x, 0, width, axis=dim)
        before = lax.ppermute(last, axis, up)
        after = lax.ppermute(first, axis, down)
        x = jnp.concatenate([before, x, after], axis=dim)
    return x


def apply_op(padded):
    center = padded[1:-1, 1:-1, :]
    beside = padded[2:, 1:-1, :] + padded[:-2, 1:-1, :]
    beside = beside + padded[1:-1, 2:, :] + padded[1:-1, :-2, :]
    blank_plane = jnp.zeros(center.shape[:2] + (1,), jnp.float32)
    beside = beside + jnp.concatenate([center[:, :, 1:], blank_plane], 2)
    beside = beside + jnp.concatenate([blank_plane, center[:, :, :-1]], 2)
    return (shift_kappa + 6.0) * center - beside


def on_device(log_density, weights, observed, inverse_var, star_counts, block_ids):
    cells_x, cells_y, depth = log_density.shape
    blocks_dev, slots, stars, width = weights.shape
    size_x = lax.axis_size("gx")
    size_y = lax.axis_size("gy")
    devices = size_x * size_y
    requests = blocks_dev * slots
    capacity = 2 * requests // devices
    local_blocks = cells_x * cells_y * (depth // width)
    flat_ids = block_ids.reshape(requests)
    target = flat_ids // local_blocks
    within = flat_ids % local_blocks
    onehot = (target[:, None] == jnp.arange(devices, dtype=jnp.int32)[None, :]).astype(jnp.int32)
    ranked = jnp.sum(jnp.cumsum(onehot, 0) * onehot, 1) - 1
    position = target * capacity + ranked
    outgoing = jnp.full((devices * capacity,), -1, jnp.int32).at[position].set(within)
    incoming = lax.all_to_all(
        outgoing.reshape(devices, capacity), ("gx", "gy"), split_axis=0, concat_axis=0, tiled=True
    ).reshape(-1)
    dens_field = jnp.exp(log_density)
    table = dens_field.astype(jnp.bfloat16).reshape(local_blocks, width)
    present = incoming >= 0
    served = jnp.where(
        present[:, None], table[jnp.maximum(incoming, 0)], jnp.zeros((), jnp.bfloat16)
    )
    returned = lax.all_to_all(
        served.reshape(devices, capacity, width),
        ("gx", "gy"),
        split_axis=0,
        concat_axis=0,
        tiled=True,
    )
    fetched = returned.reshape(devices * capacity, width)[position].reshape(
        blocks_dev, slots, width
    )
    extinction = jnp.einsum("bksv,bkv->bs", weights, fetched, preferred_element_type=jnp.float32)
    live = jnp.arange(stars)[None, :] < star_counts[:, None]
    weighted = jnp.where(live, inverse_var * (extinction - observed), 0.0).astype(jnp.bfloat16)
    sens = jnp.einsum(
        "bksv,bs->bkv", weights, weighted, preferred_element_type=jnp.float32
    ).reshape(requests, width)
    parcel = jnp.zeros((devices * capacity, width), jnp.float32).at[position].set(sens)
    arrived = lax.all_to_all(
        parcel.reshape(devices, capacity, width),
        ("gx", "gy"),
        split_axis=0,
        concat_axis=0,
        tiled=True,
    )
    arrived = arrived.reshape(devices * capacity, width)
    first_pad = extended(log_density, (("gx", 0), ("gy", 1)), 1)
    smooth = apply_op(first_pad)
    second_pad = extended(smooth, (("gx", 0), ("gy", 1)), 1)
    prior_grad = apply_op(second_pad)
    slot_target = jnp.where(present, incoming, local_blocks)
    collected = (
        jnp.zeros((local_blocks, width), jnp.float32).at[slot_target].add(arrived, mode="drop")
    )
    data_grad = collected.reshape(cells_x, cells_y, depth) * dens_field
    new_log_density = log_density - step_rate * (data_grad + prior_weight * prior_grad)
    return (new_log_density, extinction)


def solution(mesh):
    placed = (
        P("gx", "gy", None),
        P(("gx", "gy"), None, None, None),
        P(("gx", "gy"), None),
        P(("gx", "gy"), None),
        P(("gx", "gy")),
        P(("gx", "gy"), None),
    )
    return jax.shard_map(
        on_device,
        mesh=mesh,
        in_specs=placed,
        out_specs=(P("gx", "gy", None), P(("gx", "gy"), None)),
        check_vma=False,
    )
```

profile of v0, /device:TPU:1, one launch (start us, length us, event | category | flops | bytes accessed | tf_op | source)
XLA Modules:
  0.0 240.7 jit_solution(3158117413192023690)
XLA Ops:
  1.6 4.5 %collective-permute-start.1 = (f32[1,64,512]{2,1,0:T(8,128)S(1)}, f32[1,64,512]{2,1,0:T(8,128)S(1)}, u32[]{:S(2)}, u32[]{:S(2)}) collective-permute-start(f32[1,64,512]{2,1,0:T(8,128)S(1)} %get-tuple-element.17), channel_id=1, source_target_pairs={{0,4},{4,8},{8,12},{12,16},{16,20},{20,24},{24,28},{1,5},{5,9},{9,... | collective-permute-start | bytes 393224 | tf_op jit(solution)/shard_map/ppermute | solution.py:18
  6.1 1.9 collective-permute-start
  9.1 9.1 %reduce-window.6 = s32[32,16,128]{2,1,0:T(8,128)S(1)} reduce-window(s32[32,16,128]{2,1,0:T(8,128)S(1)} %fusion.24, s32[]{:T(128)} %constant.47.clone.1), window={size=1x1x128 pad=0_0x0_0x127_0}, to_apply=%region_0.1 | reduce-window | flops 8323072 | bytes 524292 | tf_op jit(solution)/shard_map/reduce-window
  19.1 8.6 %scatter_custom_fusion = s32[4096]{0:T(1024)} fusion(s32[2048]{0:T(1024)S(1)} %bitcast.56, s32[2048]{0:T(1024)S(1)} %get-tuple-element.20, s32[]{:T(128)} %constant.27.clone.1), kind=kCustom, calls=%fused_computation.76 | custom fusion | bytes 16388 | tf_op jit(solution)/shard_map/scatter | solution.py:49
  27.8 6.2 %all-to-all-start = ((s32[32,1,128]{2,1,0:T(1,128)}), s32[32,1,128]{2,1,0:T(1,128)S(1)}, u32[]{:S(2)}, u32[]{:S(2)}) async-start(s32[32,1,128]{2,1,0:T(1,128)} %bitcast.5), calls=%async_computation | async-start | bytes 32768 | tf_op jit(solution)/shard_map/all_to_all | solution.py:50
  34.0 8.1 %fusion.35 = (f32[32,64,511]{2,1,0:T(8,128)}, f32[32,64,511]{2,1,0:T(8,128)}) fusion(f32[32,64,512]{2,1,0:T(8,128)} %param.6), kind=kLoop, calls=%fused_computation.89 | loop fusion | bytes 16744448 | tf_op jit(solution)/shard_map/slice | solution.py:29
  42.2 2.8 %constant_dynamic-update-slice_fusion.1 = f32[34,64,512]{2,1,0:T(8,128)S(1)} fusion(f32[34,64,512]{2,1,0:T(8,128)S(1)} %constant_dynamic-update-slice_fusion.2, f32[32,64,512]{2,1,0:T(8,128)} %param.6), kind=kLoop, calls=%fused_computation.81 | loop fusion | bytes 8388608
  45.2 1.4 collective-permute-start.2
  46.6 4.0 %collective-permute-start.3 = (f32[34,1,512]{2,0,1:T(8,128)S(1)}, f32[34,1,512]{2,0,1:T(8,128)S(1)}, u32[]{:S(2)}, u32[]{:S(2)}) collective-permute-start(f32[34,1,512]{2,0,1:T(8,128)S(1)} %copy.38), channel_id=1, source_target_pairs={{0,1},{1,2},{2,3},{4,5},{5,6},{6,7},{8,9},{9,10},{10,11},{12,13},{... | collective-permute-start | bytes 208904 | tf_op jit(solution)/shard_map/ppermute | solution.py:18
  52.2 9.2 %exponential_convert_fusion = (bf16[32,64,512]{2,1,0:T(8,128)(2,1)}, f32[32,64,512]{2,1,0:T(8,128)}) fusion(f32[32,64,512]{2,1,0:T(8,128)S(1)} %copy-done, f32[32,64,511]{2,1,0:T(8,128)} %get-tuple-element.15, f32[32,64,511]{2,1,0:T(8,128)S(1)} %copy-done.2, f32[34,64,512]{2,1,0:T(8,128)S(1)} %constant_dynamic-update-slice_fusion, ...), kind=kLoop, calls=%fused_computation.33 | loop fusion | flops 12582912 | bytes 23715840 | tf_op jit(solution)/shard_map/convert_element_type | solution.py:54
  61.4 3.1 %reshape.221 = bf16[8192,128]{1,0:T(8,128)(2,1)S(1)} reshape(bf16[32,64,512]{2,1,0:T(8,128)(2,1)} %get-tuple-element.8) | data formatting | bytes 4194304 | tf_op jit(solution)/shard_map/reshape | solution.py:54
  64.5 12.1 %gather_fusion = bf16[4096,128]{1,0:T(8,128)(2,1)S(1)} fusion(bf16[8192,128]{1,0:T(8,128)(2,1)S(1)} %reshape.221, s32[4096]{0:T(1024)S(1)} %broadcast_clamp_fusion), kind=kCustom, calls=%fused_computation | custom fusion | bytes 2113536 | tf_op jit(solution)/shard_map/gather | solution.py:57
  76.7 1.5 broadcast_select_fusion
  78.2 7.8 %all-to-all-start.1 = ((bf16[32,128,128]{2,1,0:T(8,128)(2,1)}), bf16[32,128,128]{2,1,0:T(8,128)(2,1)S(1)}, u32[]{:S(2)}, u32[]{:S(2)}) async-start(bf16[32,128,128]{2,1,0:T(8,128)(2,1)} %broadcast_select_fusion), calls=%async_computation.1 | async-start | bytes 2097152 | tf_op jit(solution)/shard_map/all_to_all | solution.py:59
  86.0 26.3 %all-to-all-done.1 = bf16[32,128,128]{2,1,0:T(8,128)(2,1)S(1)} async-done(((bf16[32,128,128]{2,1,0:T(8,128)(2,1)}), bf16[32,128,128]{2,1,0:T(8,128)(2,1)S(1)}, u32[]{:S(2)}, u32[]{:S(2)}) %all-to-all-start.1) | async-done | bytes 1048608 | tf_op jit(solution)/shard_map/all_to_all | solution.py:59
  112.3 6.2 %gather_fusion.1 = bf16[2048,128]{1,0:T(8,128)(2,1)S(1)} fusion(bf16[4096,128]{1,0:T(8,128)(2,1)S(1)} %bitcast.45, s32[2048]{0:T(1024)S(1)} %broadcast_clamp_fusion.1), kind=kCustom, calls=%fused_computation.1 | custom fusion | bytes 1056768 | tf_op jit(solution)/shard_map/gather | solution.py:66
  118.6 8.2 %fusion.18 = f32[64,1,32,1]{2,1,3,0:T(1,128)S(1)} fusion(bf16[64,32,32,128]{3,2,1,0:T(8,128)(2,1)} %param.7, bf16[64,32,128,1]{2,1,0,3:T(8,128)(2,1)S(1)} %bitcast.50), kind=kOutput, calls=%fused_computation.36 | convolution fusion | flops 16777216 | bytes 17309696 | tf_op jit(solution)/shard_map/bksv,bkv->bs/dot_general | solution.py:69
  127.0 8.0 %fusion.37 = f32[64,1,32,128]{3,1,2,0:T(1,128)S(1)} fusion(bf16[64,32,1,1]{1,2,3,0:T(2,128)(2,1)S(1)} %copy.46, bf16[64,32,32,128]{3,2,1,0:T(8,128)(2,1)} %param.7), kind=kOutput, calls=%fused_computation.91 | convolution fusion | flops 16777216 | bytes 17829888 | tf_op jit(solution)/shard_map/bksv,bs->bkv/dot_general | solution.py:72
  135.1 7.0 %scatter_custom_fusion.1 = f32[4096,128]{1,0:T(8,128)} fusion(s32[2048]{0:T(1024)S(1)} %bitcast.58, f32[2048,128]{1,0:T(8,128)S(1)} %bitcast.47, f32[]{:T(128)} %constant.23.clone.1), kind=kCustom, calls=%fused_computation.38 | custom fusion | bytes 2097156 | tf_op jit(solution)/shard_map/scatter | solution.py:75
  142.0 3.2 %all-to-all-start.2 = ((f32[32,128,128]{2,1,0:T(8,128)}), f32[32,128,128]{2,1,0:T(8,128)S(1)}, u32[]{:S(2)}, u32[]{:S(2)}) async-start(f32[32,128,128]{2,1,0:T(8,128)} %bitcast.20), calls=%async_computation.2 | async-start | bytes 4194304 | tf_op jit(solution)/shard_map/all_to_all | solution.py:76
  146.4 2.3 collective-permute-start.4
  148.7 3.4 %collective-permute-start.5 = (f32[1,64,512]{2,1,0:T(8,128)S(1)}, f32[1,64,512]{2,1,0:T(8,128)S(1)}, u32[]{:S(2)}, u32[]{:S(2)}) collective-permute-start(f32[1,64,512]{2,1,0:T(8,128)S(1)} %get-tuple-element.12), channel_id=1, source_target_pairs={{0,4},{4,8},{8,12},{12,16},{16,20},{20,24},{24,28},{1,5},{5,9},{9,... | collective-permute-start | bytes 393224 | tf_op jit(solution)/shard_map/ppermute | solution.py:18
  152.1 14.4 %collective-permute-done.4 = f32[1,64,512]{2,1,0:T(8,128)S(1)} collective-permute-done((f32[1,64,512]{2,1,0:T(8,128)S(1)}, f32[1,64,512]{2,1,0:T(8,128)S(1)}, u32[]{:S(2)}, u32[]{:S(2)}) %collective-permute-start.4) | collective-permute-done | bytes 131104 | tf_op jit(solution)/shard_map/ppermute | solution.py:19
  166.4 1.3 pad_maximum_fusion.14
  167.8 1.3 collective-permute-start.6
  169.1 4.0 %collective-permute-start.7 = (f32[34,1,512]{2,0,1:T(8,128)S(1)}, f32[34,1,512]{2,0,1:T(8,128)S(1)}, u32[]{:S(2)}, u32[]{:S(2)}) collective-permute-start(f32[34,1,512]{2,0,1:T(8,128)S(1)} %copy.42), channel_id=1, source_target_pairs={{0,1},{1,2},{2,3},{4,5},{5,6},{6,7},{8,9},{9,10},{10,11},{12,13},{... | collective-permute-start | bytes 208904 | tf_op jit(solution)/shard_map/ppermute | solution.py:18
  173.1 4.8 %fusion.33 = (f32[32,64,511]{2,1,0:T(8,128)}, f32[32,64,511]{2,1,0:T(8,128)}) fusion(f32[32,64,512]{2,1,0:T(8,128)S(1)} %copy-done.1), kind=kLoop, calls=%fused_computation.87 | loop fusion | bytes 16744448 | tf_op jit(solution)/shard_map/slice | solution.py:29
  178.0 3.7 %collective-permute-done.7 = f32[34,1,512]{2,0,1:T(8,128)S(1)} collective-permute-done((f32[34,1,512]{2,0,1:T(8,128)S(1)}, f32[34,1,512]{2,0,1:T(8,128)S(1)}, u32[]{:S(2)}, u32[]{:S(2)}) %collective-permute-start.7) | collective-permute-done | bytes 69664 | tf_op jit(solution)/shard_map/ppermute | solution.py:18
  181.7 11.8 %all-to-all-done.2 = f32[32,128,128]{2,1,0:T(8,128)S(1)} async-done(((f32[32,128,128]{2,1,0:T(8,128)}), f32[32,128,128]{2,1,0:T(8,128)S(1)}, u32[]{:S(2)}, u32[]{:S(2)}) %all-to-all-start.2) | async-done | bytes 2097184 | tf_op jit(solution)/shard_map/all_to_all | solution.py:76
  193.5 24.6 %scatter_custom_fusion.2 = f32[8192,128]{1,0:T(8,128)} fusion(s32[4096]{0:T(1024)S(1)} %bitcast.60, f32[4096,128]{1,0:T(8,128)S(1)} %bitcast.48, f32[]{:T(128)} %constant.23.clone.1), kind=kCustom, calls=%fused_computation.34 | custom fusion | flops 524288 | bytes 4194308 | tf_op jit(solution)/shard_map/scatter-add | solution.py:90
  218.0 4.9 %reshape.227 = f32[32,64,512]{2,1,0:T(8,128)} reshape(f32[8192,128]{1,0:T(8,128)} %scatter_custom_fusion.2) | data formatting | bytes 8388608 | tf_op jit(solution)/shard_map/reshape | solution.py:92
  223.0 17.8 %fusion.7 = f32[32,64,512]{2,1,0:T(8,128)} fusion(f32[32,64,512]{2,1,0:T(8,128)} %param.6, f32[34,1,512]{2,1,0:T(1,128)S(1)} %copy.43, f32[1,64,512]{2,1,0:T(8,128)S(1)} %collective-permute-done.4, f32[32,64,512]{2,1,0:T(8,128)} %get-tuple-element.9, f32[1,64,512]{2,1,0:T(8,128)S(1)} %collective-permute-done.5, f32[34,1,512]{2,1,0:T(1,128)S(1)} %copy.41, ...), kind=kLoop, calls=%fused_computation.13 | loop fusion | flops 20971520 | bytes 25550848 | tf_op jit(solution)/shard_map/sub | solution.py:93
  (55 shorter events, 6.2 us)
Async XLA Ops:
  1.6 40.5 %collective-permute-start.1 = (f32[1,64,512]{2,1,0:T(8,128)S(1)}, f32[1,64,512]{2,1,0:T(8,128)S(1)}, u32[]{:S(2)}, u32[]{:S(2)}) collective-permute-start(f32[1,64,512]{2,1,0:T(8,128)S(1)} %get-tuple-element.17), channel_id=1, source_target_pairs={{0,4},{4,8},{8,12},{12,16},{16,20},{20,24},{24,28},{1,5},{5,9},{9,... | collective-permute-start | bytes 393224 | tf_op jit(solution)/shard_map/ppermute | solution.py:18
  6.1 38.9 %collective-permute-start = (f32[1,64,512]{2,1,0:T(8,128)S(1)}, f32[1,64,512]{2,1,0:T(8,128)S(1)}, u32[]{:S(2)}, u32[]{:S(2)}) collective-permute-start(f32[1,64,512]{2,1,0:T(8,128)S(1)} %get-tuple-element.16), channel_id=1, source_target_pairs={{4,0},{8,4},{12,8},{16,12},{20,16},{24,20},{28,24},{5,1},{9,5},{13... | collective-permute-start | bytes 393224 | tf_op jit(solution)/shard_map/ppermute | solution.py:19
  27.8 14.3 %all-to-all-start = ((s32[32,1,128]{2,1,0:T(1,128)}), s32[32,1,128]{2,1,0:T(1,128)S(1)}, u32[]{:S(2)}, u32[]{:S(2)}) async-start(s32[32,1,128]{2,1,0:T(1,128)} %bitcast.5), calls=%async_computation | async-start | bytes 32768 | tf_op jit(solution)/shard_map/all_to_all | solution.py:50
  42.2 10.0 %copy-start = (f32[32,64,512]{2,1,0:T(8,128)S(1)}, f32[32,64,512]{2,1,0:T(8,128)}, u32[]{:S(2)}) copy-start(f32[32,64,512]{2,1,0:T(8,128)} %param.6) | copy-start | bytes 12582916
  42.2 10.0 %copy-start.2 = (f32[32,64,511]{2,1,0:T(8,128)S(1)}, f32[32,64,511]{2,1,0:T(8,128)}, u32[]{:S(2)}) copy-start(f32[32,64,511]{2,1,0:T(8,128)} %get-tuple-element.14) | copy-start | bytes 12558340
  45.2 5.8 %collective-permute-start.2 = (f32[34,1,512]{2,0,1:T(8,128)S(1)}, f32[34,1,512]{2,0,1:T(8,128)S(1)}, u32[]{:S(2)}, u32[]{:S(2)}) collective-permute-start(f32[34,1,512]{2,0,1:T(8,128)S(1)} %copy.36), channel_id=1, source_target_pairs={{1,0},{2,1},{3,2},{5,4},{6,5},{7,6},{9,8},{10,9},{11,10},{13,12},{... | collective-permute-start | bytes 208904 | tf_op jit(solution)/shard_map/ppermute | solution.py:19
  46.6 5.5 %collective-permute-start.3 = (f32[34,1,512]{2,0,1:T(8,128)S(1)}, f32[34,1,512]{2,0,1:T(8,128)S(1)}, u32[]{:S(2)}, u32[]{:S(2)}) collective-permute-start(f32[34,1,512]{2,0,1:T(8,128)S(1)} %copy.38), channel_id=1, source_target_pairs={{0,1},{1,2},{2,3},{4,5},{5,6},{6,7},{8,9},{9,10},{10,11},{12,13},{... | collective-permute-start | bytes 208904 | tf_op jit(solution)/shard_map/ppermute | solution.py:18
  78.2 34.2 %all-to-all-start.1 = ((bf16[32,128,128]{2,1,0:T(8,128)(2,1)}), bf16[32,128,128]{2,1,0:T(8,128)(2,1)S(1)}, u32[]{:S(2)}, u32[]{:S(2)}) async-start(bf16[32,128,128]{2,1,0:T(8,128)(2,1)} %broadcast_select_fusion), calls=%async_computation.1 | async-start | bytes 2097152 | tf_op jit(solution)/shard_map/all_to_all | solution.py:59
  118.5 8.3 %copy-start.4 = (f32[64,32]{0,1:T(8,128)S(1)}, f32[64,32]{0,1:T(8,128)}, u32[]{:S(2)}) copy-start(f32[64,32]{0,1:T(8,128)} %param.9) | copy-start | bytes 24580
  118.5 8.3 %copy-start.5 = (f32[64,32]{0,1:T(8,128)S(1)}, f32[64,32]{0,1:T(8,128)}, u32[]{:S(2)}) copy-start(f32[64,32]{0,1:T(8,128)} %param.8) | copy-start | bytes 24580
  118.5 8.3 %copy-start.6 = (s32[64]{0:T(128)S(1)}, s32[64]{0:T(128)}, u32[]{:S(2)}) copy-start(s32[64]{0:T(128)} %param.10) | copy-start | bytes 772
  126.9 8.2 %copy-start.3 = (f32[64,1,32,1]{0,2,1,3:T(8,128)}, f32[64,1,32,1]{0,2,1,3:T(8,128)S(1)}, u32[]{:S(2)}) copy-start(f32[64,1,32,1]{0,2,1,3:T(8,128)S(1)} %copy.45) | copy-start | bytes 24580
  142.0 51.4 %all-to-all-start.2 = ((f32[32,128,128]{2,1,0:T(8,128)}), f32[32,128,128]{2,1,0:T(8,128)S(1)}, u32[]{:S(2)}, u32[]{:S(2)}) async-start(f32[32,128,128]{2,1,0:T(8,128)} %bitcast.20), calls=%async_computation.2 | async-start | bytes 4194304 | tf_op jit(solution)/shard_map/all_to_all | solution.py:76
  145.2 27.9 %copy-start.1 = (f32[32,64,512]{2,1,0:T(8,128)S(1)}, f32[32,64,512]{2,1,0:T(8,128)}, u32[]{:S(2)}) copy-start(f32[32,64,512]{2,1,0:T(8,128)} %get-tuple-element.9) | copy-start | bytes 12582916
  146.4 20.1 %collective-permute-start.4 = (f32[1,64,512]{2,1,0:T(8,128)S(1)}, f32[1,64,512]{2,1,0:T(8,128)S(1)}, u32[]{:S(2)}, u32[]{:S(2)}) collective-permute-start(f32[1,64,512]{2,1,0:T(8,128)S(1)} %get-tuple-element.13), channel_id=1, source_target_pairs={{4,0},{8,4},{12,8},{16,12},{20,16},{24,20},{28,24},{5,1},{9,5},{13... | collective-permute-start | bytes 393224 | tf_op jit(solution)/shard_map/ppermute | solution.py:19
  148.7 17.8 %collective-permute-start.5 = (f32[1,64,512]{2,1,0:T(8,128)S(1)}, f32[1,64,512]{2,1,0:T(8,128)S(1)}, u32[]{:S(2)}, u32[]{:S(2)}) collective-permute-start(f32[1,64,512]{2,1,0:T(8,128)S(1)} %get-tuple-element.12), channel_id=1, source_target_pairs={{0,4},{4,8},{8,12},{12,16},{16,20},{20,24},{24,28},{1,5},{5,9},{9,... | collective-permute-start | bytes 393224 | tf_op jit(solution)/shard_map/ppermute | solution.py:18
  167.8 10.1 %collective-permute-start.6 = (f32[34,1,512]{2,0,1:T(8,128)S(1)}, f32[34,1,512]{2,0,1:T(8,128)S(1)}, u32[]{:S(2)}, u32[]{:S(2)}) collective-permute-start(f32[34,1,512]{2,0,1:T(8,128)S(1)} %copy.40), channel_id=1, source_target_pairs={{1,0},{2,1},{3,2},{5,4},{6,5},{7,6},{9,8},{10,9},{11,10},{13,12},{... | collective-permute-start | bytes 208904 | tf_op jit(solution)/shard_map/ppermute | solution.py:19
  169.1 12.5 %collective-permute-start.7 = (f32[34,1,512]{2,0,1:T(8,128)S(1)}, f32[34,1,512]{2,0,1:T(8,128)S(1)}, u32[]{:S(2)}, u32[]{:S(2)}) collective-permute-start(f32[34,1,512]{2,0,1:T(8,128)S(1)} %copy.42), channel_id=1, source_target_pairs={{0,1},{1,2},{2,3},{4,5},{5,6},{6,7},{8,9},{9,10},{10,11},{12,13},{... | collective-permute-start | bytes 208904 | tf_op jit(solution)/shard_map/ppermute | solution.py:18
where the time goes:
time: 242 us; the launch traced here: 241 us
  other arithmetic  64.1 us (26%)
  local copies, waits for them, and re-layouts  61.8 us (26%)
  waiting for transfers between devices  57.5 us (24%)
  starting transfers between devices  40 us (17%)
  matrix products  16.3 us (7%)
    all_to_all x1, waiting for transfers between devices, on_device(): lax.all_to_all(served.reshape(devices, capacity, width), ('gx', 'gy'), sp...  26.3 us
    scatter-add x1, other arithmetic, on_device(): jnp.zeros((local_blocks, width), jnp.float32).at[slot_target]  24.6 us
    sub x1, other arithmetic, on_device(): log_density - step_rate * (data_grad + prior_weight * prior_grad)  17.8 us
    ppermute x4, starting transfers between devices, extended(): before = lax.ppermute(last, axis, up)  15.9 us
    ppermute x4, waiting for transfers between devices, extended(): after = lax.ppermute(first, axis, down)  14.7 us
    slice x2, local copies, waits for them, and re-layouts, apply_op(): beside = beside + jnp.concatenate([center[:, :, 1:], blank_plane], 2)  12.9 us
    gather x1, local copies, waits for them, and re-layouts, on_device(): table[jnp.maximum(incoming, 0)]  12.1 us
    all_to_all x1, waiting for transfers between devices, on_device(): lax.all_to_all(parcel.reshape(devices, capacity, width), ('gx', 'gy'), sp...  11.8 us
  transfers between devices with their start and end apart: 11, of which 6 were waited for; matrix products, arithmetic and copies ran while one was open for 16% of the time, Pallas kernels for 0%

commit v1 on v0

v1 whole, which is shorter than its diff:
```python
import functools

import jax
import jax.numpy as jnp
from jax import lax
from jax.experimental import pallas as pl
from jax.experimental.pallas import tpu as pltpu
from jax.sharding import PartitionSpec as P

shift_kappa = 0.5
prior_weight = 0.05
step_rate = 2.0

LANES = 128
GROUP = 16
MIB = 1 << 20

CONTRACT_LANES = (((1,), (1,)), ((), ()))


def split_by(value, size):
    if size & (size - 1) == 0:
        high = value >> (size.bit_length() - 1)
        return high, value & (size - 1)
    high = value // size
    return high, value - high * size


def route_kernel(ids_ref, outgoing_ref, position_ref, *, devices, capacity, blocks, per_column):
    lane = lax.broadcasted_iota(jnp.int32, (LANES, LANES), 1)
    row = lax.broadcasted_iota(jnp.int32, (LANES, LANES), 0)
    upper = jnp.where(row <= lane, 1.0, 0.0).astype(jnp.bfloat16)
    tile_no = lax.broadcasted_iota(jnp.int32, (devices, LANES), 0)
    slot_no = lax.broadcasted_iota(jnp.int32, (capacity, LANES), 0)
    before = jnp.zeros((devices, 1), jnp.float32)
    lists = jnp.zeros((2 * devices, capacity), jnp.float32)
    for chunk in range(ids_ref.shape[0]):
        target, local = split_by(ids_ref[chunk : chunk + 1, :], blocks)
        column, part = split_by(local, per_column)
        local = ((column >> 3) * per_column + part) * 8 + (column & 7)
        hit = tile_no == target
        onehot = jnp.where(hit, 1.0, 0.0)
        upto = before + jnp.dot(
            onehot.astype(jnp.bfloat16), upper, preferred_element_type=jnp.float32
        )
        before = upto[:, LANES - 1 :]
        rank = jnp.sum(onehot * upto, axis=0, keepdims=True).astype(jnp.int32) - 1
        in_slot = jnp.where(slot_no == rank, 1.0, 0.0).astype(jnp.bfloat16)
        high = ((local >> 7) + 1).astype(jnp.float32)
        low = (local & 127).astype(jnp.float32)
        digits = jnp.concatenate([jnp.where(hit, high, 0.0), jnp.where(hit, low, 0.0)], axis=0)
        lists = lists + lax.dot_general(
            digits.astype(jnp.bfloat16),
            in_slot,
            CONTRACT_LANES,
            preferred_element_type=jnp.float32,
        )
        position_ref[chunk : chunk + 1, :] = target * capacity + rank
    high, low = lists[:devices], lists[devices:]
    wanted = ((high - 1.0) * 128.0 + low).astype(jnp.int32)
    outgoing_ref[...] = jnp.where(high > 0.5, wanted, blocks + before.astype(jnp.int32))


def filled_groups(incoming_ref, source, capacity, blocks):
    last = incoming_ref[source, capacity - 1]
    filled = jnp.where(last < blocks, capacity, last - blocks)
    return (filled + GROUP - 1) // GROUP


def serve_kernel(incoming_ref, table_ref, served_ref, rows_ref, *, capacity, blocks):
    sources = incoming_ref.shape[0]

    def one_source(source, carry):
        base = pl.multiple_of(source * capacity, capacity)

        def one_group(group, carry):
            first = pl.multiple_of(group * GROUP, GROUP)
            for j in range(GROUP):
                at = jnp.minimum(incoming_ref[source, first + j], blocks - 1)
                rows_ref[pl.ds(base + first + j, 1), :] = table_ref[pl.ds(at, 1), :]
            return carry

        lax.fori_loop(0, filled_groups(incoming_ref, source, capacity, blocks), one_group, 0)
        span = pl.ds(base, capacity)
        served_ref[span, :] = jnp.exp(rows_ref[span, :]).astype(jnp.bfloat16)
        return carry

    lax.fori_loop(0, sources, one_source, 0)


def match_kernel(incoming_ref, match_ref):
    lane = lax.broadcasted_iota(jnp.int32, (LANES, LANES), 1)
    row = lax.broadcasted_iota(jnp.int32, (LANES, LANES), 0)
    ones = jnp.ones((LANES, LANES), jnp.bfloat16)
    same_group = (lane // GROUP) == (row // GROUP)

    def one_row(i, carry):
        wanted = incoming_ref[pl.ds(i, 1), :]
        high = jnp.where(lane == row, (wanted >> 7).astype(jnp.float32), 0.0).astype(jnp.bfloat16)
        low = jnp.where(lane == row, (wanted & 127).astype(jnp.float32), 0.0).astype(jnp.bfloat16)
        down = 128.0 * jnp.dot(high, ones, preferred_element_type=jnp.float32)
        down = down + jnp.dot(low, ones, preferred_element_type=jnp.float32)
        same = (down == wanted.astype(jnp.float32)) & same_group
        match_ref[pl.ds(pl.multiple_of(i * LANES, LANES), LANES), :] = jnp.where(
            same, 1.0, 0.0
        ).astype(jnp.bfloat16)
        return carry

    lax.fori_loop(0, incoming_ref.shape[0], one_row, 0)


def star_kernel(
    position_ref,
    returned_ref,
    observed_ref,
    inverse_ref,
    weights_hbm,
    extinction_ref,
    parcel_ref,
    weights_ref,
    fetched_ref,
    sens_ref,
    sems,
):
    blocks_dev, slots, stars, width = weights_ref.shape
    chunks = extinction_ref.shape[0]
    per = blocks_dev // chunks

    def load(chunk):
        span = pl.ds(chunk * per, per)
        return pltpu.make_async_copy(weights_hbm.at[span], weights_ref.at[span], sems.at[chunk])

    for chunk in range(chunks):
        load(chunk).start()
    fetched_ref[...] = returned_ref[...].astype(jnp.float32)
    sens_ref[...] = jnp.zeros_like(sens_ref)
    lane = lax.broadcasted_iota(jnp.int32, (8, LANES), 1)
    row = lax.broadcasted_iota(jnp.int32, (8, LANES), 0)
    star_group = lane // stars

    def extinctions(chunk):
        sums = []
        for b in range(per):
            total = jnp.zeros((stars, width), jnp.float32)
            for k in range(slots):
                at = position_ref[chunk, b * slots + k]
                total = total + weights_ref[chunk * per + b, k].astype(jnp.float32) * fetched_ref[
                    pl.ds(at, 1), :
                ]
            sums.append(total)
        extinction = lax.dot_general(
            jnp.ones((8, width), jnp.float32),
            jnp.concatenate(sums, axis=0),
            CONTRACT_LANES,
            precision=lax.Precision.HIGHEST,
            preferred_element_type=jnp.float32,
        )
        extinction_ref[pl.ds(chunk, 1), :] = extinction[:1]
        here = pl.ds(chunk, 1)
        return inverse_ref[here, :] * (extinction - observed_ref[here, :])

    def sensitivities(chunk, weighted):
        for b in range(per):
            spread = jnp.where(star_group == b, weighted, 0.0)
            shift = stars
            while shift < LANES:
                spread = spread + pltpu.roll(spread, shift, 1)
                shift *= 2
            left = jnp.concatenate(
                [jnp.where(row == star_group + per * h, spread, 0.0) for h in range(8 // per)],
                axis=1,
            ).astype(jnp.bfloat16)
            for j in range(slots // 8):
                right = weights_ref[chunk * per + b, 8 * j : 8 * j + 8].reshape(8 * stars, width)
                sens = jnp.dot(left, right, preferred_element_type=jnp.float32)
                for r in range(8):
                    at = position_ref[chunk, b * slots + 8 * j + r]
                    sens_ref[pl.ds(at, 1), :] = sens[r : r + 1, :]

    load(0).wait()
    first = extinctions(0)

    def step(chunk, weighted):
        load(chunk).wait()
        following = extinctions(chunk)
        sensitivities(chunk - 1, weighted)
        return following

    last = lax.fori_loop(1, chunks, step, first)
    sensitivities(chunks - 1, last)
    parcel_ref[...] = sens_ref[...].astype(jnp.bfloat16)


def prior_kernel(field_ref, xlo_ref, xhi_ref, ylo_ref, yhi_ref, out_ref, padded, smooth):
    cells_x, cells_y, depth = field_ref.shape
    rows = padded.shape[1]
    gx, gy = lax.axis_index("gx"), lax.axis_index("gy")
    last_gx, last_gy = lax.axis_size("gx") - 1, lax.axis_size("gy") - 1
    z = lax.broadcasted_iota(jnp.int32, (rows, depth), 1)
    y = lax.broadcasted_iota(jnp.int32, (rows, depth), 0) - 8
    inside_y = ((y >= 0) | (gy > 0)) & ((y < cells_y) | (gy < last_gy))

    def operate(center, below, above):
        beside = below + above
        beside = beside + pltpu.roll(center, 1, 0) + pltpu.roll(center, rows - 1, 0)
        beside = beside + jnp.where(z == 0, 0.0, pltpu.roll(center, 1, 1))
        beside = beside + jnp.where(z == depth - 1, 0.0, pltpu.roll(center, depth - 1, 1))
        return (shift_kappa + 6.0) * center - beside

    def fill(plane, source):
        padded[plane, 8 : 8 + cells_y, :] = source
        padded[plane, 0:8, :] = jnp.zeros((8, depth), jnp.float32)
        padded[plane, 8 + cells_y :, :] = jnp.zeros((8, depth), jnp.float32)
        for h in range(2):
            padded[plane, 6 + h : 7 + h, :] = ylo_ref[h, pl.ds(plane, 1), :]
            padded[plane, 8 + cells_y + h : 9 + cells_y + h, :] = yhi_ref[h, pl.ds(plane, 1), :]

    for h in range(2):
        fill(h, xlo_ref[h])
        fill(cells_x + 2 + h, xhi_ref[h])

    def fill_own(x, carry):
        fill(x + 2, field_ref[x])
        return carry

    lax.fori_loop(0, cells_x, fill_own, 0)

    def smooth_plane(plane, carry):
        value = operate(padded[plane], padded[plane - 1], padded[plane + 1])
        inside = ((plane > 1) | (gx > 0)) & ((plane < cells_x + 2) | (gx < last_gx))
        smooth[plane - 1] = jnp.where(inside_y & inside, value, 0.0)
        return carry

    lax.fori_loop(1, cells_x + 3, smooth_plane, 0)

    def out_plane(x, carry):
        prior = operate(smooth[x + 1], smooth[x], smooth[x + 2])
        out_ref[x] = field_ref[x] - (step_rate * prior_weight) * prior[8 : 8 + cells_y]
        return carry

    lax.fori_loop(0, cells_x, out_plane, 0)


def finish_kernel(
    incoming_ref,
    match_ref,
    arrived_ref,
    field_hbm,
    base_hbm,
    out_hbm,
    collected,
    rows_ref,
    field_ref,
    base_ref,
    out_ref,
    in_sems,
    out_sems,
    *,
    capacity,
    blocks,
):
    cells_x, cells_y, depth = field_ref.shape
    sources = incoming_ref.shape[0]
    parts = out_sems.shape[0]
    planes = cells_x // parts
    loads = [
        pltpu.make_async_copy(field_hbm, field_ref, in_sems.at[0]),
        pltpu.make_async_copy(base_hbm, base_ref, in_sems.at[1]),
    ]
    for load in loads:
        load.start()

    def clear(i, carry):
        collected[pl.ds(pl.multiple_of(i * LANES, LANES), LANES), :] = jnp.zeros(
            (LANES, LANES), jnp.float32
        )
        return carry

    lax.fori_loop(0, blocks // LANES, clear, 0)

    def merge(i, carry):
        span = pl.ds(pl.multiple_of(i * LANES, LANES), LANES)
        rows_ref[span, :] = jnp.dot(
            match_ref[span, :], arrived_ref[span, :], preferred_element_type=jnp.float32
        )
        return carry

    lax.fori_loop(0, rows_ref.shape[0] // LANES, merge, 0)

    def one_source(source, carry):
        def one_group(group, carry):
            first = pl.multiple_of(group * GROUP, GROUP)
            places = [
                pl.ds(jnp.minimum(incoming_ref[source, first + j], blocks), 1)
                for j in range(GROUP)
            ]
            start = source * capacity + first
            sums = [
                collected[places[j], :] + rows_ref[pl.ds(start + j, 1), :] for j in range(GROUP)
            ]
            for j in range(GROUP):
                collected[places[j], :] = sums[j]
            return carry

        return lax.fori_loop(
            0, filled_groups(incoming_ref, source, capacity, blocks), one_group, carry
        )

    lax.fori_loop(0, sources, one_source, 0)
    for load in loads:
        load.wait()
    per_column = depth // LANES

    def store(part):
        span = pl.ds(part * planes, planes)
        return pltpu.make_async_copy(out_ref.at[span], out_hbm.at[span], out_sems.at[part])

    def one_plane(x, carry):
        for yb in range(cells_y // 8):
            for part in range(per_column):
                at = ((x * (cells_y // 8) + yb) * per_column + part) * 8
                grad = collected[pl.ds(pl.multiple_of(at, 8), 8), :]
                where = (x, slice(8 * yb, 8 * yb + 8), slice(part * LANES, (part + 1) * LANES))
                out_ref[where] = base_ref[where] - step_rate * (grad * jnp.exp(field_ref[where]))
        return carry

    for part in range(parts):
        lax.fori_loop(part * planes, (part + 1) * planes, one_plane, 0)
        store(part).start()
    for part in range(parts):
        store(part).wait()


def halo(field):
    def both_ways(first, last, axis):
        peers = lax.axis_size(axis)
        up = [(i, i + 1) for i in range(peers - 1)]
        down = [(j, i) for i, j in up]
        return lax.ppermute(last, axis, up), lax.ppermute(first, axis, down)

    xlo, xhi = both_ways(field[:2], field[-2:], "gx")

    def rows(at):
        return jnp.concatenate([xlo[:, at], field[:, at], xhi[:, at]], axis=0).transpose(1, 0, 2)

    ylo, yhi = both_ways(rows(slice(0, 2)), rows(slice(-2, None)), "gy")
    return xlo, xhi, ylo, yhi


VMEM = pl.BlockSpec(memory_space=pltpu.VMEM)
SMEM = pl.BlockSpec(memory_space=pltpu.SMEM)
ANY = pl.BlockSpec(memory_space=pl.ANY)


def on_device(log_density, weights, observed, inverse_var, star_counts, block_ids):
    cells_x, cells_y, depth = log_density.shape
    blocks_dev, slots, stars, width = weights.shape
    devices = lax.axis_size("gx") * lax.axis_size("gy")
    requests = blocks_dev * slots
    capacity = 2 * requests // devices
    all_slots = devices * capacity
    per_column = depth // width
    blocks = cells_x * cells_y * per_column
    cells = log_density.size
    mesh_axes = ("gx", "gy")
    f32, bf16, i32 = jnp.float32, jnp.bfloat16, jnp.int32
    shape = jax.ShapeDtypeStruct

    def exchange(x):
        return lax.all_to_all(x, mesh_axes, split_axis=0, concat_axis=0, tiled=True)

    outgoing, position = pl.pallas_call(
        functools.partial(
            route_kernel,
            devices=devices,
            capacity=capacity,
            blocks=blocks,
            per_column=per_column,
        ),
        out_shape=[shape((devices, capacity), i32), shape((requests // LANES, LANES), i32)],
        in_specs=[VMEM],
        out_specs=[VMEM, VMEM],
        name="route",
    )(block_ids.reshape(requests // LANES, LANES))
    incoming = exchange(outgoing)

    table = (
        log_density.reshape(cells_x, cells_y // 8, 8, per_column, width)
        .transpose(0, 1, 3, 2, 4)
        .reshape(blocks, width)
    )
    served = pl.pallas_call(
        functools.partial(serve_kernel, capacity=capacity, blocks=blocks),
        out_shape=shape((all_slots, width), bf16),
        in_specs=[SMEM, VMEM],
        out_specs=VMEM,
        scratch_shapes=[pltpu.VMEM((all_slots, width), f32)],
        compiler_params=pltpu.CompilerParams(vmem_limit_bytes=16 * MIB),
        cost_estimate=pl.CostEstimate(flops=0, bytes_accessed=5 * MIB, transcendentals=0),
        name="serve",
    )(incoming, table)
    returned = exchange(served.reshape(devices, capacity, width)).reshape(all_slots, width)

    field, incoming_late, _ = lax.optimization_barrier((log_density, incoming, served))
    match = pl.pallas_call(
        match_kernel,
        out_shape=shape((all_slots, LANES), bf16),
        in_specs=[VMEM],
        out_specs=VMEM,
        compiler_params=pltpu.CompilerParams(vmem_limit_bytes=8 * MIB),
        cost_estimate=pl.CostEstimate(flops=10**9, bytes_accessed=MIB, transcendentals=0),
        name="match",
    )(incoming_late.reshape(all_slots // LANES, LANES))
    xlo, xhi, ylo, yhi = halo(field)
    base = pl.pallas_call(
        prior_kernel,
        out_shape=shape((cells_x, cells_y, depth), f32),
        in_specs=[VMEM] * 5,
        out_specs=VMEM,
        scratch_shapes=[
            pltpu.VMEM((cells_x + 4, cells_y + 16, depth), f32),
            pltpu.VMEM((cells_x + 2, cells_y + 16, depth), f32),
        ],
        compiler_params=pltpu.CompilerParams(vmem_limit_bytes=32 * MIB),
        cost_estimate=pl.CostEstimate(
            flops=30 * cells, bytes_accessed=8 * cells, transcendentals=0
        ),
        name="prior",
    )(field, xlo, xhi, ylo, yhi)

    chunks = blocks_dev * stars // LANES
    live = jnp.arange(stars)[None, :] < star_counts[:, None]
    live_inverse = jnp.where(live, inverse_var, 0.0).reshape(chunks, LANES)
    extinction, parcel = pl.pallas_call(
        star_kernel,
        out_shape=[shape((chunks, LANES), f32), shape((all_slots, width), bf16)],
        in_specs=[SMEM, VMEM, VMEM, VMEM, ANY],
        out_specs=[VMEM, VMEM],
        scratch_shapes=[
            pltpu.VMEM(weights.shape, bf16),
            pltpu.VMEM((all_slots, width), f32),
            pltpu.VMEM((all_slots, width), f32),
            pltpu.SemaphoreType.DMA((chunks,)),
        ],
        compiler_params=pltpu.CompilerParams(vmem_limit_bytes=32 * MIB),
        cost_estimate=pl.CostEstimate(
            flops=4 * weights.size, bytes_accessed=2 * weights.size, transcendentals=0
        ),
        name="stars",
    )(position, returned, observed.reshape(chunks, LANES), live_inverse, weights)
    arrived = exchange(parcel.reshape(devices, capacity, width)).reshape(all_slots, width)

    parts = 8
    new_log_density = pl.pallas_call(
        functools.partial(finish_kernel, capacity=capacity, blocks=blocks),
        out_shape=shape((cells_x, cells_y, depth), f32),
        in_specs=[SMEM, VMEM, VMEM, ANY, ANY],
        out_specs=ANY,
        scratch_shapes=[
            pltpu.VMEM((blocks + 8, width), f32),
            pltpu.VMEM((all_slots, width), f32),
            pltpu.VMEM((cells_x, cells_y, depth), f32),
            pltpu.VMEM((cells_x, cells_y, depth), f32),
            pltpu.VMEM((cells_x, cells_y, depth), f32),
            pltpu.SemaphoreType.DMA((2,)),
            pltpu.SemaphoreType.DMA((parts,)),
        ],
        compiler_params=pltpu.CompilerParams(vmem_limit_bytes=32 * MIB),
        cost_estimate=pl.CostEstimate(
            flops=4 * cells, bytes_accessed=12 * cells, transcendentals=cells
        ),
        name="finish",
    )(incoming, match, arrived, log_density, base)
    return new_log_density, extinction.reshape(blocks_dev, stars)


def solution(mesh):
    placed = (
        P("gx", "gy", None),
        P(("gx", "gy"), None, None, None),
        P(("gx", "gy"), None),
        P(("gx", "gy"), None),
        P(("gx", "gy")),
        P(("gx", "gy"), None),
    )
    return jax.shard_map(
        on_device,
        mesh=mesh,
        in_specs=placed,
        out_specs=(P("gx", "gy", None), P(("gx", "gy"), None)),
        check_vma=False,
    )
```

time: 242 us -> 148 us (0.61)
  other arithmetic: 64.1 us -> 0.06 us
  Pallas kernels: 0 us -> 58.5 us
  local copies, waits for them, and re-layouts: 61.8 us -> 21.9 us
  starting transfers between devices: 40 us -> 17.2 us
  waiting for transfers between devices: 57.5 us -> 35.4 us
  matrix products: 16.3 us -> 0 us
  blocking collectives: 0 us -> 13.7 us
    pallas_call x0 -> x6, Pallas kernels: none -> 58.5 us  [the longest x1 17 us: on_device(): pl.pallas_call(functools.partial(finish_kernel, capacity=capacity, blocks...]
    scatter-add x1 -> x0, other arithmetic: 24.6 us -> none  [on_device(): jnp.zeros((local_blocks, width), jnp.float32).at[slot_target]]
    gather x2 -> x0, local copies, waits for them, and re-layouts: 18.3 us -> none  [the longest x1 12.1 us: on_device(): table[jnp.maximum(incoming, 0)]]
    sub x2 -> x0, other arithmetic: 17.8 us -> none  [the longest x1 17.8 us: on_device(): log_density - step_rate * (data_grad + prior_weight * prior_grad)]
    dot_general x2 -> x0, matrix products: 16.3 us -> none  [the longest x1 8.21 us: on_device(): jnp.einsum('bksv,bkv->bs', weights, fetched, preferred_element_type=jnp.f...]
    scatter x2 -> x0, local copies, waits for them, and re-layouts: 15.6 us -> none  [the longest x1 8.62 us: on_device(): jnp.full((devices * capacity,), -1, jnp.int32).at[position].set(within)]
    slice x10 -> x4, local copies, waits for them, and re-layouts: 15.3 us -> 0.27 us  [the longest x1 0.25 us: halo(): xlo, xhi = both_ways(field[:2], field[-2:], 'gx')]
    all_to_all x0 -> x1, blocking collectives: none -> 13.7 us  [exchange(): return lax.all_to_all(x, mesh_axes, split_axis=0, concat_axis=0, tiled=True)]
  transfers between devices with their start and end apart: 11 -> 6, of which waited for: 6 -> 3; matrix products, arithmetic and copies ran while one was open for 16% -> 4% of each run, Pallas kernels for 0% -> 11%
where the time goes in v1:
time: 148 us
  Pallas kernels  58.5 us (40%)
  waiting for transfers between devices  35.4 us (24%)
  local copies, waits for them, and re-layouts  21.9 us (15%)
  starting transfers between devices  17.2 us (12%)
  blocking collectives  13.7 us (9%)
    all_to_all x2, waiting for transfers between devices, exchange(): return lax.all_to_all(x, mesh_axes, split_axis=0, concat_axis=0, tiled=True)  26.1 us
    pallas_call x1, Pallas kernels, on_device(): pl.pallas_call(functools.partial(finish_kernel, capacity=capacity, blocks...  17 us
    unnamed x23, local copies, waits for them, and re-layouts  15.9 us
    all_to_all x1, blocking collectives, exchange(): return lax.all_to_all(x, mesh_axes, split_axis=0, concat_axis=0, tiled=True)  13.7 us
    pallas_call x1, Pallas kernels, on_device(): pl.pallas_call(star_kernel, out_shape=[shape((chunks, LANES), f32), shape...  13.1 us
    ppermute x4, starting transfers between devices, both_ways(): return (lax.ppermute(last, axis, up), lax.ppermute(first, axis, down))  11.4 us
    pallas_call x1, Pallas kernels, on_device(): pl.pallas_call(prior_kernel, out_shape=shape((cells_x, cells_y, depth), f...  10.7 us
    pallas_call x1, Pallas kernels, on_device(): pl.pallas_call(functools.partial(serve_kernel, capacity=capacity, blocks=...  9.8 us
  transfers between devices with their start and end apart: 6, of which 3 were waited for; matrix products, arithmetic and copies ran while one was open for 4% of the time, Pallas kernels for 11%

profile of v1, /device:TPU:1, one launch (start us, length us, event | category | flops | bytes accessed | tf_op | source)
XLA Modules:
  0.0 147.6 jit_solution(15368144921363108529)
XLA Ops:
  0.7 0.8 copy.28
  1.5 0.7 reshape.37.ids_ref
  2.2 3.0 %route.1 = (s32[32,128]{1,0:T(8,128)}, s32[16,128]{1,0:T(8,128)}) custom-call(s32[16,128]{1,0:T(8,128)} %reshape.37.ids_ref), custom_call_target="tpu_custom_call" | custom-call | tf_op jit(solution)/shard_map/route/pallas_call | solution.py:372
  5.2 13.7 %all_to_all.21 = s32[32,1,128]{2,1,0:T(1,128)S(1)} all-to-all(s32[32,1,128]{2,1,0:T(1,128)} %bitcast.23), channel_id=1, replica_groups=mesh['gx'=8,'gy'=4] {'gx','gy'}, dimensions={0} | all-to-all | bytes 32768 | tf_op jit(solution)/shard_map/all_to_all | solution.py:370
  18.9 2.2 %copy-done = f32[32,64,512]{2,1,0:T(8,128)S(1)} copy-done((f32[32,64,512]{2,1,0:T(8,128)S(1)}, f32[32,64,512]{2,1,0:T(8,128)}, u32[]{:S(2)}) %copy-start) | copy-done | bytes 4194328
  21.1 9.8 %serve.1 = bf16[4096,128]{1,0:T(8,128)(2,1)} custom-call(s32[32,128]{1,0:T(8,128)S(1)} %bitcast.20, f32[8192,128]{1,0:T(8,128)S(1)} %bitcast.17), custom_call_target="tpu_custom_call" | custom-call | bytes 5242880 | tf_op jit(solution)/shard_map/serve/pallas_call | solution.py:392
  30.9 2.7 %all-to-all-start.1 = ((bf16[32,128,128]{2,1,0:T(8,128)(2,1)}), bf16[32,128,128]{2,1,0:T(8,128)(2,1)S(1)}, u32[]{:S(2)}, u32[]{:S(2)}) async-start(bf16[32,128,128]{2,1,0:T(8,128)(2,1)} %bitcast.6), calls=%async_computation.1 | async-start | bytes 2097152 | tf_op jit(solution)/shard_map/all_to_all | solution.py:370
  33.6 0.1 copy.31
  33.7 0.1 reshape.43.inverse_ref
  33.8 0.1 copy.30
  33.9 0.1 reshape.42.observed_ref
  33.9 26.1 %all-to-all-done.1 = bf16[32,128,128]{2,1,0:T(8,128)(2,1)S(1)} async-done(((bf16[32,128,128]{2,1,0:T(8,128)(2,1)}), bf16[32,128,128]{2,1,0:T(8,128)(2,1)S(1)}, u32[]{:S(2)}, u32[]{:S(2)}) %all-to-all-start.1) | async-done | bytes 1048608 | tf_op jit(solution)/shard_map/all_to_all | solution.py:370
  60.1 5.8 %copy-done.3 = bf16[64,32,32,128]{3,2,1,0:T(8,128)(2,1)S(1)} copy-done((bf16[64,32,32,128]{3,2,1,0:T(8,128)(2,1)S(1)}, bf16[64,32,32,128]{3,2,1,0:T(8,128)(2,1)}, u32[]{:S(2)}) %copy-start.3) | copy-done | bytes 16777240
  65.9 13.1 %stars.1 = (f32[16,128]{1,0:T(8,128)S(1)}, bf16[4096,128]{1,0:T(8,128)(2,1)}) custom-call(s32[16,128]{1,0:T(8,128)S(1)} %copy-done.6, bf16[4096,128]{1,0:T(8,128)(2,1)S(1)} %bitcast.19, f32[16,128]{1,0:T(8,128)S(1)} %reshape.42.observed_ref, f32[16,128]{1,0:T(8,128)S(1)} %reshape.43.inverse_ref, bf16[64,32,32,128]{3,2,1,0:T(8,128)(2,1)S(1)} %copy-done.3), custom_call_target="tpu_custom_call" | custom-call | flops 33554432 | bytes 16777216 | tf_op jit(solution)/shard_map/stars/pallas_call | solution.py:434
  78.9 3.1 %all-to-all-start.2 = ((bf16[32,128,128]{2,1,0:T(8,128)(2,1)}), bf16[32,128,128]{2,1,0:T(8,128)(2,1)S(1)}, u32[]{:S(2)}, u32[]{:S(2)}) async-start(bf16[32,128,128]{2,1,0:T(8,128)(2,1)} %bitcast.8), calls=%async_computation.2 | async-start | bytes 2097152 | tf_op jit(solution)/shard_map/all_to_all | solution.py:370
  82.0 4.6 %copy.32 = f32[32,64,512]{2,0,1:T(8,128)S(1)} copy(f32[32,64,512]{2,1,0:T(8,128)} %field_hbm.1) | data formatting | bytes 8388608 | tf_op jit(solution)/shard_map/optimization_barrier | solution.py:404
  86.6 0.2 fusion.2
  86.9 3.8 %collective-permute-start = (f32[2,64,512]{2,0,1:T(2,128)S(1)}, f32[2,64,512]{2,0,1:T(2,128)S(1)}, u32[]{:S(2)}, u32[]{:S(2)}) collective-permute-start(f32[2,64,512]{2,0,1:T(2,128)S(1)} %get-tuple-element.23), channel_id=1, source_target_pairs={{0,4},{4,8},{8,12},{12,16},{16,20},{20,24},{24,28},{1,5},{5,9},{9,... | collective-permute-start | bytes 786440 | tf_op jit(solution)/shard_map/ppermute | solution.py:339
  90.7 1.9 %collective-permute-start.1 = (f32[2,64,512]{2,0,1:T(2,128)S(1)}, f32[2,64,512]{2,0,1:T(2,128)S(1)}, u32[]{:S(2)}, u32[]{:S(2)}) collective-permute-start(f32[2,64,512]{2,0,1:T(2,128)S(1)} %get-tuple-element.22), channel_id=1, source_target_pairs={{4,0},{8,4},{12,8},{16,12},{20,16},{24,20},{28,24},{5,1},{9,5},{13... | collective-permute-start | bytes 786440 | tf_op jit(solution)/shard_map/ppermute | solution.py:339
  92.7 3.2 %collective-permute-done = f32[2,64,512]{2,0,1:T(2,128)S(1)} collective-permute-done((f32[2,64,512]{2,0,1:T(2,128)S(1)}, f32[2,64,512]{2,0,1:T(2,128)S(1)}, u32[]{:S(2)}, u32[]{:S(2)}) %collective-permute-start) | collective-permute-done | bytes 262176 | tf_op jit(solution)/shard_map/ppermute | solution.py:339
  95.9 6.1 %collective-permute-done.1 = f32[2,64,512]{2,0,1:T(2,128)S(1)} collective-permute-done((f32[2,64,512]{2,0,1:T(2,128)S(1)}, f32[2,64,512]{2,0,1:T(2,128)S(1)}, u32[]{:S(2)}, u32[]{:S(2)}) %collective-permute-start.1) | collective-permute-done | bytes 262176 | tf_op jit(solution)/shard_map/ppermute | solution.py:339
  102.0 1.3 collective-permute-start.3
  103.3 4.4 %collective-permute-start.2 = (f32[2,36,512]{2,1,0:T(8,128)S(1)}, f32[2,36,512]{2,1,0:T(8,128)S(1)}, u32[]{:S(2)}, u32[]{:S(2)}) collective-permute-start(f32[2,36,512]{2,1,0:T(8,128)S(1)} %maximum_bitcast_fusion), channel_id=1, source_target_pairs={{0,1},{1,2},{2,3},{4,5},{5,6},{6,7},{8,9},{9,10},{10,11},{12,13},{... | collective-permute-start | bytes 442376 | tf_op jit(solution)/shard_map/ppermute | solution.py:339
  107.7 4.9 %match.1.match_ref = bf16[4096,128]{1,0:T(8,128)(2,1)S(1)} custom-call(s32[32,128]{1,0:T(8,128)S(1)} %bitcast.21), custom_call_target="tpu_custom_call" | custom-call | flops 1000000000 | bytes 1048576 | tf_op jit(solution)/shard_map/match/pallas_call | solution.py:405
  112.6 0.1 copy.36.xlo_ref
  112.7 10.7 %prior.1.base_hbm = f32[32,64,512]{2,1,0:T(8,128)S(1)} custom-call(f32[32,64,512]{2,1,0:T(8,128)S(1)} %copy-done.1, f32[2,64,512]{2,1,0:T(8,128)S(1)} %copy.36.xlo_ref, f32[2,64,512]{2,1,0:T(8,128)S(1)} %copy.37.xhi_ref, f32[2,36,512]{2,1,0:T(8,128)S(1)} %collective-permute-done.2.ylo_ref, f32[2,36,512]{2,1,0:T(8,128)S(1)} %collective-permute-done.3.yhi_ref), custom_call_target="tpu_custom_call" | custom-call | flops 31457280 | bytes 8388608 | tf_op jit(solution)/shard_map/prior/pallas_call | solution.py:415
  123.5 2.0 %copy-done.4 = f32[32,64,512]{2,1,0:T(8,128)} copy-done((f32[32,64,512]{2,1,0:T(8,128)}, f32[32,64,512]{2,1,0:T(8,128)S(1)}, u32[]{:S(2)}) %copy-start.4) | copy-done | bytes 4194328
  125.5 0.1 reshape.46
  125.6 0.7 copy.38
  126.3 2.2 %copy-done.2 = f32[32,64,512]{2,1,0:T(8,128)S(1)} copy-done((f32[32,64,512]{2,1,0:T(8,128)S(1)}, f32[32,64,512]{2,1,0:T(8,128)}, u32[]{:S(2)}) %copy-start.2) | copy-done | bytes 4194328
  128.5 2.2 %copy-done.5 = f32[32,64,512]{2,1,0:T(8,128)S(1)} copy-done((f32[32,64,512]{2,1,0:T(8,128)S(1)}, f32[32,64,512]{2,1,0:T(8,128)}, u32[]{:S(2)}) %copy-start.5) | copy-done | bytes 4194328
  130.6 17.0 %finish.1 = f32[32,64,512]{2,1,0:T(8,128)} custom-call(s32[32,128]{1,0:T(8,128)S(1)} %bitcast.22, bf16[4096,128]{1,0:T(8,128)(2,1)S(1)} %match.1.match_ref, bf16[4096,128]{1,0:T(8,128)(2,1)S(1)} %bitcast.18, f32[32,64,512]{2,1,0:T(8,128)S(1)} %copy-done.2, f32[32,64,512]{2,1,0:T(8,128)S(1)} %copy-done.5), custom_call_target="tpu_custom_call" | custom-call | flops 4194304 | bytes 12582912 | tf_op jit(solution)/shard_map/finish/pallas_call | solution.py:454
  (25 shorter events, 0.2 us)
Async XLA Ops:
  0.6 33.0 %copy-start.9 = (s32[64]{0:T(128)S(1)}, s32[64]{0:T(128)}, u32[]{:S(2)}) copy-start(s32[64]{0:T(128)} %param.10) | copy-start | bytes 772
  0.6 33.0 %copy-start.8 = (f32[64,32]{0,1:T(8,128)S(1)}, f32[64,32]{0,1:T(8,128)}, u32[]{:S(2)}) copy-start(f32[64,32]{0,1:T(8,128)} %param.9) | copy-start | bytes 24580
  0.7 33.1 %copy-start.7 = (f32[64,32]{0,1:T(8,128)S(1)}, f32[64,32]{0,1:T(8,128)}, u32[]{:S(2)}) copy-start(f32[64,32]{0,1:T(8,128)} %param.8) | copy-start | bytes 24580
  5.2 54.9 %copy-start.6 = (s32[16,128]{1,0:T(8,128)S(1)}, s32[16,128]{1,0:T(8,128)}, u32[]{:S(2)}) copy-start(s32[16,128]{1,0:T(8,128)} %get-tuple-element.10.position_ref) | copy-start | bytes 24580
  18.9 2.2 %copy-start = (f32[32,64,512]{2,1,0:T(8,128)S(1)}, f32[32,64,512]{2,1,0:T(8,128)}, u32[]{:S(2)}) copy-start(f32[32,64,512]{2,1,0:T(8,128)} %field_hbm.1) | copy-start | bytes 12582916
  30.9 29.2 %all-to-all-start.1 = ((bf16[32,128,128]{2,1,0:T(8,128)(2,1)}), bf16[32,128,128]{2,1,0:T(8,128)(2,1)S(1)}, u32[]{:S(2)}, u32[]{:S(2)}) async-start(bf16[32,128,128]{2,1,0:T(8,128)(2,1)} %bitcast.6), calls=%async_computation.1 | async-start | bytes 2097152 | tf_op jit(solution)/shard_map/all_to_all | solution.py:370
  60.1 5.8 %copy-start.3 = (bf16[64,32,32,128]{3,2,1,0:T(8,128)(2,1)S(1)}, bf16[64,32,32,128]{3,2,1,0:T(8,128)(2,1)}, u32[]{:S(2)}) copy-start(bf16[64,32,32,128]{3,2,1,0:T(8,128)(2,1)} %weights_hbm.1) | copy-start | bytes 50331652
  78.9 47.3 %all-to-all-start.2 = ((bf16[32,128,128]{2,1,0:T(8,128)(2,1)}), bf16[32,128,128]{2,1,0:T(8,128)(2,1)S(1)}, u32[]{:S(2)}, u32[]{:S(2)}) async-start(bf16[32,128,128]{2,1,0:T(8,128)(2,1)} %bitcast.8), calls=%async_computation.2 | async-start | bytes 2097152 | tf_op jit(solution)/shard_map/all_to_all | solution.py:370
  86.6 26.1 %copy-start.1 = (f32[32,64,512]{2,1,0:T(8,128)S(1)}, f32[32,64,512]{2,1,0:T(8,128)}, u32[]{:S(2)}) copy-start(f32[32,64,512]{2,1,0:T(8,128)} %field_hbm.1) | copy-start | bytes 12582916
  86.9 9.0 %collective-permute-start = (f32[2,64,512]{2,0,1:T(2,128)S(1)}, f32[2,64,512]{2,0,1:T(2,128)S(1)}, u32[]{:S(2)}, u32[]{:S(2)}) collective-permute-start(f32[2,64,512]{2,0,1:T(2,128)S(1)} %get-tuple-element.23), channel_id=1, source_target_pairs={{0,4},{4,8},{8,12},{12,16},{16,20},{20,24},{24,28},{1,5},{5,9},{9,... | collective-permute-start | bytes 786440 | tf_op jit(solution)/shard_map/ppermute | solution.py:339
  90.7 11.3 %collective-permute-start.1 = (f32[2,64,512]{2,0,1:T(2,128)S(1)}, f32[2,64,512]{2,0,1:T(2,128)S(1)}, u32[]{:S(2)}, u32[]{:S(2)}) collective-permute-start(f32[2,64,512]{2,0,1:T(2,128)S(1)} %get-tuple-element.22), channel_id=1, source_target_pairs={{4,0},{8,4},{12,8},{16,12},{20,16},{24,20},{28,24},{5,1},{9,5},{13... | collective-permute-start | bytes 786440 | tf_op jit(solution)/shard_map/ppermute | solution.py:339
  102.0 10.7 %collective-permute-start.3 = (f32[2,36,512]{2,1,0:T(8,128)S(1)}, f32[2,36,512]{2,1,0:T(8,128)S(1)}, u32[]{:S(2)}, u32[]{:S(2)}) collective-permute-start(f32[2,36,512]{2,1,0:T(8,128)S(1)} %maximum_bitcast_fusion.1), channel_id=1, source_target_pairs={{1,0},{2,1},{3,2},{5,4},{6,5},{7,6},{9,8},{10,9},{11,10},{13,12},{... | collective-permute-start | bytes 442376 | tf_op jit(solution)/shard_map/ppermute | solution.py:339
  103.3 9.4 %collective-permute-start.2 = (f32[2,36,512]{2,1,0:T(8,128)S(1)}, f32[2,36,512]{2,1,0:T(8,128)S(1)}, u32[]{:S(2)}, u32[]{:S(2)}) collective-permute-start(f32[2,36,512]{2,1,0:T(8,128)S(1)} %maximum_bitcast_fusion), channel_id=1, source_target_pairs={{0,1},{1,2},{2,3},{4,5},{5,6},{6,7},{8,9},{9,10},{10,11},{12,13},{... | collective-permute-start | bytes 442376 | tf_op jit(solution)/shard_map/ppermute | solution.py:339
  123.5 2.0 %copy-start.4 = (f32[32,64,512]{2,1,0:T(8,128)}, f32[32,64,512]{2,1,0:T(8,128)S(1)}, u32[]{:S(2)}) copy-start(f32[32,64,512]{2,1,0:T(8,128)S(1)} %prior.1.base_hbm) | copy-start | bytes 12582916
  126.3 2.2 %copy-start.2 = (f32[32,64,512]{2,1,0:T(8,128)S(1)}, f32[32,64,512]{2,1,0:T(8,128)}, u32[]{:S(2)}) copy-start(f32[32,64,512]{2,1,0:T(8,128)} %field_hbm.1) | copy-start | bytes 12582916
  128.5 2.2 %copy-start.5 = (f32[32,64,512]{2,1,0:T(8,128)S(1)}, f32[32,64,512]{2,1,0:T(8,128)}, u32[]{:S(2)}) copy-start(f32[32,64,512]{2,1,0:T(8,128)} %copy-done.4) | copy-start | bytes 12582916

commit v2 on v1

--- a/solution.py
+++ b/solution.py
@@ -27,6 +27,8 @@
 
 
 def route_kernel(ids_ref, outgoing_ref, position_ref, *, devices, capacity, blocks, per_column):
+    half = ids_ref.shape[0] // 2
+    ids = jnp.concatenate([ids_ref[:half, :], ids_ref[half:, :]], axis=1)
     lane = lax.broadcasted_iota(jnp.int32, (LANES, LANES), 1)
     row = lax.broadcasted_iota(jnp.int32, (LANES, LANES), 0)
     upper = jnp.where(row <= lane, 1.0, 0.0).astype(jnp.bfloat16)
@@ -34,8 +36,8 @@
     slot_no = lax.broadcasted_iota(jnp.int32, (capacity, LANES), 0)
     before = jnp.zeros((devices, 1), jnp.float32)
     lists = jnp.zeros((2 * devices, capacity), jnp.float32)
-    for chunk in range(ids_ref.shape[0]):
-        target, local = split_by(ids_ref[chunk : chunk + 1, :], blocks)
+    for chunk in range(half):
+        target, local = split_by(ids[chunk : chunk + 1, :], blocks)
         column, part = split_by(local, per_column)
         local = ((column >> 3) * per_column + part) * 8 + (column & 7)
         hit = tile_no == target
@@ -61,6 +63,29 @@
     outgoing_ref[...] = jnp.where(high > 0.5, wanted, blocks + before.astype(jnp.int32))
 
 
+def table_kernel(field_ref, table_ref, xfirst_ref, xlast_ref, yfirst_ref, ylast_ref):
+    cells_x, cells_y, depth = field_ref.shape
+    per_column = depth // LANES
+    xfirst_ref[...] = field_ref[:2]
+    xlast_ref[...] = field_ref[cells_x - 2 :]
+
+    def one_plane(x, carry):
+        for yb in range(cells_y // 8):
+            for part in range(per_column):
+                at = pl.multiple_of(((x * (cells_y // 8) + yb) * per_column + part) * 8, 8)
+                table_ref[pl.ds(at, 8), :] = jnp.exp(
+                    field_ref[x, 8 * yb : 8 * yb + 8, part * LANES : (part + 1) * LANES]
+                )
+        for h in range(2):
+            yfirst_ref[h, pl.ds(x, 1), :] = field_ref[x, h : h + 1, :]
+            ylast_ref[h, pl.ds(x, 1), :] = field_ref[x, cells_y - 2 + h : cells_y - 1 + h, :]
+        return carry
+
+    lax.fori_loop(0, cells_x, one_plane, 0)
+    pad = table_ref.shape[0] - cells_x * cells_y * per_column
+    table_ref[cells_x * cells_y * per_column :, :] = jnp.zeros((pad, LANES), jnp.float32)
+
+
 def filled_groups(incoming_ref, source, capacity, blocks):
     last = incoming_ref[source, capacity - 1]
     filled = jnp.where(last < blocks, capacity, last - blocks)
@@ -68,24 +93,23 @@
 
 
 def serve_kernel(incoming_ref, table_ref, served_ref, rows_ref, *, capacity, blocks):
-    sources = incoming_ref.shape[0]
-
     def one_source(source, carry):
-        base = pl.multiple_of(source * capacity, capacity)
-
         def one_group(group, carry):
             first = pl.multiple_of(group * GROUP, GROUP)
+            rows = [
+                table_ref[pl.ds(incoming_ref[source, first + j], 1), :] for j in range(GROUP)
+            ]
+            start = source * capacity + first
             for j in range(GROUP):
-                at = jnp.minimum(incoming_ref[source, first + j], blocks - 1)
-                rows_ref[pl.ds(base + first + j, 1), :] = table_ref[pl.ds(at, 1), :]
+                rows_ref[pl.ds(start + j, 1), :] = rows[j]
             return carry
 
-        lax.fori_loop(0, filled_groups(incoming_ref, source, capacity, blocks), one_group, 0)
-        span = pl.ds(base, capacity)
-        served_ref[span, :] = jnp.exp(rows_ref[span, :]).astype(jnp.bfloat16)
-        return carry
-
-    lax.fori_loop(0, sources, one_source, 0)
+        return lax.fori_loop(
+            0, filled_groups(incoming_ref, source, capacity, blocks), one_group, carry
+        )
+
+    lax.fori_loop(0, incoming_ref.shape[0], one_source, 0)
+    served_ref[...] = rows_ref[...].astype(jnp.bfloat16)
 
 
 def match_kernel(incoming_ref, match_ref):
@@ -125,6 +149,10 @@
     blocks_dev, slots, stars, width = weights_ref.shape
     chunks = extinction_ref.shape[0]
     per = blocks_dev // chunks
+    half = position_ref.shape[0]
+
+    def place(block, slot):
+        return position_ref[slot % half, (slot // half) * blocks_dev + block]
 
     def load(chunk):
         span = pl.ds(chunk * per, per)
@@ -143,7 +171,7 @@
         for b in range(per):
             total = jnp.zeros((stars, width), jnp.float32)
             for k in range(slots):
-                at = position_ref[chunk, b * slots + k]
+                at = place(chunk * per + b, k)
                 total = total + weights_ref[chunk * per + b, k].astype(jnp.float32) * fetched_ref[
                     pl.ds(at, 1), :
                 ]
@@ -174,7 +202,7 @@
                 right = weights_ref[chunk * per + b, 8 * j : 8 * j + 8].reshape(8 * stars, width)
                 sens = jnp.dot(left, right, preferred_element_type=jnp.float32)
                 for r in range(8):
-                    at = position_ref[chunk, b * slots + 8 * j + r]
+                    at = place(chunk * per + b, 8 * j + r)
                     sens_ref[pl.ds(at, 1), :] = sens[r : r + 1, :]
 
     load(0).wait()
@@ -245,105 +273,70 @@
     incoming_ref,
     match_ref,
     arrived_ref,
-    field_hbm,
+    table_hbm,
     base_hbm,
     out_hbm,
-    collected,
     rows_ref,
-    field_ref,
-    base_ref,
+    table_ref,
     out_ref,
-    in_sems,
-    out_sems,
+    sems,
     *,
     capacity,
     blocks,
 ):
-    cells_x, cells_y, depth = field_ref.shape
-    sources = incoming_ref.shape[0]
-    parts = out_sems.shape[0]
-    planes = cells_x // parts
+    own = pl.ds(0, blocks)
     loads = [
-        pltpu.make_async_copy(field_hbm, field_ref, in_sems.at[0]),
-        pltpu.make_async_copy(base_hbm, base_ref, in_sems.at[1]),
+        pltpu.make_async_copy(table_hbm, table_ref, sems.at[0]),
+        pltpu.make_async_copy(base_hbm, out_ref.at[own], sems.at[1]),
     ]
     for load in loads:
         load.start()
-
-    def clear(i, carry):
-        collected[pl.ds(pl.multiple_of(i * LANES, LANES), LANES), :] = jnp.zeros(
-            (LANES, LANES), jnp.float32
-        )
-        return carry
-
-    lax.fori_loop(0, blocks // LANES, clear, 0)
-
-    def merge(i, carry):
-        span = pl.ds(pl.multiple_of(i * LANES, LANES), LANES)
-        rows_ref[span, :] = jnp.dot(
+    for i in range(rows_ref.shape[0] // LANES):
+        span = slice(i * LANES, (i + 1) * LANES)
+        rows_ref[span, :] = -step_rate * jnp.dot(
             match_ref[span, :], arrived_ref[span, :], preferred_element_type=jnp.float32
         )
-        return carry
-
-    lax.fori_loop(0, rows_ref.shape[0] // LANES, merge, 0)
+    for load in loads:
+        load.wait()
 
     def one_source(source, carry):
         def one_group(group, carry):
             first = pl.multiple_of(group * GROUP, GROUP)
-            places = [
-                pl.ds(jnp.minimum(incoming_ref[source, first + j], blocks), 1)
+            places = [pl.ds(incoming_ref[source, first + j], 1) for j in range(GROUP)]
+            start = source * capacity + first
+            sums = [
+                out_ref[places[j], :] + table_ref[places[j], :] * rows_ref[pl.ds(start + j, 1), :]
                 for j in range(GROUP)
             ]
-            start = source * capacity + first
-            sums = [
-                collected[places[j], :] + rows_ref[pl.ds(start + j, 1), :] for j in range(GROUP)
-            ]
             for j in range(GROUP):
-                collected[places[j], :] = sums[j]
+                out_ref[places[j], :] = sums[j]
             return carry
 
         return lax.fori_loop(
             0, filled_groups(incoming_ref, source, capacity, blocks), one_group, carry
         )
 
-    lax.fori_loop(0, sources, one_source, 0)
-    for load in loads:
-        load.wait()
-    per_column = depth // LANES
-
-    def store(part):
-        span = pl.ds(part * planes, planes)
-        return pltpu.make_async_copy(out_ref.at[span], out_hbm.at[span], out_sems.at[part])
-
-    def one_plane(x, carry):
-        for yb in range(cells_y // 8):
-            for part in range(per_column):
-                at = ((x * (cells_y // 8) + yb) * per_column + part) * 8
-                grad = collected[pl.ds(pl.multiple_of(at, 8), 8), :]
-                where = (x, slice(8 * yb, 8 * yb + 8), slice(part * LANES, (part + 1) * LANES))
-                out_ref[where] = base_ref[where] - step_rate * (grad * jnp.exp(field_ref[where]))
-        return carry
-
-    for part in range(parts):
-        lax.fori_loop(part * planes, (part + 1) * planes, one_plane, 0)
-        store(part).start()
-    for part in range(parts):
-        store(part).wait()
-
-
-def halo(field):
+    lax.fori_loop(0, incoming_ref.shape[0], one_source, 0)
+    store = pltpu.make_async_copy(out_ref.at[own], out_hbm, sems.at[2])
+    store.start()
+    store.wait()
+
+
+def halo(xfirst, xlast, yfirst, ylast):
     def both_ways(first, last, axis):
         peers = lax.axis_size(axis)
         up = [(i, i + 1) for i in range(peers - 1)]
         down = [(j, i) for i, j in up]
         return lax.ppermute(last, axis, up), lax.ppermute(first, axis, down)
 
-    xlo, xhi = both_ways(field[:2], field[-2:], "gx")
-
-    def rows(at):
-        return jnp.concatenate([xlo[:, at], field[:, at], xhi[:, at]], axis=0).transpose(1, 0, 2)
-
-    ylo, yhi = both_ways(rows(slice(0, 2)), rows(slice(-2, None)), "gy")
+    xlo, xhi = both_ways(xfirst, xlast, "gx")
+
+    def rows(own, at):
+        return jnp.concatenate(
+            [xlo[:, at].transpose(1, 0, 2), own, xhi[:, at].transpose(1, 0, 2)], axis=1
+        )
+
+    ylo, yhi = both_ways(rows(yfirst, slice(0, 2)), rows(ylast, slice(-2, None)), "gy")
     return xlo, xhi, ylo, yhi
 
 
@@ -366,6 +359,14 @@
     f32, bf16, i32 = jnp.float32, jnp.bfloat16, jnp.int32
     shape = jax.ShapeDtypeStruct
 
+    def to_rows(x):
+        x = x.reshape(cells_x, cells_y // 8, 8, per_column, width)
+        return x.transpose(0, 1, 3, 2, 4).reshape(blocks, width)
+
+    def to_field(rows):
+        x = rows.reshape(cells_x, cells_y // 8, per_column, 8, width)
+        return x.transpose(0, 1, 3, 2, 4).reshape(cells_x, cells_y, depth)
+
     def exchange(x):
         return lax.all_to_all(x, mesh_axes, split_axis=0, concat_axis=0, tiled=True)
 
@@ -381,14 +382,28 @@
         in_specs=[VMEM],
         out_specs=[VMEM, VMEM],
         name="route",
-    )(block_ids.reshape(requests // LANES, LANES))
+    )(block_ids.T)
     incoming = exchange(outgoing)
 
-    table = (
-        log_density.reshape(cells_x, cells_y // 8, 8, per_column, width)
-        .transpose(0, 1, 3, 2, 4)
-        .reshape(blocks, width)
-    )
+    field, _ = lax.optimization_barrier((log_density, outgoing))
+    table, xfirst, xlast, yfirst, ylast = pl.pallas_call(
+        table_kernel,
+        out_shape=[
+            shape((blocks + capacity, width), f32),
+            shape((2, cells_y, depth), f32),
+            shape((2, cells_y, depth), f32),
+            shape((2, cells_x, depth), f32),
+            shape((2, cells_x, depth), f32),
+        ],
+        in_specs=[VMEM],
+        out_specs=[VMEM] * 5,
+        compiler_params=pltpu.CompilerParams(vmem_limit_bytes=16 * MIB),
+        cost_estimate=pl.CostEstimate(
+            flops=8 * cells, bytes_accessed=8 * cells, transcendentals=cells
+        ),
+        name="table",
+    )(field)
+
     served = pl.pallas_call(
         functools.partial(serve_kernel, capacity=capacity, blocks=blocks),
         out_shape=shape((all_slots, width), bf16),
@@ -401,7 +416,33 @@
     )(incoming, table)
     returned = exchange(served.reshape(devices, capacity, width)).reshape(all_slots, width)
 
-    field, incoming_late, _ = lax.optimization_barrier((log_density, incoming, served))
+    *edges, _ = lax.optimization_barrier((xfirst, xlast, yfirst, ylast, served))
+    sides = halo(*edges)
+    returned, *sides = lax.optimization_barrier((returned, *sides))
+
+    chunks = blocks_dev * stars // LANES
+    live = jnp.arange(stars)[None, :] < star_counts[:, None]
+    live_inverse = jnp.where(live, inverse_var, 0.0).reshape(chunks, LANES)
+    extinction, parcel = pl.pallas_call(
+        star_kernel,
+        out_shape=[shape((chunks, LANES), f32), shape((all_slots, width), bf16)],
+        in_specs=[SMEM, VMEM, VMEM, VMEM, ANY],
+        out_specs=[VMEM, VMEM],
+        scratch_shapes=[
+            pltpu.VMEM(weights.shape, bf16),
+            pltpu.VMEM((all_slots, width), f32),
+            pltpu.VMEM((all_slots, width), f32),
+            pltpu.SemaphoreType.DMA((chunks,)),
+        ],
+        compiler_params=pltpu.CompilerParams(vmem_limit_bytes=56 * MIB),
+        cost_estimate=pl.CostEstimate(
+            flops=4 * weights.size, bytes_accessed=2 * weights.size, transcendentals=0
+        ),
+        name="stars",
+    )(position, returned, observed.reshape(chunks, LANES), live_inverse, weights)
+    arrived = exchange(parcel.reshape(devices, capacity, width)).reshape(all_slots, width)
+
+    field_late, incoming_late, _ = lax.optimization_barrier((log_density, incoming, parcel))
     match = pl.pallas_call(
         match_kernel,
         out_shape=shape((all_slots, LANES), bf16),
@@ -411,7 +452,6 @@
         cost_estimate=pl.CostEstimate(flops=10**9, bytes_accessed=MIB, transcendentals=0),
         name="match",
     )(incoming_late.reshape(all_slots // LANES, LANES))
-    xlo, xhi, ylo, yhi = halo(field)
     base = pl.pallas_call(
         prior_kernel,
         out_shape=shape((cells_x, cells_y, depth), f32),
@@ -426,52 +466,26 @@
             flops=30 * cells, bytes_accessed=8 * cells, transcendentals=0
         ),
         name="prior",
-    )(field, xlo, xhi, ylo, yhi)
-
-    chunks = blocks_dev * stars // LANES
-    live = jnp.arange(stars)[None, :] < star_counts[:, None]
-    live_inverse = jnp.where(live, inverse_var, 0.0).reshape(chunks, LANES)
-    extinction, parcel = pl.pallas_call(
-        star_kernel,
-        out_shape=[shape((chunks, LANES), f32), shape((all_slots, width), bf16)],
-        in_specs=[SMEM, VMEM, VMEM, VMEM, ANY],
-        out_specs=[VMEM, VMEM],
-        scratch_shapes=[
-            pltpu.VMEM(weights.shape, bf16),
-            pltpu.VMEM((all_slots, width), f32),
-            pltpu.VMEM((all_slots, width), f32),
-            pltpu.SemaphoreType.DMA((chunks,)),
-        ],
-        compiler_params=pltpu.CompilerParams(vmem_limit_bytes=32 * MIB),
-        cost_estimate=pl.CostEstimate(
-            flops=4 * weights.size, bytes_accessed=2 * weights.size, transcendentals=0
-        ),
-        name="stars",
-    )(position, returned, observed.reshape(chunks, LANES), live_inverse, weights)
-    arrived = exchange(parcel.reshape(devices, capacity, width)).reshape(all_slots, width)
-
-    parts = 8
-    new_log_density = pl.pallas_call(
+    )(field_late, *sides)
+
+    new_rows = pl.pallas_call(
         functools.partial(finish_kernel, capacity=capacity, blocks=blocks),
-        out_shape=shape((cells_x, cells_y, depth), f32),
+        out_shape=shape((blocks, width), f32),
         in_specs=[SMEM, VMEM, VMEM, ANY, ANY],
         out_specs=ANY,
         scratch_shapes=[
-            pltpu.VMEM((blocks + 8, width), f32),
             pltpu.VMEM((all_slots, width), f32),
-            pltpu.VMEM((cells_x, cells_y, depth), f32),
-            pltpu.VMEM((cells_x, cells_y, depth), f32),
-            pltpu.VMEM((cells_x, cells_y, depth), f32),
-            pltpu.SemaphoreType.DMA((2,)),
-            pltpu.SemaphoreType.DMA((parts,)),
+            pltpu.VMEM((blocks + capacity, width), f32),
+            pltpu.VMEM((blocks + capacity, width), f32),
+            pltpu.SemaphoreType.DMA((3,)),
         ],
-        compiler_params=pltpu.CompilerParams(vmem_limit_bytes=32 * MIB),
+        compiler_params=pltpu.CompilerParams(vmem_limit_bytes=56 * MIB),
         cost_estimate=pl.CostEstimate(
-            flops=4 * cells, bytes_accessed=12 * cells, transcendentals=cells
+            flops=4 * cells, bytes_accessed=12 * cells, transcendentals=0
         ),
         name="finish",
-    )(incoming, match, arrived, log_density, base)
-    return new_log_density, extinction.reshape(blocks_dev, stars)
+    )(incoming, match, arrived, table, to_rows(base))
+    return to_field(new_rows), extinction.reshape(blocks_dev, stars)
 
 
 def solution(mesh):

time: 148 us -> 123 us (0.83)
  waiting for transfers between devices: 35.4 us -> 17.8 us
  blocking collectives: 13.7 us -> 0 us
  starting transfers between devices: 17.2 us -> 29.5 us
  local copies, waits for them, and re-layouts: 21.9 us -> 17.1 us
  Pallas kernels: 58.5 us -> 56.7 us
    all_to_all x2 -> x3, waiting for transfers between devices: 26.1 us -> 6.04 us  [exchange(): return lax.all_to_all(x, mesh_axes, split_axis=0, concat_axis=0, tiled=True)]
    all_to_all x1 -> x0, blocking collectives: 13.7 us -> none  [exchange(): return lax.all_to_all(x, mesh_axes, split_axis=0, concat_axis=0, tiled=True)]
    all_to_all x2 -> x3, starting transfers between devices: 5.79 us -> 17.4 us  [exchange(): return lax.all_to_all(x, mesh_axes, split_axis=0, concat_axis=0, tiled=True)]
    optimization_barrier x1 -> x4, local copies, waits for them, and re-layouts: 4.62 us -> 0.51 us  [the longest x2 0.41 us: on_device(): *edges, _ = lax.optimization_barrier((xfirst, xlast, yfirst, ylast, served))]
    ppermute x4, waiting for transfers between devices: 9.3 us -> 11.7 us  [both_ways(): return (lax.ppermute(last, axis, up), lax.ppermute(first, axis, down))]
    pallas_call x1, Pallas kernels: 9.8 us -> 8.1 us  [on_device(): pl.pallas_call(functools.partial(serve_kernel, capacity=capacity, blocks=...]
    unnamed x23 -> x26, local copies, waits for them, and re-layouts: 15.9 us -> 14.3 us
  transfers between devices with their start and end apart: 6 -> 7, of which waited for: 3 -> 7; matrix products, arithmetic and copies ran while one was open for 4% -> 3% of each run, Pallas kernels for 11% -> 13%
where the time goes in v2:
time: 123 us; the launch traced here: 122 us
  Pallas kernels  56.7 us (46%)
  starting transfers between devices  29.5 us (24%)
  waiting for transfers between devices  17.8 us (14%)
  local copies, waits for them, and re-layouts  17.1 us (14%)
    all_to_all x3, starting transfers between devices, exchange(): return lax.all_to_all(x, mesh_axes, split_axis=0, concat_axis=0, tiled=True)  17.4 us
    pallas_call x1, Pallas kernels, on_device(): pl.pallas_call(functools.partial(finish_kernel, capacity=capacity, blocks...  15.6 us
    unnamed x26, local copies, waits for them, and re-layouts  14.3 us
    pallas_call x1, Pallas kernels, on_device(): pl.pallas_call(star_kernel, out_shape=[shape((chunks, LANES), f32), shape...  13.5 us
    ppermute x4, starting transfers between devices, both_ways(): return (lax.ppermute(last, axis, up), lax.ppermute(first, axis, down))  12.1 us
    ppermute x4, waiting for transfers between devices, both_ways(): return (lax.ppermute(last, axis, up), lax.ppermute(first, axis, down))  11.7 us
    pallas_call x1, Pallas kernels, on_device(): pl.pallas_call(prior_kernel, out_shape=shape((cells_x, cells_y, depth), f...  10.7 us
    pallas_call x1, Pallas kernels, on_device(): pl.pallas_call(functools.partial(serve_kernel, capacity=capacity, blocks=...  8.1 us
  transfers between devices with their start and end apart: 7, of which 7 were waited for; matrix products, arithmetic and copies ran while one was open for 3% of the time, Pallas kernels for 13%

profile of v2, /device:TPU:1, one launch (start us, length us, event | category | flops | bytes accessed | tf_op | source)
XLA Modules:
  0.0 122.0 jit_solution(13437665779886336209)
XLA Ops:
  0.6 3.1 %route.1 = (s32[32,128]{1,0:T(8,128)}, s32[16,128]{1,0:T(8,128)}) custom-call(s32[32,64]{1,0:T(8,128)} %bitcast.35), custom_call_target="tpu_custom_call" | custom-call | tf_op jit(solution)/shard_map/route/pallas_call | solution.py:373
  3.7 7.1 %all-to-all-start = ((s32[32,1,128]{2,1,0:T(1,128)}), s32[32,1,128]{2,1,0:T(1,128)S(1)}, u32[]{:S(2)}, u32[]{:S(2)}) async-start(s32[32,1,128]{2,1,0:T(1,128)} %bitcast.36), calls=%async_computation | async-start | bytes 32768 | tf_op jit(solution)/shard_map/all_to_all | solution.py:371
  10.8 2.2 %copy-done.2 = f32[32,64,512]{2,1,0:T(8,128)S(1)} copy-done((f32[32,64,512]{2,1,0:T(8,128)S(1)}, f32[32,64,512]{2,1,0:T(8,128)}, u32[]{:S(2)}) %copy-start.2) | copy-done | bytes 4194328
  13.0 0.8 table.1
  13.9 2.0 %copy-done = f32[8320,128]{1,0:T(8,128)} copy-done((f32[8320,128]{1,0:T(8,128)}, f32[8320,128]{1,0:T(8,128)S(1)}, u32[]{:S(2)}) %copy-start) | copy-done | bytes 4259864
  15.8 1.6 %all-to-all-done = s32[32,1,128]{2,1,0:T(1,128)S(1)} async-done(((s32[32,1,128]{2,1,0:T(1,128)}), s32[32,1,128]{2,1,0:T(1,128)S(1)}, u32[]{:S(2)}, u32[]{:S(2)}) %all-to-all-start) | async-done | bytes 16416 | tf_op jit(solution)/shard_map/all_to_all | solution.py:371
  17.4 2.2 %copy-done.1 = f32[8320,128]{1,0:T(8,128)S(1)} copy-done((f32[8320,128]{1,0:T(8,128)S(1)}, f32[8320,128]{1,0:T(8,128)}, u32[]{:S(2)}) %copy-start.1) | copy-done | bytes 4259864
  19.7 8.1 %serve.1 = bf16[4096,128]{1,0:T(8,128)(2,1)} custom-call(s32[32,128]{1,0:T(8,128)S(1)} %bitcast.28, f32[8320,128]{1,0:T(8,128)S(1)} %copy-done.1), custom_call_target="tpu_custom_call" | custom-call | bytes 5242880 | tf_op jit(solution)/shard_map/serve/pallas_call | solution.py:407
  27.7 4.3 %all-to-all-start.1 = ((bf16[32,128,128]{2,1,0:T(8,128)(2,1)}), bf16[32,128,128]{2,1,0:T(8,128)(2,1)S(1)}, u32[]{:S(2)}, u32[]{:S(2)}) async-start(bf16[32,128,128]{2,1,0:T(8,128)(2,1)} %bitcast.4), calls=%async_computation.1 | async-start | bytes 2097152 | tf_op jit(solution)/shard_map/all_to_all | solution.py:371
  32.3 3.5 %collective-permute-start = (f32[2,64,512]{2,0,1:T(2,128)S(1)}, f32[2,64,512]{2,0,1:T(2,128)S(1)}, u32[]{:S(2)}, u32[]{:S(2)}) collective-permute-start(f32[2,64,512]{2,0,1:T(2,128)S(1)} %copy.23), channel_id=1, source_target_pairs={{0,4},{4,8},{8,12},{12,16},{16,20},{20,24},{24,28},{1,5},{5,9},{9,... | collective-permute-start | bytes 786440 | tf_op jit(solution)/shard_map/ppermute | solution.py:330
  36.0 1.9 %collective-permute-start.1 = (f32[2,64,512]{2,0,1:T(2,128)S(1)}, f32[2,64,512]{2,0,1:T(2,128)S(1)}, u32[]{:S(2)}, u32[]{:S(2)}) collective-permute-start(f32[2,64,512]{2,0,1:T(2,128)S(1)} %copy.24), channel_id=1, source_target_pairs={{4,0},{8,4},{12,8},{16,12},{20,16},{24,20},{28,24},{5,1},{9,5},{13... | collective-permute-start | bytes 786440 | tf_op jit(solution)/shard_map/ppermute | solution.py:330
  37.9 4.8 %collective-permute-done = f32[2,64,512]{2,0,1:T(2,128)S(1)} collective-permute-done((f32[2,64,512]{2,0,1:T(2,128)S(1)}, f32[2,64,512]{2,0,1:T(2,128)S(1)}, u32[]{:S(2)}, u32[]{:S(2)}) %collective-permute-start) | collective-permute-done | bytes 262176 | tf_op jit(solution)/shard_map/ppermute | solution.py:330
  42.8 6.2 %collective-permute-done.1 = f32[2,64,512]{2,0,1:T(2,128)S(1)} collective-permute-done((f32[2,64,512]{2,0,1:T(2,128)S(1)}, f32[2,64,512]{2,0,1:T(2,128)S(1)}, u32[]{:S(2)}, u32[]{:S(2)}) %collective-permute-start.1) | collective-permute-done | bytes 262176 | tf_op jit(solution)/shard_map/ppermute | solution.py:330
  49.0 1.3 %collective-permute-start.3 = (f32[2,36,512]{2,1,0:T(8,128)S(1)}, f32[2,36,512]{2,1,0:T(8,128)S(1)}, u32[]{:S(2)}, u32[]{:S(2)}) collective-permute-start(f32[2,36,512]{2,1,0:T(8,128)S(1)} %pad_maximum_fusion.1), channel_id=1, source_target_pairs={{1,0},{2,1},{3,2},{5,4},{6,5},{7,6},{9,8},{10,9},{11,10},{13,12},{... | collective-permute-start | bytes 442376 | tf_op jit(solution)/shard_map/ppermute | solution.py:330
  50.3 5.4 %collective-permute-start.2 = (f32[2,36,512]{2,1,0:T(8,128)S(1)}, f32[2,36,512]{2,1,0:T(8,128)S(1)}, u32[]{:S(2)}, u32[]{:S(2)}) collective-permute-start(f32[2,36,512]{2,1,0:T(8,128)S(1)} %pad_maximum_fusion), channel_id=1, source_target_pairs={{0,1},{1,2},{2,3},{4,5},{5,6},{6,7},{8,9},{9,10},{10,11},{12,13},{... | collective-permute-start | bytes 442376 | tf_op jit(solution)/shard_map/ppermute | solution.py:330
  55.8 0.7 reshape.43.inverse_ref
  56.6 0.7 reshape.42.observed_ref
  57.3 0.6 collective-permute-done.3.yhi_ref
  58.0 0.5 all-to-all-done.1
  58.5 1.0 copy-done.7
  59.5 13.5 %stars.1 = (f32[16,128]{1,0:T(8,128)}, bf16[4096,128]{1,0:T(8,128)(2,1)}) custom-call(s32[16,128]{1,0:T(8,128)} %get-tuple-element.24.position_ref, bf16[4096,128]{1,0:T(8,128)(2,1)} %bitcast.31, f32[16,128]{1,0:T(8,128)} %reshape.42.observed_ref, f32[16,128]{1,0:T(8,128)} %reshape.43.inverse_ref, bf16[64,32,32,128]{3,2,1,0:T(8,128)(2,1)} %weights_hbm.1), custom_call_target="tpu_custom_call" | custom-call | flops 33554432 | bytes 16777216 | tf_op jit(solution)/shard_map/stars/pallas_call | solution.py:426
  73.0 6.0 %all-to-all-start.2 = ((bf16[32,128,128]{2,1,0:T(8,128)(2,1)}), bf16[32,128,128]{2,1,0:T(8,128)(2,1)S(1)}, u32[]{:S(2)}, u32[]{:S(2)}) async-start(bf16[32,128,128]{2,1,0:T(8,128)(2,1)} %bitcast.34), calls=%async_computation.2 | async-start | bytes 2097152 | tf_op jit(solution)/shard_map/all_to_all | solution.py:371
  79.2 0.8 reshape.50
  79.9 0.7 copy.29
  80.6 2.2 %copy-done.3 = f32[32,64,512]{2,1,0:T(8,128)S(1)} copy-done((f32[32,64,512]{2,1,0:T(8,128)S(1)}, f32[32,64,512]{2,1,0:T(8,128)}, u32[]{:S(2)}) %copy-start.3) | copy-done | bytes 4194328
  82.8 10.7 %prior.1 = f32[32,64,512]{2,1,0:T(8,128)S(1)} custom-call(f32[32,64,512]{2,1,0:T(8,128)S(1)} %copy-done.3, f32[2,64,512]{2,1,0:T(8,128)S(1)} %copy.27.xlo_ref, f32[2,64,512]{2,1,0:T(8,128)S(1)} %copy.28.xhi_ref, f32[2,36,512]{2,1,0:T(8,128)S(1)} %collective-permute-done.2.ylo_ref, f32[2,36,512]{2,1,0:T(8,128)S(1)} %collective-permute-done.3.yhi_ref), custom_call_target="tpu_custom_call" | custom-call | flops 31457280 | bytes 8388608 | tf_op jit(solution)/shard_map/prior/pallas_call | solution.py:455
  93.6 2.0 %copy-done.4 = f32[32,64,512]{2,1,0:T(8,128)} copy-done((f32[32,64,512]{2,1,0:T(8,128)}, f32[32,64,512]{2,1,0:T(8,128)S(1)}, u32[]{:S(2)}) %copy-start.4) | copy-done | bytes 4194328
  95.6 4.9 %match.1.match_ref = bf16[4096,128]{1,0:T(8,128)(2,1)S(1)} custom-call(s32[32,128]{1,0:T(8,128)S(1)} %bitcast.29), custom_call_target="tpu_custom_call" | custom-call | flops 1000000000 | bytes 1048576 | tf_op jit(solution)/shard_map/match/pallas_call | solution.py:446
  100.5 1.0 copy-done.5
  101.5 3.9 %all-to-all-done.2 = bf16[32,128,128]{2,1,0:T(8,128)(2,1)S(1)} async-done(((bf16[32,128,128]{2,1,0:T(8,128)(2,1)}), bf16[32,128,128]{2,1,0:T(8,128)(2,1)S(1)}, u32[]{:S(2)}, u32[]{:S(2)}) %all-to-all-start.2) | async-done | bytes 1048608 | tf_op jit(solution)/shard_map/all_to_all | solution.py:371
  105.4 1.0 copy-done.8
  106.4 15.6 %finish.1 = f32[8192,128]{1,0:T(8,128)} custom-call(s32[32,128]{1,0:T(8,128)} %bitcast.30, bf16[4096,128]{1,0:T(8,128)(2,1)} %copy-done.5, bf16[4096,128]{1,0:T(8,128)(2,1)} %bitcast.32, f32[8320,128]{1,0:T(8,128)} %copy-done, f32[8192,128]{1,0:T(8,128)} %bitcast.27), custom_call_target="tpu_custom_call" | custom-call | flops 4194304 | bytes 12582912 | tf_op jit(solution)/shard_map/finish/pallas_call | solution.py:471
  (28 shorter events, 0.9 us)
Async XLA Ops:
  3.7 13.7 %all-to-all-start = ((s32[32,1,128]{2,1,0:T(1,128)}), s32[32,1,128]{2,1,0:T(1,128)S(1)}, u32[]{:S(2)}, u32[]{:S(2)}) async-start(s32[32,1,128]{2,1,0:T(1,128)} %bitcast.36), calls=%async_computation | async-start | bytes 32768 | tf_op jit(solution)/shard_map/all_to_all | solution.py:371
  10.8 2.2 %copy-start.2 = (f32[32,64,512]{2,1,0:T(8,128)S(1)}, f32[32,64,512]{2,1,0:T(8,128)}, u32[]{:S(2)}) copy-start(f32[32,64,512]{2,1,0:T(8,128)} %field_ref.1) | copy-start | bytes 12582916
  13.9 2.0 %copy-start = (f32[8320,128]{1,0:T(8,128)}, f32[8320,128]{1,0:T(8,128)S(1)}, u32[]{:S(2)}) copy-start(f32[8320,128]{1,0:T(8,128)S(1)} %get-tuple-element.26.table_ref.table_hbm) | copy-start | bytes 12779524
  17.4 76.1 %copy-start.6 = (s32[32,1,128]{2,1,0:T(1,128)}, s32[32,1,128]{2,1,0:T(1,128)S(1)}, u32[]{:S(2)}) copy-start(s32[32,1,128]{2,1,0:T(1,128)S(1)} %all-to-all-done) | copy-start | bytes 49156
  17.4 2.2 %copy-start.1 = (f32[8320,128]{1,0:T(8,128)S(1)}, f32[8320,128]{1,0:T(8,128)}, u32[]{:S(2)}) copy-start(f32[8320,128]{1,0:T(8,128)} %copy-done) | copy-start | bytes 12779524
  19.6 36.1 %copy-start.10 = (f32[64,32]{0,1:T(8,128)S(1)}, f32[64,32]{0,1:T(8,128)}, u32[]{:S(2)}) copy-start(f32[64,32]{0,1:T(8,128)} %param.9) | copy-start | bytes 24580
  19.6 36.1 %copy-start.11 = (s32[64]{0:T(128)S(1)}, s32[64]{0:T(128)}, u32[]{:S(2)}) copy-start(s32[64]{0:T(128)} %param.10) | copy-start | bytes 772
  19.6 36.9 %copy-start.9 = (f32[64,32]{0,1:T(8,128)S(1)}, f32[64,32]{0,1:T(8,128)}, u32[]{:S(2)}) copy-start(f32[64,32]{0,1:T(8,128)} %param.8) | copy-start | bytes 24580
  27.7 30.8 %all-to-all-start.1 = ((bf16[32,128,128]{2,1,0:T(8,128)(2,1)}), bf16[32,128,128]{2,1,0:T(8,128)(2,1)S(1)}, u32[]{:S(2)}, u32[]{:S(2)}) async-start(bf16[32,128,128]{2,1,0:T(8,128)(2,1)} %bitcast.4), calls=%async_computation.1 | async-start | bytes 2097152 | tf_op jit(solution)/shard_map/all_to_all | solution.py:371
  32.3 10.5 %collective-permute-start = (f32[2,64,512]{2,0,1:T(2,128)S(1)}, f32[2,64,512]{2,0,1:T(2,128)S(1)}, u32[]{:S(2)}, u32[]{:S(2)}) collective-permute-start(f32[2,64,512]{2,0,1:T(2,128)S(1)} %copy.23), channel_id=1, source_target_pairs={{0,4},{4,8},{8,12},{12,16},{16,20},{20,24},{24,28},{1,5},{5,9},{9,... | collective-permute-start | bytes 786440 | tf_op jit(solution)/shard_map/ppermute | solution.py:330
  36.0 13.0 %collective-permute-start.1 = (f32[2,64,512]{2,0,1:T(2,128)S(1)}, f32[2,64,512]{2,0,1:T(2,128)S(1)}, u32[]{:S(2)}, u32[]{:S(2)}) collective-permute-start(f32[2,64,512]{2,0,1:T(2,128)S(1)} %copy.24), channel_id=1, source_target_pairs={{4,0},{8,4},{12,8},{16,12},{20,16},{24,20},{28,24},{5,1},{9,5},{13... | collective-permute-start | bytes 786440 | tf_op jit(solution)/shard_map/ppermute | solution.py:330
  49.0 8.8 %collective-permute-start.3 = (f32[2,36,512]{2,1,0:T(8,128)S(1)}, f32[2,36,512]{2,1,0:T(8,128)S(1)}, u32[]{:S(2)}, u32[]{:S(2)}) collective-permute-start(f32[2,36,512]{2,1,0:T(8,128)S(1)} %pad_maximum_fusion.1), channel_id=1, source_target_pairs={{1,0},{2,1},{3,2},{5,4},{6,5},{7,6},{9,8},{10,9},{11,10},{13,12},{... | collective-permute-start | bytes 442376 | tf_op jit(solution)/shard_map/ppermute | solution.py:330
  50.3 7.6 %collective-permute-start.2 = (f32[2,36,512]{2,1,0:T(8,128)S(1)}, f32[2,36,512]{2,1,0:T(8,128)S(1)}, u32[]{:S(2)}, u32[]{:S(2)}) collective-permute-start(f32[2,36,512]{2,1,0:T(8,128)S(1)} %pad_maximum_fusion), channel_id=1, source_target_pairs={{0,1},{1,2},{2,3},{4,5},{5,6},{6,7},{8,9},{9,10},{10,11},{12,13},{... | collective-permute-start | bytes 442376 | tf_op jit(solution)/shard_map/ppermute | solution.py:330
  58.5 1.0 copy-start.7
  73.0 32.4 %all-to-all-start.2 = ((bf16[32,128,128]{2,1,0:T(8,128)(2,1)}), bf16[32,128,128]{2,1,0:T(8,128)(2,1)S(1)}, u32[]{:S(2)}, u32[]{:S(2)}) async-start(bf16[32,128,128]{2,1,0:T(8,128)(2,1)} %bitcast.34), calls=%async_computation.2 | async-start | bytes 2097152 | tf_op jit(solution)/shard_map/all_to_all | solution.py:371
  80.6 2.2 %copy-start.3 = (f32[32,64,512]{2,1,0:T(8,128)S(1)}, f32[32,64,512]{2,1,0:T(8,128)}, u32[]{:S(2)}) copy-start(f32[32,64,512]{2,1,0:T(8,128)} %field_ref.1) | copy-start | bytes 12582916
  93.6 2.0 %copy-start.4 = (f32[32,64,512]{2,1,0:T(8,128)}, f32[32,64,512]{2,1,0:T(8,128)S(1)}, u32[]{:S(2)}) copy-start(f32[32,64,512]{2,1,0:T(8,128)S(1)} %prior.1) | copy-start | bytes 12582916
  100.5 1.0 copy-start.5
  105.4 1.0 copy-start.8

commit v3 on v2

--- a/solution.py
+++ b/solution.py
@@ -66,6 +66,7 @@
 def table_kernel(field_ref, table_ref, xfirst_ref, xlast_ref, yfirst_ref, ylast_ref):
     cells_x, cells_y, depth = field_ref.shape
     per_column = depth // LANES
+    rows_ref = table_ref.reshape(table_ref.shape[0], LANES)
     xfirst_ref[...] = field_ref[:2]
     xlast_ref[...] = field_ref[cells_x - 2 :]
 
@@ -73,7 +74,7 @@
         for yb in range(cells_y // 8):
             for part in range(per_column):
                 at = pl.multiple_of(((x * (cells_y // 8) + yb) * per_column + part) * 8, 8)
-                table_ref[pl.ds(at, 8), :] = jnp.exp(
+                rows_ref[pl.ds(at, 8), :] = jnp.exp(
                     field_ref[x, 8 * yb : 8 * yb + 8, part * LANES : (part + 1) * LANES]
                 )
         for h in range(2):
@@ -82,8 +83,8 @@
         return carry
 
     lax.fori_loop(0, cells_x, one_plane, 0)
-    pad = table_ref.shape[0] - cells_x * cells_y * per_column
-    table_ref[cells_x * cells_y * per_column :, :] = jnp.zeros((pad, LANES), jnp.float32)
+    blocks = cells_x * cells_y * per_column
+    rows_ref[blocks:, :] = jnp.zeros((table_ref.shape[0] - blocks, LANES), jnp.float32)
 
 
 def filled_groups(incoming_ref, source, capacity, blocks):
@@ -96,10 +97,8 @@
     def one_source(source, carry):
         def one_group(group, carry):
             first = pl.multiple_of(group * GROUP, GROUP)
-            rows = [
-                table_ref[pl.ds(incoming_ref[source, first + j], 1), :] for j in range(GROUP)
-            ]
-            start = source * capacity + first
+            rows = [table_ref[incoming_ref[source, first + j]] for j in range(GROUP)]
+            start = pl.multiple_of(source * capacity + first, GROUP)
             for j in range(GROUP):
                 rows_ref[pl.ds(start + j, 1), :] = rows[j]
             return carry
@@ -118,7 +117,7 @@
     ones = jnp.ones((LANES, LANES), jnp.bfloat16)
     same_group = (lane // GROUP) == (row // GROUP)
 
-    def one_row(i, carry):
+    def one_row(i):
         wanted = incoming_ref[pl.ds(i, 1), :]
         high = jnp.where(lane == row, (wanted >> 7).astype(jnp.float32), 0.0).astype(jnp.bfloat16)
         low = jnp.where(lane == row, (wanted & 127).astype(jnp.float32), 0.0).astype(jnp.bfloat16)
@@ -128,9 +127,13 @@
         match_ref[pl.ds(pl.multiple_of(i * LANES, LANES), LANES), :] = jnp.where(
             same, 1.0, 0.0
         ).astype(jnp.bfloat16)
+
+    def some_rows(i, carry):
+        for j in range(4):
+            one_row(4 * i + j)
         return carry
 
-    lax.fori_loop(0, incoming_ref.shape[0], one_row, 0)
+    lax.fori_loop(0, incoming_ref.shape[0] // 4, some_rows, 0)
 
 
 def star_kernel(
@@ -142,84 +145,110 @@
     extinction_ref,
     parcel_ref,
     weights_ref,
+    returned_rows,
     fetched_ref,
     sens_ref,
+    parcel_rows,
     sems,
 ):
     blocks_dev, slots, stars, width = weights_ref.shape
-    chunks = extinction_ref.shape[0]
+    chunks = sems.shape[0]
     per = blocks_dev // chunks
     half = position_ref.shape[0]
-
-    def place(block, slot):
-        return position_ref[slot % half, (slot // half) * blocks_dev + block]
+    fold = LANES // stars
+    all_slots = parcel_rows.shape[0]
+    lane = lax.broadcasted_iota(jnp.int32, (8, LANES), 1)
+    row = lax.broadcasted_iota(jnp.int32, (8, LANES), 0)
+    own_slot = [row == lane // stars + fold * h for h in range(8 // fold)]
 
     def load(chunk):
         span = pl.ds(chunk * per, per)
         return pltpu.make_async_copy(weights_hbm.at[span], weights_ref.at[span], sems.at[chunk])
 
+    def place(block, slot):
+        return position_ref[slot % half, (slot // half) * blocks_dev + block]
+
+    def start_of(chunk):
+        return pl.multiple_of(chunk * per * slots, per * slots)
+
+    def eight_slots(chunk, b, j):
+        return weights_ref[chunk * per + b, 8 * j : 8 * j + 8].reshape(8 * stars, width)
+
+    def gather(chunk):
+        rows = [returned_rows[place(chunk * per + b, k)] for b in range(per) for k in range(slots)]
+        for i, value in enumerate(rows):
+            fetched_ref[pl.ds(start_of(chunk) + i, 1), :] = value
+
+    def extinctions(chunk):
+        weighted = []
+        for b in range(per):
+            total = jnp.zeros((8, 8 * stars), jnp.float32)
+            for j in range(slots // 8):
+                eight = fetched_ref[pl.ds(start_of(chunk) + b * slots + 8 * j, 8), :]
+                total = total + lax.dot_general(
+                    eight.astype(jnp.bfloat16),
+                    eight_slots(chunk, b, j),
+                    CONTRACT_LANES,
+                    preferred_element_type=jnp.float32,
+                )
+            folded = jnp.zeros((8, LANES), jnp.float32)
+            for h, own in enumerate(own_slot):
+                folded = folded + jnp.where(own, total[:, h * LANES : (h + 1) * LANES], 0.0)
+            extinction = jnp.sum(folded, axis=0, keepdims=True)
+            shift = stars
+            while shift < LANES:
+                extinction = extinction + pltpu.roll(extinction, shift, 1)
+                shift *= 2
+            here = pl.ds(chunk * per + b, 1)
+            extinction_ref[here, :] = extinction
+            weighted.append(inverse_ref[here, :] * (extinction - observed_ref[here, :]))
+        return weighted
+
+    def sensitivities(chunk, weighted):
+        for b in range(per):
+            left = jnp.concatenate(
+                [jnp.where(own, weighted[b], 0.0) for own in own_slot], axis=1
+            ).astype(jnp.bfloat16)
+            for j in range(slots // 8):
+                sens_ref[pl.ds(start_of(chunk) + b * slots + 8 * j, 8), :] = jnp.dot(
+                    left, eight_slots(chunk, b, j), preferred_element_type=jnp.float32
+                )
+
+    def scatter(chunk):
+        for b in range(per):
+            for k in range(slots):
+                at = pl.ds(start_of(chunk) + b * slots + k, 1)
+                parcel_rows[place(chunk * per + b, k)] = sens_ref[at, :]
+
     for chunk in range(chunks):
         load(chunk).start()
-    fetched_ref[...] = returned_ref[...].astype(jnp.float32)
-    sens_ref[...] = jnp.zeros_like(sens_ref)
-    lane = lax.broadcasted_iota(jnp.int32, (8, LANES), 1)
-    row = lax.broadcasted_iota(jnp.int32, (8, LANES), 0)
-    star_group = lane // stars
-
-    def extinctions(chunk):
-        sums = []
-        for b in range(per):
-            total = jnp.zeros((stars, width), jnp.float32)
-            for k in range(slots):
-                at = place(chunk * per + b, k)
-                total = total + weights_ref[chunk * per + b, k].astype(jnp.float32) * fetched_ref[
-                    pl.ds(at, 1), :
-                ]
-            sums.append(total)
-        extinction = lax.dot_general(
-            jnp.ones((8, width), jnp.float32),
-            jnp.concatenate(sums, axis=0),
-            CONTRACT_LANES,
-            precision=lax.Precision.HIGHEST,
-            preferred_element_type=jnp.float32,
-        )
-        extinction_ref[pl.ds(chunk, 1), :] = extinction[:1]
-        here = pl.ds(chunk, 1)
-        return inverse_ref[here, :] * (extinction - observed_ref[here, :])
-
-    def sensitivities(chunk, weighted):
-        for b in range(per):
-            spread = jnp.where(star_group == b, weighted, 0.0)
-            shift = stars
-            while shift < LANES:
-                spread = spread + pltpu.roll(spread, shift, 1)
-                shift *= 2
-            left = jnp.concatenate(
-                [jnp.where(row == star_group + per * h, spread, 0.0) for h in range(8 // per)],
-                axis=1,
-            ).astype(jnp.bfloat16)
-            for j in range(slots // 8):
-                right = weights_ref[chunk * per + b, 8 * j : 8 * j + 8].reshape(8 * stars, width)
-                sens = jnp.dot(left, right, preferred_element_type=jnp.float32)
-                for r in range(8):
-                    at = place(chunk * per + b, 8 * j + r)
-                    sens_ref[pl.ds(at, 1), :] = sens[r : r + 1, :]
-
+    returned_rows.reshape(all_slots, width)[...] = returned_ref[...].astype(jnp.float32)
+    parcel_rows.reshape(all_slots, width)[...] = jnp.zeros((all_slots, width), jnp.float32)
+    gather(0)
     load(0).wait()
-    first = extinctions(0)
+    weighted = extinctions(0)
+    gather(1)
+    load(1).wait()
+    following = extinctions(1)
+    sensitivities(0, weighted)
+    gather(2)
 
     def step(chunk, weighted):
         load(chunk).wait()
         following = extinctions(chunk)
         sensitivities(chunk - 1, weighted)
+        scatter(chunk - 2)
+        gather(jnp.minimum(chunk + 1, chunks - 1))
         return following
 
-    last = lax.fori_loop(1, chunks, step, first)
-    sensitivities(chunks - 1, last)
-    parcel_ref[...] = sens_ref[...].astype(jnp.bfloat16)
-
-
-def prior_kernel(field_ref, xlo_ref, xhi_ref, ylo_ref, yhi_ref, out_ref, padded, smooth):
+    weighted = lax.fori_loop(2, chunks, step, following)
+    sensitivities(chunks - 1, weighted)
+    scatter(chunks - 2)
+    scatter(chunks - 1)
+    parcel_ref[...] = parcel_rows.reshape(all_slots, width)[...].astype(jnp.bfloat16)
+
+
+def prior_kernel(field_ref, xlo_ref, xhi_ref, ylo_ref, yhi_ref, out_ref, exp_ref, padded, smooth):
     cells_x, cells_y, depth = field_ref.shape
     rows = padded.shape[1]
     gx, gy = lax.axis_index("gx"), lax.axis_index("gy")
@@ -264,6 +293,7 @@
     def out_plane(x, carry):
         prior = operate(smooth[x + 1], smooth[x], smooth[x + 2])
         out_ref[x] = field_ref[x] - (step_rate * prior_weight) * prior[8 : 8 + cells_y]
+        exp_ref[x] = jnp.exp(field_ref[x])
         return carry
 
     lax.fori_loop(0, cells_x, out_plane, 0)
@@ -273,11 +303,11 @@
     incoming_ref,
     match_ref,
     arrived_ref,
-    table_hbm,
+    exp_hbm,
     base_hbm,
     out_hbm,
     rows_ref,
-    table_ref,
+    exp_ref,
     out_ref,
     sems,
     *,
@@ -286,7 +316,7 @@
 ):
     own = pl.ds(0, blocks)
     loads = [
-        pltpu.make_async_copy(table_hbm, table_ref, sems.at[0]),
+        pltpu.make_async_copy(exp_hbm, exp_ref.at[own], sems.at[0]),
         pltpu.make_async_copy(base_hbm, out_ref.at[own], sems.at[1]),
     ]
     for load in loads:
@@ -302,14 +332,14 @@
     def one_source(source, carry):
         def one_group(group, carry):
             first = pl.multiple_of(group * GROUP, GROUP)
-            places = [pl.ds(incoming_ref[source, first + j], 1) for j in range(GROUP)]
-            start = source * capacity + first
+            places = [incoming_ref[source, first + j] for j in range(GROUP)]
+            start = pl.multiple_of(source * capacity + first, GROUP)
             sums = [
-                out_ref[places[j], :] + table_ref[places[j], :] * rows_ref[pl.ds(start + j, 1), :]
+                out_ref[places[j]] + exp_ref[places[j]] * rows_ref[pl.ds(start + j, 1), :]
                 for j in range(GROUP)
             ]
             for j in range(GROUP):
-                out_ref[places[j], :] = sums[j]
+                out_ref[places[j]] = sums[j]
             return carry
 
         return lax.fori_loop(
@@ -361,7 +391,7 @@
 
     def to_rows(x):
         x = x.reshape(cells_x, cells_y // 8, 8, per_column, width)
-        return x.transpose(0, 1, 3, 2, 4).reshape(blocks, width)
+        return x.transpose(0, 1, 3, 2, 4).reshape(blocks, 1, width)
 
     def to_field(rows):
         x = rows.reshape(cells_x, cells_y // 8, per_column, 8, width)
@@ -389,7 +419,7 @@
     table, xfirst, xlast, yfirst, ylast = pl.pallas_call(
         table_kernel,
         out_shape=[
-            shape((blocks + capacity, width), f32),
+            shape((blocks + capacity, 1, width), f32),
             shape((2, cells_y, depth), f32),
             shape((2, cells_y, depth), f32),
             shape((2, cells_x, depth), f32),
@@ -416,33 +446,10 @@
     )(incoming, table)
     returned = exchange(served.reshape(devices, capacity, width)).reshape(all_slots, width)
 
-    *edges, _ = lax.optimization_barrier((xfirst, xlast, yfirst, ylast, served))
+    *edges, incoming_late, _ = lax.optimization_barrier(
+        (xfirst, xlast, yfirst, ylast, incoming, served)
+    )
     sides = halo(*edges)
-    returned, *sides = lax.optimization_barrier((returned, *sides))
-
-    chunks = blocks_dev * stars // LANES
-    live = jnp.arange(stars)[None, :] < star_counts[:, None]
-    live_inverse = jnp.where(live, inverse_var, 0.0).reshape(chunks, LANES)
-    extinction, parcel = pl.pallas_call(
-        star_kernel,
-        out_shape=[shape((chunks, LANES), f32), shape((all_slots, width), bf16)],
-        in_specs=[SMEM, VMEM, VMEM, VMEM, ANY],
-        out_specs=[VMEM, VMEM],
-        scratch_shapes=[
-            pltpu.VMEM(weights.shape, bf16),
-            pltpu.VMEM((all_slots, width), f32),
-            pltpu.VMEM((all_slots, width), f32),
-            pltpu.SemaphoreType.DMA((chunks,)),
-        ],
-        compiler_params=pltpu.CompilerParams(vmem_limit_bytes=56 * MIB),
-        cost_estimate=pl.CostEstimate(
-            flops=4 * weights.size, bytes_accessed=2 * weights.size, transcendentals=0
-        ),
-        name="stars",
-    )(position, returned, observed.reshape(chunks, LANES), live_inverse, weights)
-    arrived = exchange(parcel.reshape(devices, capacity, width)).reshape(all_slots, width)
-
-    field_late, incoming_late, _ = lax.optimization_barrier((log_density, incoming, parcel))
     match = pl.pallas_call(
         match_kernel,
         out_shape=shape((all_slots, LANES), bf16),
@@ -452,40 +459,73 @@
         cost_estimate=pl.CostEstimate(flops=10**9, bytes_accessed=MIB, transcendentals=0),
         name="match",
     )(incoming_late.reshape(all_slots // LANES, LANES))
-    base = pl.pallas_call(
+    returned, match, *sides = lax.optimization_barrier((returned, match, *sides))
+
+    chunks = blocks_dev * stars // LANES
+    live = jnp.arange(stars)[None, :] < star_counts[:, None]
+    live_inverse = jnp.where(live, inverse_var, 0.0)
+    extinction, parcel = pl.pallas_call(
+        star_kernel,
+        out_shape=[shape((blocks_dev, LANES), f32), shape((all_slots, width), bf16)],
+        in_specs=[SMEM, VMEM, VMEM, VMEM, ANY],
+        out_specs=[VMEM, VMEM],
+        scratch_shapes=[
+            pltpu.VMEM(weights.shape, bf16),
+            pltpu.VMEM((all_slots, 1, width), f32),
+            pltpu.VMEM((requests, width), f32),
+            pltpu.VMEM((requests, width), f32),
+            pltpu.VMEM((all_slots, 1, width), f32),
+            pltpu.SemaphoreType.DMA((chunks,)),
+        ],
+        compiler_params=pltpu.CompilerParams(vmem_limit_bytes=50 * MIB),
+        cost_estimate=pl.CostEstimate(
+            flops=4 * weights.size, bytes_accessed=2 * weights.size, transcendentals=0
+        ),
+        name="stars",
+    )(
+        position,
+        returned,
+        jnp.tile(observed, (1, LANES // stars)),
+        jnp.tile(live_inverse, (1, LANES // stars)),
+        weights,
+    )
+    arrived = exchange(parcel.reshape(devices, capacity, width)).reshape(all_slots, width)
+
+    field_late, _ = lax.optimization_barrier((log_density, parcel))
+    base, scale = pl.pallas_call(
         prior_kernel,
-        out_shape=shape((cells_x, cells_y, depth), f32),
+        out_shape=[shape((cells_x, cells_y, depth), f32)] * 2,
         in_specs=[VMEM] * 5,
-        out_specs=VMEM,
+        out_specs=[VMEM] * 2,
         scratch_shapes=[
             pltpu.VMEM((cells_x + 4, cells_y + 16, depth), f32),
             pltpu.VMEM((cells_x + 2, cells_y + 16, depth), f32),
         ],
         compiler_params=pltpu.CompilerParams(vmem_limit_bytes=32 * MIB),
         cost_estimate=pl.CostEstimate(
-            flops=30 * cells, bytes_accessed=8 * cells, transcendentals=0
+            flops=30 * cells, bytes_accessed=12 * cells, transcendentals=cells
         ),
         name="prior",
     )(field_late, *sides)
 
     new_rows = pl.pallas_call(
         functools.partial(finish_kernel, capacity=capacity, blocks=blocks),
-        out_shape=shape((blocks, width), f32),
+        out_shape=shape((blocks, 1, width), f32),
         in_specs=[SMEM, VMEM, VMEM, ANY, ANY],
         out_specs=ANY,
         scratch_shapes=[
             pltpu.VMEM((all_slots, width), f32),
-            pltpu.VMEM((blocks + capacity, width), f32),
-            pltpu.VMEM((blocks + capacity, width), f32),
+            pltpu.VMEM((blocks + capacity, 1, width), f32),
+            pltpu.VMEM((blocks + capacity, 1, width), f32),
             pltpu.SemaphoreType.DMA((3,)),
         ],
-        compiler_params=pltpu.CompilerParams(vmem_limit_bytes=56 * MIB),
+        compiler_params=pltpu.CompilerParams(vmem_limit_bytes=50 * MIB),
         cost_estimate=pl.CostEstimate(
             flops=4 * cells, bytes_accessed=12 * cells, transcendentals=0
         ),
         name="finish",
-    )(incoming, match, arrived, table, to_rows(base))
-    return to_field(new_rows), extinction.reshape(blocks_dev, stars)
+    )(incoming, match, arrived, to_rows(scale), to_rows(base))
+    return to_field(new_rows), extinction[:, :stars]
 
 
 def solution(mesh):

time: 123 us -> 122 us (level)
  waiting for transfers between devices: 17.8 us -> 24.9 us
  local copies, waits for them, and re-layouts: 17.1 us -> 13.9 us
  Pallas kernels: 56.7 us -> 53.6 us
  starting transfers between devices: 29.5 us -> 26.9 us
    all_to_all x3, waiting for transfers between devices: 6.04 us -> 10.9 us  [exchange(): return lax.all_to_all(x, mesh_axes, split_axis=0, concat_axis=0, tiled=True)]
    ppermute x4, starting transfers between devices: 12.1 us -> 8.51 us  [both_ways(): return (lax.ppermute(last, axis, up), lax.ppermute(first, axis, down))]
    pallas_call x1, Pallas kernels: 4.86 us -> 1.8 us  [on_device(): pl.pallas_call(match_kernel, out_shape=shape((all_slots, LANES), bf16), i...]
    ppermute x4, waiting for transfers between devices: 11.7 us -> 14 us  [both_ways(): return (lax.ppermute(last, axis, up), lax.ppermute(first, axis, down))]
    reshape x3 -> x0, local copies, waits for them, and re-layouts: 2.12 us -> none  [the longest x1 0.77 us: on_device(): return (to_field(new_rows), extinction.reshape(blocks_dev, stars))]
    unnamed x26 -> x21, local copies, waits for them, and re-layouts: 14.3 us -> 13.2 us
  transfers between devices with their start and end apart: 7 -> 7, of which waited for: 7 -> 5; matrix products, arithmetic and copies ran while one was open for 3% -> 2% of each run, Pallas kernels for 13% -> 11%
where the time goes in v3:
time: 122 us; the launch traced here: 121 us
  Pallas kernels  53.6 us (44%)
  starting transfers between devices  26.9 us (22%)
  waiting for transfers between devices  24.9 us (20%)
  local copies, waits for them, and re-layouts  13.9 us (11%)
    all_to_all x3, starting transfers between devices, exchange(): return lax.all_to_all(x, mesh_axes, split_axis=0, concat_axis=0, tiled=True)  18.4 us
    pallas_call x1, Pallas kernels, on_device(): pl.pallas_call(functools.partial(finish_kernel, capacity=capacity, blocks...  14.9 us
    pallas_call x1, Pallas kernels, on_device(): pl.pallas_call(star_kernel, out_shape=[shape((blocks_dev, LANES), f32), s...  14.3 us
    ppermute x4, waiting for transfers between devices, both_ways(): return (lax.ppermute(last, axis, up), lax.ppermute(first, axis, down))  14 us
    unnamed x21, local copies, waits for them, and re-layouts  13.2 us
    all_to_all x3, waiting for transfers between devices, exchange(): return lax.all_to_all(x, mesh_axes, split_axis=0, concat_axis=0, tiled=True)  10.9 us
    pallas_call x1, Pallas kernels, on_device(): pl.pallas_call(prior_kernel, out_shape=[shape((cells_x, cells_y, depth),...  10.7 us
    ppermute x4, starting transfers between devices, both_ways(): return (lax.ppermute(last, axis, up), lax.ppermute(first, axis, down))  8.51 us
  transfers between devices with their start and end apart: 7, of which 5 were waited for; matrix products, arithmetic and copies ran while one was open for 2% of the time, Pallas kernels for 11%

profile of v3, /device:TPU:1, one launch (start us, length us, event | category | flops | bytes accessed | tf_op | source)
XLA Modules:
  0.0 120.8 jit_solution(5665959713060623941)
XLA Ops:
  0.6 3.1 %route.1 = (s32[32,128]{1,0:T(8,128)}, s32[16,128]{1,0:T(8,128)}) custom-call(s32[32,64]{1,0:T(8,128)} %bitcast.46), custom_call_target="tpu_custom_call" | custom-call | tf_op jit(solution)/shard_map/route/pallas_call | solution.py:403
  3.7 7.1 %all-to-all-start = ((s32[32,1,128]{2,1,0:T(1,128)}), s32[32,1,128]{2,1,0:T(1,128)S(1)}, u32[]{:S(2)}, u32[]{:S(2)}) async-start(s32[32,1,128]{2,1,0:T(1,128)} %bitcast.47), calls=%async_computation | async-start | bytes 32768 | tf_op jit(solution)/shard_map/all_to_all | solution.py:401
  10.8 2.2 %copy-done = f32[32,64,512]{2,1,0:T(8,128)S(1)} copy-done((f32[32,64,512]{2,1,0:T(8,128)S(1)}, f32[32,64,512]{2,1,0:T(8,128)}, u32[]{:S(2)}) %copy-start) | copy-done | bytes 4194328
  13.0 0.8 table.1
  13.9 2.0 %copy-done.2 = f32[8320,1,128]{2,1,0:T(1,128)} copy-done((f32[8320,1,128]{2,1,0:T(1,128)}, f32[8320,1,128]{2,1,0:T(1,128)S(1)}, u32[]{:S(2)}) %copy-start.2) | copy-done | bytes 4259864
  15.8 1.6 %all-to-all-done = s32[32,1,128]{2,1,0:T(1,128)S(1)} async-done(((s32[32,1,128]{2,1,0:T(1,128)}), s32[32,1,128]{2,1,0:T(1,128)S(1)}, u32[]{:S(2)}, u32[]{:S(2)}) %all-to-all-start) | async-done | bytes 16416 | tf_op jit(solution)/shard_map/all_to_all | solution.py:401
  17.4 2.2 %copy-done.3 = f32[8320,1,128]{2,1,0:T(1,128)S(1)} copy-done((f32[8320,1,128]{2,1,0:T(1,128)S(1)}, f32[8320,1,128]{2,1,0:T(1,128)}, u32[]{:S(2)}) %copy-start.3) | copy-done | bytes 4259864
  19.6 7.9 %serve.1 = bf16[4096,128]{1,0:T(8,128)(2,1)} custom-call(s32[32,128]{1,0:T(8,128)S(1)} %bitcast.39, f32[8320,1,128]{2,1,0:T(1,128)S(1)} %copy-done.3), custom_call_target="tpu_custom_call" | custom-call | bytes 5242880 | tf_op jit(solution)/shard_map/serve/pallas_call | solution.py:437
  27.6 4.4 %all-to-all-start.1 = ((bf16[32,128,128]{2,1,0:T(8,128)(2,1)}), bf16[32,128,128]{2,1,0:T(8,128)(2,1)S(1)}, u32[]{:S(2)}, u32[]{:S(2)}) async-start(bf16[32,128,128]{2,1,0:T(8,128)(2,1)} %bitcast.4), calls=%async_computation.1 | async-start | bytes 2097152 | tf_op jit(solution)/shard_map/all_to_all | solution.py:401
  32.0 0.2 copy.24
  32.2 2.2 %collective-permute-start.1 = (f32[2,64,512]{2,0,1:T(2,128)S(1)}, f32[2,64,512]{2,0,1:T(2,128)S(1)}, u32[]{:S(2)}, u32[]{:S(2)}) collective-permute-start(f32[2,64,512]{2,0,1:T(2,128)S(1)} %copy.24), channel_id=1, source_target_pairs={{4,0},{8,4},{12,8},{16,12},{20,16},{24,20},{28,24},{5,1},{9,5},{13... | collective-permute-start | bytes 786440 | tf_op jit(solution)/shard_map/ppermute | solution.py:360
  34.4 0.2 copy.23
  34.6 3.4 %collective-permute-start = (f32[2,64,512]{2,0,1:T(2,128)S(1)}, f32[2,64,512]{2,0,1:T(2,128)S(1)}, u32[]{:S(2)}, u32[]{:S(2)}) collective-permute-start(f32[2,64,512]{2,0,1:T(2,128)S(1)} %copy.23), channel_id=1, source_target_pairs={{0,4},{4,8},{8,12},{12,16},{16,20},{20,24},{24,28},{1,5},{5,9},{9,... | collective-permute-start | bytes 786440 | tf_op jit(solution)/shard_map/ppermute | solution.py:360
  38.0 9.4 %collective-permute-done.1 = f32[2,64,512]{2,0,1:T(2,128)S(1)} collective-permute-done((f32[2,64,512]{2,0,1:T(2,128)S(1)}, f32[2,64,512]{2,0,1:T(2,128)S(1)}, u32[]{:S(2)}, u32[]{:S(2)}) %collective-permute-start.1) | collective-permute-done | bytes 262176 | tf_op jit(solution)/shard_map/ppermute | solution.py:360
  47.5 1.7 %collective-permute-start.2 = (f32[2,36,512]{2,1,0:T(8,128)S(1)}, f32[2,36,512]{2,1,0:T(8,128)S(1)}, u32[]{:S(2)}, u32[]{:S(2)}) collective-permute-start(f32[2,36,512]{2,1,0:T(8,128)S(1)} %pad_maximum_fusion), channel_id=1, source_target_pairs={{0,1},{1,2},{2,3},{4,5},{5,6},{6,7},{8,9},{9,10},{10,11},{12,13},{... | collective-permute-start | bytes 442376 | tf_op jit(solution)/shard_map/ppermute | solution.py:360
  49.2 0.7 pad_maximum_fusion.1
  49.8 1.3 %collective-permute-start.3 = (f32[2,36,512]{2,1,0:T(8,128)}, f32[2,36,512]{2,1,0:T(8,128)S(1)}, u32[]{:S(2)}, u32[]{:S(2)}) collective-permute-start(f32[2,36,512]{2,1,0:T(8,128)} %pad_maximum_fusion.1), channel_id=1, source_target_pairs={{1,0},{2,1},{3,2},{5,4},{6,5},{7,6},{9,8},{10,9},{11,10},{13,12},{... | collective-permute-start | bytes 442376 | tf_op jit(solution)/shard_map/ppermute | solution.py:360
  51.2 0.1 copy.26.inverse_ref
  51.3 0.1 copy.25.observed_ref
  51.3 1.8 %match.1.match_ref = bf16[4096,128]{1,0:T(8,128)(2,1)S(1)} custom-call(s32[32,128]{1,0:T(8,128)S(1)} %bitcast.40), custom_call_target="tpu_custom_call" | custom-call | flops 1000000000 | bytes 1048576 | tf_op jit(solution)/shard_map/match/pallas_call | solution.py:453
  53.2 4.6 %collective-permute-done.3.yhi_ref = f32[2,36,512]{2,1,0:T(8,128)S(1)} collective-permute-done((f32[2,36,512]{2,1,0:T(8,128)}, f32[2,36,512]{2,1,0:T(8,128)S(1)}, u32[]{:S(2)}, u32[]{:S(2)}) %collective-permute-start.3) | collective-permute-done | bytes 147488 | tf_op jit(solution)/shard_map/ppermute | solution.py:360
  57.7 0.7 all-to-all-done.1
  58.4 14.3 %stars.1 = (f32[64,128]{1,0:T(8,128)S(1)}, bf16[4096,128]{1,0:T(8,128)(2,1)}) custom-call(s32[16,128]{1,0:T(8,128)S(1)} %copy-done.6, bf16[4096,128]{1,0:T(8,128)(2,1)S(1)} %bitcast.35, f32[64,128]{1,0:T(8,128)S(1)} %copy.25.observed_ref, f32[64,128]{1,0:T(8,128)S(1)} %copy.26.inverse_ref, bf16[64,32,32,128]{3,2,1,0:T(8,128)(2,1)} %weights_hbm.1), custom_call_target="tpu_custom_call" | custom-call | flops 33554432 | bytes 16777216 | tf_op jit(solution)/shard_map/stars/pallas_call | solution.py:467
  72.7 6.8 %all-to-all-start.2 = ((bf16[32,128,128]{2,1,0:T(8,128)(2,1)}), bf16[32,128,128]{2,1,0:T(8,128)(2,1)S(1)}, u32[]{:S(2)}, u32[]{:S(2)}) async-start(bf16[32,128,128]{2,1,0:T(8,128)(2,1)} %bitcast.12), calls=%async_computation.2 | async-start | bytes 2097152 | tf_op jit(solution)/shard_map/all_to_all | solution.py:401
  79.5 0.1 copy.27.xlo_ref
  79.7 0.7 copy.29
  80.3 2.2 %copy-done.1 = f32[32,64,512]{2,1,0:T(8,128)S(1)} copy-done((f32[32,64,512]{2,1,0:T(8,128)S(1)}, f32[32,64,512]{2,1,0:T(8,128)}, u32[]{:S(2)}) %copy-start.1) | copy-done | bytes 4194328
  82.5 10.7 %prior.1 = (f32[32,64,512]{2,1,0:T(8,128)S(1)}, f32[32,64,512]{2,1,0:T(8,128)S(1)}) custom-call(f32[32,64,512]{2,1,0:T(8,128)S(1)} %copy-done.1, f32[2,64,512]{2,1,0:T(8,128)S(1)} %copy.27.xlo_ref, f32[2,64,512]{2,1,0:T(8,128)S(1)} %copy.28.xhi_ref, f32[2,36,512]{2,1,0:T(8,128)S(1)} %collective-permute-done.2.ylo_ref, ...), custom_call_target="tpu_custom_call" | custom-call | flops 31457280 | bytes 12582912 | tf_op jit(solution)/shard_map/prior/pallas_call | solution.py:495
  93.3 2.0 %copy-done.4 = f32[32,64,512]{2,1,0:T(8,128)} copy-done((f32[32,64,512]{2,1,0:T(8,128)}, f32[32,64,512]{2,1,0:T(8,128)S(1)}, u32[]{:S(2)}) %copy-start.4) | copy-done | bytes 4194328
  95.3 1.9 %copy-done.5 = f32[32,64,512]{2,1,0:T(8,128)} copy-done((f32[32,64,512]{2,1,0:T(8,128)}, f32[32,64,512]{2,1,0:T(8,128)S(1)}, u32[]{:S(2)}) %copy-start.5) | copy-done | bytes 4194328
  97.2 8.7 %all-to-all-done.2 = bf16[32,128,128]{2,1,0:T(8,128)(2,1)S(1)} async-done(((bf16[32,128,128]{2,1,0:T(8,128)(2,1)}), bf16[32,128,128]{2,1,0:T(8,128)(2,1)S(1)}, u32[]{:S(2)}, u32[]{:S(2)}) %all-to-all-start.2) | async-done | bytes 1048608 | tf_op jit(solution)/shard_map/all_to_all | solution.py:401
  105.9 14.9 %finish.1 = f32[8192,1,128]{2,1,0:T(1,128)} custom-call(s32[32,128]{1,0:T(8,128)S(1)} %bitcast.41, bf16[4096,128]{1,0:T(8,128)(2,1)S(1)} %match.1.match_ref, bf16[4096,128]{1,0:T(8,128)(2,1)S(1)} %bitcast.36, f32[8192,1,128]{2,1,0:T(1,128)} %bitcast.38, f32[8192,1,128]{2,1,0:T(1,128)} %bitcast.37), custom_call_target="tpu_custom_call" | custom-call | flops 4194304 | bytes 12582912 | tf_op jit(solution)/shard_map/finish/pallas_call | solution.py:511
  (23 shorter events, 0.1 us)
Async XLA Ops:
  3.7 13.7 %all-to-all-start = ((s32[32,1,128]{2,1,0:T(1,128)}), s32[32,1,128]{2,1,0:T(1,128)S(1)}, u32[]{:S(2)}, u32[]{:S(2)}) async-start(s32[32,1,128]{2,1,0:T(1,128)} %bitcast.47), calls=%async_computation | async-start | bytes 32768 | tf_op jit(solution)/shard_map/all_to_all | solution.py:401
  10.8 2.2 %copy-start = (f32[32,64,512]{2,1,0:T(8,128)S(1)}, f32[32,64,512]{2,1,0:T(8,128)}, u32[]{:S(2)}) copy-start(f32[32,64,512]{2,1,0:T(8,128)} %field_ref.1) | copy-start | bytes 12582916
  13.9 2.0 %copy-start.2 = (f32[8320,1,128]{2,1,0:T(1,128)}, f32[8320,1,128]{2,1,0:T(1,128)S(1)}, u32[]{:S(2)}) copy-start(f32[8320,1,128]{2,1,0:T(1,128)S(1)} %get-tuple-element.28.table_ref) | copy-start | bytes 12779524
  17.4 2.2 %copy-start.3 = (f32[8320,1,128]{2,1,0:T(1,128)S(1)}, f32[8320,1,128]{2,1,0:T(1,128)}, u32[]{:S(2)}) copy-start(f32[8320,1,128]{2,1,0:T(1,128)} %copy-done.2) | copy-start | bytes 12779524
  19.6 31.5 %copy-start.8 = (f32[64,32]{0,1:T(8,128)S(1)}, f32[64,32]{0,1:T(8,128)}, u32[]{:S(2)}) copy-start(f32[64,32]{0,1:T(8,128)} %param.9) | copy-start | bytes 24580
  19.6 31.5 %copy-start.9 = (s32[64]{0:T(128)S(1)}, s32[64]{0:T(128)}, u32[]{:S(2)}) copy-start(s32[64]{0:T(128)} %param.10) | copy-start | bytes 772
  19.6 31.6 %copy-start.7 = (f32[64,32]{0,1:T(8,128)S(1)}, f32[64,32]{0,1:T(8,128)}, u32[]{:S(2)}) copy-start(f32[64,32]{0,1:T(8,128)} %param.8) | copy-start | bytes 24580
  27.6 30.8 %copy-start.6 = (s32[16,128]{1,0:T(8,128)S(1)}, s32[16,128]{1,0:T(8,128)}, u32[]{:S(2)}) copy-start(s32[16,128]{1,0:T(8,128)} %get-tuple-element.39.position_ref) | copy-start | bytes 24580
  27.6 30.8 %all-to-all-start.1 = ((bf16[32,128,128]{2,1,0:T(8,128)(2,1)}), bf16[32,128,128]{2,1,0:T(8,128)(2,1)S(1)}, u32[]{:S(2)}, u32[]{:S(2)}) async-start(bf16[32,128,128]{2,1,0:T(8,128)(2,1)} %bitcast.4), calls=%async_computation.1 | async-start | bytes 2097152 | tf_op jit(solution)/shard_map/all_to_all | solution.py:401
  32.2 15.2 %collective-permute-start.1 = (f32[2,64,512]{2,0,1:T(2,128)S(1)}, f32[2,64,512]{2,0,1:T(2,128)S(1)}, u32[]{:S(2)}, u32[]{:S(2)}) collective-permute-start(f32[2,64,512]{2,0,1:T(2,128)S(1)} %copy.24), channel_id=1, source_target_pairs={{4,0},{8,4},{12,8},{16,12},{20,16},{24,20},{28,24},{5,1},{9,5},{13... | collective-permute-start | bytes 786440 | tf_op jit(solution)/shard_map/ppermute | solution.py:360
  34.6 12.8 %collective-permute-start = (f32[2,64,512]{2,0,1:T(2,128)S(1)}, f32[2,64,512]{2,0,1:T(2,128)S(1)}, u32[]{:S(2)}, u32[]{:S(2)}) collective-permute-start(f32[2,64,512]{2,0,1:T(2,128)S(1)} %copy.23), channel_id=1, source_target_pairs={{0,4},{4,8},{8,12},{12,16},{16,20},{20,24},{24,28},{1,5},{5,9},{9,... | collective-permute-start | bytes 786440 | tf_op jit(solution)/shard_map/ppermute | solution.py:360
  47.5 5.7 %collective-permute-start.2 = (f32[2,36,512]{2,1,0:T(8,128)S(1)}, f32[2,36,512]{2,1,0:T(8,128)S(1)}, u32[]{:S(2)}, u32[]{:S(2)}) collective-permute-start(f32[2,36,512]{2,1,0:T(8,128)S(1)} %pad_maximum_fusion), channel_id=1, source_target_pairs={{0,1},{1,2},{2,3},{4,5},{5,6},{6,7},{8,9},{9,10},{10,11},{12,13},{... | collective-permute-start | bytes 442376 | tf_op jit(solution)/shard_map/ppermute | solution.py:360
  49.8 7.9 %collective-permute-start.3 = (f32[2,36,512]{2,1,0:T(8,128)}, f32[2,36,512]{2,1,0:T(8,128)S(1)}, u32[]{:S(2)}, u32[]{:S(2)}) collective-permute-start(f32[2,36,512]{2,1,0:T(8,128)} %pad_maximum_fusion.1), channel_id=1, source_target_pairs={{1,0},{2,1},{3,2},{5,4},{6,5},{7,6},{9,8},{10,9},{11,10},{13,12},{... | collective-permute-start | bytes 442376 | tf_op jit(solution)/shard_map/ppermute | solution.py:360
  72.7 33.2 %all-to-all-start.2 = ((bf16[32,128,128]{2,1,0:T(8,128)(2,1)}), bf16[32,128,128]{2,1,0:T(8,128)(2,1)S(1)}, u32[]{:S(2)}, u32[]{:S(2)}) async-start(bf16[32,128,128]{2,1,0:T(8,128)(2,1)} %bitcast.12), calls=%async_computation.2 | async-start | bytes 2097152 | tf_op jit(solution)/shard_map/all_to_all | solution.py:401
  80.3 2.2 %copy-start.1 = (f32[32,64,512]{2,1,0:T(8,128)S(1)}, f32[32,64,512]{2,1,0:T(8,128)}, u32[]{:S(2)}) copy-start(f32[32,64,512]{2,1,0:T(8,128)} %field_ref.1) | copy-start | bytes 12582916
  93.3 2.0 %copy-start.4 = (f32[32,64,512]{2,1,0:T(8,128)}, f32[32,64,512]{2,1,0:T(8,128)S(1)}, u32[]{:S(2)}) copy-start(f32[32,64,512]{2,1,0:T(8,128)S(1)} %get-tuple-element.48) | copy-start | bytes 12582916
  95.3 1.9 %copy-start.5 = (f32[32,64,512]{2,1,0:T(8,128)}, f32[32,64,512]{2,1,0:T(8,128)S(1)}, u32[]{:S(2)}) copy-start(f32[32,64,512]{2,1,0:T(8,128)S(1)} %get-tuple-element.47) | copy-start | bytes 12582916

commit v4 on v3

v4 whole, which is shorter than its diff:
```python
import functools

import jax
import jax.numpy as jnp
from jax import lax
from jax.experimental import pallas as pl
from jax.experimental.pallas import tpu as pltpu
from jax.sharding import PartitionSpec as P

shift_kappa = 0.5
prior_weight = 0.05
step_rate = 2.0

LANES = 128
GROUP = 16
MIB = 1 << 20
MARK = 1 << 16

CONTRACT_LANES = (((1,), (1,)), ((), ()))


def split_by(value, size):
    if size & (size - 1) == 0:
        high = value >> (size.bit_length() - 1)
        return high, value & (size - 1)
    high = value // size
    return high, value - high * size


def route_kernel(
    ids_ref, outgoing_ref, position_ref, *, devices, capacity, first_slots, blocks, per_column
):
    half = ids_ref.shape[0] // 2
    ids = jnp.concatenate([ids_ref[:half, :], ids_ref[half:, :]], axis=1)
    lane = lax.broadcasted_iota(jnp.int32, (LANES, LANES), 1)
    row = lax.broadcasted_iota(jnp.int32, (LANES, LANES), 0)
    upper = jnp.where(row <= lane, 1.0, 0.0).astype(jnp.bfloat16)
    tile_no = lax.broadcasted_iota(jnp.int32, (devices, LANES), 0)
    slot_no = lax.broadcasted_iota(jnp.int32, (capacity, LANES), 0)
    before = jnp.zeros((devices, 1), jnp.float32)
    lists = jnp.zeros((2 * devices, capacity), jnp.float32)
    for chunk in range(half):
        target, local = split_by(ids[chunk : chunk + 1, :], blocks)
        column, part = split_by(local, per_column)
        local = ((column >> 3) * per_column + part) * 8 + (column & 7)
        hit = tile_no == target
        onehot = jnp.where(hit, 1.0, 0.0)
        upto = before + jnp.dot(
            onehot.astype(jnp.bfloat16), upper, preferred_element_type=jnp.float32
        )
        before = upto[:, LANES - 1 :]
        rank = jnp.sum(onehot * upto, axis=0, keepdims=True).astype(jnp.int32) - 1
        in_slot = jnp.where(slot_no == rank, 1.0, 0.0).astype(jnp.bfloat16)
        high = ((local >> 7) + 1).astype(jnp.float32)
        low = (local & 127).astype(jnp.float32)
        digits = jnp.concatenate([jnp.where(hit, high, 0.0), jnp.where(hit, low, 0.0)], axis=0)
        lists = lists + lax.dot_general(
            digits.astype(jnp.bfloat16),
            in_slot,
            CONTRACT_LANES,
            preferred_element_type=jnp.float32,
        )
        last_slots = capacity - first_slots
        position_ref[chunk : chunk + 1, :] = jnp.where(
            rank < first_slots,
            target * first_slots + rank,
            devices * first_slots + target * last_slots + rank - first_slots,
        )
    high, low = lists[:devices], lists[devices:]
    wanted = ((high - 1.0) * 128.0 + low).astype(jnp.int32)
    filled = before.astype(jnp.int32)
    me = lax.axis_index("gx") * lax.axis_size("gy") + lax.axis_index("gy")
    fullest = jnp.max(jnp.where(tile_no[:, :1] == me, 0.0, before), axis=0, keepdims=True)
    listed = jnp.where(high > 0.5, wanted, blocks + filled)
    if first_slots < capacity:
        slot = lax.broadcasted_iota(jnp.int32, (devices, capacity), 1)
        mark = fullest.astype(jnp.int32) * MARK
        listed = listed + jnp.where(slot == capacity - 1, mark, 0)
    outgoing_ref[...] = listed


def edges_kernel(field_ref, xfirst_ref, xlast_ref, yfirst_ref, ylast_ref):
    cells_x, cells_y, _ = field_ref.shape
    xfirst_ref[...] = field_ref[:2]
    xlast_ref[...] = field_ref[cells_x - 2 :]
    for h in range(2):
        for x in range(cells_x):
            yfirst_ref[h, x : x + 1, :] = field_ref[x, h : h + 1, :]
            ylast_ref[h, x : x + 1, :] = field_ref[x, cells_y - 2 + h : cells_y - 1 + h, :]


def for_each_group(incoming_ref, visit, capacity, first_slots, blocks):
    sources = incoming_ref.shape[0]
    last_slots = capacity - first_slots
    together = 4

    def groups_of(source):
        last = incoming_ref[source, capacity - 1] & (MARK - 1)
        return (jnp.where(last < blocks, capacity, last - blocks) + GROUP - 1) // GROUP

    def some_sources(quad, carry):
        own = [quad * together + i for i in range(together)]
        most = functools.reduce(jnp.maximum, [groups_of(source) for source in own])

        def one_group(group, carry):
            slot = pl.multiple_of(group * GROUP, GROUP)
            for source in own:
                wanted = [incoming_ref[source, slot + j] for j in range(GROUP)]
                visit(wanted, pl.multiple_of(source * first_slots + slot, GROUP))
            return carry

        return lax.fori_loop(0, jnp.minimum(most, first_slots // GROUP), one_group, carry)

    lax.fori_loop(0, sources // together, some_sources, 0)
    if last_slots == 0:
        return

    def one_source(source, carry):
        def one_group(group, carry):
            slot = pl.multiple_of(group * GROUP, GROUP)
            row = (sources - 1) * first_slots + source * last_slots + slot
            wanted = [incoming_ref[source, slot + j] & (MARK - 1) for j in range(GROUP)]
            visit(wanted, pl.multiple_of(row, GROUP))
            return carry

        return lax.fori_loop(first_slots // GROUP, groups_of(source), one_group, carry)

    lax.fori_loop(0, sources, one_source, 0)


def serve_kernel(incoming_ref, field_ref, *refs, capacity, first_slots):
    *served_refs, table_ref, rows_ref = refs
    cells_x, cells_y, depth = field_ref.shape
    per_column = depth // LANES
    table_rows = table_ref.reshape(table_ref.shape[0], LANES)
    blocks = cells_x * cells_y * per_column
    table_rows[blocks:, :] = jnp.zeros((table_ref.shape[0] - blocks, LANES), jnp.float32)

    def one_plane(x, carry):
        for yb in range(cells_y // 8):
            for part in range(per_column):
                at = pl.multiple_of(((x * (cells_y // 8) + yb) * per_column + part) * 8, 8)
                table_rows[pl.ds(at, 8), :] = jnp.exp(
                    field_ref[x, 8 * yb : 8 * yb + 8, part * LANES : (part + 1) * LANES]
                )
        return carry

    lax.fori_loop(0, cells_x, one_plane, 0)

    def visit(wanted, row):
        rows = [table_ref[at] for at in wanted]
        for j in range(GROUP):
            rows_ref[pl.ds(row + j, 1), :] = rows[j]

    for_each_group(incoming_ref, visit, capacity, first_slots, blocks)
    start = 0
    for served_ref in served_refs:
        size = served_ref.shape[0]
        served_ref[...] = rows_ref[start : start + size, :].astype(jnp.bfloat16)
        start += size


def match_kernel(incoming_ref, match_ref):
    lane = lax.broadcasted_iota(jnp.int32, (LANES, LANES), 1)
    row = lax.broadcasted_iota(jnp.int32, (LANES, LANES), 0)
    ones = jnp.ones((LANES, LANES), jnp.bfloat16)
    same_group = (lane // GROUP) == (row // GROUP)

    def one_row(i):
        wanted = incoming_ref[pl.ds(i, 1), :]
        high = jnp.where(lane == row, (wanted >> 7).astype(jnp.float32), 0.0).astype(jnp.bfloat16)
        low = jnp.where(lane == row, (wanted & 127).astype(jnp.float32), 0.0).astype(jnp.bfloat16)
        down = 128.0 * jnp.dot(high, ones, preferred_element_type=jnp.float32)
        down = down + jnp.dot(low, ones, preferred_element_type=jnp.float32)
        same = (down == wanted.astype(jnp.float32)) & same_group
        match_ref[pl.ds(pl.multiple_of(i * LANES, LANES), LANES), :] = jnp.where(
            same, 1.0, 0.0
        ).astype(jnp.bfloat16)

    def some_rows(i, carry):
        for j in range(4):
            one_row(4 * i + j)
        return carry

    lax.fori_loop(0, incoming_ref.shape[0] // 4, some_rows, 0)


def star_kernel(position_ref, observed_ref, inverse_ref, weights_hbm, *refs, exchanges):
    returned_refs, refs = refs[:exchanges], refs[exchanges:]
    extinction_ref, refs = refs[0], refs[1:]
    parcel_refs, refs = refs[:exchanges], refs[exchanges:]
    weights_ref, returned_rows, fetched_ref, sens_ref, parcel_rows, sems = refs
    blocks_dev, slots, stars, width = weights_ref.shape
    chunks = sems.shape[0]
    per = blocks_dev // chunks
    half = position_ref.shape[0]
    fold = LANES // stars
    all_slots = parcel_rows.shape[0]
    lane = lax.broadcasted_iota(jnp.int32, (8, LANES), 1)
    row = lax.broadcasted_iota(jnp.int32, (8, LANES), 0)
    own_slot = [row == lane // stars + fold * h for h in range(8 // fold)]

    def load(chunk):
        span = pl.ds(chunk * per, per)
        return pltpu.make_async_copy(weights_hbm.at[span], weights_ref.at[span], sems.at[chunk])

    def place(block, slot):
        return position_ref[slot % half, (slot // half) * blocks_dev + block]

    def start_of(chunk):
        return pl.multiple_of(chunk * per * slots, per * slots)

    def matrix_of(chunk, b):
        eights = [weights_ref[chunk * per + b, 8 * j : 8 * j + 8] for j in range(slots // 8)]
        return jnp.concatenate([x.reshape(8 * stars, width) for x in eights], axis=1)

    def gather(chunk):
        rows = [returned_rows[place(chunk * per + b, k)] for b in range(per) for k in range(slots)]
        for i, value in enumerate(rows):
            fetched_ref[pl.ds(start_of(chunk) + i, 1), :] = value

    def extinctions(chunk):
        weighted = []
        for b in range(per):
            left = jnp.concatenate(
                [
                    fetched_ref[pl.ds(start_of(chunk) + b * slots + 8 * j, 8), :]
                    for j in range(slots // 8)
                ],
                axis=1,
            )
            total = lax.dot_general(
                left.astype(jnp.bfloat16),
                matrix_of(chunk, b),
                CONTRACT_LANES,
                preferred_element_type=jnp.float32,
            )
            folded = jnp.zeros((8, LANES), jnp.float32)
            for h, own in enumerate(own_slot):
                folded = folded + jnp.where(own, total[:, h * LANES : (h + 1) * LANES], 0.0)
            extinction = jnp.sum(folded, axis=0, keepdims=True)
            shift = stars
            while shift < LANES:
                extinction = extinction + pltpu.roll(extinction, shift, 1)
                shift *= 2
            here = pl.ds(chunk * per + b, 1)
            extinction_ref[here, :] = extinction
            weighted.append(inverse_ref[here, :] * (extinction - observed_ref[here, :]))
        return weighted

    def sensitivities(chunk, weighted):
        for b in range(per):
            left = jnp.concatenate(
                [jnp.where(own, weighted[b], 0.0) for own in own_slot], axis=1
            ).astype(jnp.bfloat16)
            sens = jnp.dot(left, matrix_of(chunk, b), preferred_element_type=jnp.float32)
            for j in range(slots // 8):
                sens_ref[pl.ds(start_of(chunk) + b * slots + 8 * j, 8), :] = sens[
                    :, j * width : (j + 1) * width
                ]

    def scatter(chunk):
        for b in range(per):
            for k in range(slots):
                at = pl.ds(start_of(chunk) + b * slots + k, 1)
                parcel_rows[place(chunk * per + b, k)] = sens_ref[at, :]

    for chunk in range(chunks):
        load(chunk).start()
    start = 0
    for returned_ref in returned_refs:
        span = slice(start, start + returned_ref.shape[0])
        returned_rows.reshape(all_slots, width)[span, :] = returned_ref[...].astype(jnp.float32)
        start = span.stop
    parcel_rows.reshape(all_slots, width)[...] = jnp.zeros((all_slots, width), jnp.float32)
    gather(0)
    load(0).wait()
    weighted = extinctions(0)
    gather(1)
    load(1).wait()
    following = extinctions(1)
    sensitivities(0, weighted)
    gather(2)

    def step(chunk, weighted):
        load(chunk).wait()
        following = extinctions(chunk)
        sensitivities(chunk - 1, weighted)
        scatter(chunk - 2)
        gather(jnp.minimum(chunk + 1, chunks - 1))
        return following

    weighted = lax.fori_loop(2, chunks, step, following)
    sensitivities(chunks - 1, weighted)
    scatter(chunks - 2)
    scatter(chunks - 1)
    start = 0
    for parcel_ref in parcel_refs:
        span = slice(start, start + parcel_ref.shape[0])
        parcel_ref[...] = parcel_rows.reshape(all_slots, width)[span, :].astype(jnp.bfloat16)
        start = span.stop


def prior_kernel(field_ref, xlo_ref, xhi_ref, ylo_ref, yhi_ref, out_ref, padded, smooth):
    cells_x, cells_y, depth = field_ref.shape
    rows = padded.shape[1]
    gx, gy = lax.axis_index("gx"), lax.axis_index("gy")
    last_gx, last_gy = lax.axis_size("gx") - 1, lax.axis_size("gy") - 1
    z = lax.broadcasted_iota(jnp.int32, (rows, depth), 1)
    y = lax.broadcasted_iota(jnp.int32, (rows, depth), 0) - 8
    inside_y = ((y >= 0) | (gy > 0)) & ((y < cells_y) | (gy < last_gy))

    def operate(center, below, above):
        beside = below + above
        beside = beside + pltpu.roll(center, 1, 0) + pltpu.roll(center, rows - 1, 0)
        beside = beside + jnp.where(z == 0, 0.0, pltpu.roll(center, 1, 1))
        beside = beside + jnp.where(z == depth - 1, 0.0, pltpu.roll(center, depth - 1, 1))
        return (shift_kappa + 6.0) * center - beside

    def fill(plane, source):
        padded[plane, 8 : 8 + cells_y, :] = source
        padded[plane, 0:8, :] = jnp.zeros((8, depth), jnp.float32)
        padded[plane, 8 + cells_y :, :] = jnp.zeros((8, depth), jnp.float32)
        for h in range(2):
            padded[plane, 6 + h : 7 + h, :] = ylo_ref[h, pl.ds(plane, 1), :]
            padded[plane, 8 + cells_y + h : 9 + cells_y + h, :] = yhi_ref[h, pl.ds(plane, 1), :]

    for h in range(2):
        fill(h, xlo_ref[h])
        fill(cells_x + 2 + h, xhi_ref[h])

    def fill_own(x, carry):
        fill(x + 2, field_ref[x])
        return carry

    lax.fori_loop(0, cells_x, fill_own, 0)

    def smooth_plane(plane, carry):
        value = operate(padded[plane], padded[plane - 1], padded[plane + 1])
        inside = ((plane > 1) | (gx > 0)) & ((plane < cells_x + 2) | (gx < last_gx))
        smooth[plane - 1] = jnp.where(inside_y & inside, value, 0.0)
        return carry

    lax.fori_loop(1, cells_x + 3, smooth_plane, 0)

    def out_plane(x, carry):
        prior = operate(smooth[x + 1], smooth[x], smooth[x + 2])
        out_ref[x] = field_ref[x] - (step_rate * prior_weight) * prior[8 : 8 + cells_y]
        return carry

    lax.fori_loop(0, cells_x, out_plane, 0)


def finish_kernel(
    incoming_ref, match_ref, field_hbm, base_hbm, *refs, exchanges, capacity, first_slots
):
    arrived_refs, refs = refs[:exchanges], refs[exchanges:]
    out_hbm, collected, rows_ref, field_ref, base_ref, out_ref, in_sems, out_sems = refs
    cells_x, cells_y, depth = field_ref.shape
    per_column = depth // LANES
    parts = out_sems.shape[0]
    planes = cells_x // parts
    blocks = cells_x * cells_y * per_column
    loads = [
        pltpu.make_async_copy(field_hbm, field_ref, in_sems.at[0]),
        pltpu.make_async_copy(base_hbm, base_ref, in_sems.at[1]),
    ]
    for load in loads:
        load.start()
    collected_rows = collected.reshape(collected.shape[0], LANES)
    start = 0
    for arrived_ref in arrived_refs:
        for i in range(arrived_ref.shape[0] // LANES):
            span = slice(start + i * LANES, start + (i + 1) * LANES)
            rows_ref[span, :] = -step_rate * jnp.dot(
                match_ref[span, :],
                arrived_ref[i * LANES : (i + 1) * LANES, :],
                preferred_element_type=jnp.float32,
            )
        start += arrived_ref.shape[0]
    collected_rows[...] = jnp.zeros_like(collected_rows)

    def visit(wanted, row):
        sums = [collected[wanted[j]] + rows_ref[pl.ds(row + j, 1), :] for j in range(GROUP)]
        for j in range(GROUP):
            collected[wanted[j]] = sums[j]

    for_each_group(incoming_ref, visit, capacity, first_slots, blocks)
    for load in loads:
        load.wait()

    def store(part):
        span = pl.ds(part * planes, planes)
        return pltpu.make_async_copy(out_ref.at[span], out_hbm.at[span], out_sems.at[part])

    def one_plane(x, carry):
        for yb in range(cells_y // 8):
            for part in range(per_column):
                at = pl.multiple_of(((x * (cells_y // 8) + yb) * per_column + part) * 8, 8)
                here = (x, slice(8 * yb, 8 * yb + 8), slice(part * LANES, (part + 1) * LANES))
                out_ref[here] = base_ref[here] + collected_rows[pl.ds(at, 8), :] * jnp.exp(
                    field_ref[here]
                )
        return carry

    for part in range(parts):
        lax.fori_loop(part * planes, (part + 1) * planes, one_plane, 0)
        store(part).start()
    for part in range(parts):
        store(part).wait()


def both_ways(first, last, axis):
    peers = lax.axis_size(axis)
    up = [(i, i + 1) for i in range(peers - 1)]
    down = [(j, i) for i, j in up]
    return lax.ppermute(last, axis, up), lax.ppermute(first, axis, down)


def halo_y(xlo, xhi, yfirst, ylast):
    def rows(own, at):
        return jnp.concatenate(
            [xlo[:, at].transpose(1, 0, 2), own, xhi[:, at].transpose(1, 0, 2)], axis=1
        )

    return both_ways(rows(yfirst, slice(0, 2)), rows(ylast, slice(-2, None)), "gy")


VMEM = pl.BlockSpec(memory_space=pltpu.VMEM)
SMEM = pl.BlockSpec(memory_space=pltpu.SMEM)
ANY = pl.BlockSpec(memory_space=pl.ANY)


def on_device(log_density, weights, observed, inverse_var, star_counts, block_ids):
    cells_x, cells_y, depth = log_density.shape
    blocks_dev, slots, stars, width = weights.shape
    devices = lax.axis_size("gx") * lax.axis_size("gy")
    requests = blocks_dev * slots
    capacity = 2 * requests // devices
    first_slots = min(capacity, -(-3 * capacity // (4 * GROUP)) * GROUP)
    slots_of = [n for n in (first_slots, capacity - first_slots) if n > 0]
    exchanges = len(slots_of)
    all_slots = devices * capacity
    per_column = depth // width
    blocks = cells_x * cells_y * per_column
    cells = log_density.size
    field_shape = (cells_x, cells_y, depth)
    mesh_axes = ("gx", "gy")
    f32, bf16, i32 = jnp.float32, jnp.bfloat16, jnp.int32
    shape = jax.ShapeDtypeStruct

    def exchange(x):
        return lax.all_to_all(x, mesh_axes, split_axis=0, concat_axis=0, tiled=True)

    def exchange_rows(parts, crowded):
        moved = [parts[0].reshape(devices, first_slots, width)]
        moved[0] = exchange(moved[0])
        for part in parts[1:]:
            part = part.reshape(devices, capacity - first_slots, width)
            moved.append(lax.cond(crowded, exchange, lambda x: x, part))
        return [x.reshape(-1, width) for x in moved]

    outgoing, position = pl.pallas_call(
        functools.partial(
            route_kernel,
            devices=devices,
            capacity=capacity,
            first_slots=first_slots,
            blocks=blocks,
            per_column=per_column,
        ),
        out_shape=[shape((devices, capacity), i32), shape((requests // LANES, LANES), i32)],
        in_specs=[VMEM],
        out_specs=[VMEM, VMEM],
        name="route",
    )(block_ids.T)
    incoming = exchange(outgoing)

    field, _ = lax.optimization_barrier((log_density, outgoing))
    xfirst, xlast, yfirst, ylast = pl.pallas_call(
        edges_kernel,
        out_shape=[
            shape((2, cells_y, depth), f32),
            shape((2, cells_y, depth), f32),
            shape((2, cells_x, depth), f32),
            shape((2, cells_x, depth), f32),
        ],
        in_specs=[VMEM],
        out_specs=[VMEM] * 4,
        compiler_params=pltpu.CompilerParams(vmem_limit_bytes=8 * MIB),
        cost_estimate=pl.CostEstimate(flops=0, bytes_accessed=2 * MIB, transcendentals=0),
        name="edges",
    )(field)
    xlo, xhi = both_ways(xfirst, xlast, "gx")

    served = pl.pallas_call(
        functools.partial(serve_kernel, capacity=capacity, first_slots=first_slots),
        out_shape=[shape((devices * n, width), bf16) for n in slots_of],
        in_specs=[SMEM, VMEM],
        out_specs=[VMEM] * exchanges,
        scratch_shapes=[
            pltpu.VMEM((blocks + capacity, 1, width), f32),
            pltpu.VMEM((all_slots, width), f32),
        ],
        compiler_params=pltpu.CompilerParams(vmem_limit_bytes=24 * MIB),
        cost_estimate=pl.CostEstimate(
            flops=cells, bytes_accessed=6 * MIB, transcendentals=cells
        ),
        name="serve",
    )(incoming, field)
    crowded = jnp.max(incoming[:, capacity - 1]) >= (first_slots + 1) * MARK
    returned = exchange_rows(served, crowded)

    incoming_late, xlo, xhi, yfirst, ylast, _ = lax.optimization_barrier(
        (incoming, xlo, xhi, yfirst, ylast, served[0])
    )
    sides = halo_y(xlo, xhi, yfirst, ylast)
    slot_lists = [
        incoming_late[:, :first_slots].reshape(-1, LANES),
        (incoming_late[:, first_slots:] & (MARK - 1)).reshape(-1, LANES),
    ][:exchanges]
    match = pl.pallas_call(
        match_kernel,
        out_shape=shape((all_slots, LANES), bf16),
        in_specs=[VMEM],
        out_specs=VMEM,
        compiler_params=pltpu.CompilerParams(vmem_limit_bytes=8 * MIB),
        cost_estimate=pl.CostEstimate(flops=10**9, bytes_accessed=MIB, transcendentals=0),
        name="match",
    )(jnp.concatenate(slot_lists, axis=0))
    *returned, match, xlo, xhi, ylo, yhi = lax.optimization_barrier(
        (*returned, match, xlo, xhi, *sides)
    )

    chunks = blocks_dev * stars // LANES
    live = jnp.arange(stars)[None, :] < star_counts[:, None]
    live_inverse = jnp.where(live, inverse_var, 0.0)
    extinction, *parcel = pl.pallas_call(
        functools.partial(star_kernel, exchanges=exchanges),
        out_shape=[shape((blocks_dev, LANES), f32)]
        + [shape((devices * n, width), bf16) for n in slots_of],
        in_specs=[SMEM, VMEM, VMEM, ANY] + [VMEM] * exchanges,
        out_specs=[VMEM] * (1 + exchanges),
        scratch_shapes=[
            pltpu.VMEM(weights.shape, bf16),
            pltpu.VMEM((all_slots, 1, width), f32),
            pltpu.VMEM((requests, width), f32),
            pltpu.VMEM((requests, width), f32),
            pltpu.VMEM((all_slots, 1, width), f32),
            pltpu.SemaphoreType.DMA((chunks,)),
        ],
        compiler_params=pltpu.CompilerParams(vmem_limit_bytes=50 * MIB),
        cost_estimate=pl.CostEstimate(
            flops=4 * weights.size, bytes_accessed=2 * weights.size, transcendentals=0
        ),
        name="stars",
    )(
        position,
        jnp.tile(observed, (1, LANES // stars)),
        jnp.tile(live_inverse, (1, LANES // stars)),
        weights,
        *returned,
    )
    arrived = exchange_rows(parcel, crowded)

    field_late, _ = lax.optimization_barrier((log_density, parcel[0]))
    base = pl.pallas_call(
        prior_kernel,
        out_shape=shape(field_shape, f32),
        in_specs=[VMEM] * 5,
        out_specs=VMEM,
        scratch_shapes=[
            pltpu.VMEM((cells_x + 4, cells_y + 16, depth), f32),
            pltpu.VMEM((cells_x + 2, cells_y + 16, depth), f32),
        ],
        compiler_params=pltpu.CompilerParams(vmem_limit_bytes=32 * MIB),
        cost_estimate=pl.CostEstimate(
            flops=30 * cells, bytes_accessed=8 * cells, transcendentals=0
        ),
        name="prior",
    )(field_late, xlo, xhi, ylo, yhi)

    parts = 8
    new_log_density = pl.pallas_call(
        functools.partial(
            finish_kernel, exchanges=exchanges, capacity=capacity, first_slots=first_slots
        ),
        out_shape=shape(field_shape, f32),
        in_specs=[SMEM, VMEM, ANY, ANY] + [VMEM] * exchanges,
        out_specs=ANY,
        scratch_shapes=[
            pltpu.VMEM((blocks + capacity, 1, width), f32),
            pltpu.VMEM((all_slots, width), f32),
            pltpu.VMEM(field_shape, f32),
            pltpu.VMEM(field_shape, f32),
            pltpu.VMEM(field_shape, f32),
            pltpu.SemaphoreType.DMA((2,)),
            pltpu.SemaphoreType.DMA((parts,)),
        ],
        compiler_params=pltpu.CompilerParams(vmem_limit_bytes=50 * MIB),
        cost_estimate=pl.CostEstimate(
            flops=4 * cells, bytes_accessed=12 * cells, transcendentals=cells
        ),
        name="finish",
    )(incoming, match, log_density, base, *arrived)
    return new_log_density, extinction[:, :stars]


def solution(mesh):
    placed = (
        P("gx", "gy", None),
        P(("gx", "gy"), None, None, None),
        P(("gx", "gy"), None),
        P(("gx", "gy"), None),
        P(("gx", "gy")),
        P(("gx", "gy"), None),
    )
    return jax.shard_map(
        on_device,
        mesh=mesh,
        in_specs=placed,
        out_specs=(P("gx", "gy", None), P(("gx", "gy"), None)),
        check_vma=False,
    )
```

time: 122 us -> 112 us (0.918)
  waiting for transfers between devices: 24.9 us -> 18.4 us
  local copies, waits for them, and re-layouts: 13.9 us -> 9.99 us
  starting transfers between devices: 26.9 us -> 30.6 us
  Pallas kernels: 53.6 us -> 50.2 us
    ppermute x4, waiting for transfers between devices: 14 us -> 6.63 us  [both_ways(): return (lax.ppermute(last, axis, up), lax.ppermute(first, axis, down))]
    unnamed x21 -> x17, local copies, waits for them, and re-layouts: 13.2 us -> 9.19 us
    pallas_call x5, Pallas kernels: 48.7 us -> 45.3 us  [the longest x1 14.1 us: on_device(): pl.pallas_call(functools.partial(star_kernel, exchanges=exchanges), out_s...]
    ppermute x4, starting transfers between devices: 8.51 us -> 11.9 us  [both_ways(): return (lax.ppermute(last, axis, up), lax.ppermute(first, axis, down))]
  transfers between devices with their start and end apart: 7 -> 7, of which waited for: 5 -> 4; matrix products, arithmetic and copies ran while one was open for 2% -> 1% of each run, Pallas kernels for 11% -> 11%
where the time goes in v4:
time: 112 us
  Pallas kernels  50.2 us (45%)
  starting transfers between devices  30.6 us (27%)
  waiting for transfers between devices  18.4 us (16%)
  local copies, waits for them, and re-layouts  9.99 us (9%)
  between operations  1.52 us (1%)
    all_to_all x3, starting transfers between devices, exchange(): return lax.all_to_all(x, mesh_axes, split_axis=0, concat_axis=0, tiled=True)  18.7 us
    pallas_call x1, Pallas kernels, on_device(): pl.pallas_call(functools.partial(star_kernel, exchanges=exchanges), out_s...  14.1 us
    ppermute x4, starting transfers between devices, both_ways(): return (lax.ppermute(last, axis, up), lax.ppermute(first, axis, down))  11.9 us
    all_to_all x3, waiting for transfers between devices, exchange(): return lax.all_to_all(x, mesh_axes, split_axis=0, concat_axis=0, tiled=True)  11.8 us
    pallas_call x1, Pallas kernels, on_device(): pl.pallas_call(functools.partial(finish_kernel, exchanges=exchanges, capa...  11.5 us
    pallas_call x1, Pallas kernels, on_device(): pl.pallas_call(prior_kernel, out_shape=shape(field_shape, f32), in_specs=...  10.7 us
    unnamed x17, local copies, waits for them, and re-layouts  9.19 us
    pallas_call x1, Pallas kernels, on_device(): pl.pallas_call(functools.partial(serve_kernel, capacity=capacity, first_s...  8.86 us
  transfers between devices with their start and end apart: 7, of which 4 were waited for; matrix products, arithmetic and copies ran while one was open for 1% of the time, Pallas kernels for 11%

profile of v4, /device:TPU:1, one launch (start us, length us, event | category | flops | bytes accessed | tf_op | source)
XLA Modules:
  0.0 111.5 jit_solution(15013548484327682166)
XLA Ops:
  0.6 3.1 %route.1 = (s32[32,128]{1,0:T(8,128)}, s32[16,128]{1,0:T(8,128)}) custom-call(s32[32,64]{1,0:T(8,128)} %bitcast.41), custom_call_target="tpu_custom_call" | custom-call | tf_op jit(solution)/shard_map/route/pallas_call | solution.py:463
  3.7 7.1 %all-to-all-start.2 = ((s32[32,1,128]{2,1,0:T(1,128)}), s32[32,1,128]{2,1,0:T(1,128)S(1)}, u32[]{:S(2)}, u32[]{:S(2)}) async-start(s32[32,1,128]{2,1,0:T(1,128)} %bitcast.42), calls=%async_computation.2 | async-start | bytes 32768 | tf_op jit(solution)/shard_map/all_to_all | solution.py:453
  10.8 6.6 %all-to-all-done.2 = s32[32,1,128]{2,1,0:T(1,128)S(1)} async-done(((s32[32,1,128]{2,1,0:T(1,128)}), s32[32,1,128]{2,1,0:T(1,128)S(1)}, u32[]{:S(2)}, u32[]{:S(2)}) %all-to-all-start.2) | async-done | bytes 16416 | tf_op jit(solution)/shard_map/all_to_all | solution.py:453
  17.4 0.7 slice_reduce_fusion
  18.8 2.2 %copy-done = f32[32,64,512]{2,1,0:T(8,128)S(1)} copy-done((f32[32,64,512]{2,1,0:T(8,128)S(1)}, f32[32,64,512]{2,1,0:T(8,128)}, u32[]{:S(2)}) %copy-start) | copy-done | bytes 4194328
  21.0 8.9 %serve.1 = (bf16[3072,128]{1,0:T(8,128)(2,1)}, bf16[1024,128]{1,0:T(8,128)(2,1)S(1)}) custom-call(s32[32,128]{1,0:T(8,128)S(1)} %bitcast.28, f32[32,64,512]{2,1,0:T(8,128)S(1)} %copy-done), custom_call_target="tpu_custom_call" | custom-call | flops 1048576 | bytes 6291456 | tf_op jit(solution)/shard_map/serve/pallas_call | solution.py:496
  29.8 3.4 %all-to-all-start.3 = ((bf16[32,96,128]{2,1,0:T(8,128)(2,1)}), bf16[32,96,128]{2,1,0:T(8,128)(2,1)S(1)}, u32[]{:S(2)}, u32[]{:S(2)}) async-start(bf16[32,96,128]{2,1,0:T(8,128)(2,1)} %bitcast.4), calls=%async_computation.3 | async-start | bytes 1572864 | tf_op jit(solution)/shard_map/all_to_all | solution.py:453
  33.2 2.2 %copy-done.1 = f32[32,64,512]{2,1,0:T(8,128)S(1)} copy-done((f32[32,64,512]{2,1,0:T(8,128)S(1)}, f32[32,64,512]{2,1,0:T(8,128)}, u32[]{:S(2)}) %copy-start.1) | copy-done | bytes 4194328
  35.4 0.1 edges.1
  35.5 0.2 copy.24
  35.7 2.3 %collective-permute-start.1 = (f32[2,64,512]{2,0,1:T(2,128)S(1)}, f32[2,64,512]{2,0,1:T(2,128)S(1)}, u32[]{:S(2)}, u32[]{:S(2)}) collective-permute-start(f32[2,64,512]{2,0,1:T(2,128)S(1)} %copy.24), channel_id=1, source_target_pairs={{4,0},{8,4},{12,8},{16,12},{20,16},{24,20},{28,24},{5,1},{9,5},{13... | collective-permute-start | bytes 786440 | tf_op jit(solution)/shard_map/ppermute | solution.py:417
  38.1 0.2 copy.23
  38.3 3.3 %collective-permute-start = (f32[2,64,512]{2,0,1:T(2,128)S(1)}, f32[2,64,512]{2,0,1:T(2,128)S(1)}, u32[]{:S(2)}, u32[]{:S(2)}) collective-permute-start(f32[2,64,512]{2,0,1:T(2,128)S(1)} %copy.23), channel_id=1, source_target_pairs={{0,4},{4,8},{8,12},{12,16},{16,20},{20,24},{24,28},{1,5},{5,9},{9,... | collective-permute-start | bytes 786440 | tf_op jit(solution)/shard_map/ppermute | solution.py:417
  41.6 0.1 copy.26.inverse_ref
  41.7 0.1 copy.25.observed_ref
  41.7 3.6 %collective-permute-done.1 = f32[2,64,512]{2,0,1:T(2,128)S(1)} collective-permute-done((f32[2,64,512]{2,0,1:T(2,128)S(1)}, f32[2,64,512]{2,0,1:T(2,128)S(1)}, u32[]{:S(2)}, u32[]{:S(2)}) %collective-permute-start.1) | collective-permute-done | bytes 262176 | tf_op jit(solution)/shard_map/ppermute | solution.py:417
  45.4 0.1 reshape.67
  45.5 0.1 slice_and_fusion
  45.6 0.1 reshape.68
  45.7 5.0 %collective-permute-start.2 = (f32[2,36,512]{2,1,0:T(8,128)S(1)}, f32[2,36,512]{2,1,0:T(8,128)S(1)}, u32[]{:S(2)}, u32[]{:S(2)}) collective-permute-start(f32[2,36,512]{2,1,0:T(8,128)S(1)} %pad_maximum_fusion), channel_id=1, source_target_pairs={{0,1},{1,2},{2,3},{4,5},{5,6},{6,7},{8,9},{9,10},{10,11},{12,13},{... | collective-permute-start | bytes 442376 | tf_op jit(solution)/shard_map/ppermute | solution.py:417
  50.8 1.3 %collective-permute-start.3 = (f32[2,36,512]{2,1,0:T(8,128)S(1)}, f32[2,36,512]{2,1,0:T(8,128)S(1)}, u32[]{:S(2)}, u32[]{:S(2)}) collective-permute-start(f32[2,36,512]{2,1,0:T(8,128)S(1)} %pad_maximum_fusion.1), channel_id=1, source_target_pairs={{1,0},{2,1},{3,2},{5,4},{6,5},{7,6},{9,8},{10,9},{11,10},{13,12},{... | collective-permute-start | bytes 442376 | tf_op jit(solution)/shard_map/ppermute | solution.py:417
  52.1 1.8 %match.1.match_ref = bf16[4096,128]{1,0:T(8,128)(2,1)S(1)} custom-call(s32[32,128]{1,0:T(8,128)S(1)} %pad_add_fusion.incoming_ref), custom_call_target="tpu_custom_call" | custom-call | flops 1000000000 | bytes 1048576 | tf_op jit(solution)/shard_map/match/pallas_call | solution.py:522
  53.9 3.0 %collective-permute-done.3.yhi_ref = f32[2,36,512]{2,1,0:T(8,128)S(1)} collective-permute-done((f32[2,36,512]{2,1,0:T(8,128)S(1)}, f32[2,36,512]{2,1,0:T(8,128)S(1)}, u32[]{:S(2)}, u32[]{:S(2)}) %collective-permute-start.3) | collective-permute-done | bytes 147488 | tf_op jit(solution)/shard_map/ppermute | solution.py:417
  56.8 14.1 %stars.1 = (f32[64,128]{1,0:T(8,128)S(1)}, bf16[3072,128]{1,0:T(8,128)(2,1)}, bf16[1024,128]{1,0:T(8,128)(2,1)S(1)}) custom-call(s32[16,128]{1,0:T(8,128)S(1)} %copy-done.4, f32[64,128]{1,0:T(8,128)S(1)} %copy.25.observed_ref, f32[64,128]{1,0:T(8,128)S(1)} %copy.26.inverse_ref, bf16[64,32,32,128]{3,2,1,0:T(8,128)(2,1)} %weights_hbm.1, ...), custom_call_target="tpu_custom_call" | custom-call | flops 33554432 | bytes 16777216 | tf_op jit(solution)/shard_map/stars/pallas_call | solution.py:538
  71.0 8.2 %all-to-all-start.4 = ((bf16[32,96,128]{2,1,0:T(8,128)(2,1)}), bf16[32,96,128]{2,1,0:T(8,128)(2,1)S(1)}, u32[]{:S(2)}, u32[]{:S(2)}) async-start(bf16[32,96,128]{2,1,0:T(8,128)(2,1)} %bitcast.14), calls=%async_computation.4 | async-start | bytes 1572864 | tf_op jit(solution)/shard_map/all_to_all | solution.py:453
  79.3 0.1 copy.28.xhi_ref
  79.3 0.7 copy.29
  80.0 2.2 %copy-done.2 = f32[32,64,512]{2,1,0:T(8,128)S(1)} copy-done((f32[32,64,512]{2,1,0:T(8,128)S(1)}, f32[32,64,512]{2,1,0:T(8,128)}, u32[]{:S(2)}) %copy-start.2) | copy-done | bytes 4194328
  82.2 10.7 %prior.1.base_hbm = f32[32,64,512]{2,1,0:T(8,128)S(1)} custom-call(f32[32,64,512]{2,1,0:T(8,128)S(1)} %copy-done.2, f32[2,64,512]{2,1,0:T(8,128)S(1)} %copy.27.xlo_ref, f32[2,64,512]{2,1,0:T(8,128)S(1)} %copy.28.xhi_ref, f32[2,36,512]{2,1,0:T(8,128)S(1)} %collective-permute-done.2.ylo_ref, f32[2,36,512]{2,1,0:T(8,128)S(1)} %collective-permute-done.3.yhi_ref), custom_call_target="tpu_custom_call" | custom-call | flops 31457280 | bytes 8388608 | tf_op jit(solution)/shard_map/prior/pallas_call | solution.py:567
  93.0 1.9 %copy-done.3 = f32[32,64,512]{2,1,0:T(8,128)} copy-done((f32[32,64,512]{2,1,0:T(8,128)}, f32[32,64,512]{2,1,0:T(8,128)S(1)}, u32[]{:S(2)}) %copy-start.3) | copy-done | bytes 4194328
  94.9 5.2 %all-to-all-done.4 = bf16[32,96,128]{2,1,0:T(8,128)(2,1)S(1)} async-done(((bf16[32,96,128]{2,1,0:T(8,128)(2,1)}), bf16[32,96,128]{2,1,0:T(8,128)(2,1)S(1)}, u32[]{:S(2)}, u32[]{:S(2)}) %all-to-all-start.4) | async-done | bytes 786464 | tf_op jit(solution)/shard_map/all_to_all | solution.py:453
  100.0 11.5 %finish.1 = f32[32,64,512]{2,1,0:T(8,128)} custom-call(s32[32,128]{1,0:T(8,128)S(1)} %bitcast.31, bf16[4096,128]{1,0:T(8,128)(2,1)S(1)} %match.1.match_ref, f32[32,64,512]{2,1,0:T(8,128)} %field_hbm.1, f32[32,64,512]{2,1,0:T(8,128)} %copy-done.3, bf16[3072,128]{1,0:T(8,128)(2,1)S(1)} %bitcast.26, bf16[1024,128]{1,0:T(8,128)(2,1)S(1)} %bitcast.35), custom_call_target="tpu_custom_call" | custom-call | flops 4194304 | bytes 12582912 | tf_op jit(solution)/shard_map/finish/pallas_call | solution.py:584
  (25 shorter events, 0.2 us)
Async XLA Ops:
  3.7 13.7 %all-to-all-start.2 = ((s32[32,1,128]{2,1,0:T(1,128)}), s32[32,1,128]{2,1,0:T(1,128)S(1)}, u32[]{:S(2)}, u32[]{:S(2)}) async-start(s32[32,1,128]{2,1,0:T(1,128)} %bitcast.42), calls=%async_computation.2 | async-start | bytes 32768 | tf_op jit(solution)/shard_map/all_to_all | solution.py:453
  18.8 2.2 %copy-start = (f32[32,64,512]{2,1,0:T(8,128)S(1)}, f32[32,64,512]{2,1,0:T(8,128)}, u32[]{:S(2)}) copy-start(f32[32,64,512]{2,1,0:T(8,128)} %field_hbm.1) | copy-start | bytes 12582916
  29.8 11.7 %copy-start.6 = (f32[64,32]{0,1:T(8,128)S(1)}, f32[64,32]{0,1:T(8,128)}, u32[]{:S(2)}) copy-start(f32[64,32]{0,1:T(8,128)} %param.13) | copy-start | bytes 24580
  29.8 11.7 %copy-start.7 = (s32[64]{0:T(128)S(1)}, s32[64]{0:T(128)}, u32[]{:S(2)}) copy-start(s32[64]{0:T(128)} %param.14) | copy-start | bytes 772
  29.8 11.8 %copy-start.5 = (f32[64,32]{0,1:T(8,128)S(1)}, f32[64,32]{0,1:T(8,128)}, u32[]{:S(2)}) copy-start(f32[64,32]{0,1:T(8,128)} %param.12) | copy-start | bytes 24580
  29.8 27.0 %all-to-all-start.3 = ((bf16[32,96,128]{2,1,0:T(8,128)(2,1)}), bf16[32,96,128]{2,1,0:T(8,128)(2,1)S(1)}, u32[]{:S(2)}, u32[]{:S(2)}) async-start(bf16[32,96,128]{2,1,0:T(8,128)(2,1)} %bitcast.4), calls=%async_computation.3 | async-start | bytes 1572864 | tf_op jit(solution)/shard_map/all_to_all | solution.py:453
  33.2 2.2 %copy-start.1 = (f32[32,64,512]{2,1,0:T(8,128)S(1)}, f32[32,64,512]{2,1,0:T(8,128)}, u32[]{:S(2)}) copy-start(f32[32,64,512]{2,1,0:T(8,128)} %field_hbm.1) | copy-start | bytes 12582916
  35.4 21.4 %copy-start.4 = (s32[16,128]{1,0:T(8,128)S(1)}, s32[16,128]{1,0:T(8,128)}, u32[]{:S(2)}) copy-start(s32[16,128]{1,0:T(8,128)} %get-tuple-element.63.position_ref) | copy-start | bytes 24580
  35.7 9.6 %collective-permute-start.1 = (f32[2,64,512]{2,0,1:T(2,128)S(1)}, f32[2,64,512]{2,0,1:T(2,128)S(1)}, u32[]{:S(2)}, u32[]{:S(2)}) collective-permute-start(f32[2,64,512]{2,0,1:T(2,128)S(1)} %copy.24), channel_id=1, source_target_pairs={{4,0},{8,4},{12,8},{16,12},{20,16},{24,20},{28,24},{5,1},{9,5},{13... | collective-permute-start | bytes 786440 | tf_op jit(solution)/shard_map/ppermute | solution.py:417
  38.3 7.2 %collective-permute-start = (f32[2,64,512]{2,0,1:T(2,128)S(1)}, f32[2,64,512]{2,0,1:T(2,128)S(1)}, u32[]{:S(2)}, u32[]{:S(2)}) collective-permute-start(f32[2,64,512]{2,0,1:T(2,128)S(1)} %copy.23), channel_id=1, source_target_pairs={{0,4},{4,8},{8,12},{12,16},{16,20},{20,24},{24,28},{1,5},{5,9},{9,... | collective-permute-start | bytes 786440 | tf_op jit(solution)/shard_map/ppermute | solution.py:417
  45.7 8.2 %collective-permute-start.2 = (f32[2,36,512]{2,1,0:T(8,128)S(1)}, f32[2,36,512]{2,1,0:T(8,128)S(1)}, u32[]{:S(2)}, u32[]{:S(2)}) collective-permute-start(f32[2,36,512]{2,1,0:T(8,128)S(1)} %pad_maximum_fusion), channel_id=1, source_target_pairs={{0,1},{1,2},{2,3},{4,5},{5,6},{6,7},{8,9},{9,10},{10,11},{12,13},{... | collective-permute-start | bytes 442376 | tf_op jit(solution)/shard_map/ppermute | solution.py:417
  50.8 6.1 %collective-permute-start.3 = (f32[2,36,512]{2,1,0:T(8,128)S(1)}, f32[2,36,512]{2,1,0:T(8,128)S(1)}, u32[]{:S(2)}, u32[]{:S(2)}) collective-permute-start(f32[2,36,512]{2,1,0:T(8,128)S(1)} %pad_maximum_fusion.1), channel_id=1, source_target_pairs={{1,0},{2,1},{3,2},{5,4},{6,5},{7,6},{9,8},{10,9},{11,10},{13,12},{... | collective-permute-start | bytes 442376 | tf_op jit(solution)/shard_map/ppermute | solution.py:417
  71.0 29.0 %all-to-all-start.4 = ((bf16[32,96,128]{2,1,0:T(8,128)(2,1)}), bf16[32,96,128]{2,1,0:T(8,128)(2,1)S(1)}, u32[]{:S(2)}, u32[]{:S(2)}) async-start(bf16[32,96,128]{2,1,0:T(8,128)(2,1)} %bitcast.14), calls=%async_computation.4 | async-start | bytes 1572864 | tf_op jit(solution)/shard_map/all_to_all | solution.py:453
  80.0 2.2 %copy-start.2 = (f32[32,64,512]{2,1,0:T(8,128)S(1)}, f32[32,64,512]{2,1,0:T(8,128)}, u32[]{:S(2)}) copy-start(f32[32,64,512]{2,1,0:T(8,128)} %field_hbm.1) | copy-start | bytes 12582916
  92.9 1.9 %copy-start.3 = (f32[32,64,512]{2,1,0:T(8,128)}, f32[32,64,512]{2,1,0:T(8,128)S(1)}, u32[]{:S(2)}) copy-start(f32[32,64,512]{2,1,0:T(8,128)S(1)} %prior.1.base_hbm) | copy-start | bytes 12582916

commit v5 on v4

--- a/solution.py
+++ b/solution.py
@@ -61,11 +61,12 @@
             preferred_element_type=jnp.float32,
         )
         last_slots = capacity - first_slots
-        position_ref[chunk : chunk + 1, :] = jnp.where(
+        position = jnp.where(
             rank < first_slots,
             target * first_slots + rank,
             devices * first_slots + target * last_slots + rank - first_slots,
         )
+        position_ref[chunk : chunk + 1, :] = position + MARK * pltpu.roll(position, LANES // 2, 1)
     high, low = lists[:devices], lists[devices:]
     wanted = ((high - 1.0) * 128.0 + low).astype(jnp.int32)
     filled = before.astype(jnp.int32)
@@ -90,12 +91,12 @@
 
 
 def for_each_group(incoming_ref, visit, capacity, first_slots, blocks):
-    sources = incoming_ref.shape[0]
+    sources = incoming_ref.shape[0] // capacity
     last_slots = capacity - first_slots
     together = 4
 
     def groups_of(source):
-        last = incoming_ref[source, capacity - 1] & (MARK - 1)
+        last = incoming_ref[source * capacity + capacity - 1] & (MARK - 1)
         return (jnp.where(last < blocks, capacity, last - blocks) + GROUP - 1) // GROUP
 
     def some_sources(quad, carry):
@@ -103,10 +104,10 @@
         most = functools.reduce(jnp.maximum, [groups_of(source) for source in own])
 
         def one_group(group, carry):
-            slot = pl.multiple_of(group * GROUP, GROUP)
+            slot = group * GROUP
             for source in own:
-                wanted = [incoming_ref[source, slot + j] for j in range(GROUP)]
-                visit(wanted, pl.multiple_of(source * first_slots + slot, GROUP))
+                wanted = [incoming_ref[source * capacity + slot + j] for j in range(GROUP)]
+                visit(wanted, pl.multiple_of(source * first_slots + slot, GROUP), 0)
             return carry
 
         return lax.fori_loop(0, jnp.minimum(most, first_slots // GROUP), one_group, carry)
@@ -117,10 +118,11 @@
 
     def one_source(source, carry):
         def one_group(group, carry):
-            slot = pl.multiple_of(group * GROUP, GROUP)
-            row = (sources - 1) * first_slots + source * last_slots + slot
-            wanted = [incoming_ref[source, slot + j] & (MARK - 1) for j in range(GROUP)]
-            visit(wanted, pl.multiple_of(row, GROUP))
+            slot = group * GROUP
+            wanted = [
+                incoming_ref[source * capacity + slot + j] & (MARK - 1) for j in range(GROUP)
+            ]
+            visit(wanted, pl.multiple_of(source * last_slots + slot - first_slots, GROUP), 1)
             return carry
 
         return lax.fori_loop(first_slots // GROUP, groups_of(source), one_group, carry)
@@ -129,7 +131,7 @@
 
 
 def serve_kernel(incoming_ref, field_ref, *refs, capacity, first_slots):
-    *served_refs, table_ref, rows_ref = refs
+    *served_refs, table_ref = refs
     cells_x, cells_y, depth = field_ref.shape
     per_column = depth // LANES
     table_rows = table_ref.reshape(table_ref.shape[0], LANES)
@@ -147,17 +149,11 @@
 
     lax.fori_loop(0, cells_x, one_plane, 0)
 
-    def visit(wanted, row):
-        rows = [table_ref[at] for at in wanted]
-        for j in range(GROUP):
-            rows_ref[pl.ds(row + j, 1), :] = rows[j]
+    def visit(wanted, row, list_part):
+        rows = jnp.concatenate([table_ref[at] for at in wanted], axis=0)
+        served_refs[list_part][pl.ds(row, GROUP), :] = rows.astype(jnp.bfloat16)
 
     for_each_group(incoming_ref, visit, capacity, first_slots, blocks)
-    start = 0
-    for served_ref in served_refs:
-        size = served_ref.shape[0]
-        served_ref[...] = rows_ref[start : start + size, :].astype(jnp.bfloat16)
-        start += size
 
 
 def match_kernel(incoming_ref, match_ref):
@@ -193,7 +189,7 @@
     blocks_dev, slots, stars, width = weights_ref.shape
     chunks = sems.shape[0]
     per = blocks_dev // chunks
-    half = position_ref.shape[0]
+    half = slots // 2
     fold = LANES // stars
     all_slots = parcel_rows.shape[0]
     lane = lax.broadcasted_iota(jnp.int32, (8, LANES), 1)
@@ -204,8 +200,14 @@
         span = pl.ds(chunk * per, per)
         return pltpu.make_async_copy(weights_hbm.at[span], weights_ref.at[span], sems.at[chunk])
 
-    def place(block, slot):
-        return position_ref[slot % half, (slot // half) * blocks_dev + block]
+    def places(chunk):
+        found = {}
+        for b in range(per):
+            for k in range(half):
+                both = position_ref[k * 2 * blocks_dev + chunk * per + b]
+                found[b, k] = both & (MARK - 1)
+                found[b, k + half] = both >> 16
+        return found
 
     def start_of(chunk):
         return pl.multiple_of(chunk * per * slots, per * slots)
@@ -215,9 +217,8 @@
         return jnp.concatenate([x.reshape(8 * stars, width) for x in eights], axis=1)
 
     def gather(chunk):
-        rows = [returned_rows[place(chunk * per + b, k)] for b in range(per) for k in range(slots)]
-        for i, value in enumerate(rows):
-            fetched_ref[pl.ds(start_of(chunk) + i, 1), :] = value
+        for (b, k), at in places(chunk).items():
+            fetched_ref[pl.ds(start_of(chunk) + b * slots + k, 1), :] = returned_rows[at]
 
     def extinctions(chunk):
         weighted = []
@@ -260,10 +261,8 @@
                 ]
 
     def scatter(chunk):
-        for b in range(per):
-            for k in range(slots):
-                at = pl.ds(start_of(chunk) + b * slots + k, 1)
-                parcel_rows[place(chunk * per + b, k)] = sens_ref[at, :]
+        for (b, k), at in places(chunk).items():
+            parcel_rows[at] = sens_ref[pl.ds(start_of(chunk) + b * slots + k, 1), :]
 
     for chunk in range(chunks):
         load(chunk).start()
@@ -380,7 +379,10 @@
         start += arrived_ref.shape[0]
     collected_rows[...] = jnp.zeros_like(collected_rows)
 
-    def visit(wanted, row):
+    part_starts = [0, arrived_refs[0].shape[0]]
+
+    def visit(wanted, row, list_part):
+        row = row + part_starts[list_part]
         sums = [collected[wanted[j]] + rows_ref[pl.ds(row + j, 1), :] for j in range(GROUP)]
         for j in range(GROUP):
             collected[wanted[j]] = sums[j]
@@ -492,6 +494,8 @@
         name="edges",
     )(field)
     xlo, xhi = both_ways(xfirst, xlast, "gx")
+    incoming, yfirst, ylast = lax.optimization_barrier((incoming, yfirst, ylast))
+    wanted = incoming.reshape(-1)
 
     served = pl.pallas_call(
         functools.partial(serve_kernel, capacity=capacity, first_slots=first_slots),
@@ -500,21 +504,20 @@
         out_specs=[VMEM] * exchanges,
         scratch_shapes=[
             pltpu.VMEM((blocks + capacity, 1, width), f32),
-            pltpu.VMEM((all_slots, width), f32),
         ],
         compiler_params=pltpu.CompilerParams(vmem_limit_bytes=24 * MIB),
         cost_estimate=pl.CostEstimate(
             flops=cells, bytes_accessed=6 * MIB, transcendentals=cells
         ),
         name="serve",
-    )(incoming, field)
-    crowded = jnp.max(incoming[:, capacity - 1]) >= (first_slots + 1) * MARK
-    returned = exchange_rows(served, crowded)
+    )(wanted, field)
 
     incoming_late, xlo, xhi, yfirst, ylast, _ = lax.optimization_barrier(
         (incoming, xlo, xhi, yfirst, ylast, served[0])
     )
-    sides = halo_y(xlo, xhi, yfirst, ylast)
+    crowded = jnp.max(incoming_late[:, capacity - 1]) >= (first_slots + 1) * MARK
+    returned = exchange_rows(served, crowded)
+    ylo, yhi = halo_y(xlo, xhi, yfirst, ylast)
     slot_lists = [
         incoming_late[:, :first_slots].reshape(-1, LANES),
         (incoming_late[:, first_slots:] & (MARK - 1)).reshape(-1, LANES),
@@ -528,9 +531,7 @@
         cost_estimate=pl.CostEstimate(flops=10**9, bytes_accessed=MIB, transcendentals=0),
         name="match",
     )(jnp.concatenate(slot_lists, axis=0))
-    *returned, match, xlo, xhi, ylo, yhi = lax.optimization_barrier(
-        (*returned, match, xlo, xhi, *sides)
-    )
+    *returned, match, xlo, xhi = lax.optimization_barrier((*returned, match, xlo, xhi))
 
     chunks = blocks_dev * stars // LANES
     live = jnp.arange(stars)[None, :] < star_counts[:, None]
@@ -555,7 +556,7 @@
         ),
         name="stars",
     )(
-        position,
+        position.reshape(requests),
         jnp.tile(observed, (1, LANES // stars)),
         jnp.tile(live_inverse, (1, LANES // stars)),
         weights,
@@ -602,7 +603,7 @@
             flops=4 * cells, bytes_accessed=12 * cells, transcendentals=cells
         ),
         name="finish",
-    )(incoming, match, log_density, base, *arrived)
+    )(wanted, match, log_density, base, *arrived)
     return new_log_density, extinction[:, :stars]
 
 

time: 112 us -> 120 us (1.071)
  the two profiles are of different devices: /device:TPU:1 before, /device:TPU:12 now
where the time goes in v5:
time: 120 us
  Pallas kernels  44.8 us (37%)
  waiting for transfers between devices  32.5 us (27%)
  starting transfers between devices  19.7 us (16%)
  blocking collectives  11.1 us (9%)
  local copies, waits for them, and re-layouts  7.85 us (7%)
  other arithmetic  2.17 us (2%)
  between operations  1.52 us (1%)
    all_to_all x2, waiting for transfers between devices, exchange(): return lax.all_to_all(x, mesh_axes, split_axis=0, concat_axis=0, tiled=True)  17.6 us
    ppermute x4, waiting for transfers between devices, both_ways(): return (lax.ppermute(last, axis, up), lax.ppermute(first, axis, down))  14.9 us
    pallas_call x1, Pallas kernels, on_device(): pl.pallas_call(functools.partial(star_kernel, exchanges=exchanges), out_s...  14.2 us
    all_to_all x1, blocking collectives, exchange(): return lax.all_to_all(x, mesh_axes, split_axis=0, concat_axis=0, tiled=True)  11.1 us
    ppermute x4, starting transfers between devices, both_ways(): return (lax.ppermute(last, axis, up), lax.ppermute(first, axis, down))  10.8 us
    pallas_call x1, Pallas kernels, on_device(): pl.pallas_call(prior_kernel, out_shape=shape(field_shape, f32), in_specs=...  10.7 us
    all_to_all x2, starting transfers between devices, exchange(): return lax.all_to_all(x, mesh_axes, split_axis=0, concat_axis=0, tiled=True)  8.94 us
    pallas_call x1, Pallas kernels, on_device(): pl.pallas_call(functools.partial(finish_kernel, exchanges=exchanges, capa...  8.38 us
  transfers between devices with their start and end apart: 6, of which 3 were waited for; matrix products, arithmetic and copies ran while one was open for 2% of the time, Pallas kernels for 16%

profile of v5, /device:TPU:12, one launch (start us, length us, event | category | flops | bytes accessed | tf_op | source)
XLA Modules:
  0.0 119.6 jit_solution(1916469662123358533)
XLA Ops:
  0.6 3.1 %route.1 = (s32[32,128]{1,0:T(8,128)}, s32[16,128]{1,0:T(8,128)}) custom-call(s32[32,64]{1,0:T(8,128)} %bitcast.44), custom_call_target="tpu_custom_call" | custom-call | tf_op jit(solution)/shard_map/route/pallas_call | solution.py:465
  3.7 2.2 %copy-done = f32[32,64,512]{2,1,0:T(8,128)S(1)} copy-done((f32[32,64,512]{2,1,0:T(8,128)S(1)}, f32[32,64,512]{2,1,0:T(8,128)}, u32[]{:S(2)}) %copy-start) | copy-done | bytes 4194328
  5.9 0.1 edges.1
  6.0 0.2 copy.24
  6.3 3.0 %collective-permute-start.1 = (f32[2,64,512]{2,0,1:T(2,128)S(1)}, f32[2,64,512]{2,0,1:T(2,128)S(1)}, u32[]{:S(2)}, u32[]{:S(2)}) collective-permute-start(f32[2,64,512]{2,0,1:T(2,128)S(1)} %copy.24), channel_id=1, source_target_pairs={{4,0},{8,4},{12,8},{16,12},{20,16},{24,20},{28,24},{5,1},{9,5},{13... | collective-permute-start | bytes 786440 | tf_op jit(solution)/shard_map/ppermute | solution.py:419
  9.3 0.2 copy.23
  9.5 1.9 %collective-permute-start = (f32[2,64,512]{2,0,1:T(2,128)S(1)}, f32[2,64,512]{2,0,1:T(2,128)S(1)}, u32[]{:S(2)}, u32[]{:S(2)}) collective-permute-start(f32[2,64,512]{2,0,1:T(2,128)S(1)} %copy.23), channel_id=1, source_target_pairs={{0,4},{4,8},{8,12},{12,16},{16,20},{20,24},{24,28},{1,5},{5,9},{9,... | collective-permute-start | bytes 786440 | tf_op jit(solution)/shard_map/ppermute | solution.py:419
  11.5 11.1 %all_to_all.32 = s32[32,1,128]{2,1,0:T(1,128)S(1)} all-to-all(s32[32,1,128]{2,1,0:T(1,128)S(1)} %bitcast.45), channel_id=1, replica_groups=mesh['gx'=8,'gy'=4] {'gx','gy'}, dimensions={0} | all-to-all | bytes 32768 | tf_op jit(solution)/shard_map/all_to_all | solution.py:455
  22.5 6.5 %serve.1 = (bf16[3072,128]{1,0:T(8,128)(2,1)}, bf16[1024,128]{1,0:T(8,128)(2,1)S(1)}) custom-call(s32[4096]{0:T(1024)S(1)} %bitcast.29, f32[32,64,512]{2,1,0:T(8,128)S(1)} %copy-done.1), custom_call_target="tpu_custom_call" | custom-call | flops 1048576 | bytes 6291456 | tf_op jit(solution)/shard_map/serve/pallas_call | solution.py:500
  29.0 0.7 slice_reduce_fusion
  30.4 4.8 %all-to-all-start.3 = ((bf16[32,96,128]{2,1,0:T(8,128)(2,1)}), bf16[32,96,128]{2,1,0:T(8,128)(2,1)S(1)}, u32[]{:S(2)}, u32[]{:S(2)}) async-start(bf16[32,96,128]{2,1,0:T(8,128)(2,1)} %bitcast.5), calls=%async_computation.3 | async-start | bytes 1572864 | tf_op jit(solution)/shard_map/all_to_all | solution.py:455
  35.3 0.1 copy.26.inverse_ref
  35.4 0.1 copy.25.observed_ref
  35.4 0.1 reshape.74
  35.5 0.1 slice_and_fusion
  35.6 0.1 reshape.75
  35.7 1.8 %match.1.match_ref = bf16[4096,128]{1,0:T(8,128)(2,1)S(1)} custom-call(s32[32,128]{1,0:T(8,128)S(1)} %pad_add_fusion.incoming_ref), custom_call_target="tpu_custom_call" | custom-call | flops 1000000000 | bytes 1048576 | tf_op jit(solution)/shard_map/match/pallas_call | solution.py:525
  37.5 17.6 %all-to-all-done.3 = bf16[32,96,128]{2,1,0:T(8,128)(2,1)S(1)} async-done(((bf16[32,96,128]{2,1,0:T(8,128)(2,1)}), bf16[32,96,128]{2,1,0:T(8,128)(2,1)S(1)}, u32[]{:S(2)}, u32[]{:S(2)}) %all-to-all-start.3) | async-done | bytes 786464 | tf_op jit(solution)/shard_map/all_to_all | solution.py:455
  55.1 14.2 %stars.1 = (f32[64,128]{1,0:T(8,128)S(1)}, bf16[3072,128]{1,0:T(8,128)(2,1)}, bf16[1024,128]{1,0:T(8,128)(2,1)S(1)}) custom-call(s32[2048]{0:T(1024)S(1)} %bitcast.35, f32[64,128]{1,0:T(8,128)S(1)} %copy.25.observed_ref, f32[64,128]{1,0:T(8,128)S(1)} %copy.26.inverse_ref, bf16[64,32,32,128]{3,2,1,0:T(8,128)(2,1)} %weights_hbm.1, ...), custom_call_target="tpu_custom_call" | custom-call | flops 33554432 | bytes 16777216 | tf_op jit(solution)/shard_map/stars/pallas_call | solution.py:539
  69.3 4.1 %all-to-all-start.4 = ((bf16[32,96,128]{2,1,0:T(8,128)(2,1)}), bf16[32,96,128]{2,1,0:T(8,128)(2,1)S(1)}, u32[]{:S(2)}, u32[]{:S(2)}) async-start(bf16[32,96,128]{2,1,0:T(8,128)(2,1)} %bitcast.16), calls=%async_computation.4 | async-start | bytes 1572864 | tf_op jit(solution)/shard_map/all_to_all | solution.py:455
  73.4 0.7 pad_maximum_fusion
  74.1 3.4 %collective-permute-start.2 = (f32[2,36,512]{2,1,0:T(8,128)}, f32[2,36,512]{2,1,0:T(8,128)S(1)}, u32[]{:S(2)}, u32[]{:S(2)}) collective-permute-start(f32[2,36,512]{2,1,0:T(8,128)} %pad_maximum_fusion), channel_id=1, source_target_pairs={{0,1},{1,2},{2,3},{4,5},{5,6},{6,7},{8,9},{9,10},{10,11},{12,13},{... | collective-permute-start | bytes 442376 | tf_op jit(solution)/shard_map/ppermute | solution.py:419
  77.5 0.7 pad_maximum_fusion.1
  78.2 2.4 %collective-permute-start.3 = (f32[2,36,512]{2,1,0:T(8,128)}, f32[2,36,512]{2,1,0:T(8,128)S(1)}, u32[]{:S(2)}, u32[]{:S(2)}) collective-permute-start(f32[2,36,512]{2,1,0:T(8,128)} %pad_maximum_fusion.1), channel_id=1, source_target_pairs={{1,0},{2,1},{3,2},{5,4},{6,5},{7,6},{9,8},{10,9},{11,10},{13,12},{... | collective-permute-start | bytes 442376 | tf_op jit(solution)/shard_map/ppermute | solution.py:419
  80.7 0.1 copy.27.xlo_ref
  80.8 0.7 copy.29
  81.5 13.1 %collective-permute-done.2.ylo_ref = f32[2,36,512]{2,1,0:T(8,128)S(1)} collective-permute-done((f32[2,36,512]{2,1,0:T(8,128)}, f32[2,36,512]{2,1,0:T(8,128)S(1)}, u32[]{:S(2)}, u32[]{:S(2)}) %collective-permute-start.2) | collective-permute-done | bytes 147488 | tf_op jit(solution)/shard_map/ppermute | solution.py:419
  94.5 1.8 %collective-permute-done.3.yhi_ref = f32[2,36,512]{2,1,0:T(8,128)S(1)} collective-permute-done((f32[2,36,512]{2,1,0:T(8,128)}, f32[2,36,512]{2,1,0:T(8,128)S(1)}, u32[]{:S(2)}, u32[]{:S(2)}) %collective-permute-start.3) | collective-permute-done | bytes 147488 | tf_op jit(solution)/shard_map/ppermute | solution.py:419
  96.4 2.2 %copy-done.2 = f32[32,64,512]{2,1,0:T(8,128)S(1)} copy-done((f32[32,64,512]{2,1,0:T(8,128)S(1)}, f32[32,64,512]{2,1,0:T(8,128)}, u32[]{:S(2)}) %copy-start.2) | copy-done | bytes 4194328
  98.6 10.7 %prior.1.base_hbm = f32[32,64,512]{2,1,0:T(8,128)S(1)} custom-call(f32[32,64,512]{2,1,0:T(8,128)S(1)} %copy-done.2, f32[2,64,512]{2,1,0:T(8,128)S(1)} %copy.27.xlo_ref, f32[2,64,512]{2,1,0:T(8,128)S(1)} %copy.28.xhi_ref, f32[2,36,512]{2,1,0:T(8,128)S(1)} %collective-permute-done.2.ylo_ref, f32[2,36,512]{2,1,0:T(8,128)S(1)} %collective-permute-done.3.yhi_ref), custom_call_target="tpu_custom_call" | custom-call | flops 31457280 | bytes 8388608 | tf_op jit(solution)/shard_map/prior/pallas_call | solution.py:568
  109.3 1.9 %copy-done.3 = f32[32,64,512]{2,1,0:T(8,128)} copy-done((f32[32,64,512]{2,1,0:T(8,128)}, f32[32,64,512]{2,1,0:T(8,128)S(1)}, u32[]{:S(2)}) %copy-start.3) | copy-done | bytes 4194328
  111.3 8.4 %finish.1 = f32[32,64,512]{2,1,0:T(8,128)} custom-call(s32[4096]{0:T(1024)S(1)} %bitcast.33, bf16[4096,128]{1,0:T(8,128)(2,1)S(1)} %match.1.match_ref, f32[32,64,512]{2,1,0:T(8,128)} %field_hbm.1, f32[32,64,512]{2,1,0:T(8,128)} %copy-done.3, bf16[3072,128]{1,0:T(8,128)(2,1)S(1)} %bitcast.27, bf16[1024,128]{1,0:T(8,128)(2,1)S(1)} %bitcast.41), custom_call_target="tpu_custom_call" | custom-call | flops 4194304 | bytes 12582912 | tf_op jit(solution)/shard_map/finish/pallas_call | solution.py:585
  (26 shorter events, 0.2 us)
Async XLA Ops:
  3.7 2.2 %copy-start = (f32[32,64,512]{2,1,0:T(8,128)S(1)}, f32[32,64,512]{2,1,0:T(8,128)}, u32[]{:S(2)}) copy-start(f32[32,64,512]{2,1,0:T(8,128)} %field_hbm.1) | copy-start | bytes 12582916
  5.9 5.6 %copy-start.7 = (s32[32,128]{1,0:T(8,128)S(1)}, s32[32,128]{1,0:T(8,128)}, u32[]{:S(2)}) copy-start(s32[32,128]{1,0:T(8,128)} %get-tuple-element.50) | copy-start | bytes 49156
  5.9 16.6 %copy-start.1 = (f32[32,64,512]{2,1,0:T(8,128)S(1)}, f32[32,64,512]{2,1,0:T(8,128)}, u32[]{:S(2)}) copy-start(f32[32,64,512]{2,1,0:T(8,128)} %field_hbm.1) | copy-start | bytes 12582916
  6.0 29.2 %copy-start.6 = (f32[64,32]{0,1:T(8,128)S(1)}, f32[64,32]{0,1:T(8,128)}, u32[]{:S(2)}) copy-start(f32[64,32]{0,1:T(8,128)} %param.13) | copy-start | bytes 24580
  6.0 29.2 %copy-start.8 = (s32[64]{0:T(128)S(1)}, s32[64]{0:T(128)}, u32[]{:S(2)}) copy-start(s32[64]{0:T(128)} %param.14) | copy-start | bytes 772
  6.0 29.3 %copy-start.5 = (f32[64,32]{0,1:T(8,128)S(1)}, f32[64,32]{0,1:T(8,128)}, u32[]{:S(2)}) copy-start(f32[64,32]{0,1:T(8,128)} %param.12) | copy-start | bytes 24580
  6.3 22.8 %collective-permute-start.1 = (f32[2,64,512]{2,0,1:T(2,128)S(1)}, f32[2,64,512]{2,0,1:T(2,128)S(1)}, u32[]{:S(2)}, u32[]{:S(2)}) collective-permute-start(f32[2,64,512]{2,0,1:T(2,128)S(1)} %copy.24), channel_id=1, source_target_pairs={{4,0},{8,4},{12,8},{16,12},{20,16},{24,20},{28,24},{5,1},{9,5},{13... | collective-permute-start | bytes 786440 | tf_op jit(solution)/shard_map/ppermute | solution.py:419
  9.5 19.5 %collective-permute-start = (f32[2,64,512]{2,0,1:T(2,128)S(1)}, f32[2,64,512]{2,0,1:T(2,128)S(1)}, u32[]{:S(2)}, u32[]{:S(2)}) collective-permute-start(f32[2,64,512]{2,0,1:T(2,128)S(1)} %copy.23), channel_id=1, source_target_pairs={{0,4},{4,8},{8,12},{12,16},{16,20},{20,24},{24,28},{1,5},{5,9},{9,... | collective-permute-start | bytes 786440 | tf_op jit(solution)/shard_map/ppermute | solution.py:419
  29.0 26.1 %copy-start.4 = (s32[16,128]{1,0:T(8,128)S(1)}, s32[16,128]{1,0:T(8,128)}, u32[]{:S(2)}) copy-start(s32[16,128]{1,0:T(8,128)} %get-tuple-element.65) | copy-start | bytes 24580
  30.4 24.7 %all-to-all-start.3 = ((bf16[32,96,128]{2,1,0:T(8,128)(2,1)}), bf16[32,96,128]{2,1,0:T(8,128)(2,1)S(1)}, u32[]{:S(2)}, u32[]{:S(2)}) async-start(bf16[32,96,128]{2,1,0:T(8,128)(2,1)} %bitcast.5), calls=%async_computation.3 | async-start | bytes 1572864 | tf_op jit(solution)/shard_map/all_to_all | solution.py:455
  69.3 41.9 %all-to-all-start.4 = ((bf16[32,96,128]{2,1,0:T(8,128)(2,1)}), bf16[32,96,128]{2,1,0:T(8,128)(2,1)S(1)}, u32[]{:S(2)}, u32[]{:S(2)}) async-start(bf16[32,96,128]{2,1,0:T(8,128)(2,1)} %bitcast.16), calls=%async_computation.4 | async-start | bytes 1572864 | tf_op jit(solution)/shard_map/all_to_all | solution.py:455
  74.1 20.4 %collective-permute-start.2 = (f32[2,36,512]{2,1,0:T(8,128)}, f32[2,36,512]{2,1,0:T(8,128)S(1)}, u32[]{:S(2)}, u32[]{:S(2)}) collective-permute-start(f32[2,36,512]{2,1,0:T(8,128)} %pad_maximum_fusion), channel_id=1, source_target_pairs={{0,1},{1,2},{2,3},{4,5},{5,6},{6,7},{8,9},{9,10},{10,11},{12,13},{... | collective-permute-start | bytes 442376 | tf_op jit(solution)/shard_map/ppermute | solution.py:419
  78.2 18.2 %collective-permute-start.3 = (f32[2,36,512]{2,1,0:T(8,128)}, f32[2,36,512]{2,1,0:T(8,128)S(1)}, u32[]{:S(2)}, u32[]{:S(2)}) collective-permute-start(f32[2,36,512]{2,1,0:T(8,128)} %pad_maximum_fusion.1), channel_id=1, source_target_pairs={{1,0},{2,1},{3,2},{5,4},{6,5},{7,6},{9,8},{10,9},{11,10},{13,12},{... | collective-permute-start | bytes 442376 | tf_op jit(solution)/shard_map/ppermute | solution.py:419
  96.4 2.2 %copy-start.2 = (f32[32,64,512]{2,1,0:T(8,128)S(1)}, f32[32,64,512]{2,1,0:T(8,128)}, u32[]{:S(2)}) copy-start(f32[32,64,512]{2,1,0:T(8,128)} %field_hbm.1) | copy-start | bytes 12582916
  109.3 1.9 %copy-start.3 = (f32[32,64,512]{2,1,0:T(8,128)}, f32[32,64,512]{2,1,0:T(8,128)S(1)}, u32[]{:S(2)}) copy-start(f32[32,64,512]{2,1,0:T(8,128)S(1)} %prior.1.base_hbm) | copy-start | bytes 12582916

commit v6 on v5

--- a/solution.py
+++ b/solution.py
@@ -61,12 +61,11 @@
             preferred_element_type=jnp.float32,
         )
         last_slots = capacity - first_slots
-        position = jnp.where(
+        position_ref[chunk : chunk + 1, :] = jnp.where(
             rank < first_slots,
             target * first_slots + rank,
             devices * first_slots + target * last_slots + rank - first_slots,
         )
-        position_ref[chunk : chunk + 1, :] = position + MARK * pltpu.roll(position, LANES // 2, 1)
     high, low = lists[:devices], lists[devices:]
     wanted = ((high - 1.0) * 128.0 + low).astype(jnp.int32)
     filled = before.astype(jnp.int32)
@@ -82,8 +81,8 @@
 
 def edges_kernel(field_ref, xfirst_ref, xlast_ref, yfirst_ref, ylast_ref):
     cells_x, cells_y, _ = field_ref.shape
-    xfirst_ref[...] = field_ref[:2]
-    xlast_ref[...] = field_ref[cells_x - 2 :]
+    xfirst_ref[...] = field_ref[:2].astype(xfirst_ref.dtype)
+    xlast_ref[...] = field_ref[cells_x - 2 :].astype(xlast_ref.dtype)
     for h in range(2):
         for x in range(cells_x):
             yfirst_ref[h, x : x + 1, :] = field_ref[x, h : h + 1, :]
@@ -106,7 +105,8 @@
         def one_group(group, carry):
             slot = group * GROUP
             for source in own:
-                wanted = [incoming_ref[source * capacity + slot + j] for j in range(GROUP)]
+                listed = incoming_ref.at[pl.ds(source * capacity + slot, GROUP)]
+                wanted = [listed[j] for j in range(GROUP)]
                 visit(wanted, pl.multiple_of(source * first_slots + slot, GROUP), 0)
             return carry
 
@@ -119,9 +119,8 @@
     def one_source(source, carry):
         def one_group(group, carry):
             slot = group * GROUP
-            wanted = [
-                incoming_ref[source * capacity + slot + j] & (MARK - 1) for j in range(GROUP)
-            ]
+            listed = incoming_ref.at[pl.ds(source * capacity + slot, GROUP)]
+            wanted = [listed[j] & (MARK - 1) for j in range(GROUP)]
             visit(wanted, pl.multiple_of(source * last_slots + slot - first_slots, GROUP), 1)
             return carry
 
@@ -156,7 +155,10 @@
     for_each_group(incoming_ref, visit, capacity, first_slots, blocks)
 
 
-def match_kernel(incoming_ref, match_ref):
+def match_kernel(incoming_ref, marked_ref, match_ref, fullest_ref):
+    marks = marked_ref[:, marked_ref.shape[1] - 1 :] >> 16
+    fullest = jnp.max(marks, axis=0, keepdims=True)
+    fullest_ref[...] = jnp.broadcast_to(fullest, fullest_ref.shape)
     lane = lax.broadcasted_iota(jnp.int32, (LANES, LANES), 1)
     row = lax.broadcasted_iota(jnp.int32, (LANES, LANES), 0)
     ones = jnp.ones((LANES, LANES), jnp.bfloat16)
@@ -185,84 +187,70 @@
     returned_refs, refs = refs[:exchanges], refs[exchanges:]
     extinction_ref, refs = refs[0], refs[1:]
     parcel_refs, refs = refs[:exchanges], refs[exchanges:]
-    weights_ref, returned_rows, fetched_ref, sens_ref, parcel_rows, sems = refs
+    weights_ref, returned_rows, sens_ref, parcel_rows, sems = refs
     blocks_dev, slots, stars, width = weights_ref.shape
     chunks = sems.shape[0]
     per = blocks_dev // chunks
-    half = slots // 2
     fold = LANES // stars
     all_slots = parcel_rows.shape[0]
     lane = lax.broadcasted_iota(jnp.int32, (8, LANES), 1)
     row = lax.broadcasted_iota(jnp.int32, (8, LANES), 0)
-    own_slot = [row == lane // stars + fold * h for h in range(8 // fold)]
+    star_group = lane // stars
+    own_slot = [row == star_group + fold * h for h in range(8 // fold)]
 
     def load(chunk):
         span = pl.ds(chunk * per, per)
         return pltpu.make_async_copy(weights_hbm.at[span], weights_ref.at[span], sems.at[chunk])
 
-    def places(chunk):
-        found = {}
-        for b in range(per):
-            for k in range(half):
-                both = position_ref[k * 2 * blocks_dev + chunk * per + b]
-                found[b, k] = both & (MARK - 1)
-                found[b, k + half] = both >> 16
-        return found
-
     def start_of(chunk):
         return pl.multiple_of(chunk * per * slots, per * slots)
 
-    def matrix_of(chunk, b):
-        eights = [weights_ref[chunk * per + b, 8 * j : 8 * j + 8] for j in range(slots // 8)]
-        return jnp.concatenate([x.reshape(8 * stars, width) for x in eights], axis=1)
-
-    def gather(chunk):
-        for (b, k), at in places(chunk).items():
-            fetched_ref[pl.ds(start_of(chunk) + b * slots + k, 1), :] = returned_rows[at]
+    def positions(chunk):
+        return position_ref.at[pl.ds(start_of(chunk), per * slots)]
 
     def extinctions(chunk):
-        weighted = []
+        places = positions(chunk)
+        sums = []
         for b in range(per):
-            left = jnp.concatenate(
-                [
-                    fetched_ref[pl.ds(start_of(chunk) + b * slots + 8 * j, 8), :]
-                    for j in range(slots // 8)
-                ],
-                axis=1,
-            )
-            total = lax.dot_general(
-                left.astype(jnp.bfloat16),
-                matrix_of(chunk, b),
-                CONTRACT_LANES,
-                preferred_element_type=jnp.float32,
-            )
-            folded = jnp.zeros((8, LANES), jnp.float32)
-            for h, own in enumerate(own_slot):
-                folded = folded + jnp.where(own, total[:, h * LANES : (h + 1) * LANES], 0.0)
-            extinction = jnp.sum(folded, axis=0, keepdims=True)
+            total = jnp.zeros((stars, width), jnp.float32)
+            for k in range(slots):
+                fetched = returned_rows[places[b * slots + k]]
+                total = total + weights_ref[chunk * per + b, k].astype(jnp.float32) * fetched
+            sums.append(total)
+        extinction = lax.dot_general(
+            jnp.ones((8, width), jnp.float32),
+            jnp.concatenate(sums, axis=0),
+            CONTRACT_LANES,
+            precision=lax.Precision.HIGHEST,
+            preferred_element_type=jnp.float32,
+        )
+        here = pl.ds(chunk, 1)
+        extinction_ref[here, :] = extinction[:1]
+        return inverse_ref[here, :] * (extinction - observed_ref[here, :])
+
+    def sensitivities(chunk, weighted):
+        for b in range(per):
+            spread = jnp.where(star_group == b, weighted, 0.0)
             shift = stars
             while shift < LANES:
-                extinction = extinction + pltpu.roll(extinction, shift, 1)
+                spread = spread + pltpu.roll(spread, shift, 1)
                 shift *= 2
-            here = pl.ds(chunk * per + b, 1)
-            extinction_ref[here, :] = extinction
-            weighted.append(inverse_ref[here, :] * (extinction - observed_ref[here, :]))
-        return weighted
-
-    def sensitivities(chunk, weighted):
-        for b in range(per):
             left = jnp.concatenate(
-                [jnp.where(own, weighted[b], 0.0) for own in own_slot], axis=1
+                [jnp.where(own, spread, 0.0) for own in own_slot], axis=1
             ).astype(jnp.bfloat16)
-            sens = jnp.dot(left, matrix_of(chunk, b), preferred_element_type=jnp.float32)
+            eights = [weights_ref[chunk * per + b, 8 * j : 8 * j + 8] for j in range(slots // 8)]
+            right = jnp.concatenate([x.reshape(8 * stars, width) for x in eights], axis=1)
+            sens = jnp.dot(left, right, preferred_element_type=jnp.float32)
             for j in range(slots // 8):
                 sens_ref[pl.ds(start_of(chunk) + b * slots + 8 * j, 8), :] = sens[
                     :, j * width : (j + 1) * width
                 ]
 
     def scatter(chunk):
-        for (b, k), at in places(chunk).items():
-            parcel_rows[at] = sens_ref[pl.ds(start_of(chunk) + b * slots + k, 1), :]
+        places = positions(chunk)
+        rows = sens_ref.at[pl.ds(start_of(chunk), per * slots)]
+        for i in range(per * slots):
+            parcel_rows[places[i]] = rows[i : i + 1, :]
 
     for chunk in range(chunks):
         load(chunk).start()
@@ -272,21 +260,17 @@
         returned_rows.reshape(all_slots, width)[span, :] = returned_ref[...].astype(jnp.float32)
         start = span.stop
     parcel_rows.reshape(all_slots, width)[...] = jnp.zeros((all_slots, width), jnp.float32)
-    gather(0)
     load(0).wait()
     weighted = extinctions(0)
-    gather(1)
     load(1).wait()
     following = extinctions(1)
     sensitivities(0, weighted)
-    gather(2)
 
     def step(chunk, weighted):
         load(chunk).wait()
         following = extinctions(chunk)
         sensitivities(chunk - 1, weighted)
         scatter(chunk - 2)
-        gather(jnp.minimum(chunk + 1, chunks - 1))
         return following
 
     weighted = lax.fori_loop(2, chunks, step, following)
@@ -325,8 +309,8 @@
             padded[plane, 8 + cells_y + h : 9 + cells_y + h, :] = yhi_ref[h, pl.ds(plane, 1), :]
 
     for h in range(2):
-        fill(h, xlo_ref[h])
-        fill(cells_x + 2 + h, xhi_ref[h])
+        fill(h, xlo_ref[h].astype(jnp.float32))
+        fill(cells_x + 2 + h, xhi_ref[h].astype(jnp.float32))
 
     def fill_own(x, carry):
         fill(x + 2, field_ref[x])
@@ -382,8 +366,9 @@
     part_starts = [0, arrived_refs[0].shape[0]]
 
     def visit(wanted, row, list_part):
-        row = row + part_starts[list_part]
-        sums = [collected[wanted[j]] + rows_ref[pl.ds(row + j, 1), :] for j in range(GROUP)]
+        row = pl.multiple_of(row + part_starts[list_part], GROUP)
+        rows = rows_ref.at[pl.ds(row, GROUP)]
+        sums = [collected[wanted[j]] + rows[j : j + 1, :] for j in range(GROUP)]
         for j in range(GROUP):
             collected[wanted[j]] = sums[j]
 
@@ -419,13 +404,15 @@
     return lax.ppermute(last, axis, up), lax.ppermute(first, axis, down)
 
 
-def halo_y(xlo, xhi, yfirst, ylast):
+def halo(xfirst, xlast, yfirst, ylast):
+    xlo, xhi = both_ways(xfirst, xlast, "gx")
+
     def rows(own, at):
-        return jnp.concatenate(
-            [xlo[:, at].transpose(1, 0, 2), own, xhi[:, at].transpose(1, 0, 2)], axis=1
-        )
-
-    return both_ways(rows(yfirst, slice(0, 2)), rows(ylast, slice(-2, None)), "gy")
+        ends = [x[:, at].transpose(1, 0, 2) for x in (xlo, xhi)]
+        return jnp.concatenate([ends[0], own.astype(xlo.dtype), ends[1]], axis=1)
+
+    ylo, yhi = both_ways(rows(yfirst, slice(0, 2)), rows(ylast, slice(-2, None)), "gy")
+    return xlo, xhi, ylo.astype(jnp.float32), yhi.astype(jnp.float32)
 
 
 VMEM = pl.BlockSpec(memory_space=pltpu.VMEM)
@@ -482,8 +469,8 @@
     xfirst, xlast, yfirst, ylast = pl.pallas_call(
         edges_kernel,
         out_shape=[
-            shape((2, cells_y, depth), f32),
-            shape((2, cells_y, depth), f32),
+            shape((2, cells_y, depth), bf16),
+            shape((2, cells_y, depth), bf16),
             shape((2, cells_x, depth), f32),
             shape((2, cells_x, depth), f32),
         ],
@@ -493,8 +480,7 @@
         cost_estimate=pl.CostEstimate(flops=0, bytes_accessed=2 * MIB, transcendentals=0),
         name="edges",
     )(field)
-    xlo, xhi = both_ways(xfirst, xlast, "gx")
-    incoming, yfirst, ylast = lax.optimization_barrier((incoming, yfirst, ylast))
+    incoming, *edges = lax.optimization_barrier((incoming, xfirst, xlast, yfirst, ylast))
     wanted = incoming.reshape(-1)
 
     served = pl.pallas_call(
@@ -512,40 +498,37 @@
         name="serve",
     )(wanted, field)
 
-    incoming_late, xlo, xhi, yfirst, ylast, _ = lax.optimization_barrier(
-        (incoming, xlo, xhi, yfirst, ylast, served[0])
-    )
-    crowded = jnp.max(incoming_late[:, capacity - 1]) >= (first_slots + 1) * MARK
-    returned = exchange_rows(served, crowded)
-    ylo, yhi = halo_y(xlo, xhi, yfirst, ylast)
+    incoming_late, *edges, _ = lax.optimization_barrier((incoming, *edges, served[0]))
     slot_lists = [
         incoming_late[:, :first_slots].reshape(-1, LANES),
         (incoming_late[:, first_slots:] & (MARK - 1)).reshape(-1, LANES),
     ][:exchanges]
-    match = pl.pallas_call(
+    match, fullest = pl.pallas_call(
         match_kernel,
-        out_shape=shape((all_slots, LANES), bf16),
-        in_specs=[VMEM],
-        out_specs=VMEM,
+        out_shape=[shape((all_slots, LANES), bf16), shape((8, LANES), i32)],
+        in_specs=[VMEM] * 2,
+        out_specs=[VMEM] * 2,
         compiler_params=pltpu.CompilerParams(vmem_limit_bytes=8 * MIB),
         cost_estimate=pl.CostEstimate(flops=10**9, bytes_accessed=MIB, transcendentals=0),
         name="match",
-    )(jnp.concatenate(slot_lists, axis=0))
-    *returned, match, xlo, xhi = lax.optimization_barrier((*returned, match, xlo, xhi))
+    )(jnp.concatenate(slot_lists, axis=0), incoming_late)
+    crowded = fullest[0, 0] > first_slots
+    returned = exchange_rows(served, crowded)
+    xlo, xhi, ylo, yhi = halo(*edges)
+    *returned, match, ylo, yhi = lax.optimization_barrier((*returned, match, ylo, yhi))
 
     chunks = blocks_dev * stars // LANES
     live = jnp.arange(stars)[None, :] < star_counts[:, None]
     live_inverse = jnp.where(live, inverse_var, 0.0)
     extinction, *parcel = pl.pallas_call(
         functools.partial(star_kernel, exchanges=exchanges),
-        out_shape=[shape((blocks_dev, LANES), f32)]
+        out_shape=[shape((chunks, LANES), f32)]
         + [shape((devices * n, width), bf16) for n in slots_of],
         in_specs=[SMEM, VMEM, VMEM, ANY] + [VMEM] * exchanges,
         out_specs=[VMEM] * (1 + exchanges),
         scratch_shapes=[
             pltpu.VMEM(weights.shape, bf16),
             pltpu.VMEM((all_slots, 1, width), f32),
-            pltpu.VMEM((requests, width), f32),
             pltpu.VMEM((requests, width), f32),
             pltpu.VMEM((all_slots, 1, width), f32),
             pltpu.SemaphoreType.DMA((chunks,)),
@@ -556,9 +539,9 @@
         ),
         name="stars",
     )(
-        position.reshape(requests),
-        jnp.tile(observed, (1, LANES // stars)),
-        jnp.tile(live_inverse, (1, LANES // stars)),
+        position.reshape(slots // 2, 2, blocks_dev).transpose(2, 1, 0).reshape(requests),
+        observed.reshape(chunks, LANES),
+        live_inverse.reshape(chunks, LANES),
         weights,
         *returned,
     )
@@ -604,7 +587,7 @@
         ),
         name="finish",
     )(wanted, match, log_density, base, *arrived)
-    return new_log_density, extinction[:, :stars]
+    return new_log_density, extinction.reshape(blocks_dev, stars)
 
 
 def solution(mesh):

time: 120 us -> 101 us (0.84)
  the two profiles are of different devices: /device:TPU:12 before, /device:TPU:1 now
where the time goes in v6:
time: 101 us
  Pallas kernels  44.6 us (44%)
  starting transfers between devices  25.2 us (25%)
  waiting for transfers between devices  18.5 us (18%)
  local copies, waits for them, and re-layouts  10.9 us (11%)
  between operations  1.53 us (2%)
    all_to_all x3, starting transfers between devices, exchange(): return lax.all_to_all(x, mesh_axes, split_axis=0, concat_axis=0, tiled=True)  14.2 us
    pallas_call x1, Pallas kernels, on_device(): pl.pallas_call(functools.partial(star_kernel, exchanges=exchanges), out_s...  13.5 us
    all_to_all x3, waiting for transfers between devices, exchange(): return lax.all_to_all(x, mesh_axes, split_axis=0, concat_axis=0, tiled=True)  12 us
    ppermute x4, starting transfers between devices, both_ways(): return (lax.ppermute(last, axis, up), lax.ppermute(first, axis, down))  11 us
    pallas_call x1, Pallas kernels, on_device(): pl.pallas_call(prior_kernel, out_shape=shape(field_shape, f32), in_specs=...  10.7 us
    unnamed x18, local copies, waits for them, and re-layouts  9.28 us
    pallas_call x1, Pallas kernels, on_device(): pl.pallas_call(functools.partial(finish_kernel, exchanges=exchanges, capa...  8.76 us
    pallas_call x1, Pallas kernels, on_device(): pl.pallas_call(functools.partial(serve_kernel, capacity=capacity, first_s...  6.54 us
  transfers between devices with their start and end apart: 7, of which 6 were waited for; matrix products, arithmetic and copies ran while one was open for 2% of the time, Pallas kernels for 11%

profile of v6, /device:TPU:1, one launch (start us, length us, event | category | flops | bytes accessed | tf_op | source)
XLA Modules:
  0.0 100.9 jit_solution(13731170879448298374)
XLA Ops:
  0.6 3.1 %route.1 = (s32[32,128]{1,0:T(8,128)}, s32[16,128]{1,0:T(8,128)}) custom-call(s32[32,64]{1,0:T(8,128)} %bitcast.39), custom_call_target="tpu_custom_call" | custom-call | tf_op jit(solution)/shard_map/route/pallas_call | solution.py:452
  3.7 7.1 %all-to-all-start.2 = ((s32[32,1,128]{2,1,0:T(1,128)}), s32[32,1,128]{2,1,0:T(1,128)S(1)}, u32[]{:S(2)}, u32[]{:S(2)}) async-start(s32[32,1,128]{2,1,0:T(1,128)} %bitcast.40), calls=%async_computation.2 | async-start | bytes 32768 | tf_op jit(solution)/shard_map/all_to_all | solution.py:442
  10.8 2.2 %copy-done = f32[32,64,512]{2,1,0:T(8,128)S(1)} copy-done((f32[32,64,512]{2,1,0:T(8,128)S(1)}, f32[32,64,512]{2,1,0:T(8,128)}, u32[]{:S(2)}) %copy-start) | copy-done | bytes 4194328
  13.0 0.1 edges.1
  13.1 4.3 %all-to-all-done.2 = s32[32,1,128]{2,1,0:T(1,128)S(1)} async-done(((s32[32,1,128]{2,1,0:T(1,128)}), s32[32,1,128]{2,1,0:T(1,128)S(1)}, u32[]{:S(2)}, u32[]{:S(2)}) %all-to-all-start.2) | async-done | bytes 16416 | tf_op jit(solution)/shard_map/all_to_all | solution.py:442
  17.4 2.2 %copy-done.1 = f32[32,64,512]{2,1,0:T(8,128)S(1)} copy-done((f32[32,64,512]{2,1,0:T(8,128)S(1)}, f32[32,64,512]{2,1,0:T(8,128)}, u32[]{:S(2)}) %copy-start.1) | copy-done | bytes 4194328
  19.6 6.5 %serve.1 = (bf16[3072,128]{1,0:T(8,128)(2,1)}, bf16[1024,128]{1,0:T(8,128)(2,1)S(1)}) custom-call(s32[4096]{0:T(1024)S(1)} %bitcast.27, f32[32,64,512]{2,1,0:T(8,128)S(1)} %copy-done.1), custom_call_target="tpu_custom_call" | custom-call | flops 1048576 | bytes 6291456 | tf_op jit(solution)/shard_map/serve/pallas_call | solution.py:486
  26.4 1.9 %match.1 = (bf16[4096,128]{1,0:T(8,128)(2,1)S(1)}, s32[8,128]{1,0:T(8,128)S(1)}) custom-call(s32[32,128]{1,0:T(8,128)S(1)} %pad_add_fusion.incoming_ref, s32[32,128]{1,0:T(8,128)S(1)} %bitcast.30), custom_call_target="tpu_custom_call" | custom-call | flops 1000000000 | bytes 1048576 | tf_op jit(solution)/shard_map/match/pallas_call | solution.py:506
  28.3 0.5 slice.23
  29.4 2.9 %all-to-all-start.3 = ((bf16[32,96,128]{2,1,0:T(8,128)(2,1)}), bf16[32,96,128]{2,1,0:T(8,128)(2,1)S(1)}, u32[]{:S(2)}, u32[]{:S(2)}) async-start(bf16[32,96,128]{2,1,0:T(8,128)(2,1)} %bitcast.5), calls=%async_computation.3 | async-start | bytes 1572864 | tf_op jit(solution)/shard_map/all_to_all | solution.py:442
  32.4 0.1 copy.24
  32.5 3.5 %collective-permute-start = (bf16[2,64,512]{2,0,1:T(2,128)(2,1)S(1)}, bf16[2,64,512]{2,0,1:T(2,128)(2,1)S(1)}, u32[]{:S(2)}, u32[]{:S(2)}) collective-permute-start(bf16[2,64,512]{2,0,1:T(2,128)(2,1)S(1)} %copy.24), channel_id=1, source_target_pairs={{0,4},{4,8},{8,12},{12,16},{16,20},{20,24},{24,28},{1,5},{5,9},{9,... | collective-permute-start | bytes 393224 | tf_op jit(solution)/shard_map/ppermute | solution.py:404
  36.1 0.1 copy.25
  36.2 1.9 %collective-permute-start.1 = (bf16[2,64,512]{2,0,1:T(2,128)(2,1)S(1)}, bf16[2,64,512]{2,0,1:T(2,128)(2,1)S(1)}, u32[]{:S(2)}, u32[]{:S(2)}) collective-permute-start(bf16[2,64,512]{2,0,1:T(2,128)(2,1)S(1)} %copy.25), channel_id=1, source_target_pairs={{4,0},{8,4},{12,8},{16,12},{20,16},{24,20},{28,24},{5,1},{9,5},{13... | collective-permute-start | bytes 393224 | tf_op jit(solution)/shard_map/ppermute | solution.py:404
  38.2 0.9 collective-permute-done
  39.1 4.8 %collective-permute-done.1 = bf16[2,64,512]{2,0,1:T(2,128)(2,1)S(1)} collective-permute-done((bf16[2,64,512]{2,0,1:T(2,128)(2,1)S(1)}, bf16[2,64,512]{2,0,1:T(2,128)(2,1)S(1)}, u32[]{:S(2)}, u32[]{:S(2)}) %collective-permute-start.1) | collective-permute-done | bytes 131104 | tf_op jit(solution)/shard_map/ppermute | solution.py:404
  44.0 1.3 %collective-permute-start.3 = (bf16[2,36,512]{2,1,0:T(8,128)(2,1)S(1)}, bf16[2,36,512]{2,1,0:T(8,128)(2,1)S(1)}, u32[]{:S(2)}, u32[]{:S(2)}) collective-permute-start(bf16[2,36,512]{2,1,0:T(8,128)(2,1)S(1)} %pad_maximum_fusion.1), channel_id=1, source_target_pairs={{1,0},{2,1},{3,2},{5,4},{6,5},{7,6},{9,8},{10,9},{11,10},{13,12},{... | collective-permute-start | bytes 221192 | tf_op jit(solution)/shard_map/ppermute | solution.py:404
  45.3 4.2 %collective-permute-start.2 = (bf16[2,36,512]{2,1,0:T(8,128)(2,1)S(1)}, bf16[2,36,512]{2,1,0:T(8,128)(2,1)S(1)}, u32[]{:S(2)}, u32[]{:S(2)}) collective-permute-start(bf16[2,36,512]{2,1,0:T(8,128)(2,1)S(1)} %pad_maximum_fusion), channel_id=1, source_target_pairs={{0,1},{1,2},{2,3},{4,5},{5,6},{6,7},{8,9},{9,10},{10,11},{12,13},{... | collective-permute-start | bytes 221192 | tf_op jit(solution)/shard_map/ppermute | solution.py:404
  49.6 0.1 reshape.84
  49.7 0.1 copy.26
  49.8 0.1 reshape.85.position_ref
  50.0 0.1 copy.27
  50.2 0.8 collective-permute-done.3
  51.0 2.5 %all-to-all-done.3 = bf16[32,96,128]{2,1,0:T(8,128)(2,1)S(1)} async-done(((bf16[32,96,128]{2,1,0:T(8,128)(2,1)}), bf16[32,96,128]{2,1,0:T(8,128)(2,1)S(1)}, u32[]{:S(2)}, u32[]{:S(2)}) %all-to-all-start.3) | async-done | bytes 786464 | tf_op jit(solution)/shard_map/all_to_all | solution.py:442
  53.5 13.5 %stars.1 = (f32[16,128]{1,0:T(8,128)S(1)}, bf16[3072,128]{1,0:T(8,128)(2,1)}, bf16[1024,128]{1,0:T(8,128)(2,1)S(1)}) custom-call(s32[2048]{0:T(1024)S(1)} %reshape.85.position_ref, f32[16,128]{1,0:T(8,128)S(1)} %reshape.86.observed_ref, f32[16,128]{1,0:T(8,128)S(1)} %reshape.87.inverse_ref, bf16[64,32,32,128]{3,2,1,0:T(8,128)(2,1)} %weights_hbm.1, ...), custom_call_target="tpu_custom_call" | custom-call | flops 33554432 | bytes 16777216 | tf_op jit(solution)/shard_map/stars/pallas_call | solution.py:523
  67.1 4.2 %all-to-all-start.4 = ((bf16[32,96,128]{2,1,0:T(8,128)(2,1)}), bf16[32,96,128]{2,1,0:T(8,128)(2,1)S(1)}, u32[]{:S(2)}, u32[]{:S(2)}) async-start(bf16[32,96,128]{2,1,0:T(8,128)(2,1)} %bitcast.15), calls=%async_computation.4 | async-start | bytes 1572864 | tf_op jit(solution)/shard_map/all_to_all | solution.py:442
  71.4 0.7 copy.31
  72.1 2.2 %copy-done.2 = f32[32,64,512]{2,1,0:T(8,128)S(1)} copy-done((f32[32,64,512]{2,1,0:T(8,128)S(1)}, f32[32,64,512]{2,1,0:T(8,128)}, u32[]{:S(2)}) %copy-start.2) | copy-done | bytes 4194328
  74.3 10.7 %prior.1.base_hbm = f32[32,64,512]{2,1,0:T(8,128)S(1)} custom-call(f32[32,64,512]{2,1,0:T(8,128)S(1)} %copy-done.2, bf16[2,64,512]{2,1,0:T(8,128)(2,1)S(1)} %copy.29.xlo_ref, bf16[2,64,512]{2,1,0:T(8,128)(2,1)S(1)} %copy.30.xhi_ref, f32[2,36,512]{2,1,0:T(8,128)S(1)} %convert_element_type.22.ylo_ref, f32[2,36,512]{2,1,0:T(8,128)S(1)} %convert_element_type.24.yhi_ref), custom_call_target="tpu_custom_call" | custom-call | flops 31457280 | bytes 8388608 | tf_op jit(solution)/shard_map/prior/pallas_call | solution.py:551
  85.0 1.9 %copy-done.3 = f32[32,64,512]{2,1,0:T(8,128)} copy-done((f32[32,64,512]{2,1,0:T(8,128)}, f32[32,64,512]{2,1,0:T(8,128)S(1)}, u32[]{:S(2)}) %copy-start.3) | copy-done | bytes 4194328
  86.9 5.1 %all-to-all-done.4 = bf16[32,96,128]{2,1,0:T(8,128)(2,1)S(1)} async-done(((bf16[32,96,128]{2,1,0:T(8,128)(2,1)}), bf16[32,96,128]{2,1,0:T(8,128)(2,1)S(1)}, u32[]{:S(2)}, u32[]{:S(2)}) %all-to-all-start.4) | async-done | bytes 786464 | tf_op jit(solution)/shard_map/all_to_all | solution.py:442
  92.1 8.8 %finish.1 = f32[32,64,512]{2,1,0:T(8,128)} custom-call(s32[4096]{0:T(1024)S(1)} %bitcast.31, bf16[4096,128]{1,0:T(8,128)(2,1)S(1)} %get-tuple-element.74.match_ref, f32[32,64,512]{2,1,0:T(8,128)} %field_hbm.1, f32[32,64,512]{2,1,0:T(8,128)} %copy-done.3, bf16[3072,128]{1,0:T(8,128)(2,1)S(1)} %bitcast.26, bf16[1024,128]{1,0:T(8,128)(2,1)S(1)} %bitcast.37), custom_call_target="tpu_custom_call" | custom-call | flops 4194304 | bytes 12582912 | tf_op jit(solution)/shard_map/finish/pallas_call | solution.py:568
  (34 shorter events, 0.7 us)
Async XLA Ops:
  3.7 13.7 %all-to-all-start.2 = ((s32[32,1,128]{2,1,0:T(1,128)}), s32[32,1,128]{2,1,0:T(1,128)S(1)}, u32[]{:S(2)}, u32[]{:S(2)}) async-start(s32[32,1,128]{2,1,0:T(1,128)} %bitcast.40), calls=%async_computation.2 | async-start | bytes 32768 | tf_op jit(solution)/shard_map/all_to_all | solution.py:442
  10.8 2.2 %copy-start = (f32[32,64,512]{2,1,0:T(8,128)S(1)}, f32[32,64,512]{2,1,0:T(8,128)}, u32[]{:S(2)}) copy-start(f32[32,64,512]{2,1,0:T(8,128)} %field_hbm.1) | copy-start | bytes 12582916
  17.4 2.2 %copy-start.1 = (f32[32,64,512]{2,1,0:T(8,128)S(1)}, f32[32,64,512]{2,1,0:T(8,128)}, u32[]{:S(2)}) copy-start(f32[32,64,512]{2,1,0:T(8,128)} %field_hbm.1) | copy-start | bytes 12582916
  26.2 23.4 %copy-start.5 = (f32[64,32]{0,1:T(8,128)S(1)}, f32[64,32]{0,1:T(8,128)}, u32[]{:S(2)}) copy-start(f32[64,32]{0,1:T(8,128)} %param.13) | copy-start | bytes 24580
  26.2 23.4 %copy-start.7 = (s32[64]{0:T(128)S(1)}, s32[64]{0:T(128)}, u32[]{:S(2)}) copy-start(s32[64]{0:T(128)} %param.14) | copy-start | bytes 772
  26.2 23.4 %copy-start.6 = (s32[16,128]{1,0:T(8,128)S(1)}, s32[16,128]{1,0:T(8,128)}, u32[]{:S(2)}) copy-start(s32[16,128]{1,0:T(8,128)} %get-tuple-element.75) | copy-start | bytes 24580
  26.2 23.9 %copy-start.4 = (f32[64,32]{0,1:T(8,128)S(1)}, f32[64,32]{0,1:T(8,128)}, u32[]{:S(2)}) copy-start(f32[64,32]{0,1:T(8,128)} %param.12) | copy-start | bytes 24580
  29.4 24.1 %all-to-all-start.3 = ((bf16[32,96,128]{2,1,0:T(8,128)(2,1)}), bf16[32,96,128]{2,1,0:T(8,128)(2,1)S(1)}, u32[]{:S(2)}, u32[]{:S(2)}) async-start(bf16[32,96,128]{2,1,0:T(8,128)(2,1)} %bitcast.5), calls=%async_computation.3 | async-start | bytes 1572864 | tf_op jit(solution)/shard_map/all_to_all | solution.py:442
  32.5 6.6 %collective-permute-start = (bf16[2,64,512]{2,0,1:T(2,128)(2,1)S(1)}, bf16[2,64,512]{2,0,1:T(2,128)(2,1)S(1)}, u32[]{:S(2)}, u32[]{:S(2)}) collective-permute-start(bf16[2,64,512]{2,0,1:T(2,128)(2,1)S(1)} %copy.24), channel_id=1, source_target_pairs={{0,4},{4,8},{8,12},{12,16},{16,20},{20,24},{24,28},{1,5},{5,9},{9,... | collective-permute-start | bytes 393224 | tf_op jit(solution)/shard_map/ppermute | solution.py:404
  36.2 7.7 %collective-permute-start.1 = (bf16[2,64,512]{2,0,1:T(2,128)(2,1)S(1)}, bf16[2,64,512]{2,0,1:T(2,128)(2,1)S(1)}, u32[]{:S(2)}, u32[]{:S(2)}) collective-permute-start(bf16[2,64,512]{2,0,1:T(2,128)(2,1)S(1)} %copy.25), channel_id=1, source_target_pairs={{4,0},{8,4},{12,8},{16,12},{20,16},{24,20},{28,24},{5,1},{9,5},{13... | collective-permute-start | bytes 393224 | tf_op jit(solution)/shard_map/ppermute | solution.py:404
  44.0 7.0 %collective-permute-start.3 = (bf16[2,36,512]{2,1,0:T(8,128)(2,1)S(1)}, bf16[2,36,512]{2,1,0:T(8,128)(2,1)S(1)}, u32[]{:S(2)}, u32[]{:S(2)}) collective-permute-start(bf16[2,36,512]{2,1,0:T(8,128)(2,1)S(1)} %pad_maximum_fusion.1), channel_id=1, source_target_pairs={{1,0},{2,1},{3,2},{5,4},{6,5},{7,6},{9,8},{10,9},{11,10},{13,12},{... | collective-permute-start | bytes 221192 | tf_op jit(solution)/shard_map/ppermute | solution.py:404
  45.3 5.7 %collective-permute-start.2 = (bf16[2,36,512]{2,1,0:T(8,128)(2,1)S(1)}, bf16[2,36,512]{2,1,0:T(8,128)(2,1)S(1)}, u32[]{:S(2)}, u32[]{:S(2)}) collective-permute-start(bf16[2,36,512]{2,1,0:T(8,128)(2,1)S(1)} %pad_maximum_fusion), channel_id=1, source_target_pairs={{0,1},{1,2},{2,3},{4,5},{5,6},{6,7},{8,9},{9,10},{10,11},{12,13},{... | collective-permute-start | bytes 221192 | tf_op jit(solution)/shard_map/ppermute | solution.py:404
  67.1 25.0 %all-to-all-start.4 = ((bf16[32,96,128]{2,1,0:T(8,128)(2,1)}), bf16[32,96,128]{2,1,0:T(8,128)(2,1)S(1)}, u32[]{:S(2)}, u32[]{:S(2)}) async-start(bf16[32,96,128]{2,1,0:T(8,128)(2,1)} %bitcast.15), calls=%async_computation.4 | async-start | bytes 1572864 | tf_op jit(solution)/shard_map/all_to_all | solution.py:442
  72.1 2.2 %copy-start.2 = (f32[32,64,512]{2,1,0:T(8,128)S(1)}, f32[32,64,512]{2,1,0:T(8,128)}, u32[]{:S(2)}) copy-start(f32[32,64,512]{2,1,0:T(8,128)} %field_hbm.1) | copy-start | bytes 12582916
  85.0 1.9 %copy-start.3 = (f32[32,64,512]{2,1,0:T(8,128)}, f32[32,64,512]{2,1,0:T(8,128)S(1)}, u32[]{:S(2)}) copy-start(f32[32,64,512]{2,1,0:T(8,128)S(1)} %prior.1.base_hbm) | copy-start | bytes 12582916

commit v7 on v6

--- a/solution.py
+++ b/solution.py
@@ -79,14 +79,28 @@
     outgoing_ref[...] = listed
 
 
-def edges_kernel(field_ref, xfirst_ref, xlast_ref, yfirst_ref, ylast_ref):
-    cells_x, cells_y, _ = field_ref.shape
-    xfirst_ref[...] = field_ref[:2].astype(xfirst_ref.dtype)
-    xlast_ref[...] = field_ref[cells_x - 2 :].astype(xlast_ref.dtype)
+def edges_kernel(
+    field_hbm, xfirst_ref, xlast_ref, yfirst_ref, ylast_ref, planes_ref, strips_ref, sems
+):
+    cells_x, cells_y, _ = field_hbm.shape
+    copies = [
+        pltpu.make_async_copy(field_hbm.at[pl.ds(0, 2)], planes_ref.at[0], sems.at[0]),
+        pltpu.make_async_copy(field_hbm.at[pl.ds(cells_x - 2, 2)], planes_ref.at[1], sems.at[1]),
+        pltpu.make_async_copy(field_hbm.at[:, pl.ds(0, 8)], strips_ref.at[0], sems.at[2]),
+        pltpu.make_async_copy(
+            field_hbm.at[:, pl.ds(cells_y - 8, 8)], strips_ref.at[1], sems.at[3]
+        ),
+    ]
+    for copy in copies:
+        copy.start()
+    for copy in copies:
+        copy.wait()
+    xfirst_ref[...] = planes_ref[0].astype(xfirst_ref.dtype)
+    xlast_ref[...] = planes_ref[1].astype(xlast_ref.dtype)
     for h in range(2):
         for x in range(cells_x):
-            yfirst_ref[h, x : x + 1, :] = field_ref[x, h : h + 1, :]
-            ylast_ref[h, x : x + 1, :] = field_ref[x, cells_y - 2 + h : cells_y - 1 + h, :]
+            yfirst_ref[h, x : x + 1, :] = strips_ref[0, x, h : h + 1, :]
+            ylast_ref[h, x : x + 1, :] = strips_ref[1, x, 6 + h : 7 + h, :]
 
 
 def for_each_group(incoming_ref, visit, capacity, first_slots, blocks):
@@ -129,10 +143,25 @@
     lax.fori_loop(0, sources, one_source, 0)
 
 
-def serve_kernel(incoming_ref, field_ref, *refs, capacity, first_slots):
-    *served_refs, table_ref = refs
+def serve_kernel(incoming_ref, field_hbm, *refs, capacity, first_slots):
+    *served_refs, crowded_ref, field_ref, table_ref, sems = refs
     cells_x, cells_y, depth = field_ref.shape
     per_column = depth // LANES
+    parts = sems.shape[0]
+    planes = cells_x // parts
+
+    def load(part):
+        span = pl.ds(part * planes, planes)
+        return pltpu.make_async_copy(field_hbm.at[span], field_ref.at[span], sems.at[part])
+
+    for part in range(parts):
+        load(part).start()
+
+    def mark_of(source, most):
+        return jnp.maximum(most, incoming_ref[source * capacity + capacity - 1] >> 16)
+
+    fullest = lax.fori_loop(0, incoming_ref.shape[0] // capacity, mark_of, jnp.int32(0))
+    crowded_ref[0] = jnp.where(fullest > first_slots, 1, 0)
     table_rows = table_ref.reshape(table_ref.shape[0], LANES)
     blocks = cells_x * cells_y * per_column
     table_rows[blocks:, :] = jnp.zeros((table_ref.shape[0] - blocks, LANES), jnp.float32)
@@ -146,7 +175,9 @@
                 )
         return carry
 
-    lax.fori_loop(0, cells_x, one_plane, 0)
+    for part in range(parts):
+        load(part).wait()
+        lax.fori_loop(part * planes, (part + 1) * planes, one_plane, 0)
 
     def visit(wanted, row, list_part):
         rows = jnp.concatenate([table_ref[at] for at in wanted], axis=0)
@@ -155,10 +186,7 @@
     for_each_group(incoming_ref, visit, capacity, first_slots, blocks)
 
 
-def match_kernel(incoming_ref, marked_ref, match_ref, fullest_ref):
-    marks = marked_ref[:, marked_ref.shape[1] - 1 :] >> 16
-    fullest = jnp.max(marks, axis=0, keepdims=True)
-    fullest_ref[...] = jnp.broadcast_to(fullest, fullest_ref.shape)
+def match_kernel(incoming_ref, match_ref):
     lane = lax.broadcasted_iota(jnp.int32, (LANES, LANES), 1)
     row = lax.broadcasted_iota(jnp.int32, (LANES, LANES), 0)
     ones = jnp.ones((LANES, LANES), jnp.bfloat16)
@@ -188,9 +216,10 @@
     extinction_ref, refs = refs[0], refs[1:]
     parcel_refs, refs = refs[:exchanges], refs[exchanges:]
     weights_ref, returned_rows, sens_ref, parcel_rows, sems = refs
-    blocks_dev, slots, stars, width = weights_ref.shape
-    chunks = sems.shape[0]
-    per = blocks_dev // chunks
+    sets, in_set, per, slots, stars, width = weights_ref.shape
+    chunks = extinction_ref.shape[0]
+    rounds = chunks // (sets * in_set)
+    per_chunk = per * slots
     fold = LANES // stars
     all_slots = parcel_rows.shape[0]
     lane = lax.broadcasted_iota(jnp.int32, (8, LANES), 1)
@@ -198,24 +227,23 @@
     star_group = lane // stars
     own_slot = [row == star_group + fold * h for h in range(8 // fold)]
 
-    def load(chunk):
-        span = pl.ds(chunk * per, per)
-        return pltpu.make_async_copy(weights_hbm.at[span], weights_ref.at[span], sems.at[chunk])
-
-    def start_of(chunk):
-        return pl.multiple_of(chunk * per * slots, per * slots)
-
-    def positions(chunk):
-        return position_ref.at[pl.ds(start_of(chunk), per * slots)]
-
-    def extinctions(chunk):
-        places = positions(chunk)
+    def load(one_round, one_set):
+        return [
+            pltpu.make_async_copy(
+                weights_hbm.at[pl.ds(((one_round * sets + one_set) * in_set + u) * per, per)],
+                weights_ref.at[one_set, u],
+                sems.at[one_set, u],
+            )
+            for u in range(in_set)
+        ]
+
+    def extinctions(one_set, u, chunk, places):
         sums = []
         for b in range(per):
             total = jnp.zeros((stars, width), jnp.float32)
             for k in range(slots):
-                fetched = returned_rows[places[b * slots + k]]
-                total = total + weights_ref[chunk * per + b, k].astype(jnp.float32) * fetched
+                fetched = returned_rows[places[u * per_chunk + b * slots + k]]
+                total = total + weights_ref[one_set, u, b, k].astype(jnp.float32) * fetched
             sums.append(total)
         extinction = lax.dot_general(
             jnp.ones((8, width), jnp.float32),
@@ -228,7 +256,7 @@
         extinction_ref[here, :] = extinction[:1]
         return inverse_ref[here, :] * (extinction - observed_ref[here, :])
 
-    def sensitivities(chunk, weighted):
+    def sensitivities(one_set, u, weighted):
         for b in range(per):
             spread = jnp.where(star_group == b, weighted, 0.0)
             shift = stars
@@ -238,45 +266,54 @@
             left = jnp.concatenate(
                 [jnp.where(own, spread, 0.0) for own in own_slot], axis=1
             ).astype(jnp.bfloat16)
-            eights = [weights_ref[chunk * per + b, 8 * j : 8 * j + 8] for j in range(slots // 8)]
+            eights = [weights_ref[one_set, u, b, 8 * j : 8 * j + 8] for j in range(slots // 8)]
             right = jnp.concatenate([x.reshape(8 * stars, width) for x in eights], axis=1)
             sens = jnp.dot(left, right, preferred_element_type=jnp.float32)
             for j in range(slots // 8):
-                sens_ref[pl.ds(start_of(chunk) + b * slots + 8 * j, 8), :] = sens[
-                    :, j * width : (j + 1) * width
-                ]
-
-    def scatter(chunk):
-        places = positions(chunk)
-        rows = sens_ref.at[pl.ds(start_of(chunk), per * slots)]
-        for i in range(per * slots):
-            parcel_rows[places[i]] = rows[i : i + 1, :]
-
-    for chunk in range(chunks):
-        load(chunk).start()
+                first = u * per_chunk + b * slots + 8 * j
+                sens_ref[first : first + 8, :] = sens[:, j * width : (j + 1) * width]
+
+    def scatter(u, places):
+        for i in range(u * per_chunk, (u + 1) * per_chunk):
+            parcel_rows[places[i]] = sens_ref[i : i + 1, :]
+
+    def work(one_round, one_set):
+        first = (one_round * sets + one_set) * in_set
+        size = in_set * per_chunk
+        places = position_ref.at[pl.ds(pl.multiple_of(first * per_chunk, size), size)]
+        weighted = {}
+        for u in range(in_set + 2):
+            if u < in_set:
+                weighted[u] = extinctions(one_set, u, first + u, places)
+            if 1 <= u <= in_set:
+                sensitivities(one_set, u - 1, weighted[u - 1])
+            if u >= 2:
+                scatter(u - 2, places)
+
+    for one_set in range(sets):
+        for copy in load(0, one_set):
+            copy.start()
     start = 0
     for returned_ref in returned_refs:
         span = slice(start, start + returned_ref.shape[0])
         returned_rows.reshape(all_slots, width)[span, :] = returned_ref[...].astype(jnp.float32)
         start = span.stop
     parcel_rows.reshape(all_slots, width)[...] = jnp.zeros((all_slots, width), jnp.float32)
-    load(0).wait()
-    weighted = extinctions(0)
-    load(1).wait()
-    following = extinctions(1)
-    sensitivities(0, weighted)
-
-    def step(chunk, weighted):
-        load(chunk).wait()
-        following = extinctions(chunk)
-        sensitivities(chunk - 1, weighted)
-        scatter(chunk - 2)
-        return following
-
-    weighted = lax.fori_loop(2, chunks, step, following)
-    sensitivities(chunks - 1, weighted)
-    scatter(chunks - 2)
-    scatter(chunks - 1)
+
+    def one_round(i, carry):
+        for one_set in range(sets):
+            for copy in load(i, one_set):
+                copy.wait()
+            work(i, one_set)
+
+            @pl.when(i + 1 < rounds)
+            def _():
+                for copy in load(i + 1, one_set):
+                    copy.start()
+
+        return carry
+
+    lax.fori_loop(0, rounds, one_round, 0)
     start = 0
     for parcel_ref in parcel_refs:
         span = slice(start, start + parcel_ref.shape[0])
@@ -474,50 +511,59 @@
             shape((2, cells_x, depth), f32),
             shape((2, cells_x, depth), f32),
         ],
-        in_specs=[VMEM],
+        in_specs=[ANY],
         out_specs=[VMEM] * 4,
-        compiler_params=pltpu.CompilerParams(vmem_limit_bytes=8 * MIB),
+        scratch_shapes=[
+            pltpu.VMEM((2, 2, cells_y, depth), f32),
+            pltpu.VMEM((2, cells_x, 8, depth), f32),
+            pltpu.SemaphoreType.DMA((4,)),
+        ],
+        compiler_params=pltpu.CompilerParams(vmem_limit_bytes=56 * MIB),
         cost_estimate=pl.CostEstimate(flops=0, bytes_accessed=2 * MIB, transcendentals=0),
         name="edges",
     )(field)
     incoming, *edges = lax.optimization_barrier((incoming, xfirst, xlast, yfirst, ylast))
     wanted = incoming.reshape(-1)
 
-    served = pl.pallas_call(
+    parts = 8
+    *served, crowded = pl.pallas_call(
         functools.partial(serve_kernel, capacity=capacity, first_slots=first_slots),
-        out_shape=[shape((devices * n, width), bf16) for n in slots_of],
-        in_specs=[SMEM, VMEM],
-        out_specs=[VMEM] * exchanges,
+        out_shape=[shape((devices * n, width), bf16) for n in slots_of] + [shape((1,), i32)],
+        in_specs=[SMEM, ANY],
+        out_specs=[VMEM] * exchanges + [SMEM],
         scratch_shapes=[
+            pltpu.VMEM(field_shape, f32),
             pltpu.VMEM((blocks + capacity, 1, width), f32),
+            pltpu.SemaphoreType.DMA((parts,)),
         ],
-        compiler_params=pltpu.CompilerParams(vmem_limit_bytes=24 * MIB),
+        compiler_params=pltpu.CompilerParams(vmem_limit_bytes=56 * MIB),
         cost_estimate=pl.CostEstimate(
             flops=cells, bytes_accessed=6 * MIB, transcendentals=cells
         ),
         name="serve",
-    )(wanted, field)
+    )(wanted, log_density)
+    crowded = crowded[0] != 0
 
     incoming_late, *edges, _ = lax.optimization_barrier((incoming, *edges, served[0]))
     slot_lists = [
         incoming_late[:, :first_slots].reshape(-1, LANES),
         (incoming_late[:, first_slots:] & (MARK - 1)).reshape(-1, LANES),
     ][:exchanges]
-    match, fullest = pl.pallas_call(
+    match = pl.pallas_call(
         match_kernel,
-        out_shape=[shape((all_slots, LANES), bf16), shape((8, LANES), i32)],
-        in_specs=[VMEM] * 2,
-        out_specs=[VMEM] * 2,
+        out_shape=shape((all_slots, LANES), bf16),
+        in_specs=[VMEM],
+        out_specs=VMEM,
         compiler_params=pltpu.CompilerParams(vmem_limit_bytes=8 * MIB),
         cost_estimate=pl.CostEstimate(flops=10**9, bytes_accessed=MIB, transcendentals=0),
         name="match",
-    )(jnp.concatenate(slot_lists, axis=0), incoming_late)
-    crowded = fullest[0, 0] > first_slots
+    )(jnp.concatenate(slot_lists, axis=0))
     returned = exchange_rows(served, crowded)
     xlo, xhi, ylo, yhi = halo(*edges)
     *returned, match, ylo, yhi = lax.optimization_barrier((*returned, match, ylo, yhi))
 
     chunks = blocks_dev * stars // LANES
+    in_set = chunks // 4
     live = jnp.arange(stars)[None, :] < star_counts[:, None]
     live_inverse = jnp.where(live, inverse_var, 0.0)
     extinction, *parcel = pl.pallas_call(
@@ -527,11 +573,11 @@
         in_specs=[SMEM, VMEM, VMEM, ANY] + [VMEM] * exchanges,
         out_specs=[VMEM] * (1 + exchanges),
         scratch_shapes=[
-            pltpu.VMEM(weights.shape, bf16),
+            pltpu.VMEM((2, in_set, blocks_dev // chunks, slots, stars, width), bf16),
             pltpu.VMEM((all_slots, 1, width), f32),
-            pltpu.VMEM((requests, width), f32),
+            pltpu.VMEM((in_set * LANES // stars * slots, width), f32),
             pltpu.VMEM((all_slots, 1, width), f32),
-            pltpu.SemaphoreType.DMA((chunks,)),
+            pltpu.SemaphoreType.DMA((2, in_set)),
         ],
         compiler_params=pltpu.CompilerParams(vmem_limit_bytes=50 * MIB),
         cost_estimate=pl.CostEstimate(
@@ -564,7 +610,6 @@
         name="prior",
     )(field_late, xlo, xhi, ylo, yhi)
 
-    parts = 8
     new_log_density = pl.pallas_call(
         functools.partial(
             finish_kernel, exchanges=exchanges, capacity=capacity, first_slots=first_slots

time: 101 us -> 98.7 us (0.977)
  waiting for transfers between devices: 18.5 us -> 14.9 us
  local copies, waits for them, and re-layouts: 10.9 us -> 7.35 us
  Pallas kernels: 44.6 us -> 47.1 us
    unnamed x18 -> x26, local copies, waits for them, and re-layouts: 9.28 us -> 5.55 us
    ppermute x4, waiting for transfers between devices: 6.51 us -> 3.44 us  [both_ways(): return (lax.ppermute(last, axis, up), lax.ppermute(first, axis, down))]
    pallas_call x1, Pallas kernels: 0.09 us -> 2.27 us  [on_device(): pl.pallas_call(edges_kernel, out_shape=[shape((2, cells_y, depth), bf16),...]
    pallas_call x1, Pallas kernels: 6.54 us -> 8.17 us  [on_device(): pl.pallas_call(functools.partial(serve_kernel, capacity=capacity, first_s...]
    pallas_call x1, Pallas kernels: 13.5 us -> 12.3 us  [on_device(): pl.pallas_call(functools.partial(star_kernel, exchanges=exchanges), out_s...]
  transfers between devices with their start and end apart: 7 -> 7, of which waited for: 6 -> 4; matrix products, arithmetic and copies ran while one was open for 2% -> 4% of each run, Pallas kernels for 11% -> 15%
where the time goes in v7:
time: 98.7 us; the launch traced here: 98 us
  Pallas kernels  47.1 us (48%)
  starting transfers between devices  26.1 us (26%)
  waiting for transfers between devices  14.9 us (15%)
  local copies, waits for them, and re-layouts  7.35 us (7%)
  between operations  1.61 us (2%)
    all_to_all x3, starting transfers between devices, exchange(): return lax.all_to_all(x, mesh_axes, split_axis=0, concat_axis=0, tiled=True)  15.1 us
    pallas_call x1, Pallas kernels, on_device(): pl.pallas_call(functools.partial(star_kernel, exchanges=exchanges), out_s...  12.3 us
    all_to_all x3, waiting for transfers between devices, exchange(): return lax.all_to_all(x, mesh_axes, split_axis=0, concat_axis=0, tiled=True)  11.5 us
    ppermute x4, starting transfers between devices, both_ways(): return (lax.ppermute(last, axis, up), lax.ppermute(first, axis, down))  11 us
    pallas_call x1, Pallas kernels, on_device(): pl.pallas_call(prior_kernel, out_shape=shape(field_shape, f32), in_specs=...  10.7 us
    pallas_call x1, Pallas kernels, on_device(): pl.pallas_call(functools.partial(finish_kernel, exchanges=exchanges, capa...  8.76 us
    pallas_call x1, Pallas kernels, on_device(): pl.pallas_call(functools.partial(serve_kernel, capacity=capacity, first_s...  8.17 us
    unnamed x26, local copies, waits for them, and re-layouts  5.55 us
  transfers between devices with their start and end apart: 7, of which 4 were waited for; matrix products, arithmetic and copies ran while one was open for 4% of the time, Pallas kernels for 15%

profile of v7, /device:TPU:1, one launch (start us, length us, event | category | flops | bytes accessed | tf_op | source)
XLA Modules:
  0.0 98.0 jit_solution(15044370490807974015)
XLA Ops:
  0.6 3.1 %route.1 = (s32[32,128]{1,0:T(8,128)}, s32[16,128]{1,0:T(8,128)}) custom-call(s32[32,64]{1,0:T(8,128)} %bitcast.39), custom_call_target="tpu_custom_call" | custom-call | tf_op jit(solution)/shard_map/route/pallas_call | solution.py:489
  3.7 7.1 %all-to-all-start.2 = ((s32[32,1,128]{2,1,0:T(1,128)}), s32[32,1,128]{2,1,0:T(1,128)S(1)}, u32[]{:S(2)}, u32[]{:S(2)}) async-start(s32[32,1,128]{2,1,0:T(1,128)} %bitcast.40), calls=%async_computation.2 | async-start | bytes 32768 | tf_op jit(solution)/shard_map/all_to_all | solution.py:479
  10.8 2.3 %edges.1 = (bf16[2,64,512]{2,1,0:T(8,128)(2,1)}, bf16[2,64,512]{2,1,0:T(8,128)(2,1)}, f32[2,32,512]{2,1,0:T(8,128)}, f32[2,32,512]{2,1,0:T(8,128)}) custom-call(f32[32,64,512]{2,1,0:T(8,128)} %field_hbm.4), custom_call_target="tpu_custom_call" | custom-call | bytes 2097152 | tf_op jit(solution)/shard_map/edges/pallas_call | solution.py:506
  13.2 4.2 %all-to-all-done.2 = s32[32,1,128]{2,1,0:T(1,128)S(1)} async-done(((s32[32,1,128]{2,1,0:T(1,128)}), s32[32,1,128]{2,1,0:T(1,128)S(1)}, u32[]{:S(2)}, u32[]{:S(2)}) %all-to-all-start.2) | async-done | bytes 16416 | tf_op jit(solution)/shard_map/all_to_all | solution.py:479
  17.4 0.6 copy-done.2
  18.0 8.2 %serve.1 = (bf16[3072,128]{1,0:T(8,128)(2,1)}, bf16[1024,128]{1,0:T(8,128)(2,1)S(1)}, s32[1]{0:T(128)}) custom-call(s32[4096]{0:T(1024)} %bitcast.27, f32[32,64,512]{2,1,0:T(8,128)} %field_hbm.4), custom_call_target="tpu_custom_call" | custom-call | flops 1048576 | bytes 6291456 | tf_op jit(solution)/shard_map/serve/pallas_call | solution.py:529
  26.9 2.9 %all-to-all-start.3 = ((bf16[32,96,128]{2,1,0:T(8,128)(2,1)}), bf16[32,96,128]{2,1,0:T(8,128)(2,1)S(1)}, u32[]{:S(2)}, u32[]{:S(2)}) async-start(bf16[32,96,128]{2,1,0:T(8,128)(2,1)} %bitcast.37), calls=%async_computation.3 | async-start | bytes 1572864 | tf_op jit(solution)/shard_map/all_to_all | solution.py:479
  29.8 0.1 reshape.84
  29.9 0.1 copy.26
  30.0 0.1 reshape.85.position_ref
  30.1 0.1 copy.28
  30.2 0.1 reshape.87.inverse_ref
  30.3 0.1 copy.27
  30.5 0.1 copy.24
  30.6 3.5 %collective-permute-start = (bf16[2,64,512]{2,0,1:T(2,128)(2,1)S(1)}, bf16[2,64,512]{2,0,1:T(2,128)(2,1)S(1)}, u32[]{:S(2)}, u32[]{:S(2)}) collective-permute-start(bf16[2,64,512]{2,0,1:T(2,128)(2,1)S(1)} %copy.24), channel_id=1, source_target_pairs={{0,4},{4,8},{8,12},{12,16},{16,20},{20,24},{24,28},{1,5},{5,9},{9,... | collective-permute-start | bytes 393224 | tf_op jit(solution)/shard_map/ppermute | solution.py:441
  34.2 0.1 copy.25
  34.3 1.9 %collective-permute-start.1 = (bf16[2,64,512]{2,0,1:T(2,128)(2,1)S(1)}, bf16[2,64,512]{2,0,1:T(2,128)(2,1)S(1)}, u32[]{:S(2)}, u32[]{:S(2)}) collective-permute-start(bf16[2,64,512]{2,0,1:T(2,128)(2,1)S(1)} %copy.25), channel_id=1, source_target_pairs={{4,0},{8,4},{12,8},{16,12},{20,16},{24,20},{28,24},{5,1},{9,5},{13... | collective-permute-start | bytes 393224 | tf_op jit(solution)/shard_map/ppermute | solution.py:441
  36.3 0.8 slice_and_fusion
  37.2 0.8 reshape.82
  38.0 3.4 %collective-permute-done.1 = bf16[2,64,512]{2,0,1:T(2,128)(2,1)S(1)} collective-permute-done((bf16[2,64,512]{2,0,1:T(2,128)(2,1)S(1)}, bf16[2,64,512]{2,0,1:T(2,128)(2,1)S(1)}, u32[]{:S(2)}, u32[]{:S(2)}) %collective-permute-start.1) | collective-permute-done | bytes 131104 | tf_op jit(solution)/shard_map/ppermute | solution.py:441
  41.5 1.3 %collective-permute-start.3 = (bf16[2,36,512]{2,1,0:T(8,128)(2,1)S(1)}, bf16[2,36,512]{2,1,0:T(8,128)(2,1)S(1)}, u32[]{:S(2)}, u32[]{:S(2)}) collective-permute-start(bf16[2,36,512]{2,1,0:T(8,128)(2,1)S(1)} %pad_maximum_fusion.1), channel_id=1, source_target_pairs={{1,0},{2,1},{3,2},{5,4},{6,5},{7,6},{9,8},{10,9},{11,10},{13,12},{... | collective-permute-start | bytes 221192 | tf_op jit(solution)/shard_map/ppermute | solution.py:441
  42.8 4.2 %collective-permute-start.2 = (bf16[2,36,512]{2,1,0:T(8,128)(2,1)S(1)}, bf16[2,36,512]{2,1,0:T(8,128)(2,1)S(1)}, u32[]{:S(2)}, u32[]{:S(2)}) collective-permute-start(bf16[2,36,512]{2,1,0:T(8,128)(2,1)S(1)} %pad_maximum_fusion), channel_id=1, source_target_pairs={{0,1},{1,2},{2,3},{4,5},{5,6},{6,7},{8,9},{9,10},{10,11},{12,13},{... | collective-permute-start | bytes 221192 | tf_op jit(solution)/shard_map/ppermute | solution.py:441
  47.0 1.8 %match.1.match_ref = bf16[4096,128]{1,0:T(8,128)(2,1)S(1)} custom-call(s32[32,128]{1,0:T(8,128)S(1)} %pad_add_fusion.incoming_ref), custom_call_target="tpu_custom_call" | custom-call | flops 1000000000 | bytes 1048576 | tf_op jit(solution)/shard_map/match/pallas_call | solution.py:552
  48.9 2.1 %all-to-all-done.3 = bf16[32,96,128]{2,1,0:T(8,128)(2,1)S(1)} async-done(((bf16[32,96,128]{2,1,0:T(8,128)(2,1)}), bf16[32,96,128]{2,1,0:T(8,128)(2,1)S(1)}, u32[]{:S(2)}, u32[]{:S(2)}) %all-to-all-start.3) | async-done | bytes 786464 | tf_op jit(solution)/shard_map/all_to_all | solution.py:479
  51.0 12.3 %stars.1 = (f32[16,128]{1,0:T(8,128)S(1)}, bf16[3072,128]{1,0:T(8,128)(2,1)}, bf16[1024,128]{1,0:T(8,128)(2,1)S(1)}) custom-call(s32[2048]{0:T(1024)S(1)} %reshape.85.position_ref, f32[16,128]{1,0:T(8,128)S(1)} %reshape.86.observed_ref, f32[16,128]{1,0:T(8,128)S(1)} %reshape.87.inverse_ref, bf16[64,32,32,128]{3,2,1,0:T(8,128)(2,1)} %weights_hbm.1, ...), custom_call_target="tpu_custom_call" | custom-call | flops 33554432 | bytes 16777216 | tf_op jit(solution)/shard_map/stars/pallas_call | solution.py:569
  63.3 5.1 %all-to-all-start.4 = ((bf16[32,96,128]{2,1,0:T(8,128)(2,1)}), bf16[32,96,128]{2,1,0:T(8,128)(2,1)S(1)}, u32[]{:S(2)}, u32[]{:S(2)}) async-start(bf16[32,96,128]{2,1,0:T(8,128)(2,1)} %bitcast.15), calls=%async_computation.4 | async-start | bytes 1572864 | tf_op jit(solution)/shard_map/all_to_all | solution.py:479
  68.6 0.7 copy.31
  69.3 2.2 %copy-done = f32[32,64,512]{2,1,0:T(8,128)S(1)} copy-done((f32[32,64,512]{2,1,0:T(8,128)S(1)}, f32[32,64,512]{2,1,0:T(8,128)}, u32[]{:S(2)}) %copy-start) | copy-done | bytes 4194328
  71.5 10.7 %prior.1.base_hbm = f32[32,64,512]{2,1,0:T(8,128)S(1)} custom-call(f32[32,64,512]{2,1,0:T(8,128)S(1)} %copy-done, bf16[2,64,512]{2,1,0:T(8,128)(2,1)S(1)} %copy.29.xlo_ref, bf16[2,64,512]{2,1,0:T(8,128)(2,1)S(1)} %copy.30.xhi_ref, f32[2,36,512]{2,1,0:T(8,128)S(1)} %convert_element_type.22.ylo_ref, f32[2,36,512]{2,1,0:T(8,128)S(1)} %convert_element_type.24.yhi_ref), custom_call_target="tpu_custom_call" | custom-call | flops 31457280 | bytes 8388608 | tf_op jit(solution)/shard_map/prior/pallas_call | solution.py:597
  82.2 1.9 %copy-done.1 = f32[32,64,512]{2,1,0:T(8,128)} copy-done((f32[32,64,512]{2,1,0:T(8,128)}, f32[32,64,512]{2,1,0:T(8,128)S(1)}, u32[]{:S(2)}) %copy-start.1) | copy-done | bytes 4194328
  84.2 5.1 %all-to-all-done.4 = bf16[32,96,128]{2,1,0:T(8,128)(2,1)S(1)} async-done(((bf16[32,96,128]{2,1,0:T(8,128)(2,1)}), bf16[32,96,128]{2,1,0:T(8,128)(2,1)S(1)}, u32[]{:S(2)}, u32[]{:S(2)}) %all-to-all-start.4) | async-done | bytes 786464 | tf_op jit(solution)/shard_map/all_to_all | solution.py:479
  89.3 8.8 %finish.1 = f32[32,64,512]{2,1,0:T(8,128)} custom-call(s32[4096]{0:T(1024)S(1)} %bitcast.30, bf16[4096,128]{1,0:T(8,128)(2,1)S(1)} %match.1.match_ref, f32[32,64,512]{2,1,0:T(8,128)} %field_hbm.4, f32[32,64,512]{2,1,0:T(8,128)} %copy-done.1, bf16[3072,128]{1,0:T(8,128)(2,1)S(1)} %bitcast.26, bf16[1024,128]{1,0:T(8,128)(2,1)S(1)} %bitcast.33), custom_call_target="tpu_custom_call" | custom-call | flops 4194304 | bytes 12582912 | tf_op jit(solution)/shard_map/finish/pallas_call | solution.py:613
  (41 shorter events, 0.5 us)
Async XLA Ops:
  3.7 13.7 %all-to-all-start.2 = ((s32[32,1,128]{2,1,0:T(1,128)}), s32[32,1,128]{2,1,0:T(1,128)S(1)}, u32[]{:S(2)}, u32[]{:S(2)}) async-start(s32[32,1,128]{2,1,0:T(1,128)} %bitcast.40), calls=%async_computation.2 | async-start | bytes 32768 | tf_op jit(solution)/shard_map/all_to_all | solution.py:479
  13.1 16.7 %copy-start.10 = (s32[16,128]{1,0:T(8,128)S(1)}, s32[16,128]{1,0:T(8,128)}, u32[]{:S(2)}) copy-start(s32[16,128]{1,0:T(8,128)} %get-tuple-element.73) | copy-start | bytes 24580
  13.1 17.0 %copy-start.9 = (f32[64,32]{0,1:T(8,128)S(1)}, f32[64,32]{0,1:T(8,128)}, u32[]{:S(2)}) copy-start(f32[64,32]{0,1:T(8,128)} %param.13) | copy-start | bytes 24580
  13.1 17.0 %copy-start.11 = (s32[64]{0:T(128)S(1)}, s32[64]{0:T(128)}, u32[]{:S(2)}) copy-start(s32[64]{0:T(128)} %param.14) | copy-start | bytes 772
  13.1 17.2 %copy-start.8 = (f32[64,32]{0,1:T(8,128)S(1)}, f32[64,32]{0,1:T(8,128)}, u32[]{:S(2)}) copy-start(f32[64,32]{0,1:T(8,128)} %param.12) | copy-start | bytes 24580
  13.1 17.3 %copy-start.7 = (bf16[2,64,512]{2,1,0:T(8,128)(2,1)S(1)}, bf16[2,64,512]{2,1,0:T(8,128)(2,1)}, u32[]{:S(2)}) copy-start(bf16[2,64,512]{2,1,0:T(8,128)(2,1)} %get-tuple-element.68) | copy-start | bytes 393220
  13.1 21.0 %copy-start.6 = (bf16[2,64,512]{2,1,0:T(8,128)(2,1)S(1)}, bf16[2,64,512]{2,1,0:T(8,128)(2,1)}, u32[]{:S(2)}) copy-start(bf16[2,64,512]{2,1,0:T(8,128)(2,1)} %get-tuple-element.70) | copy-start | bytes 393220
  13.2 23.9 %copy-start.5 = (f32[2,32,512]{2,1,0:T(8,128)S(1)}, f32[2,32,512]{2,1,0:T(8,128)}, u32[]{:S(2)}) copy-start(f32[2,32,512]{2,1,0:T(8,128)} %get-tuple-element.71) | copy-start | bytes 393220
  13.2 23.9 %copy-start.4 = (f32[2,32,512]{2,1,0:T(8,128)S(1)}, f32[2,32,512]{2,1,0:T(8,128)}, u32[]{:S(2)}) copy-start(f32[2,32,512]{2,1,0:T(8,128)} %get-tuple-element.69) | copy-start | bytes 393220
  17.4 0.6 copy-start.2
  26.9 24.1 %all-to-all-start.3 = ((bf16[32,96,128]{2,1,0:T(8,128)(2,1)}), bf16[32,96,128]{2,1,0:T(8,128)(2,1)S(1)}, u32[]{:S(2)}, u32[]{:S(2)}) async-start(bf16[32,96,128]{2,1,0:T(8,128)(2,1)} %bitcast.37), calls=%async_computation.3 | async-start | bytes 1572864 | tf_op jit(solution)/shard_map/all_to_all | solution.py:479
  30.6 7.3 %collective-permute-start = (bf16[2,64,512]{2,0,1:T(2,128)(2,1)S(1)}, bf16[2,64,512]{2,0,1:T(2,128)(2,1)S(1)}, u32[]{:S(2)}, u32[]{:S(2)}) collective-permute-start(bf16[2,64,512]{2,0,1:T(2,128)(2,1)S(1)} %copy.24), channel_id=1, source_target_pairs={{0,4},{4,8},{8,12},{12,16},{16,20},{20,24},{24,28},{1,5},{5,9},{9,... | collective-permute-start | bytes 393224 | tf_op jit(solution)/shard_map/ppermute | solution.py:441
  34.3 7.1 %collective-permute-start.1 = (bf16[2,64,512]{2,0,1:T(2,128)(2,1)S(1)}, bf16[2,64,512]{2,0,1:T(2,128)(2,1)S(1)}, u32[]{:S(2)}, u32[]{:S(2)}) collective-permute-start(bf16[2,64,512]{2,0,1:T(2,128)(2,1)S(1)} %copy.25), channel_id=1, source_target_pairs={{4,0},{8,4},{12,8},{16,12},{20,16},{24,20},{28,24},{5,1},{9,5},{13... | collective-permute-start | bytes 393224 | tf_op jit(solution)/shard_map/ppermute | solution.py:441
  41.5 7.3 %collective-permute-start.3 = (bf16[2,36,512]{2,1,0:T(8,128)(2,1)S(1)}, bf16[2,36,512]{2,1,0:T(8,128)(2,1)S(1)}, u32[]{:S(2)}, u32[]{:S(2)}) collective-permute-start(bf16[2,36,512]{2,1,0:T(8,128)(2,1)S(1)} %pad_maximum_fusion.1), channel_id=1, source_target_pairs={{1,0},{2,1},{3,2},{5,4},{6,5},{7,6},{9,8},{10,9},{11,10},{13,12},{... | collective-permute-start | bytes 221192 | tf_op jit(solution)/shard_map/ppermute | solution.py:441
  42.8 6.0 %collective-permute-start.2 = (bf16[2,36,512]{2,1,0:T(8,128)(2,1)S(1)}, bf16[2,36,512]{2,1,0:T(8,128)(2,1)S(1)}, u32[]{:S(2)}, u32[]{:S(2)}) collective-permute-start(bf16[2,36,512]{2,1,0:T(8,128)(2,1)S(1)} %pad_maximum_fusion), channel_id=1, source_target_pairs={{0,1},{1,2},{2,3},{4,5},{5,6},{6,7},{8,9},{9,10},{10,11},{12,13},{... | collective-permute-start | bytes 221192 | tf_op jit(solution)/shard_map/ppermute | solution.py:441
  63.3 25.9 %all-to-all-start.4 = ((bf16[32,96,128]{2,1,0:T(8,128)(2,1)}), bf16[32,96,128]{2,1,0:T(8,128)(2,1)S(1)}, u32[]{:S(2)}, u32[]{:S(2)}) async-start(bf16[32,96,128]{2,1,0:T(8,128)(2,1)} %bitcast.15), calls=%async_computation.4 | async-start | bytes 1572864 | tf_op jit(solution)/shard_map/all_to_all | solution.py:479
  69.3 2.2 %copy-start = (f32[32,64,512]{2,1,0:T(8,128)S(1)}, f32[32,64,512]{2,1,0:T(8,128)}, u32[]{:S(2)}) copy-start(f32[32,64,512]{2,1,0:T(8,128)} %field_hbm.4) | copy-start | bytes 12582916
  71.5 17.8 %copy-start.3 = (s32[32,1,128]{2,1,0:T(1,128)S(1)}, s32[32,1,128]{2,1,0:T(1,128)}, u32[]{:S(2)}) copy-start(s32[32,1,128]{2,1,0:T(1,128)} %copy-done.2) | copy-start | bytes 49156
  82.2 2.0 %copy-start.1 = (f32[32,64,512]{2,1,0:T(8,128)}, f32[32,64,512]{2,1,0:T(8,128)S(1)}, u32[]{:S(2)}) copy-start(f32[32,64,512]{2,1,0:T(8,128)S(1)} %prior.1.base_hbm) | copy-start | bytes 12582916

commit v8 on v7

--- a/solution.py
+++ b/solution.py
@@ -35,7 +35,9 @@
     lane = lax.broadcasted_iota(jnp.int32, (LANES, LANES), 1)
     row = lax.broadcasted_iota(jnp.int32, (LANES, LANES), 0)
     upper = jnp.where(row <= lane, 1.0, 0.0).astype(jnp.bfloat16)
-    tile_no = lax.broadcasted_iota(jnp.int32, (devices, LANES), 0)
+    size_x, size_y = lax.axis_size("gx"), lax.axis_size("gy")
+    along_y, along_x = split_by(lax.broadcasted_iota(jnp.int32, (devices, LANES), 0), size_x)
+    tile_no = along_x * size_y + along_y
     slot_no = lax.broadcasted_iota(jnp.int32, (capacity, LANES), 0)
     before = jnp.zeros((devices, 1), jnp.float32)
     lists = jnp.zeros((2 * devices, capacity), jnp.float32)
@@ -69,7 +71,7 @@
     high, low = lists[:devices], lists[devices:]
     wanted = ((high - 1.0) * 128.0 + low).astype(jnp.int32)
     filled = before.astype(jnp.int32)
-    me = lax.axis_index("gx") * lax.axis_size("gy") + lax.axis_index("gy")
+    me = lax.axis_index("gx") * size_y + lax.axis_index("gy")
     fullest = jnp.max(jnp.where(tile_no[:, :1] == me, 0.0, before), axis=0, keepdims=True)
     listed = jnp.where(high > 0.5, wanted, blocks + filled)
     if first_slots < capacity:
@@ -144,44 +146,22 @@
 
 
 def serve_kernel(incoming_ref, field_hbm, *refs, capacity, first_slots):
-    *served_refs, crowded_ref, field_ref, table_ref, sems = refs
-    cells_x, cells_y, depth = field_ref.shape
-    per_column = depth // LANES
-    parts = sems.shape[0]
-    planes = cells_x // parts
-
-    def load(part):
-        span = pl.ds(part * planes, planes)
-        return pltpu.make_async_copy(field_hbm.at[span], field_ref.at[span], sems.at[part])
-
-    for part in range(parts):
-        load(part).start()
+    *served_refs, crowded_ref, rows_ref, sems = refs
+    blocks = field_hbm.shape[0]
+    load = pltpu.make_async_copy(field_hbm, rows_ref.at[pl.ds(0, blocks)], sems.at[0])
+    load.start()
 
     def mark_of(source, most):
         return jnp.maximum(most, incoming_ref[source * capacity + capacity - 1] >> 16)
 
     fullest = lax.fori_loop(0, incoming_ref.shape[0] // capacity, mark_of, jnp.int32(0))
     crowded_ref[0] = jnp.where(fullest > first_slots, 1, 0)
-    table_rows = table_ref.reshape(table_ref.shape[0], LANES)
-    blocks = cells_x * cells_y * per_column
-    table_rows[blocks:, :] = jnp.zeros((table_ref.shape[0] - blocks, LANES), jnp.float32)
-
-    def one_plane(x, carry):
-        for yb in range(cells_y // 8):
-            for part in range(per_column):
-                at = pl.multiple_of(((x * (cells_y // 8) + yb) * per_column + part) * 8, 8)
-                table_rows[pl.ds(at, 8), :] = jnp.exp(
-                    field_ref[x, 8 * yb : 8 * yb + 8, part * LANES : (part + 1) * LANES]
-                )
-        return carry
-
-    for part in range(parts):
-        load(part).wait()
-        lax.fori_loop(part * planes, (part + 1) * planes, one_plane, 0)
+    rows_ref[blocks:] = jnp.zeros((rows_ref.shape[0] - blocks, 1, LANES), jnp.float32)
+    load.wait()
 
     def visit(wanted, row, list_part):
-        rows = jnp.concatenate([table_ref[at] for at in wanted], axis=0)
-        served_refs[list_part][pl.ds(row, GROUP), :] = rows.astype(jnp.bfloat16)
+        rows = jnp.concatenate([rows_ref[at] for at in wanted], axis=0)
+        served_refs[list_part][pl.ds(row, GROUP), :] = jnp.exp(rows).astype(jnp.bfloat16)
 
     for_each_group(incoming_ref, visit, capacity, first_slots, blocks)
 
@@ -216,34 +196,28 @@
     extinction_ref, refs = refs[0], refs[1:]
     parcel_refs, refs = refs[:exchanges], refs[exchanges:]
     weights_ref, returned_rows, sens_ref, parcel_rows, sems = refs
-    sets, in_set, per, slots, stars, width = weights_ref.shape
+    held, per, slots, stars, width = weights_ref.shape
     chunks = extinction_ref.shape[0]
-    rounds = chunks // (sets * in_set)
     per_chunk = per * slots
     fold = LANES // stars
     all_slots = parcel_rows.shape[0]
+    ahead = 2
     lane = lax.broadcasted_iota(jnp.int32, (8, LANES), 1)
     row = lax.broadcasted_iota(jnp.int32, (8, LANES), 0)
     star_group = lane // stars
     own_slot = [row == star_group + fold * h for h in range(8 // fold)]
 
-    def load(one_round, one_set):
-        return [
-            pltpu.make_async_copy(
-                weights_hbm.at[pl.ds(((one_round * sets + one_set) * in_set + u) * per, per)],
-                weights_ref.at[one_set, u],
-                sems.at[one_set, u],
-            )
-            for u in range(in_set)
-        ]
-
-    def extinctions(one_set, u, chunk, places):
+    def load(chunk, u):
+        source = weights_hbm.at[pl.ds(chunk * per, per)]
+        return pltpu.make_async_copy(source, weights_ref.at[u], sems.at[u])
+
+    def extinctions(u, chunk, places):
         sums = []
         for b in range(per):
             total = jnp.zeros((stars, width), jnp.float32)
             for k in range(slots):
                 fetched = returned_rows[places[u * per_chunk + b * slots + k]]
-                total = total + weights_ref[one_set, u, b, k].astype(jnp.float32) * fetched
+                total = total + weights_ref[u, b, k].astype(jnp.float32) * fetched
             sums.append(total)
         extinction = lax.dot_general(
             jnp.ones((8, width), jnp.float32),
@@ -256,7 +230,7 @@
         extinction_ref[here, :] = extinction[:1]
         return inverse_ref[here, :] * (extinction - observed_ref[here, :])
 
-    def sensitivities(one_set, u, weighted):
+    def sensitivities(u, weighted):
         for b in range(per):
             spread = jnp.where(star_group == b, weighted, 0.0)
             shift = stars
@@ -266,7 +240,7 @@
             left = jnp.concatenate(
                 [jnp.where(own, spread, 0.0) for own in own_slot], axis=1
             ).astype(jnp.bfloat16)
-            eights = [weights_ref[one_set, u, b, 8 * j : 8 * j + 8] for j in range(slots // 8)]
+            eights = [weights_ref[u, b, 8 * j : 8 * j + 8] for j in range(slots // 8)]
             right = jnp.concatenate([x.reshape(8 * stars, width) for x in eights], axis=1)
             sens = jnp.dot(left, right, preferred_element_type=jnp.float32)
             for j in range(slots // 8):
@@ -277,22 +251,8 @@
         for i in range(u * per_chunk, (u + 1) * per_chunk):
             parcel_rows[places[i]] = sens_ref[i : i + 1, :]
 
-    def work(one_round, one_set):
-        first = (one_round * sets + one_set) * in_set
-        size = in_set * per_chunk
-        places = position_ref.at[pl.ds(pl.multiple_of(first * per_chunk, size), size)]
-        weighted = {}
-        for u in range(in_set + 2):
-            if u < in_set:
-                weighted[u] = extinctions(one_set, u, first + u, places)
-            if 1 <= u <= in_set:
-                sensitivities(one_set, u - 1, weighted[u - 1])
-            if u >= 2:
-                scatter(u - 2, places)
-
-    for one_set in range(sets):
-        for copy in load(0, one_set):
-            copy.start()
+    for u in range(ahead):
+        load(u, u).start()
     start = 0
     for returned_ref in returned_refs:
         span = slice(start, start + returned_ref.shape[0])
@@ -301,19 +261,29 @@
     parcel_rows.reshape(all_slots, width)[...] = jnp.zeros((all_slots, width), jnp.float32)
 
     def one_round(i, carry):
-        for one_set in range(sets):
-            for copy in load(i, one_set):
-                copy.wait()
-            work(i, one_set)
-
-            @pl.when(i + 1 < rounds)
-            def _():
-                for copy in load(i + 1, one_set):
-                    copy.start()
-
+        first = i * held
+        size = held * per_chunk
+        places = position_ref.at[pl.ds(pl.multiple_of(first * per_chunk, size), size)]
+        weighted = {}
+        for u in range(held + 2):
+            if u < held:
+                load(first + u, u).wait()
+                if u + ahead < held:
+                    load(first + u + ahead, u + ahead).start()
+                else:
+
+                    @pl.when(first + u + ahead < chunks)
+                    def _():
+                        load(first + u + ahead, u + ahead - held).start()
+
+                weighted[u] = extinctions(u, first + u, places)
+            if 1 <= u <= held:
+                sensitivities(u - 1, weighted[u - 1])
+            if u >= 2:
+                scatter(u - 2, places)
         return carry
 
-    lax.fori_loop(0, rounds, one_round, 0)
+    lax.fori_loop(0, chunks // held, one_round, 0)
     start = 0
     for parcel_ref in parcel_refs:
         span = slice(start, start + parcel_ref.shape[0])
@@ -475,6 +445,10 @@
     f32, bf16, i32 = jnp.float32, jnp.bfloat16, jnp.int32
     shape = jax.ShapeDtypeStruct
 
+    def to_rows(x):
+        x = x.reshape(cells_x, cells_y // 8, 8, per_column, width)
+        return x.transpose(0, 1, 3, 2, 4).reshape(blocks, 1, width)
+
     def exchange(x):
         return lax.all_to_all(x, mesh_axes, split_axis=0, concat_axis=0, tiled=True)
 
@@ -500,7 +474,10 @@
         out_specs=[VMEM, VMEM],
         name="route",
     )(block_ids.T)
-    incoming = exchange(outgoing)
+    incoming = lax.all_to_all(outgoing, "gy", split_axis=0, concat_axis=0, tiled=True)
+    incoming = incoming.reshape(lax.axis_size("gy"), lax.axis_size("gx"), capacity)
+    incoming = incoming.transpose(1, 0, 2).reshape(devices, capacity)
+    incoming = lax.all_to_all(incoming, "gx", split_axis=0, concat_axis=0, tiled=True)
 
     field, _ = lax.optimization_barrier((log_density, outgoing))
     xfirst, xlast, yfirst, ylast = pl.pallas_call(
@@ -525,23 +502,21 @@
     incoming, *edges = lax.optimization_barrier((incoming, xfirst, xlast, yfirst, ylast))
     wanted = incoming.reshape(-1)
 
-    parts = 8
     *served, crowded = pl.pallas_call(
         functools.partial(serve_kernel, capacity=capacity, first_slots=first_slots),
         out_shape=[shape((devices * n, width), bf16) for n in slots_of] + [shape((1,), i32)],
         in_specs=[SMEM, ANY],
         out_specs=[VMEM] * exchanges + [SMEM],
         scratch_shapes=[
-            pltpu.VMEM(field_shape, f32),
             pltpu.VMEM((blocks + capacity, 1, width), f32),
-            pltpu.SemaphoreType.DMA((parts,)),
+            pltpu.SemaphoreType.DMA((1,)),
         ],
         compiler_params=pltpu.CompilerParams(vmem_limit_bytes=56 * MIB),
         cost_estimate=pl.CostEstimate(
             flops=cells, bytes_accessed=6 * MIB, transcendentals=cells
         ),
         name="serve",
-    )(wanted, log_density)
+    )(wanted, to_rows(log_density))
     crowded = crowded[0] != 0
 
     incoming_late, *edges, _ = lax.optimization_barrier((incoming, *edges, served[0]))
@@ -563,7 +538,7 @@
     *returned, match, ylo, yhi = lax.optimization_barrier((*returned, match, ylo, yhi))
 
     chunks = blocks_dev * stars // LANES
-    in_set = chunks // 4
+    held = chunks // 2
     live = jnp.arange(stars)[None, :] < star_counts[:, None]
     live_inverse = jnp.where(live, inverse_var, 0.0)
     extinction, *parcel = pl.pallas_call(
@@ -573,11 +548,11 @@
         in_specs=[SMEM, VMEM, VMEM, ANY] + [VMEM] * exchanges,
         out_specs=[VMEM] * (1 + exchanges),
         scratch_shapes=[
-            pltpu.VMEM((2, in_set, blocks_dev // chunks, slots, stars, width), bf16),
+            pltpu.VMEM((held, blocks_dev // chunks, slots, stars, width), bf16),
             pltpu.VMEM((all_slots, 1, width), f32),
-            pltpu.VMEM((in_set * LANES // stars * slots, width), f32),
+            pltpu.VMEM((held * (blocks_dev // chunks) * slots, width), f32),
             pltpu.VMEM((all_slots, 1, width), f32),
-            pltpu.SemaphoreType.DMA((2, in_set)),
+            pltpu.SemaphoreType.DMA((held,)),
         ],
         compiler_params=pltpu.CompilerParams(vmem_limit_bytes=50 * MIB),
         cost_estimate=pl.CostEstimate(
@@ -610,6 +585,7 @@
         name="prior",
     )(field_late, xlo, xhi, ylo, yhi)
 
+    parts = 8
     new_log_density = pl.pallas_call(
         functools.partial(
             finish_kernel, exchanges=exchanges, capacity=capacity, first_slots=first_slots

time: 98.7 us -> 108 us (1.094)
  blocking collectives: 0 us -> 9.88 us
  waiting for transfers between devices: 14.9 us -> 12.3 us
  Pallas kernels: 47.1 us -> 49.2 us
  starting transfers between devices: 26.1 us -> 24.7 us
    all_to_all x0 -> x1, blocking collectives: none -> 9.88 us  [on_device(): lax.all_to_all(outgoing, 'gy', split_axis=0, concat_axis=0, tiled=True)]
    all_to_all x3 -> x2, starting transfers between devices: 15.1 us -> 7.88 us  [exchange(): return lax.all_to_all(x, mesh_axes, split_axis=0, concat_axis=0, tiled=True)]
    all_to_all x0 -> x1, starting transfers between devices: none -> 5.82 us  [on_device(): lax.all_to_all(incoming, 'gx', split_axis=0, concat_axis=0, tiled=True)]
    all_to_all x3 -> x2, waiting for transfers between devices: 11.5 us -> 7.22 us  [exchange(): return lax.all_to_all(x, mesh_axes, split_axis=0, concat_axis=0, tiled=True)]
    pallas_call x1, Pallas kernels: 12.3 us -> 14.4 us  [on_device(): pl.pallas_call(functools.partial(star_kernel, exchanges=exchanges), out_s...]
    all_to_all x0 -> x1, waiting for transfers between devices: none -> 1.67 us  [on_device(): lax.all_to_all(incoming, 'gx', split_axis=0, concat_axis=0, tiled=True)]
  transfers between devices with their start and end apart: 7 -> 7, of which waited for: 4 -> 4; matrix products, arithmetic and copies ran while one was open for 4% -> 3% of each run, Pallas kernels for 15% -> 14%
where the time goes in v8:
time: 108 us; the launch traced here: 107 us
  Pallas kernels  49.2 us (46%)
  starting transfers between devices  24.7 us (23%)
  waiting for transfers between devices  12.3 us (11%)
  blocking collectives  9.88 us (9%)
  local copies, waits for them, and re-layouts  7.96 us (7%)
  between operations  1.61 us (1%)
    pallas_call x1, Pallas kernels, on_device(): pl.pallas_call(functools.partial(star_kernel, exchanges=exchanges), out_s...  14.4 us
    ppermute x4, starting transfers between devices, both_ways(): return (lax.ppermute(last, axis, up), lax.ppermute(first, axis, down))  11 us
    pallas_call x1, Pallas kernels, on_device(): pl.pallas_call(prior_kernel, out_shape=shape(field_shape, f32), in_specs=...  10.7 us
    all_to_all x1, blocking collectives, on_device(): lax.all_to_all(outgoing, 'gy', split_axis=0, concat_axis=0, tiled=True)  9.88 us
    pallas_call x1, Pallas kernels, on_device(): pl.pallas_call(functools.partial(finish_kernel, exchanges=exchanges, capa...  8.86 us
    pallas_call x1, Pallas kernels, on_device(): pl.pallas_call(functools.partial(serve_kernel, capacity=capacity, first_s...  8.03 us
    all_to_all x2, starting transfers between devices, exchange(): return lax.all_to_all(x, mesh_axes, split_axis=0, concat_axis=0, tiled=True)  7.88 us
    all_to_all x2, waiting for transfers between devices, exchange(): return lax.all_to_all(x, mesh_axes, split_axis=0, concat_axis=0, tiled=True)  7.22 us
  transfers between devices with their start and end apart: 7, of which 4 were waited for; matrix products, arithmetic and copies ran while one was open for 3% of the time, Pallas kernels for 14%

profile of v8, /device:TPU:1, one launch (start us, length us, event | category | flops | bytes accessed | tf_op | source)
XLA Modules:
  0.0 106.5 jit_solution(2016998225489962714)
XLA Ops:
  0.6 3.1 %route.1 = (s32[32,128]{1,0:T(8,128)}, s32[16,128]{1,0:T(8,128)}) custom-call(s32[32,64]{1,0:T(8,128)} %bitcast.45), custom_call_target="tpu_custom_call" | custom-call | tf_op jit(solution)/shard_map/route/pallas_call | solution.py:463
  3.7 9.9 %all_to_all.38 = s32[4,8,128]{2,1,0:T(8,128)S(1)} all-to-all(s32[4,8,128]{2,1,0:T(8,128)} %bitcast.46), channel_id=1, replica_groups=mesh['gx'=8,'gy'=4] {'gy'}, dimensions={0} | all-to-all | bytes 32768 | tf_op jit(solution)/shard_map/all_to_all | solution.py:477
  13.6 0.6 copy.34
  14.2 5.8 %all-to-all-start.3 = ((s32[8,4,128]{2,1,0:T(4,128)}), s32[8,4,128]{2,1,0:T(4,128)S(1)}, u32[]{:S(2)}, u32[]{:S(2)}) async-start(s32[8,4,128]{2,1,0:T(4,128)} %copy.34), calls=%async_computation.3 | async-start | bytes 32768 | tf_op jit(solution)/shard_map/all_to_all | solution.py:480
  20.0 2.3 %edges.1 = (bf16[2,64,512]{2,1,0:T(8,128)(2,1)}, bf16[2,64,512]{2,1,0:T(8,128)(2,1)}, f32[2,32,512]{2,1,0:T(8,128)}, f32[2,32,512]{2,1,0:T(8,128)}) custom-call(f32[32,64,512]{2,1,0:T(8,128)} %field_hbm.2), custom_call_target="tpu_custom_call" | custom-call | bytes 2097152 | tf_op jit(solution)/shard_map/edges/pallas_call | solution.py:483
  22.4 1.7 %all-to-all-done.3 = s32[8,4,128]{2,1,0:T(4,128)S(1)} async-done(((s32[8,4,128]{2,1,0:T(4,128)}), s32[8,4,128]{2,1,0:T(4,128)S(1)}, u32[]{:S(2)}, u32[]{:S(2)}) %all-to-all-start.3) | async-done | bytes 16416 | tf_op jit(solution)/shard_map/all_to_all | solution.py:480
  24.1 0.6 copy-done.2
  24.7 8.0 %serve.1 = (bf16[3072,128]{1,0:T(8,128)(2,1)}, bf16[1024,128]{1,0:T(8,128)(2,1)S(1)}, s32[1]{0:T(128)}) custom-call(s32[4096]{0:T(1024)} %bitcast.32, f32[8192,1,128]{2,1,0:T(1,128)} %bitcast.29), custom_call_target="tpu_custom_call" | custom-call | flops 1048576 | bytes 6291456 | tf_op jit(solution)/shard_map/serve/pallas_call | solution.py:505
  33.4 2.8 %all-to-all-start.4 = ((bf16[32,96,128]{2,1,0:T(8,128)(2,1)}), bf16[32,96,128]{2,1,0:T(8,128)(2,1)S(1)}, u32[]{:S(2)}, u32[]{:S(2)}) async-start(bf16[32,96,128]{2,1,0:T(8,128)(2,1)} %bitcast.42), calls=%async_computation.4 | async-start | bytes 1572864 | tf_op jit(solution)/shard_map/all_to_all | solution.py:453
  36.2 0.1 copy.37
  36.3 0.1 reshape.99.position_ref
  36.5 0.1 copy.39
  36.6 0.1 copy.38
  36.8 0.1 copy.35
  37.0 3.5 %collective-permute-start = (bf16[2,64,512]{2,0,1:T(2,128)(2,1)S(1)}, bf16[2,64,512]{2,0,1:T(2,128)(2,1)S(1)}, u32[]{:S(2)}, u32[]{:S(2)}) collective-permute-start(bf16[2,64,512]{2,0,1:T(2,128)(2,1)S(1)} %copy.35), channel_id=1, source_target_pairs={{0,4},{4,8},{8,12},{12,16},{16,20},{20,24},{24,28},{1,5},{5,9},{9,... | collective-permute-start | bytes 393224 | tf_op jit(solution)/shard_map/ppermute | solution.py:411
  40.5 0.1 copy.36
  40.7 1.9 %collective-permute-start.1 = (bf16[2,64,512]{2,0,1:T(2,128)(2,1)S(1)}, bf16[2,64,512]{2,0,1:T(2,128)(2,1)S(1)}, u32[]{:S(2)}, u32[]{:S(2)}) collective-permute-start(bf16[2,64,512]{2,0,1:T(2,128)(2,1)S(1)} %copy.36), channel_id=1, source_target_pairs={{4,0},{8,4},{12,8},{16,12},{20,16},{24,20},{28,24},{5,1},{9,5},{13... | collective-permute-start | bytes 393224 | tf_op jit(solution)/shard_map/ppermute | solution.py:411
  42.6 0.8 slice_and_fusion
  43.5 0.8 reshape.96
  44.3 3.4 %collective-permute-done.1 = bf16[2,64,512]{2,0,1:T(2,128)(2,1)S(1)} collective-permute-done((bf16[2,64,512]{2,0,1:T(2,128)(2,1)S(1)}, bf16[2,64,512]{2,0,1:T(2,128)(2,1)S(1)}, u32[]{:S(2)}, u32[]{:S(2)}) %collective-permute-start.1) | collective-permute-done | bytes 131104 | tf_op jit(solution)/shard_map/ppermute | solution.py:411
  47.8 1.3 %collective-permute-start.3 = (bf16[2,36,512]{2,1,0:T(8,128)(2,1)S(1)}, bf16[2,36,512]{2,1,0:T(8,128)(2,1)S(1)}, u32[]{:S(2)}, u32[]{:S(2)}) collective-permute-start(bf16[2,36,512]{2,1,0:T(8,128)(2,1)S(1)} %pad_maximum_fusion.1), channel_id=1, source_target_pairs={{1,0},{2,1},{3,2},{5,4},{6,5},{7,6},{9,8},{10,9},{11,10},{13,12},{... | collective-permute-start | bytes 221192 | tf_op jit(solution)/shard_map/ppermute | solution.py:411
  49.1 4.2 %collective-permute-start.2 = (bf16[2,36,512]{2,1,0:T(8,128)(2,1)S(1)}, bf16[2,36,512]{2,1,0:T(8,128)(2,1)S(1)}, u32[]{:S(2)}, u32[]{:S(2)}) collective-permute-start(bf16[2,36,512]{2,1,0:T(8,128)(2,1)S(1)} %pad_maximum_fusion), channel_id=1, source_target_pairs={{0,1},{1,2},{2,3},{4,5},{5,6},{6,7},{8,9},{9,10},{10,11},{12,13},{... | collective-permute-start | bytes 221192 | tf_op jit(solution)/shard_map/ppermute | solution.py:411
  53.4 1.8 %match.1.match_ref = bf16[4096,128]{1,0:T(8,128)(2,1)S(1)} custom-call(s32[32,128]{1,0:T(8,128)S(1)} %pad_add_fusion.incoming_ref), custom_call_target="tpu_custom_call" | custom-call | flops 1000000000 | bytes 1048576 | tf_op jit(solution)/shard_map/match/pallas_call | solution.py:527
  55.2 2.1 %all-to-all-done.4 = bf16[32,96,128]{2,1,0:T(8,128)(2,1)S(1)} async-done(((bf16[32,96,128]{2,1,0:T(8,128)(2,1)}), bf16[32,96,128]{2,1,0:T(8,128)(2,1)S(1)}, u32[]{:S(2)}, u32[]{:S(2)}) %all-to-all-start.4) | async-done | bytes 786464 | tf_op jit(solution)/shard_map/all_to_all | solution.py:453
  57.3 14.4 %stars.1 = (f32[16,128]{1,0:T(8,128)S(1)}, bf16[3072,128]{1,0:T(8,128)(2,1)}, bf16[1024,128]{1,0:T(8,128)(2,1)S(1)}) custom-call(s32[2048]{0:T(1024)S(1)} %reshape.99.position_ref, f32[16,128]{1,0:T(8,128)S(1)} %reshape.100.observed_ref, f32[16,128]{1,0:T(8,128)S(1)} %reshape.101.inverse_ref, bf16[64,32,32,128]{3,2,1,0:T(8,128)(2,1)} %weights_hbm.1, ...), custom_call_target="tpu_custom_call" | custom-call | flops 33554432 | bytes 16777216 | tf_op jit(solution)/shard_map/stars/pallas_call | solution.py:544
  71.7 5.1 %all-to-all-start.5 = ((bf16[32,96,128]{2,1,0:T(8,128)(2,1)}), bf16[32,96,128]{2,1,0:T(8,128)(2,1)S(1)}, u32[]{:S(2)}, u32[]{:S(2)}) async-start(bf16[32,96,128]{2,1,0:T(8,128)(2,1)} %bitcast.18), calls=%async_computation.5 | async-start | bytes 1572864 | tf_op jit(solution)/shard_map/all_to_all | solution.py:453
  77.0 0.7 copy.42
  77.7 2.2 %copy-done = f32[32,64,512]{2,1,0:T(8,128)S(1)} copy-done((f32[32,64,512]{2,1,0:T(8,128)S(1)}, f32[32,64,512]{2,1,0:T(8,128)}, u32[]{:S(2)}) %copy-start) | copy-done | bytes 4194328
  79.9 10.7 %prior.1.base_hbm = f32[32,64,512]{2,1,0:T(8,128)S(1)} custom-call(f32[32,64,512]{2,1,0:T(8,128)S(1)} %copy-done, bf16[2,64,512]{2,1,0:T(8,128)(2,1)S(1)} %copy.40.xlo_ref, bf16[2,64,512]{2,1,0:T(8,128)(2,1)S(1)} %copy.41.xhi_ref, f32[2,36,512]{2,1,0:T(8,128)S(1)} %convert_element_type.22.ylo_ref, f32[2,36,512]{2,1,0:T(8,128)S(1)} %convert_element_type.24.yhi_ref), custom_call_target="tpu_custom_call" | custom-call | flops 31457280 | bytes 8388608 | tf_op jit(solution)/shard_map/prior/pallas_call | solution.py:572
  90.6 1.9 %copy-done.1 = f32[32,64,512]{2,1,0:T(8,128)} copy-done((f32[32,64,512]{2,1,0:T(8,128)}, f32[32,64,512]{2,1,0:T(8,128)S(1)}, u32[]{:S(2)}) %copy-start.1) | copy-done | bytes 4194328
  92.6 5.1 %all-to-all-done.5 = bf16[32,96,128]{2,1,0:T(8,128)(2,1)S(1)} async-done(((bf16[32,96,128]{2,1,0:T(8,128)(2,1)}), bf16[32,96,128]{2,1,0:T(8,128)(2,1)S(1)}, u32[]{:S(2)}, u32[]{:S(2)}) %all-to-all-start.5) | async-done | bytes 786464 | tf_op jit(solution)/shard_map/all_to_all | solution.py:453
  97.7 8.9 %finish.1 = f32[32,64,512]{2,1,0:T(8,128)} custom-call(s32[4096]{0:T(1024)S(1)} %bitcast.35, bf16[4096,128]{1,0:T(8,128)(2,1)S(1)} %match.1.match_ref, f32[32,64,512]{2,1,0:T(8,128)} %field_hbm.2, f32[32,64,512]{2,1,0:T(8,128)} %copy-done.1, bf16[3072,128]{1,0:T(8,128)(2,1)S(1)} %bitcast.31, bf16[1024,128]{1,0:T(8,128)(2,1)S(1)} %bitcast.38), custom_call_target="tpu_custom_call" | custom-call | flops 4194304 | bytes 12582912 | tf_op jit(solution)/shard_map/finish/pallas_call | solution.py:589
  (43 shorter events, 0.6 us)
Async XLA Ops:
  14.2 9.8 %all-to-all-start.3 = ((s32[8,4,128]{2,1,0:T(4,128)}), s32[8,4,128]{2,1,0:T(4,128)S(1)}, u32[]{:S(2)}, u32[]{:S(2)}) async-start(s32[8,4,128]{2,1,0:T(4,128)} %copy.34), calls=%async_computation.3 | async-start | bytes 32768 | tf_op jit(solution)/shard_map/all_to_all | solution.py:480
  22.3 13.8 %copy-start.10 = (s32[16,128]{1,0:T(8,128)S(1)}, s32[16,128]{1,0:T(8,128)}, u32[]{:S(2)}) copy-start(s32[16,128]{1,0:T(8,128)} %get-tuple-element.73) | copy-start | bytes 24580
  22.3 14.2 %copy-start.9 = (f32[64,32]{0,1:T(8,128)S(1)}, f32[64,32]{0,1:T(8,128)}, u32[]{:S(2)}) copy-start(f32[64,32]{0,1:T(8,128)} %param.13) | copy-start | bytes 24580
  22.3 14.1 %copy-start.11 = (s32[64]{0:T(128)S(1)}, s32[64]{0:T(128)}, u32[]{:S(2)}) copy-start(s32[64]{0:T(128)} %param.14) | copy-start | bytes 772
  22.3 14.3 %copy-start.8 = (f32[64,32]{0,1:T(8,128)S(1)}, f32[64,32]{0,1:T(8,128)}, u32[]{:S(2)}) copy-start(f32[64,32]{0,1:T(8,128)} %param.12) | copy-start | bytes 24580
  22.3 14.5 %copy-start.7 = (bf16[2,64,512]{2,1,0:T(8,128)(2,1)S(1)}, bf16[2,64,512]{2,1,0:T(8,128)(2,1)}, u32[]{:S(2)}) copy-start(bf16[2,64,512]{2,1,0:T(8,128)(2,1)} %get-tuple-element.68) | copy-start | bytes 393220
  22.4 18.2 %copy-start.6 = (bf16[2,64,512]{2,1,0:T(8,128)(2,1)S(1)}, bf16[2,64,512]{2,1,0:T(8,128)(2,1)}, u32[]{:S(2)}) copy-start(bf16[2,64,512]{2,1,0:T(8,128)(2,1)} %get-tuple-element.70) | copy-start | bytes 393220
  22.4 21.0 %copy-start.5 = (f32[2,32,512]{2,1,0:T(8,128)S(1)}, f32[2,32,512]{2,1,0:T(8,128)}, u32[]{:S(2)}) copy-start(f32[2,32,512]{2,1,0:T(8,128)} %get-tuple-element.71) | copy-start | bytes 393220
  22.4 21.0 %copy-start.4 = (f32[2,32,512]{2,1,0:T(8,128)S(1)}, f32[2,32,512]{2,1,0:T(8,128)}, u32[]{:S(2)}) copy-start(f32[2,32,512]{2,1,0:T(8,128)} %get-tuple-element.69) | copy-start | bytes 393220
  24.1 0.6 copy-start.2
  33.4 23.9 %all-to-all-start.4 = ((bf16[32,96,128]{2,1,0:T(8,128)(2,1)}), bf16[32,96,128]{2,1,0:T(8,128)(2,1)S(1)}, u32[]{:S(2)}, u32[]{:S(2)}) async-start(bf16[32,96,128]{2,1,0:T(8,128)(2,1)} %bitcast.42), calls=%async_computation.4 | async-start | bytes 1572864 | tf_op jit(solution)/shard_map/all_to_all | solution.py:453
  37.0 7.3 %collective-permute-start = (bf16[2,64,512]{2,0,1:T(2,128)(2,1)S(1)}, bf16[2,64,512]{2,0,1:T(2,128)(2,1)S(1)}, u32[]{:S(2)}, u32[]{:S(2)}) collective-permute-start(bf16[2,64,512]{2,0,1:T(2,128)(2,1)S(1)} %copy.35), channel_id=1, source_target_pairs={{0,4},{4,8},{8,12},{12,16},{16,20},{20,24},{24,28},{1,5},{5,9},{9,... | collective-permute-start | bytes 393224 | tf_op jit(solution)/shard_map/ppermute | solution.py:411
  40.7 7.1 %collective-permute-start.1 = (bf16[2,64,512]{2,0,1:T(2,128)(2,1)S(1)}, bf16[2,64,512]{2,0,1:T(2,128)(2,1)S(1)}, u32[]{:S(2)}, u32[]{:S(2)}) collective-permute-start(bf16[2,64,512]{2,0,1:T(2,128)(2,1)S(1)} %copy.36), channel_id=1, source_target_pairs={{4,0},{8,4},{12,8},{16,12},{20,16},{24,20},{28,24},{5,1},{9,5},{13... | collective-permute-start | bytes 393224 | tf_op jit(solution)/shard_map/ppermute | solution.py:411
  47.8 7.3 %collective-permute-start.3 = (bf16[2,36,512]{2,1,0:T(8,128)(2,1)S(1)}, bf16[2,36,512]{2,1,0:T(8,128)(2,1)S(1)}, u32[]{:S(2)}, u32[]{:S(2)}) collective-permute-start(bf16[2,36,512]{2,1,0:T(8,128)(2,1)S(1)} %pad_maximum_fusion.1), channel_id=1, source_target_pairs={{1,0},{2,1},{3,2},{5,4},{6,5},{7,6},{9,8},{10,9},{11,10},{13,12},{... | collective-permute-start | bytes 221192 | tf_op jit(solution)/shard_map/ppermute | solution.py:411
  49.1 6.0 %collective-permute-start.2 = (bf16[2,36,512]{2,1,0:T(8,128)(2,1)S(1)}, bf16[2,36,512]{2,1,0:T(8,128)(2,1)S(1)}, u32[]{:S(2)}, u32[]{:S(2)}) collective-permute-start(bf16[2,36,512]{2,1,0:T(8,128)(2,1)S(1)} %pad_maximum_fusion), channel_id=1, source_target_pairs={{0,1},{1,2},{2,3},{4,5},{5,6},{6,7},{8,9},{9,10},{10,11},{12,13},{... | collective-permute-start | bytes 221192 | tf_op jit(solution)/shard_map/ppermute | solution.py:411
  71.7 25.9 %all-to-all-start.5 = ((bf16[32,96,128]{2,1,0:T(8,128)(2,1)}), bf16[32,96,128]{2,1,0:T(8,128)(2,1)S(1)}, u32[]{:S(2)}, u32[]{:S(2)}) async-start(bf16[32,96,128]{2,1,0:T(8,128)(2,1)} %bitcast.18), calls=%async_computation.5 | async-start | bytes 1572864 | tf_op jit(solution)/shard_map/all_to_all | solution.py:453
  77.7 2.2 %copy-start = (f32[32,64,512]{2,1,0:T(8,128)S(1)}, f32[32,64,512]{2,1,0:T(8,128)}, u32[]{:S(2)}) copy-start(f32[32,64,512]{2,1,0:T(8,128)} %field_hbm.2) | copy-start | bytes 12582916
  79.9 17.8 %copy-start.3 = (s32[8,4,128]{2,1,0:T(4,128)S(1)}, s32[8,4,128]{2,1,0:T(4,128)}, u32[]{:S(2)}) copy-start(s32[8,4,128]{2,1,0:T(4,128)} %copy-done.2) | copy-start | bytes 49156
  90.6 2.0 %copy-start.1 = (f32[32,64,512]{2,1,0:T(8,128)}, f32[32,64,512]{2,1,0:T(8,128)S(1)}, u32[]{:S(2)}) copy-start(f32[32,64,512]{2,1,0:T(8,128)S(1)} %prior.1.base_hbm) | copy-start | bytes 12582916

commit v9 on v8

--- a/solution.py
+++ b/solution.py
@@ -35,9 +35,7 @@
     lane = lax.broadcasted_iota(jnp.int32, (LANES, LANES), 1)
     row = lax.broadcasted_iota(jnp.int32, (LANES, LANES), 0)
     upper = jnp.where(row <= lane, 1.0, 0.0).astype(jnp.bfloat16)
-    size_x, size_y = lax.axis_size("gx"), lax.axis_size("gy")
-    along_y, along_x = split_by(lax.broadcasted_iota(jnp.int32, (devices, LANES), 0), size_x)
-    tile_no = along_x * size_y + along_y
+    tile_no = lax.broadcasted_iota(jnp.int32, (devices, LANES), 0)
     slot_no = lax.broadcasted_iota(jnp.int32, (capacity, LANES), 0)
     before = jnp.zeros((devices, 1), jnp.float32)
     lists = jnp.zeros((2 * devices, capacity), jnp.float32)
@@ -71,7 +69,7 @@
     high, low = lists[:devices], lists[devices:]
     wanted = ((high - 1.0) * 128.0 + low).astype(jnp.int32)
     filled = before.astype(jnp.int32)
-    me = lax.axis_index("gx") * size_y + lax.axis_index("gy")
+    me = lax.axis_index("gx") * lax.axis_size("gy") + lax.axis_index("gy")
     fullest = jnp.max(jnp.where(tile_no[:, :1] == me, 0.0, before), axis=0, keepdims=True)
     listed = jnp.where(high > 0.5, wanted, blocks + filled)
     if first_slots < capacity:
@@ -105,6 +103,17 @@
             ylast_ref[h, x : x + 1, :] = strips_ref[1, x, 6 + h : 7 + h, :]
 
 
+def copies_in_parts(source, target, sems):
+    parts = sems.shape[0]
+    size = source.shape[0] // parts
+    return [
+        pltpu.make_async_copy(
+            source.at[pl.ds(i * size, size)], target.at[pl.ds(i * size, size)], sems.at[i]
+        )
+        for i in range(parts)
+    ]
+
+
 def for_each_group(incoming_ref, visit, capacity, first_slots, blocks):
     sources = incoming_ref.shape[0] // capacity
     last_slots = capacity - first_slots
@@ -148,8 +157,9 @@
 def serve_kernel(incoming_ref, field_hbm, *refs, capacity, first_slots):
     *served_refs, crowded_ref, rows_ref, sems = refs
     blocks = field_hbm.shape[0]
-    load = pltpu.make_async_copy(field_hbm, rows_ref.at[pl.ds(0, blocks)], sems.at[0])
-    load.start()
+    loads = copies_in_parts(field_hbm, rows_ref, sems)
+    for load in loads:
+        load.start()
 
     def mark_of(source, most):
         return jnp.maximum(most, incoming_ref[source * capacity + capacity - 1] >> 16)
@@ -157,7 +167,8 @@
     fullest = lax.fori_loop(0, incoming_ref.shape[0] // capacity, mark_of, jnp.int32(0))
     crowded_ref[0] = jnp.where(fullest > first_slots, 1, 0)
     rows_ref[blocks:] = jnp.zeros((rows_ref.shape[0] - blocks, 1, LANES), jnp.float32)
-    load.wait()
+    for load in loads:
+        load.wait()
 
     def visit(wanted, row, list_part):
         rows = jnp.concatenate([rows_ref[at] for at in wanted], axis=0)
@@ -201,15 +212,19 @@
     per_chunk = per * slots
     fold = LANES // stars
     all_slots = parcel_rows.shape[0]
-    ahead = 2
+    ahead = held // 2
     lane = lax.broadcasted_iota(jnp.int32, (8, LANES), 1)
     row = lax.broadcasted_iota(jnp.int32, (8, LANES), 0)
     star_group = lane // stars
     own_slot = [row == star_group + fold * h for h in range(8 // fold)]
 
     def load(chunk, u):
-        source = weights_hbm.at[pl.ds(chunk * per, per)]
-        return pltpu.make_async_copy(source, weights_ref.at[u], sems.at[u])
+        return [
+            pltpu.make_async_copy(
+                weights_hbm.at[chunk * per + b], weights_ref.at[u, b], sems.at[u, b]
+            )
+            for b in range(per)
+        ]
 
     def extinctions(u, chunk, places):
         sums = []
@@ -252,7 +267,8 @@
             parcel_rows[places[i]] = sens_ref[i : i + 1, :]
 
     for u in range(ahead):
-        load(u, u).start()
+        for copy in load(u, u):
+            copy.start()
     start = 0
     for returned_ref in returned_refs:
         span = slice(start, start + returned_ref.shape[0])
@@ -267,14 +283,18 @@
         weighted = {}
         for u in range(held + 2):
             if u < held:
-                load(first + u, u).wait()
+                for copy in load(first + u, u):
+                    copy.wait()
+                following = load(first + u + ahead, (u + ahead) % held)
                 if u + ahead < held:
-                    load(first + u + ahead, u + ahead).start()
+                    for copy in following:
+                        copy.start()
                 else:
 
                     @pl.when(first + u + ahead < chunks)
-                    def _():
-                        load(first + u + ahead, u + ahead - held).start()
+                    def _(following=following):
+                        for copy in following:
+                            copy.start()
 
                 weighted[u] = extinctions(u, first + u, places)
             if 1 <= u <= held:
@@ -351,10 +371,8 @@
     parts = out_sems.shape[0]
     planes = cells_x // parts
     blocks = cells_x * cells_y * per_column
-    loads = [
-        pltpu.make_async_copy(field_hbm, field_ref, in_sems.at[0]),
-        pltpu.make_async_copy(base_hbm, base_ref, in_sems.at[1]),
-    ]
+    loads = copies_in_parts(field_hbm, field_ref, in_sems.at[0])
+    loads += copies_in_parts(base_hbm, base_ref, in_sems.at[1])
     for load in loads:
         load.start()
     collected_rows = collected.reshape(collected.shape[0], LANES)
@@ -474,10 +492,7 @@
         out_specs=[VMEM, VMEM],
         name="route",
     )(block_ids.T)
-    incoming = lax.all_to_all(outgoing, "gy", split_axis=0, concat_axis=0, tiled=True)
-    incoming = incoming.reshape(lax.axis_size("gy"), lax.axis_size("gx"), capacity)
-    incoming = incoming.transpose(1, 0, 2).reshape(devices, capacity)
-    incoming = lax.all_to_all(incoming, "gx", split_axis=0, concat_axis=0, tiled=True)
+    incoming = exchange(outgoing)
 
     field, _ = lax.optimization_barrier((log_density, outgoing))
     xfirst, xlast, yfirst, ylast = pl.pallas_call(
@@ -509,7 +524,7 @@
         out_specs=[VMEM] * exchanges + [SMEM],
         scratch_shapes=[
             pltpu.VMEM((blocks + capacity, 1, width), f32),
-            pltpu.SemaphoreType.DMA((1,)),
+            pltpu.SemaphoreType.DMA((16,)),
         ],
         compiler_params=pltpu.CompilerParams(vmem_limit_bytes=56 * MIB),
         cost_estimate=pl.CostEstimate(
@@ -552,7 +567,7 @@
             pltpu.VMEM((all_slots, 1, width), f32),
             pltpu.VMEM((held * (blocks_dev // chunks) * slots, width), f32),
             pltpu.VMEM((all_slots, 1, width), f32),
-            pltpu.SemaphoreType.DMA((held,)),
+            pltpu.SemaphoreType.DMA((held, blocks_dev // chunks)),
         ],
         compiler_params=pltpu.CompilerParams(vmem_limit_bytes=50 * MIB),
         cost_estimate=pl.CostEstimate(
@@ -599,7 +614,7 @@
             pltpu.VMEM(field_shape, f32),
             pltpu.VMEM(field_shape, f32),
             pltpu.VMEM(field_shape, f32),
-            pltpu.SemaphoreType.DMA((2,)),
+            pltpu.SemaphoreType.DMA((2, parts)),
             pltpu.SemaphoreType.DMA((parts,)),
         ],
         compiler_params=pltpu.CompilerParams(vmem_limit_bytes=50 * MIB),

time: 108 us -> 101 us (0.935)
  blocking collectives: 9.88 us -> 0 us
  waiting for transfers between devices: 12.3 us -> 14.9 us
  starting transfers between devices: 24.7 us -> 26.2 us
    all_to_all x1 -> x0, blocking collectives: 9.88 us -> none  [on_device(): lax.all_to_all(outgoing, 'gy', split_axis=0, concat_axis=0, tiled=True)]
    all_to_all x2 -> x3, starting transfers between devices: 7.88 us -> 15.2 us  [exchange(): return lax.all_to_all(x, mesh_axes, split_axis=0, concat_axis=0, tiled=True)]
    all_to_all x1 -> x0, starting transfers between devices: 5.82 us -> none  [on_device(): lax.all_to_all(incoming, 'gx', split_axis=0, concat_axis=0, tiled=True)]
    all_to_all x2 -> x3, waiting for transfers between devices: 7.22 us -> 11.5 us  [exchange(): return lax.all_to_all(x, mesh_axes, split_axis=0, concat_axis=0, tiled=True)]
    all_to_all x1 -> x0, waiting for transfers between devices: 1.67 us -> none  [on_device(): lax.all_to_all(incoming, 'gx', split_axis=0, concat_axis=0, tiled=True)]
  transfers between devices with their start and end apart: 7 -> 7, of which waited for: 4 -> 4; matrix products, arithmetic and copies ran while one was open for 3% -> 3% of each run, Pallas kernels for 14% -> 15%
where the time goes in v9:
time: 101 us; the launch traced here: 99.9 us
  Pallas kernels  48.9 us (48%)
  starting transfers between devices  26.2 us (26%)
  waiting for transfers between devices  14.9 us (15%)
  local copies, waits for them, and re-layouts  7.35 us (7%)
  between operations  1.61 us (2%)
    all_to_all x3, starting transfers between devices, exchange(): return lax.all_to_all(x, mesh_axes, split_axis=0, concat_axis=0, tiled=True)  15.2 us
    pallas_call x1, Pallas kernels, on_device(): pl.pallas_call(functools.partial(star_kernel, exchanges=exchanges), out_s...  14.1 us
    all_to_all x3, waiting for transfers between devices, exchange(): return lax.all_to_all(x, mesh_axes, split_axis=0, concat_axis=0, tiled=True)  11.5 us
    ppermute x4, starting transfers between devices, both_ways(): return (lax.ppermute(last, axis, up), lax.ppermute(first, axis, down))  11 us
    pallas_call x1, Pallas kernels, on_device(): pl.pallas_call(prior_kernel, out_shape=shape(field_shape, f32), in_specs=...  10.7 us
    pallas_call x1, Pallas kernels, on_device(): pl.pallas_call(functools.partial(finish_kernel, exchanges=exchanges, capa...  8.9 us
    pallas_call x1, Pallas kernels, on_device(): pl.pallas_call(functools.partial(serve_kernel, capacity=capacity, first_s...  8.04 us
    unnamed x26, local copies, waits for them, and re-layouts  5.55 us
  transfers between devices with their start and end apart: 7, of which 4 were waited for; matrix products, arithmetic and copies ran while one was open for 3% of the time, Pallas kernels for 15%

profile of v9, /device:TPU:1, one launch (start us, length us, event | category | flops | bytes accessed | tf_op | source)
XLA Modules:
  0.0 99.9 jit_solution(834582623797767717)
XLA Ops:
  0.6 3.1 %route.1 = (s32[32,128]{1,0:T(8,128)}, s32[16,128]{1,0:T(8,128)}) custom-call(s32[32,64]{1,0:T(8,128)} %bitcast.45), custom_call_target="tpu_custom_call" | custom-call | tf_op jit(solution)/shard_map/route/pallas_call | solution.py:481
  3.7 7.1 %all-to-all-start.2 = ((s32[32,1,128]{2,1,0:T(1,128)}), s32[32,1,128]{2,1,0:T(1,128)S(1)}, u32[]{:S(2)}, u32[]{:S(2)}) async-start(s32[32,1,128]{2,1,0:T(1,128)} %bitcast.46), calls=%async_computation.2 | async-start | bytes 32768 | tf_op jit(solution)/shard_map/all_to_all | solution.py:471
  10.8 2.3 %edges.1 = (bf16[2,64,512]{2,1,0:T(8,128)(2,1)}, bf16[2,64,512]{2,1,0:T(8,128)(2,1)}, f32[2,32,512]{2,1,0:T(8,128)}, f32[2,32,512]{2,1,0:T(8,128)}) custom-call(f32[32,64,512]{2,1,0:T(8,128)} %field_hbm.2), custom_call_target="tpu_custom_call" | custom-call | bytes 2097152 | tf_op jit(solution)/shard_map/edges/pallas_call | solution.py:498
  13.2 4.2 %all-to-all-done.2 = s32[32,1,128]{2,1,0:T(1,128)S(1)} async-done(((s32[32,1,128]{2,1,0:T(1,128)}), s32[32,1,128]{2,1,0:T(1,128)S(1)}, u32[]{:S(2)}, u32[]{:S(2)}) %all-to-all-start.2) | async-done | bytes 16416 | tf_op jit(solution)/shard_map/all_to_all | solution.py:471
  17.4 0.6 copy-done.2
  18.0 8.0 %serve.1 = (bf16[3072,128]{1,0:T(8,128)(2,1)}, bf16[1024,128]{1,0:T(8,128)(2,1)S(1)}, s32[1]{0:T(128)}) custom-call(s32[4096]{0:T(1024)} %bitcast.33, f32[8192,1,128]{2,1,0:T(1,128)} %bitcast.30), custom_call_target="tpu_custom_call" | custom-call | flops 1048576 | bytes 6291456 | tf_op jit(solution)/shard_map/serve/pallas_call | solution.py:520
  26.7 3.0 %all-to-all-start.3 = ((bf16[32,96,128]{2,1,0:T(8,128)(2,1)}), bf16[32,96,128]{2,1,0:T(8,128)(2,1)S(1)}, u32[]{:S(2)}, u32[]{:S(2)}) async-start(bf16[32,96,128]{2,1,0:T(8,128)(2,1)} %bitcast.43), calls=%async_computation.3 | async-start | bytes 1572864 | tf_op jit(solution)/shard_map/all_to_all | solution.py:471
  29.8 0.1 reshape.92
  29.8 0.1 copy.26
  29.9 0.1 reshape.93.position_ref
  30.1 0.1 copy.28
  30.2 0.1 reshape.95.inverse_ref
  30.2 0.1 copy.27
  30.4 0.1 copy.24
  30.6 3.5 %collective-permute-start = (bf16[2,64,512]{2,0,1:T(2,128)(2,1)S(1)}, bf16[2,64,512]{2,0,1:T(2,128)(2,1)S(1)}, u32[]{:S(2)}, u32[]{:S(2)}) collective-permute-start(bf16[2,64,512]{2,0,1:T(2,128)(2,1)S(1)} %copy.24), channel_id=1, source_target_pairs={{0,4},{4,8},{8,12},{12,16},{16,20},{20,24},{24,28},{1,5},{5,9},{9,... | collective-permute-start | bytes 393224 | tf_op jit(solution)/shard_map/ppermute | solution.py:429
  34.1 0.1 copy.25
  34.3 1.9 %collective-permute-start.1 = (bf16[2,64,512]{2,0,1:T(2,128)(2,1)S(1)}, bf16[2,64,512]{2,0,1:T(2,128)(2,1)S(1)}, u32[]{:S(2)}, u32[]{:S(2)}) collective-permute-start(bf16[2,64,512]{2,0,1:T(2,128)(2,1)S(1)} %copy.25), channel_id=1, source_target_pairs={{4,0},{8,4},{12,8},{16,12},{20,16},{24,20},{28,24},{5,1},{9,5},{13... | collective-permute-start | bytes 393224 | tf_op jit(solution)/shard_map/ppermute | solution.py:429
  36.2 0.8 slice_and_fusion
  37.1 0.8 reshape.90
  37.9 3.4 %collective-permute-done.1 = bf16[2,64,512]{2,0,1:T(2,128)(2,1)S(1)} collective-permute-done((bf16[2,64,512]{2,0,1:T(2,128)(2,1)S(1)}, bf16[2,64,512]{2,0,1:T(2,128)(2,1)S(1)}, u32[]{:S(2)}, u32[]{:S(2)}) %collective-permute-start.1) | collective-permute-done | bytes 131104 | tf_op jit(solution)/shard_map/ppermute | solution.py:429
  41.4 1.3 %collective-permute-start.3 = (bf16[2,36,512]{2,1,0:T(8,128)(2,1)S(1)}, bf16[2,36,512]{2,1,0:T(8,128)(2,1)S(1)}, u32[]{:S(2)}, u32[]{:S(2)}) collective-permute-start(bf16[2,36,512]{2,1,0:T(8,128)(2,1)S(1)} %pad_maximum_fusion.1), channel_id=1, source_target_pairs={{1,0},{2,1},{3,2},{5,4},{6,5},{7,6},{9,8},{10,9},{11,10},{13,12},{... | collective-permute-start | bytes 221192 | tf_op jit(solution)/shard_map/ppermute | solution.py:429
  42.7 4.2 %collective-permute-start.2 = (bf16[2,36,512]{2,1,0:T(8,128)(2,1)S(1)}, bf16[2,36,512]{2,1,0:T(8,128)(2,1)S(1)}, u32[]{:S(2)}, u32[]{:S(2)}) collective-permute-start(bf16[2,36,512]{2,1,0:T(8,128)(2,1)S(1)} %pad_maximum_fusion), channel_id=1, source_target_pairs={{0,1},{1,2},{2,3},{4,5},{5,6},{6,7},{8,9},{9,10},{10,11},{12,13},{... | collective-permute-start | bytes 221192 | tf_op jit(solution)/shard_map/ppermute | solution.py:429
  47.0 1.8 %match.1.match_ref = bf16[4096,128]{1,0:T(8,128)(2,1)S(1)} custom-call(s32[32,128]{1,0:T(8,128)S(1)} %pad_add_fusion.incoming_ref), custom_call_target="tpu_custom_call" | custom-call | flops 1000000000 | bytes 1048576 | tf_op jit(solution)/shard_map/match/pallas_call | solution.py:542
  48.8 2.1 %all-to-all-done.3 = bf16[32,96,128]{2,1,0:T(8,128)(2,1)S(1)} async-done(((bf16[32,96,128]{2,1,0:T(8,128)(2,1)}), bf16[32,96,128]{2,1,0:T(8,128)(2,1)S(1)}, u32[]{:S(2)}, u32[]{:S(2)}) %all-to-all-start.3) | async-done | bytes 786464 | tf_op jit(solution)/shard_map/all_to_all | solution.py:471
  50.9 14.1 %stars.1 = (f32[16,128]{1,0:T(8,128)S(1)}, bf16[3072,128]{1,0:T(8,128)(2,1)}, bf16[1024,128]{1,0:T(8,128)(2,1)S(1)}) custom-call(s32[2048]{0:T(1024)S(1)} %reshape.93.position_ref, f32[16,128]{1,0:T(8,128)S(1)} %reshape.94.observed_ref, f32[16,128]{1,0:T(8,128)S(1)} %reshape.95.inverse_ref, bf16[64,32,32,128]{3,2,1,0:T(8,128)(2,1)} %weights_hbm.1, ...), custom_call_target="tpu_custom_call" | custom-call | flops 33554432 | bytes 16777216 | tf_op jit(solution)/shard_map/stars/pallas_call | solution.py:559
  65.0 5.1 %all-to-all-start.4 = ((bf16[32,96,128]{2,1,0:T(8,128)(2,1)}), bf16[32,96,128]{2,1,0:T(8,128)(2,1)S(1)}, u32[]{:S(2)}, u32[]{:S(2)}) async-start(bf16[32,96,128]{2,1,0:T(8,128)(2,1)} %bitcast.18), calls=%async_computation.4 | async-start | bytes 1572864 | tf_op jit(solution)/shard_map/all_to_all | solution.py:471
  70.2 0.7 copy.31
  70.9 2.2 %copy-done = f32[32,64,512]{2,1,0:T(8,128)S(1)} copy-done((f32[32,64,512]{2,1,0:T(8,128)S(1)}, f32[32,64,512]{2,1,0:T(8,128)}, u32[]{:S(2)}) %copy-start) | copy-done | bytes 4194328
  73.1 10.7 %prior.1.base_hbm = f32[32,64,512]{2,1,0:T(8,128)S(1)} custom-call(f32[32,64,512]{2,1,0:T(8,128)S(1)} %copy-done, bf16[2,64,512]{2,1,0:T(8,128)(2,1)S(1)} %copy.29.xlo_ref, bf16[2,64,512]{2,1,0:T(8,128)(2,1)S(1)} %copy.30.xhi_ref, f32[2,36,512]{2,1,0:T(8,128)S(1)} %convert_element_type.22.ylo_ref, f32[2,36,512]{2,1,0:T(8,128)S(1)} %convert_element_type.24.yhi_ref), custom_call_target="tpu_custom_call" | custom-call | flops 31457280 | bytes 8388608 | tf_op jit(solution)/shard_map/prior/pallas_call | solution.py:587
  83.9 1.9 %copy-done.1 = f32[32,64,512]{2,1,0:T(8,128)} copy-done((f32[32,64,512]{2,1,0:T(8,128)}, f32[32,64,512]{2,1,0:T(8,128)S(1)}, u32[]{:S(2)}) %copy-start.1) | copy-done | bytes 4194328
  85.8 5.1 %all-to-all-done.4 = bf16[32,96,128]{2,1,0:T(8,128)(2,1)S(1)} async-done(((bf16[32,96,128]{2,1,0:T(8,128)(2,1)}), bf16[32,96,128]{2,1,0:T(8,128)(2,1)S(1)}, u32[]{:S(2)}, u32[]{:S(2)}) %all-to-all-start.4) | async-done | bytes 786464 | tf_op jit(solution)/shard_map/all_to_all | solution.py:471
  91.0 8.9 %finish.1 = f32[32,64,512]{2,1,0:T(8,128)} custom-call(s32[4096]{0:T(1024)S(1)} %bitcast.36, bf16[4096,128]{1,0:T(8,128)(2,1)S(1)} %match.1.match_ref, f32[32,64,512]{2,1,0:T(8,128)} %field_hbm.2, f32[32,64,512]{2,1,0:T(8,128)} %copy-done.1, bf16[3072,128]{1,0:T(8,128)(2,1)S(1)} %bitcast.32, bf16[1024,128]{1,0:T(8,128)(2,1)S(1)} %bitcast.39), custom_call_target="tpu_custom_call" | custom-call | flops 4194304 | bytes 12582912 | tf_op jit(solution)/shard_map/finish/pallas_call | solution.py:604
  (41 shorter events, 0.5 us)
Async XLA Ops:
  3.7 13.7 %all-to-all-start.2 = ((s32[32,1,128]{2,1,0:T(1,128)}), s32[32,1,128]{2,1,0:T(1,128)S(1)}, u32[]{:S(2)}, u32[]{:S(2)}) async-start(s32[32,1,128]{2,1,0:T(1,128)} %bitcast.46), calls=%async_computation.2 | async-start | bytes 32768 | tf_op jit(solution)/shard_map/all_to_all | solution.py:471
  13.1 16.7 %copy-start.10 = (s32[16,128]{1,0:T(8,128)S(1)}, s32[16,128]{1,0:T(8,128)}, u32[]{:S(2)}) copy-start(s32[16,128]{1,0:T(8,128)} %get-tuple-element.73) | copy-start | bytes 24580
  13.1 17.0 %copy-start.9 = (f32[64,32]{0,1:T(8,128)S(1)}, f32[64,32]{0,1:T(8,128)}, u32[]{:S(2)}) copy-start(f32[64,32]{0,1:T(8,128)} %param.13) | copy-start | bytes 24580
  13.1 17.0 %copy-start.11 = (s32[64]{0:T(128)S(1)}, s32[64]{0:T(128)}, u32[]{:S(2)}) copy-start(s32[64]{0:T(128)} %param.14) | copy-start | bytes 772
  13.1 17.1 %copy-start.8 = (f32[64,32]{0,1:T(8,128)S(1)}, f32[64,32]{0,1:T(8,128)}, u32[]{:S(2)}) copy-start(f32[64,32]{0,1:T(8,128)} %param.12) | copy-start | bytes 24580
  13.1 17.3 %copy-start.7 = (bf16[2,64,512]{2,1,0:T(8,128)(2,1)S(1)}, bf16[2,64,512]{2,1,0:T(8,128)(2,1)}, u32[]{:S(2)}) copy-start(bf16[2,64,512]{2,1,0:T(8,128)(2,1)} %get-tuple-element.68) | copy-start | bytes 393220
  13.1 21.0 %copy-start.6 = (bf16[2,64,512]{2,1,0:T(8,128)(2,1)S(1)}, bf16[2,64,512]{2,1,0:T(8,128)(2,1)}, u32[]{:S(2)}) copy-start(bf16[2,64,512]{2,1,0:T(8,128)(2,1)} %get-tuple-element.70) | copy-start | bytes 393220
  13.2 23.8 %copy-start.5 = (f32[2,32,512]{2,1,0:T(8,128)S(1)}, f32[2,32,512]{2,1,0:T(8,128)}, u32[]{:S(2)}) copy-start(f32[2,32,512]{2,1,0:T(8,128)} %get-tuple-element.71) | copy-start | bytes 393220
  13.2 23.8 %copy-start.4 = (f32[2,32,512]{2,1,0:T(8,128)S(1)}, f32[2,32,512]{2,1,0:T(8,128)}, u32[]{:S(2)}) copy-start(f32[2,32,512]{2,1,0:T(8,128)} %get-tuple-element.69) | copy-start | bytes 393220
  17.4 0.6 copy-start.2
  26.7 24.2 %all-to-all-start.3 = ((bf16[32,96,128]{2,1,0:T(8,128)(2,1)}), bf16[32,96,128]{2,1,0:T(8,128)(2,1)S(1)}, u32[]{:S(2)}, u32[]{:S(2)}) async-start(bf16[32,96,128]{2,1,0:T(8,128)(2,1)} %bitcast.43), calls=%async_computation.3 | async-start | bytes 1572864 | tf_op jit(solution)/shard_map/all_to_all | solution.py:471
  30.6 7.3 %collective-permute-start = (bf16[2,64,512]{2,0,1:T(2,128)(2,1)S(1)}, bf16[2,64,512]{2,0,1:T(2,128)(2,1)S(1)}, u32[]{:S(2)}, u32[]{:S(2)}) collective-permute-start(bf16[2,64,512]{2,0,1:T(2,128)(2,1)S(1)} %copy.24), channel_id=1, source_target_pairs={{0,4},{4,8},{8,12},{12,16},{16,20},{20,24},{24,28},{1,5},{5,9},{9,... | collective-permute-start | bytes 393224 | tf_op jit(solution)/shard_map/ppermute | solution.py:429
  34.3 7.1 %collective-permute-start.1 = (bf16[2,64,512]{2,0,1:T(2,128)(2,1)S(1)}, bf16[2,64,512]{2,0,1:T(2,128)(2,1)S(1)}, u32[]{:S(2)}, u32[]{:S(2)}) collective-permute-start(bf16[2,64,512]{2,0,1:T(2,128)(2,1)S(1)} %copy.25), channel_id=1, source_target_pairs={{4,0},{8,4},{12,8},{16,12},{20,16},{24,20},{28,24},{5,1},{9,5},{13... | collective-permute-start | bytes 393224 | tf_op jit(solution)/shard_map/ppermute | solution.py:429
  41.4 7.3 %collective-permute-start.3 = (bf16[2,36,512]{2,1,0:T(8,128)(2,1)S(1)}, bf16[2,36,512]{2,1,0:T(8,128)(2,1)S(1)}, u32[]{:S(2)}, u32[]{:S(2)}) collective-permute-start(bf16[2,36,512]{2,1,0:T(8,128)(2,1)S(1)} %pad_maximum_fusion.1), channel_id=1, source_target_pairs={{1,0},{2,1},{3,2},{5,4},{6,5},{7,6},{9,8},{10,9},{11,10},{13,12},{... | collective-permute-start | bytes 221192 | tf_op jit(solution)/shard_map/ppermute | solution.py:429
  42.7 6.0 %collective-permute-start.2 = (bf16[2,36,512]{2,1,0:T(8,128)(2,1)S(1)}, bf16[2,36,512]{2,1,0:T(8,128)(2,1)S(1)}, u32[]{:S(2)}, u32[]{:S(2)}) collective-permute-start(bf16[2,36,512]{2,1,0:T(8,128)(2,1)S(1)} %pad_maximum_fusion), channel_id=1, source_target_pairs={{0,1},{1,2},{2,3},{4,5},{5,6},{6,7},{8,9},{9,10},{10,11},{12,13},{... | collective-permute-start | bytes 221192 | tf_op jit(solution)/shard_map/ppermute | solution.py:429
  65.0 26.0 %all-to-all-start.4 = ((bf16[32,96,128]{2,1,0:T(8,128)(2,1)}), bf16[32,96,128]{2,1,0:T(8,128)(2,1)S(1)}, u32[]{:S(2)}, u32[]{:S(2)}) async-start(bf16[32,96,128]{2,1,0:T(8,128)(2,1)} %bitcast.18), calls=%async_computation.4 | async-start | bytes 1572864 | tf_op jit(solution)/shard_map/all_to_all | solution.py:471
  70.9 2.2 %copy-start = (f32[32,64,512]{2,1,0:T(8,128)S(1)}, f32[32,64,512]{2,1,0:T(8,128)}, u32[]{:S(2)}) copy-start(f32[32,64,512]{2,1,0:T(8,128)} %field_hbm.2) | copy-start | bytes 12582916
  73.1 17.8 %copy-start.3 = (s32[32,1,128]{2,1,0:T(1,128)S(1)}, s32[32,1,128]{2,1,0:T(1,128)}, u32[]{:S(2)}) copy-start(s32[32,1,128]{2,1,0:T(1,128)} %copy-done.2) | copy-start | bytes 49156
  83.9 2.0 %copy-start.1 = (f32[32,64,512]{2,1,0:T(8,128)}, f32[32,64,512]{2,1,0:T(8,128)S(1)}, u32[]{:S(2)}) copy-start(f32[32,64,512]{2,1,0:T(8,128)S(1)} %prior.1.base_hbm) | copy-start | bytes 12582916

commit v10 on v7

--- a/solution.py
+++ b/solution.py
@@ -103,6 +103,17 @@
             ylast_ref[h, x : x + 1, :] = strips_ref[1, x, 6 + h : 7 + h, :]
 
 
+def copies_in_parts(source, target, sems):
+    parts = sems.shape[0]
+    size = source.shape[0] // parts
+    return [
+        pltpu.make_async_copy(
+            source.at[pl.ds(i * size, size)], target.at[pl.ds(i * size, size)], sems.at[i]
+        )
+        for i in range(parts)
+    ]
+
+
 def for_each_group(incoming_ref, visit, capacity, first_slots, blocks):
     sources = incoming_ref.shape[0] // capacity
     last_slots = capacity - first_slots
@@ -144,46 +155,34 @@
 
 
 def serve_kernel(incoming_ref, field_hbm, *refs, capacity, first_slots):
-    *served_refs, crowded_ref, field_ref, table_ref, sems = refs
-    cells_x, cells_y, depth = field_ref.shape
-    per_column = depth // LANES
-    parts = sems.shape[0]
-    planes = cells_x // parts
-
-    def load(part):
-        span = pl.ds(part * planes, planes)
-        return pltpu.make_async_copy(field_hbm.at[span], field_ref.at[span], sems.at[part])
-
-    for part in range(parts):
-        load(part).start()
+    *served_refs, crowded_ref, rows_ref, found_ref, sems = refs
+    blocks = field_hbm.shape[0]
+    loads = copies_in_parts(field_hbm, rows_ref, sems)
+    for load in loads:
+        load.start()
 
     def mark_of(source, most):
         return jnp.maximum(most, incoming_ref[source * capacity + capacity - 1] >> 16)
 
     fullest = lax.fori_loop(0, incoming_ref.shape[0] // capacity, mark_of, jnp.int32(0))
     crowded_ref[0] = jnp.where(fullest > first_slots, 1, 0)
-    table_rows = table_ref.reshape(table_ref.shape[0], LANES)
-    blocks = cells_x * cells_y * per_column
-    table_rows[blocks:, :] = jnp.zeros((table_ref.shape[0] - blocks, LANES), jnp.float32)
-
-    def one_plane(x, carry):
-        for yb in range(cells_y // 8):
-            for part in range(per_column):
-                at = pl.multiple_of(((x * (cells_y // 8) + yb) * per_column + part) * 8, 8)
-                table_rows[pl.ds(at, 8), :] = jnp.exp(
-                    field_ref[x, 8 * yb : 8 * yb + 8, part * LANES : (part + 1) * LANES]
-                )
-        return carry
-
-    for part in range(parts):
-        load(part).wait()
-        lax.fori_loop(part * planes, (part + 1) * planes, one_plane, 0)
+    rows_ref[blocks:] = jnp.zeros((rows_ref.shape[0] - blocks, 1, LANES), jnp.float32)
+    for load in loads:
+        load.wait()
+
+    part_starts = [0, served_refs[0].shape[0]]
 
     def visit(wanted, row, list_part):
-        rows = jnp.concatenate([table_ref[at] for at in wanted], axis=0)
-        served_refs[list_part][pl.ds(row, GROUP), :] = rows.astype(jnp.bfloat16)
+        rows = [rows_ref[at] for at in wanted]
+        found = found_ref.at[pl.ds(row + part_starts[list_part], GROUP)]
+        for j in range(GROUP):
+            found[j] = rows[j]
 
     for_each_group(incoming_ref, visit, capacity, first_slots, blocks)
+    found = found_ref.reshape(found_ref.shape[0], LANES)
+    for start, served_ref in zip(part_starts, served_refs):
+        span = slice(start, start + served_ref.shape[0])
+        served_ref[...] = jnp.exp(found[span, :]).astype(jnp.bfloat16)
 
 
 def match_kernel(incoming_ref, match_ref):
@@ -222,6 +221,7 @@
     per_chunk = per * slots
     fold = LANES // stars
     all_slots = parcel_rows.shape[0]
+    sens_blocks = sens_ref.reshape(sens_ref.shape[0], width)
     lane = lax.broadcasted_iota(jnp.int32, (8, LANES), 1)
     row = lax.broadcasted_iota(jnp.int32, (8, LANES), 0)
     star_group = lane // stars
@@ -240,11 +240,13 @@
     def extinctions(one_set, u, chunk, places):
         sums = []
         for b in range(per):
-            total = jnp.zeros((stars, width), jnp.float32)
+            total = jnp.zeros((stars // 8, 8, width), jnp.float32)
             for k in range(slots):
-                fetched = returned_rows[places[u * per_chunk + b * slots + k]]
-                total = total + weights_ref[one_set, u, b, k].astype(jnp.float32) * fetched
-            sums.append(total)
+                at = places[u * per_chunk + b * slots + k]
+                fetched = returned_rows[pl.ds(at, 8, stride=0), :]
+                block = weights_ref[one_set, u, b, k].astype(jnp.float32)
+                total = total + block.reshape(stars // 8, 8, width) * fetched
+            sums.append(total.reshape(stars, width))
         extinction = lax.dot_general(
             jnp.ones((8, width), jnp.float32),
             jnp.concatenate(sums, axis=0),
@@ -271,11 +273,11 @@
             sens = jnp.dot(left, right, preferred_element_type=jnp.float32)
             for j in range(slots // 8):
                 first = u * per_chunk + b * slots + 8 * j
-                sens_ref[first : first + 8, :] = sens[:, j * width : (j + 1) * width]
+                sens_blocks[first : first + 8, :] = sens[:, j * width : (j + 1) * width]
 
     def scatter(u, places):
         for i in range(u * per_chunk, (u + 1) * per_chunk):
-            parcel_rows[places[i]] = sens_ref[i : i + 1, :]
+            parcel_rows[places[i]] = sens_ref[i]
 
     def work(one_round, one_set):
         first = (one_round * sets + one_set) * in_set
@@ -296,7 +298,7 @@
     start = 0
     for returned_ref in returned_refs:
         span = slice(start, start + returned_ref.shape[0])
-        returned_rows.reshape(all_slots, width)[span, :] = returned_ref[...].astype(jnp.float32)
+        returned_rows[span, :] = returned_ref[...].astype(jnp.float32)
         start = span.stop
     parcel_rows.reshape(all_slots, width)[...] = jnp.zeros((all_slots, width), jnp.float32)
 
@@ -381,18 +383,17 @@
     parts = out_sems.shape[0]
     planes = cells_x // parts
     blocks = cells_x * cells_y * per_column
-    loads = [
-        pltpu.make_async_copy(field_hbm, field_ref, in_sems.at[0]),
-        pltpu.make_async_copy(base_hbm, base_ref, in_sems.at[1]),
-    ]
+    loads = copies_in_parts(field_hbm, field_ref, in_sems.at[0])
+    loads += copies_in_parts(base_hbm, base_ref, in_sems.at[1])
     for load in loads:
         load.start()
     collected_rows = collected.reshape(collected.shape[0], LANES)
+    merged = rows_ref.reshape(rows_ref.shape[0], LANES)
     start = 0
     for arrived_ref in arrived_refs:
         for i in range(arrived_ref.shape[0] // LANES):
             span = slice(start + i * LANES, start + (i + 1) * LANES)
-            rows_ref[span, :] = -step_rate * jnp.dot(
+            merged[span, :] = -step_rate * jnp.dot(
                 match_ref[span, :],
                 arrived_ref[i * LANES : (i + 1) * LANES, :],
                 preferred_element_type=jnp.float32,
@@ -405,7 +406,7 @@
     def visit(wanted, row, list_part):
         row = pl.multiple_of(row + part_starts[list_part], GROUP)
         rows = rows_ref.at[pl.ds(row, GROUP)]
-        sums = [collected[wanted[j]] + rows[j : j + 1, :] for j in range(GROUP)]
+        sums = [collected[wanted[j]] + rows[j] for j in range(GROUP)]
         for j in range(GROUP):
             collected[wanted[j]] = sums[j]
 
@@ -474,6 +475,10 @@
     mesh_axes = ("gx", "gy")
     f32, bf16, i32 = jnp.float32, jnp.bfloat16, jnp.int32
     shape = jax.ShapeDtypeStruct
+
+    def to_rows(x):
+        x = x.reshape(cells_x, cells_y // 8, 8, per_column, width)
+        return x.transpose(0, 1, 3, 2, 4).reshape(blocks, 1, width)
 
     def exchange(x):
         return lax.all_to_all(x, mesh_axes, split_axis=0, concat_axis=0, tiled=True)
@@ -525,23 +530,22 @@
     incoming, *edges = lax.optimization_barrier((incoming, xfirst, xlast, yfirst, ylast))
     wanted = incoming.reshape(-1)
 
-    parts = 8
     *served, crowded = pl.pallas_call(
         functools.partial(serve_kernel, capacity=capacity, first_slots=first_slots),
         out_shape=[shape((devices * n, width), bf16) for n in slots_of] + [shape((1,), i32)],
         in_specs=[SMEM, ANY],
         out_specs=[VMEM] * exchanges + [SMEM],
         scratch_shapes=[
-            pltpu.VMEM(field_shape, f32),
             pltpu.VMEM((blocks + capacity, 1, width), f32),
-            pltpu.SemaphoreType.DMA((parts,)),
+            pltpu.VMEM((all_slots, 1, width), f32),
+            pltpu.SemaphoreType.DMA((16,)),
         ],
         compiler_params=pltpu.CompilerParams(vmem_limit_bytes=56 * MIB),
         cost_estimate=pl.CostEstimate(
             flops=cells, bytes_accessed=6 * MIB, transcendentals=cells
         ),
         name="serve",
-    )(wanted, log_density)
+    )(wanted, to_rows(log_density))
     crowded = crowded[0] != 0
 
     incoming_late, *edges, _ = lax.optimization_barrier((incoming, *edges, served[0]))
@@ -574,8 +578,8 @@
         out_specs=[VMEM] * (1 + exchanges),
         scratch_shapes=[
             pltpu.VMEM((2, in_set, blocks_dev // chunks, slots, stars, width), bf16),
-            pltpu.VMEM((all_slots, 1, width), f32),
-            pltpu.VMEM((in_set * LANES // stars * slots, width), f32),
+            pltpu.VMEM((all_slots + 8, width), f32),
+            pltpu.VMEM((in_set * (blocks_dev // chunks) * slots, 1, width), f32),
             pltpu.VMEM((all_slots, 1, width), f32),
             pltpu.SemaphoreType.DMA((2, in_set)),
         ],
@@ -610,6 +614,7 @@
         name="prior",
     )(field_late, xlo, xhi, ylo, yhi)
 
+    parts = 8
     new_log_density = pl.pallas_call(
         functools.partial(
             finish_kernel, exchanges=exchanges, capacity=capacity, first_slots=first_slots
@@ -619,11 +624,11 @@
         out_specs=ANY,
         scratch_shapes=[
             pltpu.VMEM((blocks + capacity, 1, width), f32),
-            pltpu.VMEM((all_slots, width), f32),
+            pltpu.VMEM((all_slots, 1, width), f32),
             pltpu.VMEM(field_shape, f32),
             pltpu.VMEM(field_shape, f32),
             pltpu.VMEM(field_shape, f32),
-            pltpu.SemaphoreType.DMA((2,)),
+            pltpu.SemaphoreType.DMA((2, parts)),
             pltpu.SemaphoreType.DMA((parts,)),
         ],
         compiler_params=pltpu.CompilerParams(vmem_limit_bytes=50 * MIB),

time: 98.7 us -> 98.1 us (level)
  no operation moved by 1% of the time
where the time goes in v10:
time: 98.1 us; the launch traced here: 97.5 us
  Pallas kernels  46.5 us (47%)
  starting transfers between devices  26.1 us (27%)
  waiting for transfers between devices  14.9 us (15%)
  local copies, waits for them, and re-layouts  7.35 us (7%)
  between operations  1.61 us (2%)
    all_to_all x3, starting transfers between devices, exchange(): return lax.all_to_all(x, mesh_axes, split_axis=0, concat_axis=0, tiled=True)  15.2 us
    pallas_call x1, Pallas kernels, on_device(): pl.pallas_call(functools.partial(star_kernel, exchanges=exchanges), out_s...  12.2 us
    all_to_all x3, waiting for transfers between devices, exchange(): return lax.all_to_all(x, mesh_axes, split_axis=0, concat_axis=0, tiled=True)  11.5 us
    ppermute x4, starting transfers between devices, both_ways(): return (lax.ppermute(last, axis, up), lax.ppermute(first, axis, down))  11 us
    pallas_call x1, Pallas kernels, on_device(): pl.pallas_call(prior_kernel, out_shape=shape(field_shape, f32), in_specs=...  10.7 us
    pallas_call x1, Pallas kernels, on_device(): pl.pallas_call(functools.partial(finish_kernel, exchanges=exchanges, capa...  8.9 us
    pallas_call x1, Pallas kernels, on_device(): pl.pallas_call(functools.partial(serve_kernel, capacity=capacity, first_s...  7.54 us
    unnamed x26, local copies, waits for them, and re-layouts  5.55 us
  transfers between devices with their start and end apart: 7, of which 4 were waited for; matrix products, arithmetic and copies ran while one was open for 4% of the time, Pallas kernels for 15%

profile of v10, /device:TPU:1, one launch (start us, length us, event | category | flops | bytes accessed | tf_op | source)
XLA Modules:
  0.0 97.5 jit_solution(10509290634518716736)
XLA Ops:
  0.6 3.1 %route.1 = (s32[32,128]{1,0:T(8,128)}, s32[16,128]{1,0:T(8,128)}) custom-call(s32[32,64]{1,0:T(8,128)} %bitcast.45), custom_call_target="tpu_custom_call" | custom-call | tf_op jit(solution)/shard_map/route/pallas_call | solution.py:494
  3.7 7.1 %all-to-all-start.2 = ((s32[32,1,128]{2,1,0:T(1,128)}), s32[32,1,128]{2,1,0:T(1,128)S(1)}, u32[]{:S(2)}, u32[]{:S(2)}) async-start(s32[32,1,128]{2,1,0:T(1,128)} %bitcast.46), calls=%async_computation.2 | async-start | bytes 32768 | tf_op jit(solution)/shard_map/all_to_all | solution.py:484
  10.8 2.3 %edges.1 = (bf16[2,64,512]{2,1,0:T(8,128)(2,1)}, bf16[2,64,512]{2,1,0:T(8,128)(2,1)}, f32[2,32,512]{2,1,0:T(8,128)}, f32[2,32,512]{2,1,0:T(8,128)}) custom-call(f32[32,64,512]{2,1,0:T(8,128)} %field_hbm.2), custom_call_target="tpu_custom_call" | custom-call | bytes 2097152 | tf_op jit(solution)/shard_map/edges/pallas_call | solution.py:511
  13.2 4.2 %all-to-all-done.2 = s32[32,1,128]{2,1,0:T(1,128)S(1)} async-done(((s32[32,1,128]{2,1,0:T(1,128)}), s32[32,1,128]{2,1,0:T(1,128)S(1)}, u32[]{:S(2)}, u32[]{:S(2)}) %all-to-all-start.2) | async-done | bytes 16416 | tf_op jit(solution)/shard_map/all_to_all | solution.py:484
  17.4 0.6 copy-done.2
  18.0 7.5 %serve.1 = (bf16[3072,128]{1,0:T(8,128)(2,1)}, bf16[1024,128]{1,0:T(8,128)(2,1)S(1)}, s32[1]{0:T(128)}) custom-call(s32[4096]{0:T(1024)} %bitcast.33, f32[8192,1,128]{2,1,0:T(1,128)} %bitcast.30), custom_call_target="tpu_custom_call" | custom-call | flops 1048576 | bytes 6291456 | tf_op jit(solution)/shard_map/serve/pallas_call | solution.py:533
  26.2 2.9 %all-to-all-start.3 = ((bf16[32,96,128]{2,1,0:T(8,128)(2,1)}), bf16[32,96,128]{2,1,0:T(8,128)(2,1)S(1)}, u32[]{:S(2)}, u32[]{:S(2)}) async-start(bf16[32,96,128]{2,1,0:T(8,128)(2,1)} %bitcast.43), calls=%async_computation.3 | async-start | bytes 1572864 | tf_op jit(solution)/shard_map/all_to_all | solution.py:484
  29.2 0.1 reshape.92
  29.3 0.1 copy.26
  29.4 0.1 reshape.93.position_ref
  29.5 0.1 copy.28
  29.6 0.1 reshape.95.inverse_ref
  29.7 0.1 copy.27
  29.8 0.1 copy.24
  30.0 3.5 %collective-permute-start = (bf16[2,64,512]{2,0,1:T(2,128)(2,1)S(1)}, bf16[2,64,512]{2,0,1:T(2,128)(2,1)S(1)}, u32[]{:S(2)}, u32[]{:S(2)}) collective-permute-start(bf16[2,64,512]{2,0,1:T(2,128)(2,1)S(1)} %copy.24), channel_id=1, source_target_pairs={{0,4},{4,8},{8,12},{12,16},{16,20},{20,24},{24,28},{1,5},{5,9},{9,... | collective-permute-start | bytes 393224 | tf_op jit(solution)/shard_map/ppermute | solution.py:442
  33.6 0.1 copy.25
  33.7 1.9 %collective-permute-start.1 = (bf16[2,64,512]{2,0,1:T(2,128)(2,1)S(1)}, bf16[2,64,512]{2,0,1:T(2,128)(2,1)S(1)}, u32[]{:S(2)}, u32[]{:S(2)}) collective-permute-start(bf16[2,64,512]{2,0,1:T(2,128)(2,1)S(1)} %copy.25), channel_id=1, source_target_pairs={{4,0},{8,4},{12,8},{16,12},{20,16},{24,20},{28,24},{5,1},{9,5},{13... | collective-permute-start | bytes 393224 | tf_op jit(solution)/shard_map/ppermute | solution.py:442
  35.6 0.8 slice_and_fusion
  36.5 0.8 reshape.90
  37.4 3.4 %collective-permute-done.1 = bf16[2,64,512]{2,0,1:T(2,128)(2,1)S(1)} collective-permute-done((bf16[2,64,512]{2,0,1:T(2,128)(2,1)S(1)}, bf16[2,64,512]{2,0,1:T(2,128)(2,1)S(1)}, u32[]{:S(2)}, u32[]{:S(2)}) %collective-permute-start.1) | collective-permute-done | bytes 131104 | tf_op jit(solution)/shard_map/ppermute | solution.py:442
  40.9 1.3 %collective-permute-start.3 = (bf16[2,36,512]{2,1,0:T(8,128)(2,1)S(1)}, bf16[2,36,512]{2,1,0:T(8,128)(2,1)S(1)}, u32[]{:S(2)}, u32[]{:S(2)}) collective-permute-start(bf16[2,36,512]{2,1,0:T(8,128)(2,1)S(1)} %pad_maximum_fusion.1), channel_id=1, source_target_pairs={{1,0},{2,1},{3,2},{5,4},{6,5},{7,6},{9,8},{10,9},{11,10},{13,12},{... | collective-permute-start | bytes 221192 | tf_op jit(solution)/shard_map/ppermute | solution.py:442
  42.2 4.2 %collective-permute-start.2 = (bf16[2,36,512]{2,1,0:T(8,128)(2,1)S(1)}, bf16[2,36,512]{2,1,0:T(8,128)(2,1)S(1)}, u32[]{:S(2)}, u32[]{:S(2)}) collective-permute-start(bf16[2,36,512]{2,1,0:T(8,128)(2,1)S(1)} %pad_maximum_fusion), channel_id=1, source_target_pairs={{0,1},{1,2},{2,3},{4,5},{5,6},{6,7},{8,9},{9,10},{10,11},{12,13},{... | collective-permute-start | bytes 221192 | tf_op jit(solution)/shard_map/ppermute | solution.py:442
  46.4 1.8 %match.1.match_ref = bf16[4096,128]{1,0:T(8,128)(2,1)S(1)} custom-call(s32[32,128]{1,0:T(8,128)S(1)} %pad_add_fusion.incoming_ref), custom_call_target="tpu_custom_call" | custom-call | flops 1000000000 | bytes 1048576 | tf_op jit(solution)/shard_map/match/pallas_call | solution.py:556
  48.3 2.1 %all-to-all-done.3 = bf16[32,96,128]{2,1,0:T(8,128)(2,1)S(1)} async-done(((bf16[32,96,128]{2,1,0:T(8,128)(2,1)}), bf16[32,96,128]{2,1,0:T(8,128)(2,1)S(1)}, u32[]{:S(2)}, u32[]{:S(2)}) %all-to-all-start.3) | async-done | bytes 786464 | tf_op jit(solution)/shard_map/all_to_all | solution.py:484
  50.4 12.2 %stars.1 = (f32[16,128]{1,0:T(8,128)S(1)}, bf16[3072,128]{1,0:T(8,128)(2,1)}, bf16[1024,128]{1,0:T(8,128)(2,1)S(1)}) custom-call(s32[2048]{0:T(1024)S(1)} %reshape.93.position_ref, f32[16,128]{1,0:T(8,128)S(1)} %reshape.94.observed_ref, f32[16,128]{1,0:T(8,128)S(1)} %reshape.95.inverse_ref, bf16[64,32,32,128]{3,2,1,0:T(8,128)(2,1)} %weights_hbm.1, ...), custom_call_target="tpu_custom_call" | custom-call | flops 33554432 | bytes 16777216 | tf_op jit(solution)/shard_map/stars/pallas_call | solution.py:573
  62.6 5.1 %all-to-all-start.4 = ((bf16[32,96,128]{2,1,0:T(8,128)(2,1)}), bf16[32,96,128]{2,1,0:T(8,128)(2,1)S(1)}, u32[]{:S(2)}, u32[]{:S(2)}) async-start(bf16[32,96,128]{2,1,0:T(8,128)(2,1)} %bitcast.18), calls=%async_computation.4 | async-start | bytes 1572864 | tf_op jit(solution)/shard_map/all_to_all | solution.py:484
  67.9 0.7 copy.31
  68.6 2.2 %copy-done = f32[32,64,512]{2,1,0:T(8,128)S(1)} copy-done((f32[32,64,512]{2,1,0:T(8,128)S(1)}, f32[32,64,512]{2,1,0:T(8,128)}, u32[]{:S(2)}) %copy-start) | copy-done | bytes 4194328
  70.8 10.7 %prior.1.base_hbm = f32[32,64,512]{2,1,0:T(8,128)S(1)} custom-call(f32[32,64,512]{2,1,0:T(8,128)S(1)} %copy-done, bf16[2,64,512]{2,1,0:T(8,128)(2,1)S(1)} %copy.29.xlo_ref, bf16[2,64,512]{2,1,0:T(8,128)(2,1)S(1)} %copy.30.xhi_ref, f32[2,36,512]{2,1,0:T(8,128)S(1)} %convert_element_type.22.ylo_ref, f32[2,36,512]{2,1,0:T(8,128)S(1)} %convert_element_type.24.yhi_ref), custom_call_target="tpu_custom_call" | custom-call | flops 31457280 | bytes 8388608 | tf_op jit(solution)/shard_map/prior/pallas_call | solution.py:601
  81.5 1.9 %copy-done.1 = f32[32,64,512]{2,1,0:T(8,128)} copy-done((f32[32,64,512]{2,1,0:T(8,128)}, f32[32,64,512]{2,1,0:T(8,128)S(1)}, u32[]{:S(2)}) %copy-start.1) | copy-done | bytes 4194328
  83.5 5.1 %all-to-all-done.4 = bf16[32,96,128]{2,1,0:T(8,128)(2,1)S(1)} async-done(((bf16[32,96,128]{2,1,0:T(8,128)(2,1)}), bf16[32,96,128]{2,1,0:T(8,128)(2,1)S(1)}, u32[]{:S(2)}, u32[]{:S(2)}) %all-to-all-start.4) | async-done | bytes 786464 | tf_op jit(solution)/shard_map/all_to_all | solution.py:484
  88.6 8.9 %finish.1 = f32[32,64,512]{2,1,0:T(8,128)} custom-call(s32[4096]{0:T(1024)S(1)} %bitcast.36, bf16[4096,128]{1,0:T(8,128)(2,1)S(1)} %match.1.match_ref, f32[32,64,512]{2,1,0:T(8,128)} %field_hbm.2, f32[32,64,512]{2,1,0:T(8,128)} %copy-done.1, bf16[3072,128]{1,0:T(8,128)(2,1)S(1)} %bitcast.32, bf16[1024,128]{1,0:T(8,128)(2,1)S(1)} %bitcast.39), custom_call_target="tpu_custom_call" | custom-call | flops 4194304 | bytes 12582912 | tf_op jit(solution)/shard_map/finish/pallas_call | solution.py:618
  (41 shorter events, 0.5 us)
Async XLA Ops:
  3.7 13.7 %all-to-all-start.2 = ((s32[32,1,128]{2,1,0:T(1,128)}), s32[32,1,128]{2,1,0:T(1,128)S(1)}, u32[]{:S(2)}, u32[]{:S(2)}) async-start(s32[32,1,128]{2,1,0:T(1,128)} %bitcast.46), calls=%async_computation.2 | async-start | bytes 32768 | tf_op jit(solution)/shard_map/all_to_all | solution.py:484
  13.1 16.1 %copy-start.10 = (s32[16,128]{1,0:T(8,128)S(1)}, s32[16,128]{1,0:T(8,128)}, u32[]{:S(2)}) copy-start(s32[16,128]{1,0:T(8,128)} %get-tuple-element.73) | copy-start | bytes 24580
  13.1 16.4 %copy-start.9 = (f32[64,32]{0,1:T(8,128)S(1)}, f32[64,32]{0,1:T(8,128)}, u32[]{:S(2)}) copy-start(f32[64,32]{0,1:T(8,128)} %param.13) | copy-start | bytes 24580
  13.1 16.4 %copy-start.11 = (s32[64]{0:T(128)S(1)}, s32[64]{0:T(128)}, u32[]{:S(2)}) copy-start(s32[64]{0:T(128)} %param.14) | copy-start | bytes 772
  13.1 16.6 %copy-start.8 = (f32[64,32]{0,1:T(8,128)S(1)}, f32[64,32]{0,1:T(8,128)}, u32[]{:S(2)}) copy-start(f32[64,32]{0,1:T(8,128)} %param.12) | copy-start | bytes 24580
  13.1 16.7 %copy-start.7 = (bf16[2,64,512]{2,1,0:T(8,128)(2,1)S(1)}, bf16[2,64,512]{2,1,0:T(8,128)(2,1)}, u32[]{:S(2)}) copy-start(bf16[2,64,512]{2,1,0:T(8,128)(2,1)} %get-tuple-element.68) | copy-start | bytes 393220
  13.1 20.4 %copy-start.6 = (bf16[2,64,512]{2,1,0:T(8,128)(2,1)S(1)}, bf16[2,64,512]{2,1,0:T(8,128)(2,1)}, u32[]{:S(2)}) copy-start(bf16[2,64,512]{2,1,0:T(8,128)(2,1)} %get-tuple-element.70) | copy-start | bytes 393220
  13.2 23.3 %copy-start.5 = (f32[2,32,512]{2,1,0:T(8,128)S(1)}, f32[2,32,512]{2,1,0:T(8,128)}, u32[]{:S(2)}) copy-start(f32[2,32,512]{2,1,0:T(8,128)} %get-tuple-element.71) | copy-start | bytes 393220
  13.2 23.3 %copy-start.4 = (f32[2,32,512]{2,1,0:T(8,128)S(1)}, f32[2,32,512]{2,1,0:T(8,128)}, u32[]{:S(2)}) copy-start(f32[2,32,512]{2,1,0:T(8,128)} %get-tuple-element.69) | copy-start | bytes 393220
  17.4 0.6 copy-start.2
  26.2 24.1 %all-to-all-start.3 = ((bf16[32,96,128]{2,1,0:T(8,128)(2,1)}), bf16[32,96,128]{2,1,0:T(8,128)(2,1)S(1)}, u32[]{:S(2)}, u32[]{:S(2)}) async-start(bf16[32,96,128]{2,1,0:T(8,128)(2,1)} %bitcast.43), calls=%async_computation.3 | async-start | bytes 1572864 | tf_op jit(solution)/shard_map/all_to_all | solution.py:484
  30.0 7.3 %collective-permute-start = (bf16[2,64,512]{2,0,1:T(2,128)(2,1)S(1)}, bf16[2,64,512]{2,0,1:T(2,128)(2,1)S(1)}, u32[]{:S(2)}, u32[]{:S(2)}) collective-permute-start(bf16[2,64,512]{2,0,1:T(2,128)(2,1)S(1)} %copy.24), channel_id=1, source_target_pairs={{0,4},{4,8},{8,12},{12,16},{16,20},{20,24},{24,28},{1,5},{5,9},{9,... | collective-permute-start | bytes 393224 | tf_op jit(solution)/shard_map/ppermute | solution.py:442
  33.7 7.1 %collective-permute-start.1 = (bf16[2,64,512]{2,0,1:T(2,128)(2,1)S(1)}, bf16[2,64,512]{2,0,1:T(2,128)(2,1)S(1)}, u32[]{:S(2)}, u32[]{:S(2)}) collective-permute-start(bf16[2,64,512]{2,0,1:T(2,128)(2,1)S(1)} %copy.25), channel_id=1, source_target_pairs={{4,0},{8,4},{12,8},{16,12},{20,16},{24,20},{28,24},{5,1},{9,5},{13... | collective-permute-start | bytes 393224 | tf_op jit(solution)/shard_map/ppermute | solution.py:442
  40.9 7.3 %collective-permute-start.3 = (bf16[2,36,512]{2,1,0:T(8,128)(2,1)S(1)}, bf16[2,36,512]{2,1,0:T(8,128)(2,1)S(1)}, u32[]{:S(2)}, u32[]{:S(2)}) collective-permute-start(bf16[2,36,512]{2,1,0:T(8,128)(2,1)S(1)} %pad_maximum_fusion.1), channel_id=1, source_target_pairs={{1,0},{2,1},{3,2},{5,4},{6,5},{7,6},{9,8},{10,9},{11,10},{13,12},{... | collective-permute-start | bytes 221192 | tf_op jit(solution)/shard_map/ppermute | solution.py:442
  42.2 6.0 %collective-permute-start.2 = (bf16[2,36,512]{2,1,0:T(8,128)(2,1)S(1)}, bf16[2,36,512]{2,1,0:T(8,128)(2,1)S(1)}, u32[]{:S(2)}, u32[]{:S(2)}) collective-permute-start(bf16[2,36,512]{2,1,0:T(8,128)(2,1)S(1)} %pad_maximum_fusion), channel_id=1, source_target_pairs={{0,1},{1,2},{2,3},{4,5},{5,6},{6,7},{8,9},{9,10},{10,11},{12,13},{... | collective-permute-start | bytes 221192 | tf_op jit(solution)/shard_map/ppermute | solution.py:442
  62.6 26.0 %all-to-all-start.4 = ((bf16[32,96,128]{2,1,0:T(8,128)(2,1)}), bf16[32,96,128]{2,1,0:T(8,128)(2,1)S(1)}, u32[]{:S(2)}, u32[]{:S(2)}) async-start(bf16[32,96,128]{2,1,0:T(8,128)(2,1)} %bitcast.18), calls=%async_computation.4 | async-start | bytes 1572864 | tf_op jit(solution)/shard_map/all_to_all | solution.py:484
  68.6 2.2 %copy-start = (f32[32,64,512]{2,1,0:T(8,128)S(1)}, f32[32,64,512]{2,1,0:T(8,128)}, u32[]{:S(2)}) copy-start(f32[32,64,512]{2,1,0:T(8,128)} %field_hbm.2) | copy-start | bytes 12582916
  70.8 17.8 %copy-start.3 = (s32[32,1,128]{2,1,0:T(1,128)S(1)}, s32[32,1,128]{2,1,0:T(1,128)}, u32[]{:S(2)}) copy-start(s32[32,1,128]{2,1,0:T(1,128)} %copy-done.2) | copy-start | bytes 49156
  81.5 2.0 %copy-start.1 = (f32[32,64,512]{2,1,0:T(8,128)}, f32[32,64,512]{2,1,0:T(8,128)S(1)}, u32[]{:S(2)}) copy-start(f32[32,64,512]{2,1,0:T(8,128)S(1)} %prior.1.base_hbm) | copy-start | bytes 12582916

commit v11 on v10

--- a/solution.py
+++ b/solution.py
@@ -12,7 +12,7 @@
 step_rate = 2.0
 
 LANES = 128
-GROUP = 16
+GROUP = 8
 MIB = 1 << 20
 MARK = 1 << 16
 
@@ -117,7 +117,7 @@
 def for_each_group(incoming_ref, visit, capacity, first_slots, blocks):
     sources = incoming_ref.shape[0] // capacity
     last_slots = capacity - first_slots
-    together = 4
+    together = 8
 
     def groups_of(source):
         last = incoming_ref[source * capacity + capacity - 1] & (MARK - 1)
@@ -292,9 +292,8 @@
             if u >= 2:
                 scatter(u - 2, places)
 
-    for one_set in range(sets):
-        for copy in load(0, one_set):
-            copy.start()
+    for copy in load(0, 0):
+        copy.start()
     start = 0
     for returned_ref in returned_refs:
         span = slice(start, start + returned_ref.shape[0])
@@ -306,13 +305,17 @@
         for one_set in range(sets):
             for copy in load(i, one_set):
                 copy.wait()
+            if one_set + 1 < sets:
+                for copy in load(i, one_set + 1):
+                    copy.start()
+            else:
+
+                @pl.when(i + 1 < rounds)
+                def _():
+                    for copy in load(i + 1, 0):
+                        copy.start()
+
             work(i, one_set)
-
-            @pl.when(i + 1 < rounds)
-            def _():
-                for copy in load(i + 1, one_set):
-                    copy.start()
-
         return carry
 
     lax.fori_loop(0, rounds, one_round, 0)
@@ -323,9 +326,24 @@
         start = span.stop
 
 
-def prior_kernel(field_ref, xlo_ref, xhi_ref, ylo_ref, yhi_ref, out_ref, padded, smooth):
-    cells_x, cells_y, depth = field_ref.shape
+def prior_kernel(
+    field_hbm, xlo_ref, xhi_ref, ylo_ref, yhi_ref, out_hbm, padded, smooth, out_ref, sems, out_sems
+):
+    cells_x, cells_y, depth = field_hbm.shape
     rows = padded.shape[1]
+    parts = sems.shape[0]
+    planes = cells_x // parts
+    own_rows = pl.ds(8, cells_y)
+    loads = [
+        pltpu.make_async_copy(
+            field_hbm.at[pl.ds(i * planes, planes)],
+            padded.at[pl.ds(2 + i * planes, planes), own_rows],
+            sems.at[i],
+        )
+        for i in range(parts)
+    ]
+    for load in loads:
+        load.start()
     gx, gy = lax.axis_index("gx"), lax.axis_index("gy")
     last_gx, last_gy = lax.axis_size("gx") - 1, lax.axis_size("gy") - 1
     z = lax.broadcasted_iota(jnp.int32, (rows, depth), 1)
@@ -339,23 +357,21 @@
         beside = beside + jnp.where(z == depth - 1, 0.0, pltpu.roll(center, depth - 1, 1))
         return (shift_kappa + 6.0) * center - beside
 
-    def fill(plane, source):
-        padded[plane, 8 : 8 + cells_y, :] = source
+    for h in range(2):
+        padded[h, own_rows, :] = xlo_ref[h].astype(jnp.float32)
+        padded[cells_x + 2 + h, own_rows, :] = xhi_ref[h].astype(jnp.float32)
+
+    def fill_ends(plane, carry):
         padded[plane, 0:8, :] = jnp.zeros((8, depth), jnp.float32)
         padded[plane, 8 + cells_y :, :] = jnp.zeros((8, depth), jnp.float32)
         for h in range(2):
             padded[plane, 6 + h : 7 + h, :] = ylo_ref[h, pl.ds(plane, 1), :]
             padded[plane, 8 + cells_y + h : 9 + cells_y + h, :] = yhi_ref[h, pl.ds(plane, 1), :]
-
-    for h in range(2):
-        fill(h, xlo_ref[h].astype(jnp.float32))
-        fill(cells_x + 2 + h, xhi_ref[h].astype(jnp.float32))
-
-    def fill_own(x, carry):
-        fill(x + 2, field_ref[x])
         return carry
 
-    lax.fori_loop(0, cells_x, fill_own, 0)
+    lax.fori_loop(0, cells_x + 4, fill_ends, 0)
+    for load in loads:
+        load.wait()
 
     def smooth_plane(plane, carry):
         value = operate(padded[plane], padded[plane - 1], padded[plane + 1])
@@ -367,27 +383,40 @@
 
     def out_plane(x, carry):
         prior = operate(smooth[x + 1], smooth[x], smooth[x + 2])
-        out_ref[x] = field_ref[x] - (step_rate * prior_weight) * prior[8 : 8 + cells_y]
+        change = (step_rate * prior_weight) * prior[8 : 8 + cells_y]
+        out_ref[x] = padded[x + 2, own_rows, :] - change
         return carry
 
-    lax.fori_loop(0, cells_x, out_plane, 0)
+    def store(part):
+        span = pl.ds(part * planes, planes)
+        return pltpu.make_async_copy(out_ref.at[span], out_hbm.at[span], out_sems.at[part])
+
+    for part in range(parts):
+        lax.fori_loop(part * planes, (part + 1) * planes, out_plane, 0)
+        store(part).start()
+    for part in range(parts):
+        store(part).wait()
 
 
 def finish_kernel(
-    incoming_ref, match_ref, field_hbm, base_hbm, *refs, exchanges, capacity, first_slots
+    incoming_ref, match_hbm, field_hbm, base_hbm, *refs, exchanges, capacity, first_slots
 ):
     arrived_refs, refs = refs[:exchanges], refs[exchanges:]
-    out_hbm, collected, rows_ref, field_ref, base_ref, out_ref, in_sems, out_sems = refs
+    out_hbm, collected, rows_ref, match_ref, field_ref, base_ref, out_ref, in_sems, out_sems = refs
     cells_x, cells_y, depth = field_ref.shape
     per_column = depth // LANES
     parts = out_sems.shape[0]
     planes = cells_x // parts
     blocks = cells_x * cells_y * per_column
+    matches = copies_in_parts(match_hbm, match_ref, in_sems.at[2])
     loads = copies_in_parts(field_hbm, field_ref, in_sems.at[0])
     loads += copies_in_parts(base_hbm, base_ref, in_sems.at[1])
-    for load in loads:
+    for load in matches + loads:
         load.start()
     collected_rows = collected.reshape(collected.shape[0], LANES)
+    collected_rows[...] = jnp.zeros_like(collected_rows)
+    for load in matches:
+        load.wait()
     merged = rows_ref.reshape(rows_ref.shape[0], LANES)
     start = 0
     for arrived_ref in arrived_refs:
@@ -399,7 +428,6 @@
                 preferred_element_type=jnp.float32,
             )
         start += arrived_ref.shape[0]
-    collected_rows[...] = jnp.zeros_like(collected_rows)
 
     part_starts = [0, arrived_refs[0].shape[0]]
 
@@ -464,7 +492,7 @@
     devices = lax.axis_size("gx") * lax.axis_size("gy")
     requests = blocks_dev * slots
     capacity = 2 * requests // devices
-    first_slots = min(capacity, -(-3 * capacity // (4 * GROUP)) * GROUP)
+    first_slots = 11 * capacity // 16 if capacity % LANES == 0 else capacity
     slots_of = [n for n in (first_slots, capacity - first_slots) if n > 0]
     exchanges = len(slots_of)
     all_slots = devices * capacity
@@ -548,23 +576,10 @@
     )(wanted, to_rows(log_density))
     crowded = crowded[0] != 0
 
-    incoming_late, *edges, _ = lax.optimization_barrier((incoming, *edges, served[0]))
-    slot_lists = [
-        incoming_late[:, :first_slots].reshape(-1, LANES),
-        (incoming_late[:, first_slots:] & (MARK - 1)).reshape(-1, LANES),
-    ][:exchanges]
-    match = pl.pallas_call(
-        match_kernel,
-        out_shape=shape((all_slots, LANES), bf16),
-        in_specs=[VMEM],
-        out_specs=VMEM,
-        compiler_params=pltpu.CompilerParams(vmem_limit_bytes=8 * MIB),
-        cost_estimate=pl.CostEstimate(flops=10**9, bytes_accessed=MIB, transcendentals=0),
-        name="match",
-    )(jnp.concatenate(slot_lists, axis=0))
     returned = exchange_rows(served, crowded)
+    *edges, _ = lax.optimization_barrier((*edges, served[0]))
     xlo, xhi, ylo, yhi = halo(*edges)
-    *returned, match, ylo, yhi = lax.optimization_barrier((*returned, match, ylo, yhi))
+    *returned, ylo, yhi = lax.optimization_barrier((*returned, ylo, yhi))
 
     chunks = blocks_dev * stars // LANES
     in_set = chunks // 4
@@ -597,38 +612,55 @@
     )
     arrived = exchange_rows(parcel, crowded)
 
-    field_late, _ = lax.optimization_barrier((log_density, parcel[0]))
+    field_late, incoming_late, _ = lax.optimization_barrier((log_density, incoming, parcel[0]))
+    slot_lists = [
+        incoming_late[:, :first_slots].reshape(-1, LANES),
+        (incoming_late[:, first_slots:] & (MARK - 1)).reshape(-1, LANES),
+    ][:exchanges]
+    match = pl.pallas_call(
+        match_kernel,
+        out_shape=shape((all_slots, LANES), bf16),
+        in_specs=[VMEM],
+        out_specs=VMEM,
+        compiler_params=pltpu.CompilerParams(vmem_limit_bytes=8 * MIB),
+        cost_estimate=pl.CostEstimate(flops=10**9, bytes_accessed=MIB, transcendentals=0),
+        name="match",
+    )(jnp.concatenate(slot_lists, axis=0))
+    parts = 8
     base = pl.pallas_call(
         prior_kernel,
         out_shape=shape(field_shape, f32),
-        in_specs=[VMEM] * 5,
-        out_specs=VMEM,
+        in_specs=[ANY] + [VMEM] * 4,
+        out_specs=ANY,
         scratch_shapes=[
             pltpu.VMEM((cells_x + 4, cells_y + 16, depth), f32),
             pltpu.VMEM((cells_x + 2, cells_y + 16, depth), f32),
+            pltpu.VMEM(field_shape, f32),
+            pltpu.SemaphoreType.DMA((parts,)),
+            pltpu.SemaphoreType.DMA((parts,)),
         ],
-        compiler_params=pltpu.CompilerParams(vmem_limit_bytes=32 * MIB),
+        compiler_params=pltpu.CompilerParams(vmem_limit_bytes=56 * MIB),
         cost_estimate=pl.CostEstimate(
             flops=30 * cells, bytes_accessed=8 * cells, transcendentals=0
         ),
         name="prior",
     )(field_late, xlo, xhi, ylo, yhi)
 
-    parts = 8
     new_log_density = pl.pallas_call(
         functools.partial(
             finish_kernel, exchanges=exchanges, capacity=capacity, first_slots=first_slots
         ),
         out_shape=shape(field_shape, f32),
-        in_specs=[SMEM, VMEM, ANY, ANY] + [VMEM] * exchanges,
+        in_specs=[SMEM, ANY, ANY, ANY] + [VMEM] * exchanges,
         out_specs=ANY,
         scratch_shapes=[
             pltpu.VMEM((blocks + capacity, 1, width), f32),
             pltpu.VMEM((all_slots, 1, width), f32),
+            pltpu.VMEM((all_slots, LANES), bf16),
             pltpu.VMEM(field_shape, f32),
             pltpu.VMEM(field_shape, f32),
             pltpu.VMEM(field_shape, f32),
-            pltpu.SemaphoreType.DMA((2, parts)),
+            pltpu.SemaphoreType.DMA((3, parts)),
             pltpu.SemaphoreType.DMA((parts,)),
         ],
         compiler_params=pltpu.CompilerParams(vmem_limit_bytes=50 * MIB),

time: 98.1 us -> 97.5 us (level)
  Pallas kernels: 46.5 us -> 51.2 us
  waiting for transfers between devices: 14.9 us -> 11 us
  local copies, waits for them, and re-layouts: 7.35 us -> 3.81 us
  starting transfers between devices: 26.1 us -> 27.8 us
    all_to_all x3, waiting for transfers between devices: 11.5 us -> 5.66 us  [exchange(): return lax.all_to_all(x, mesh_axes, split_axis=0, concat_axis=0, tiled=True)]
    unnamed x26 -> x22, local copies, waits for them, and re-layouts: 5.55 us -> 1.42 us
    pallas_call x1, Pallas kernels: 10.7 us -> 14.5 us  [on_device(): pl.pallas_call(prior_kernel, out_shape=shape(field_shape, f32), in_specs=...]
    ppermute x4, waiting for transfers between devices: 3.44 us -> 5.34 us  [both_ways(): return (lax.ppermute(last, axis, up), lax.ppermute(first, axis, down))]
    all_to_all x3, starting transfers between devices: 15.2 us -> 16.6 us  [exchange(): return lax.all_to_all(x, mesh_axes, split_axis=0, concat_axis=0, tiled=True)]
    convert_element_type x2, other arithmetic: 0.03 us -> 1.36 us  [halo(): return (xlo, xhi, ylo.astype(jnp.float32), yhi.astype(jnp.float32))]
    ppermute x2, local copies, waits for them, and re-layouts: 0.03 us -> 1.33 us  [both_ways(): return (lax.ppermute(last, axis, up), lax.ppermute(first, axis, down))]
    pallas_call x1, Pallas kernels: 8.9 us -> 9.96 us  [on_device(): pl.pallas_call(functools.partial(finish_kernel, exchanges=exchanges, capa...]
  transfers between devices with their start and end apart: 7 -> 7, of which waited for: 4 -> 6; matrix products, arithmetic and copies ran while one was open for 4% -> 5% of each run, Pallas kernels for 15% -> 19%
where the time goes in v11:
time: 97.5 us; the launch traced here: 96.9 us
  Pallas kernels  51.2 us (53%)
  starting transfers between devices  27.8 us (29%)
  waiting for transfers between devices  11 us (11%)
  local copies, waits for them, and re-layouts  3.81 us (4%)
  other arithmetic  1.54 us (2%)
  between operations  1.49 us (2%)
    all_to_all x3, starting transfers between devices, exchange(): return lax.all_to_all(x, mesh_axes, split_axis=0, concat_axis=0, tiled=True)  16.6 us
    pallas_call x1, Pallas kernels, on_device(): pl.pallas_call(prior_kernel, out_shape=shape(field_shape, f32), in_specs=...  14.5 us
    pallas_call x1, Pallas kernels, on_device(): pl.pallas_call(functools.partial(star_kernel, exchanges=exchanges), out_s...  12.4 us
    ppermute x4, starting transfers between devices, both_ways(): return (lax.ppermute(last, axis, up), lax.ppermute(first, axis, down))  11.2 us
    pallas_call x1, Pallas kernels, on_device(): pl.pallas_call(functools.partial(finish_kernel, exchanges=exchanges, capa...  9.96 us
    pallas_call x1, Pallas kernels, on_device(): pl.pallas_call(functools.partial(serve_kernel, capacity=capacity, first_s...  7.27 us
    all_to_all x3, waiting for transfers between devices, exchange(): return lax.all_to_all(x, mesh_axes, split_axis=0, concat_axis=0, tiled=True)  5.66 us
    ppermute x4, waiting for transfers between devices, both_ways(): return (lax.ppermute(last, axis, up), lax.ppermute(first, axis, down))  5.34 us
  transfers between devices with their start and end apart: 7, of which 6 were waited for; matrix products, arithmetic and copies ran while one was open for 5% of the time, Pallas kernels for 19%

profile of v11, /device:TPU:1, one launch (start us, length us, event | category | flops | bytes accessed | tf_op | source)
XLA Modules:
  0.0 96.9 jit_solution(11586965885807649484)
XLA Ops:
  0.6 3.1 %route.1 = (s32[32,128]{1,0:T(8,128)}, s32[16,128]{1,0:T(8,128)}) custom-call(s32[32,64]{1,0:T(8,128)} %bitcast.45), custom_call_target="tpu_custom_call" | custom-call | tf_op jit(solution)/shard_map/route/pallas_call | solution.py:522
  3.7 7.1 %all-to-all-start.2 = ((s32[32,1,128]{2,1,0:T(1,128)}), s32[32,1,128]{2,1,0:T(1,128)S(1)}, u32[]{:S(2)}, u32[]{:S(2)}) async-start(s32[32,1,128]{2,1,0:T(1,128)} %bitcast.46), calls=%async_computation.2 | async-start | bytes 32768 | tf_op jit(solution)/shard_map/all_to_all | solution.py:512
  10.8 2.3 %edges.1 = (bf16[2,64,512]{2,1,0:T(8,128)(2,1)}, bf16[2,64,512]{2,1,0:T(8,128)(2,1)}, f32[2,32,512]{2,1,0:T(8,128)}, f32[2,32,512]{2,1,0:T(8,128)}) custom-call(f32[32,64,512]{2,1,0:T(8,128)} %field_hbm.3), custom_call_target="tpu_custom_call" | custom-call | bytes 2097152 | tf_op jit(solution)/shard_map/edges/pallas_call | solution.py:539
  13.2 4.3 %all-to-all-done.2 = s32[32,1,128]{2,1,0:T(1,128)S(1)} async-done(((s32[32,1,128]{2,1,0:T(1,128)}), s32[32,1,128]{2,1,0:T(1,128)S(1)}, u32[]{:S(2)}, u32[]{:S(2)}) %all-to-all-start.2) | async-done | bytes 16416 | tf_op jit(solution)/shard_map/all_to_all | solution.py:512
  17.4 0.6 copy-done
  18.0 7.3 %serve.1 = (bf16[2816,128]{1,0:T(8,128)(2,1)}, bf16[1280,128]{1,0:T(8,128)(2,1)S(1)}, s32[1]{0:T(128)}) custom-call(s32[4096]{0:T(1024)} %bitcast.32, f32[8192,1,128]{2,1,0:T(1,128)} %bitcast.36), custom_call_target="tpu_custom_call" | custom-call | flops 1048576 | bytes 6291456 | tf_op jit(solution)/shard_map/serve/pallas_call | solution.py:561
  25.9 2.9 %all-to-all-start.3 = ((bf16[32,88,128]{2,1,0:T(8,128)(2,1)}), bf16[32,88,128]{2,1,0:T(8,128)(2,1)S(1)}, u32[]{:S(2)}, u32[]{:S(2)}) async-start(bf16[32,88,128]{2,1,0:T(8,128)(2,1)} %bitcast.43), calls=%async_computation.3 | async-start | bytes 1441792 | tf_op jit(solution)/shard_map/all_to_all | solution.py:512
  28.8 0.1 copy.27
  29.0 3.5 %collective-permute-start = (bf16[2,64,512]{2,0,1:T(2,128)(2,1)S(1)}, bf16[2,64,512]{2,0,1:T(2,128)(2,1)S(1)}, u32[]{:S(2)}, u32[]{:S(2)}) collective-permute-start(bf16[2,64,512]{2,0,1:T(2,128)(2,1)S(1)} %copy.27), channel_id=1, source_target_pairs={{0,4},{4,8},{8,12},{12,16},{16,20},{20,24},{24,28},{1,5},{5,9},{9,... | collective-permute-start | bytes 393224 | tf_op jit(solution)/shard_map/ppermute | solution.py:470
  32.5 0.1 copy.28
  32.7 1.9 %collective-permute-start.1 = (bf16[2,64,512]{2,0,1:T(2,128)(2,1)S(1)}, bf16[2,64,512]{2,0,1:T(2,128)(2,1)S(1)}, u32[]{:S(2)}, u32[]{:S(2)}) collective-permute-start(bf16[2,64,512]{2,0,1:T(2,128)(2,1)S(1)} %copy.28), channel_id=1, source_target_pairs={{4,0},{8,4},{12,8},{16,12},{20,16},{24,20},{28,24},{5,1},{9,5},{13... | collective-permute-start | bytes 393224 | tf_op jit(solution)/shard_map/ppermute | solution.py:470
  34.7 0.8 collective-permute-done
  35.5 4.3 %collective-permute-done.1 = bf16[2,64,512]{2,0,1:T(2,128)(2,1)S(1)} collective-permute-done((bf16[2,64,512]{2,0,1:T(2,128)(2,1)S(1)}, bf16[2,64,512]{2,0,1:T(2,128)(2,1)S(1)}, u32[]{:S(2)}, u32[]{:S(2)}) %collective-permute-start.1) | collective-permute-done | bytes 131104 | tf_op jit(solution)/shard_map/ppermute | solution.py:470
  39.9 1.3 %collective-permute-start.3 = (bf16[2,36,512]{2,1,0:T(8,128)(2,1)S(1)}, bf16[2,36,512]{2,1,0:T(8,128)(2,1)S(1)}, u32[]{:S(2)}, u32[]{:S(2)}) collective-permute-start(bf16[2,36,512]{2,1,0:T(8,128)(2,1)S(1)} %pad_maximum_fusion.1), channel_id=1, source_target_pairs={{1,0},{2,1},{3,2},{5,4},{6,5},{7,6},{9,8},{10,9},{11,10},{13,12},{... | collective-permute-start | bytes 221192 | tf_op jit(solution)/shard_map/ppermute | solution.py:470
  41.2 4.4 %collective-permute-start.2 = (bf16[2,36,512]{2,1,0:T(8,128)(2,1)S(1)}, bf16[2,36,512]{2,1,0:T(8,128)(2,1)S(1)}, u32[]{:S(2)}, u32[]{:S(2)}) collective-permute-start(bf16[2,36,512]{2,1,0:T(8,128)(2,1)S(1)} %pad_maximum_fusion), channel_id=1, source_target_pairs={{0,1},{1,2},{2,3},{4,5},{5,6},{6,7},{8,9},{9,10},{10,11},{12,13},{... | collective-permute-start | bytes 221192 | tf_op jit(solution)/shard_map/ppermute | solution.py:470
  45.7 0.1 copy.24
  45.8 0.1 reshape.85.position_ref
  46.1 0.1 copy.25
  46.3 0.2 collective-permute-done.3
  46.5 0.7 convert_element_type.24.yhi_ref
  47.2 0.7 convert_element_type.22.ylo_ref
  47.9 0.6 all-to-all-done.3
  48.4 12.4 %stars.1 = (f32[16,128]{1,0:T(8,128)S(1)}, bf16[2816,128]{1,0:T(8,128)(2,1)}, bf16[1280,128]{1,0:T(8,128)(2,1)S(1)}) custom-call(s32[2048]{0:T(1024)S(1)} %reshape.85.position_ref, f32[16,128]{1,0:T(8,128)S(1)} %reshape.86.observed_ref, f32[16,128]{1,0:T(8,128)S(1)} %reshape.87.inverse_ref, bf16[64,32,32,128]{3,2,1,0:T(8,128)(2,1)} %weights_hbm.1, ...), custom_call_target="tpu_custom_call" | custom-call | flops 33554432 | bytes 16777216 | tf_op jit(solution)/shard_map/stars/pallas_call | solution.py:588
  60.9 6.6 %all-to-all-start.4 = ((bf16[32,88,128]{2,1,0:T(8,128)(2,1)}), bf16[32,88,128]{2,1,0:T(8,128)(2,1)S(1)}, u32[]{:S(2)}, u32[]{:S(2)}) async-start(bf16[32,88,128]{2,1,0:T(8,128)(2,1)} %bitcast.18), calls=%async_computation.4 | async-start | bytes 1441792 | tf_op jit(solution)/shard_map/all_to_all | solution.py:512
  67.5 0.7 copy.29.xlo_ref
  68.2 0.7 copy.30.xhi_ref
  68.9 0.1 reshape.95
  69.2 0.7 copy.31
  69.8 14.5 %prior.1.base_hbm = f32[32,64,512]{2,1,0:T(8,128)} custom-call(f32[32,64,512]{2,1,0:T(8,128)} %field_hbm.3, bf16[2,64,512]{2,1,0:T(8,128)(2,1)} %copy.29.xlo_ref, bf16[2,64,512]{2,1,0:T(8,128)(2,1)} %copy.30.xhi_ref, f32[2,36,512]{2,1,0:T(8,128)} %convert_element_type.22.ylo_ref, f32[2,36,512]{2,1,0:T(8,128)} %convert_element_type.24.yhi_ref), custom_call_target="tpu_custom_call" | custom-call | flops 31457280 | bytes 8388608 | tf_op jit(solution)/shard_map/prior/pallas_call | solution.py:630
  84.3 1.8 %match.1.match_hbm = bf16[4096,128]{1,0:T(8,128)(2,1)S(1)} custom-call(s32[32,128]{1,0:T(8,128)S(1)} %pad_add_fusion.incoming_ref), custom_call_target="tpu_custom_call" | custom-call | flops 1000000000 | bytes 1048576 | tf_op jit(solution)/shard_map/match/pallas_call | solution.py:620
  86.1 0.8 all-to-all-done.4
  86.9 10.0 %finish.1 = f32[32,64,512]{2,1,0:T(8,128)} custom-call(s32[4096]{0:T(1024)S(1)} %bitcast.35, bf16[4096,128]{1,0:T(8,128)(2,1)S(1)} %match.1.match_hbm, f32[32,64,512]{2,1,0:T(8,128)} %field_hbm.3, f32[32,64,512]{2,1,0:T(8,128)} %prior.1.base_hbm, bf16[2816,128]{1,0:T(8,128)(2,1)S(1)} %bitcast.31, bf16[1280,128]{1,0:T(8,128)(2,1)S(1)} %bitcast.39), custom_call_target="tpu_custom_call" | custom-call | flops 4194304 | bytes 12582912 | tf_op jit(solution)/shard_map/finish/pallas_call | solution.py:649
  (37 shorter events, 0.7 us)
Async XLA Ops:
  3.7 13.7 %all-to-all-start.2 = ((s32[32,1,128]{2,1,0:T(1,128)}), s32[32,1,128]{2,1,0:T(1,128)S(1)}, u32[]{:S(2)}, u32[]{:S(2)}) async-start(s32[32,1,128]{2,1,0:T(1,128)} %bitcast.46), calls=%async_computation.2 | async-start | bytes 32768 | tf_op jit(solution)/shard_map/all_to_all | solution.py:512
  13.1 15.7 %copy-start.5 = (bf16[2,64,512]{2,1,0:T(8,128)(2,1)S(1)}, bf16[2,64,512]{2,1,0:T(8,128)(2,1)}, u32[]{:S(2)}) copy-start(bf16[2,64,512]{2,1,0:T(8,128)(2,1)} %get-tuple-element.67) | copy-start | bytes 393220
  13.1 19.4 %copy-start.4 = (bf16[2,64,512]{2,1,0:T(8,128)(2,1)S(1)}, bf16[2,64,512]{2,1,0:T(8,128)(2,1)}, u32[]{:S(2)}) copy-start(bf16[2,64,512]{2,1,0:T(8,128)(2,1)} %get-tuple-element.69) | copy-start | bytes 393220
  13.1 21.5 %copy-start.3 = (f32[2,32,512]{2,1,0:T(8,128)S(1)}, f32[2,32,512]{2,1,0:T(8,128)}, u32[]{:S(2)}) copy-start(f32[2,32,512]{2,1,0:T(8,128)} %get-tuple-element.70) | copy-start | bytes 393220
  13.1 21.5 %copy-start.2 = (f32[2,32,512]{2,1,0:T(8,128)S(1)}, f32[2,32,512]{2,1,0:T(8,128)}, u32[]{:S(2)}) copy-start(f32[2,32,512]{2,1,0:T(8,128)} %get-tuple-element.68) | copy-start | bytes 393220
  13.1 32.5 %copy-start.7 = (f32[64,32]{0,1:T(8,128)S(1)}, f32[64,32]{0,1:T(8,128)}, u32[]{:S(2)}) copy-start(f32[64,32]{0,1:T(8,128)} %param.13) | copy-start | bytes 24580
  13.1 32.5 %copy-start.9 = (s32[64]{0:T(128)S(1)}, s32[64]{0:T(128)}, u32[]{:S(2)}) copy-start(s32[64]{0:T(128)} %param.14) | copy-start | bytes 772
  13.2 32.5 %copy-start.8 = (s32[16,128]{1,0:T(8,128)S(1)}, s32[16,128]{1,0:T(8,128)}, u32[]{:S(2)}) copy-start(s32[16,128]{1,0:T(8,128)} %get-tuple-element.59) | copy-start | bytes 24580
  17.4 0.6 copy-start
  18.0 28.1 %copy-start.6 = (f32[64,32]{0,1:T(8,128)S(1)}, f32[64,32]{0,1:T(8,128)}, u32[]{:S(2)}) copy-start(f32[64,32]{0,1:T(8,128)} %param.12) | copy-start | bytes 24580
  25.9 22.5 %all-to-all-start.3 = ((bf16[32,88,128]{2,1,0:T(8,128)(2,1)}), bf16[32,88,128]{2,1,0:T(8,128)(2,1)S(1)}, u32[]{:S(2)}, u32[]{:S(2)}) async-start(bf16[32,88,128]{2,1,0:T(8,128)(2,1)} %bitcast.43), calls=%async_computation.3 | async-start | bytes 1441792 | tf_op jit(solution)/shard_map/all_to_all | solution.py:512
  29.0 6.5 %collective-permute-start = (bf16[2,64,512]{2,0,1:T(2,128)(2,1)S(1)}, bf16[2,64,512]{2,0,1:T(2,128)(2,1)S(1)}, u32[]{:S(2)}, u32[]{:S(2)}) collective-permute-start(bf16[2,64,512]{2,0,1:T(2,128)(2,1)S(1)} %copy.27), channel_id=1, source_target_pairs={{0,4},{4,8},{8,12},{12,16},{16,20},{20,24},{24,28},{1,5},{5,9},{9,... | collective-permute-start | bytes 393224 | tf_op jit(solution)/shard_map/ppermute | solution.py:470
  32.7 7.1 %collective-permute-start.1 = (bf16[2,64,512]{2,0,1:T(2,128)(2,1)S(1)}, bf16[2,64,512]{2,0,1:T(2,128)(2,1)S(1)}, u32[]{:S(2)}, u32[]{:S(2)}) collective-permute-start(bf16[2,64,512]{2,0,1:T(2,128)(2,1)S(1)} %copy.28), channel_id=1, source_target_pairs={{4,0},{8,4},{12,8},{16,12},{20,16},{24,20},{28,24},{5,1},{9,5},{13... | collective-permute-start | bytes 393224 | tf_op jit(solution)/shard_map/ppermute | solution.py:470
  39.9 6.6 %collective-permute-start.3 = (bf16[2,36,512]{2,1,0:T(8,128)(2,1)S(1)}, bf16[2,36,512]{2,1,0:T(8,128)(2,1)S(1)}, u32[]{:S(2)}, u32[]{:S(2)}) collective-permute-start(bf16[2,36,512]{2,1,0:T(8,128)(2,1)S(1)} %pad_maximum_fusion.1), channel_id=1, source_target_pairs={{1,0},{2,1},{3,2},{5,4},{6,5},{7,6},{9,8},{10,9},{11,10},{13,12},{... | collective-permute-start | bytes 221192 | tf_op jit(solution)/shard_map/ppermute | solution.py:470
  41.2 6.0 %collective-permute-start.2 = (bf16[2,36,512]{2,1,0:T(8,128)(2,1)S(1)}, bf16[2,36,512]{2,1,0:T(8,128)(2,1)S(1)}, u32[]{:S(2)}, u32[]{:S(2)}) collective-permute-start(bf16[2,36,512]{2,1,0:T(8,128)(2,1)S(1)} %pad_maximum_fusion), channel_id=1, source_target_pairs={{0,1},{1,2},{2,3},{4,5},{5,6},{6,7},{8,9},{9,10},{10,11},{12,13},{... | collective-permute-start | bytes 221192 | tf_op jit(solution)/shard_map/ppermute | solution.py:470
  48.4 20.4 %copy-start.1 = (s32[32,1,128]{2,1,0:T(1,128)S(1)}, s32[32,1,128]{2,1,0:T(1,128)}, u32[]{:S(2)}) copy-start(s32[32,1,128]{2,1,0:T(1,128)} %copy-done) | copy-start | bytes 49156
  60.9 26.1 %all-to-all-start.4 = ((bf16[32,88,128]{2,1,0:T(8,128)(2,1)}), bf16[32,88,128]{2,1,0:T(8,128)(2,1)S(1)}, u32[]{:S(2)}, u32[]{:S(2)}) async-start(bf16[32,88,128]{2,1,0:T(8,128)(2,1)} %bitcast.18), calls=%async_computation.4 | async-start | bytes 1441792 | tf_op jit(solution)/shard_map/all_to_all | solution.py:512

commit v12 on v11

--- a/solution.py
+++ b/solution.py
@@ -99,8 +99,26 @@
     xlast_ref[...] = planes_ref[1].astype(xlast_ref.dtype)
     for h in range(2):
         for x in range(cells_x):
-            yfirst_ref[h, x : x + 1, :] = strips_ref[0, x, h : h + 1, :]
-            ylast_ref[h, x : x + 1, :] = strips_ref[1, x, 6 + h : 7 + h, :]
+            yfirst_ref[h, x + 2 : x + 3, :] = strips_ref[0, x, h : h + 1, :]
+            ylast_ref[h, x + 2 : x + 3, :] = strips_ref[1, x, 6 + h : 7 + h, :]
+
+
+def ends_kernel(
+    xlo_ref, xhi_ref, yfirst_ref, ylast_ref, first_ref, last_ref, slab_ref
+):
+    cells_y = xlo_ref.shape[1]
+    length = yfirst_ref.shape[1]
+    for own_ref, out_ref, start, row in (
+        (yfirst_ref, first_ref, 0, 0),
+        (ylast_ref, last_ref, cells_y - 16, 14),
+    ):
+        slab_ref[...] = own_ref[...]
+        for e in range(2):
+            for x_ref, at in ((xlo_ref, e), (xhi_ref, length - 2 + e)):
+                block = x_ref[e, start : start + 16, :].astype(jnp.float32)
+                for h in range(2):
+                    slab_ref[h, at : at + 1, :] = block[row + h : row + h + 1, :]
+        out_ref[...] = slab_ref[...].astype(out_ref.dtype)
 
 
 def copies_in_parts(source, target, sems):
@@ -129,10 +147,10 @@
 
         def one_group(group, carry):
             slot = group * GROUP
-            for source in own:
+            for which, source in enumerate(own):
                 listed = incoming_ref.at[pl.ds(source * capacity + slot, GROUP)]
                 wanted = [listed[j] for j in range(GROUP)]
-                visit(wanted, pl.multiple_of(source * first_slots + slot, GROUP), 0)
+                visit(wanted, pl.multiple_of(source * first_slots + slot, GROUP), 0, which)
             return carry
 
         return lax.fori_loop(0, jnp.minimum(most, first_slots // GROUP), one_group, carry)
@@ -146,7 +164,7 @@
             slot = group * GROUP
             listed = incoming_ref.at[pl.ds(source * capacity + slot, GROUP)]
             wanted = [listed[j] & (MARK - 1) for j in range(GROUP)]
-            visit(wanted, pl.multiple_of(source * last_slots + slot - first_slots, GROUP), 1)
+            visit(wanted, pl.multiple_of(source * last_slots + slot - first_slots, GROUP), 1, 0)
             return carry
 
         return lax.fori_loop(first_slots // GROUP, groups_of(source), one_group, carry)
@@ -172,7 +190,7 @@
 
     part_starts = [0, served_refs[0].shape[0]]
 
-    def visit(wanted, row, list_part):
+    def visit(wanted, row, list_part, which):
         rows = [rows_ref[at] for at in wanted]
         found = found_ref.at[pl.ds(row + part_starts[list_part], GROUP)]
         for j in range(GROUP):
@@ -327,7 +345,8 @@
 
 
 def prior_kernel(
-    field_hbm, xlo_ref, xhi_ref, ylo_ref, yhi_ref, out_hbm, padded, smooth, out_ref, sems, out_sems
+    field_hbm, xlo_ref, xhi_ref, ylo_ref, yhi_ref, out_hbm,
+    padded, smooth, out_ref, yends_ref, sems, out_sems,
 ):
     cells_x, cells_y, depth = field_hbm.shape
     rows = padded.shape[1]
@@ -361,17 +380,18 @@
         padded[h, own_rows, :] = xlo_ref[h].astype(jnp.float32)
         padded[cells_x + 2 + h, own_rows, :] = xhi_ref[h].astype(jnp.float32)
 
+    yends_ref[0] = ylo_ref[...].astype(jnp.float32)
+    yends_ref[1] = yhi_ref[...].astype(jnp.float32)
+
     def fill_ends(plane, carry):
         padded[plane, 0:8, :] = jnp.zeros((8, depth), jnp.float32)
         padded[plane, 8 + cells_y :, :] = jnp.zeros((8, depth), jnp.float32)
         for h in range(2):
-            padded[plane, 6 + h : 7 + h, :] = ylo_ref[h, pl.ds(plane, 1), :]
-            padded[plane, 8 + cells_y + h : 9 + cells_y + h, :] = yhi_ref[h, pl.ds(plane, 1), :]
+            padded[plane, 6 + h : 7 + h, :] = yends_ref[0, h, pl.ds(plane, 1), :]
+            padded[plane, 8 + cells_y + h : 9 + cells_y + h, :] = yends_ref[1, h, pl.ds(plane, 1), :]
         return carry
 
     lax.fori_loop(0, cells_x + 4, fill_ends, 0)
-    for load in loads:
-        load.wait()
 
     def smooth_plane(plane, carry):
         value = operate(padded[plane], padded[plane - 1], padded[plane + 1])
@@ -379,8 +399,6 @@
         smooth[plane - 1] = jnp.where(inside_y & inside, value, 0.0)
         return carry
 
-    lax.fori_loop(1, cells_x + 3, smooth_plane, 0)
-
     def out_plane(x, carry):
         prior = operate(smooth[x + 1], smooth[x], smooth[x + 2])
         change = (step_rate * prior_weight) * prior[8 : 8 + cells_y]
@@ -391,9 +409,17 @@
         span = pl.ds(part * planes, planes)
         return pltpu.make_async_copy(out_ref.at[span], out_hbm.at[span], out_sems.at[part])
 
+    smoothed, done = 1, 0
     for part in range(parts):
-        lax.fori_loop(part * planes, (part + 1) * planes, out_plane, 0)
-        store(part).start()
+        loads[part].wait()
+        ready = cells_x + 3 if part + 1 == parts else 1 + (part + 1) * planes
+        lax.fori_loop(smoothed, ready, smooth_plane, 0)
+        smoothed = ready
+        lax.fori_loop(done, ready - 3, out_plane, 0)
+        done = ready - 3
+        for whole in range(parts):
+            if part * planes - 2 < (whole + 1) * planes <= done:
+                store(whole).start()
     for part in range(parts):
         store(part).wait()
 
@@ -402,7 +428,7 @@
     incoming_ref, match_hbm, field_hbm, base_hbm, *refs, exchanges, capacity, first_slots
 ):
     arrived_refs, refs = refs[:exchanges], refs[exchanges:]
-    out_hbm, collected, rows_ref, match_ref, field_ref, base_ref, out_ref, in_sems, out_sems = refs
+    out_hbm, *collected, rows_ref, match_ref, field_ref, base_ref, out_ref, in_sems, out_sems = refs
     cells_x, cells_y, depth = field_ref.shape
     per_column = depth // LANES
     parts = out_sems.shape[0]
@@ -413,8 +439,9 @@
     loads += copies_in_parts(base_hbm, base_ref, in_sems.at[1])
     for load in matches + loads:
         load.start()
-    collected_rows = collected.reshape(collected.shape[0], LANES)
-    collected_rows[...] = jnp.zeros_like(collected_rows)
+    collected_rows = [ref.reshape(ref.shape[0], LANES) for ref in collected]
+    for ref in collected_rows:
+        ref[...] = jnp.zeros_like(ref)
     for load in matches:
         load.wait()
     merged = rows_ref.reshape(rows_ref.shape[0], LANES)
@@ -431,12 +458,13 @@
 
     part_starts = [0, arrived_refs[0].shape[0]]
 
-    def visit(wanted, row, list_part):
+    def visit(wanted, row, list_part, which):
         row = pl.multiple_of(row + part_starts[list_part], GROUP)
         rows = rows_ref.at[pl.ds(row, GROUP)]
-        sums = [collected[wanted[j]] + rows[j] for j in range(GROUP)]
+        into = collected[which % len(collected)]
+        sums = [into[wanted[j]] + rows[j] for j in range(GROUP)]
         for j in range(GROUP):
-            collected[wanted[j]] = sums[j]
+            into[wanted[j]] = sums[j]
 
     for_each_group(incoming_ref, visit, capacity, first_slots, blocks)
     for load in loads:
@@ -451,9 +479,8 @@
             for part in range(per_column):
                 at = pl.multiple_of(((x * (cells_y // 8) + yb) * per_column + part) * 8, 8)
                 here = (x, slice(8 * yb, 8 * yb + 8), slice(part * LANES, (part + 1) * LANES))
-                out_ref[here] = base_ref[here] + collected_rows[pl.ds(at, 8), :] * jnp.exp(
-                    field_ref[here]
-                )
+                grad = collected_rows[0][pl.ds(at, 8), :] + collected_rows[1][pl.ds(at, 8), :]
+                out_ref[here] = base_ref[here] + grad * jnp.exp(field_ref[here])
         return carry
 
     for part in range(parts):
@@ -468,17 +495,6 @@
     up = [(i, i + 1) for i in range(peers - 1)]
     down = [(j, i) for i, j in up]
     return lax.ppermute(last, axis, up), lax.ppermute(first, axis, down)
-
-
-def halo(xfirst, xlast, yfirst, ylast):
-    xlo, xhi = both_ways(xfirst, xlast, "gx")
-
-    def rows(own, at):
-        ends = [x[:, at].transpose(1, 0, 2) for x in (xlo, xhi)]
-        return jnp.concatenate([ends[0], own.astype(xlo.dtype), ends[1]], axis=1)
-
-    ylo, yhi = both_ways(rows(yfirst, slice(0, 2)), rows(ylast, slice(-2, None)), "gy")
-    return xlo, xhi, ylo.astype(jnp.float32), yhi.astype(jnp.float32)
 
 
 VMEM = pl.BlockSpec(memory_space=pltpu.VMEM)
@@ -541,8 +557,8 @@
         out_shape=[
             shape((2, cells_y, depth), bf16),
             shape((2, cells_y, depth), bf16),
-            shape((2, cells_x, depth), f32),
-            shape((2, cells_x, depth), f32),
+            shape((2, cells_x + 4, depth), f32),
+            shape((2, cells_x + 4, depth), f32),
         ],
         in_specs=[ANY],
         out_specs=[VMEM] * 4,
@@ -555,7 +571,8 @@
         cost_estimate=pl.CostEstimate(flops=0, bytes_accessed=2 * MIB, transcendentals=0),
         name="edges",
     )(field)
-    incoming, *edges = lax.optimization_barrier((incoming, xfirst, xlast, yfirst, ylast))
+    xlo, xhi = both_ways(xfirst, xlast, "gx")
+    incoming, *edges = lax.optimization_barrier((incoming, xlo, xhi, yfirst, ylast))
     wanted = incoming.reshape(-1)
 
     *served, crowded = pl.pallas_call(
@@ -577,9 +594,33 @@
     crowded = crowded[0] != 0
 
     returned = exchange_rows(served, crowded)
-    *edges, _ = lax.optimization_barrier((*edges, served[0]))
-    xlo, xhi, ylo, yhi = halo(*edges)
-    *returned, ylo, yhi = lax.optimization_barrier((*returned, ylo, yhi))
+    *edges, incoming_late, _ = lax.optimization_barrier((*edges, incoming, served[0]))
+    slabs = pl.pallas_call(
+        ends_kernel,
+        out_shape=[shape((2, cells_x + 4, depth), bf16)] * 2,
+        in_specs=[VMEM] * 4,
+        out_specs=[VMEM] * 2,
+        scratch_shapes=[pltpu.VMEM((2, cells_x + 4, depth), f32)],
+        compiler_params=pltpu.CompilerParams(vmem_limit_bytes=8 * MIB),
+        cost_estimate=pl.CostEstimate(flops=0, bytes_accessed=MIB, transcendentals=0),
+        name="ends",
+    )(*edges)
+    ylo, yhi = both_ways(*slabs, "gy")
+    xlo, xhi, *_ = edges
+    slot_lists = [
+        incoming_late[:, :first_slots].reshape(-1, LANES),
+        (incoming_late[:, first_slots:] & (MARK - 1)).reshape(-1, LANES),
+    ][:exchanges]
+    match = pl.pallas_call(
+        match_kernel,
+        out_shape=shape((all_slots, LANES), bf16),
+        in_specs=[VMEM],
+        out_specs=VMEM,
+        compiler_params=pltpu.CompilerParams(vmem_limit_bytes=8 * MIB),
+        cost_estimate=pl.CostEstimate(flops=10**9, bytes_accessed=MIB, transcendentals=0),
+        name="match",
+    )(jnp.concatenate(slot_lists, axis=0))
+    *returned, match, ylo, yhi = lax.optimization_barrier((*returned, match, ylo, yhi))
 
     chunks = blocks_dev * stars // LANES
     in_set = chunks // 4
@@ -612,20 +653,7 @@
     )
     arrived = exchange_rows(parcel, crowded)
 
-    field_late, incoming_late, _ = lax.optimization_barrier((log_density, incoming, parcel[0]))
-    slot_lists = [
-        incoming_late[:, :first_slots].reshape(-1, LANES),
-        (incoming_late[:, first_slots:] & (MARK - 1)).reshape(-1, LANES),
-    ][:exchanges]
-    match = pl.pallas_call(
-        match_kernel,
-        out_shape=shape((all_slots, LANES), bf16),
-        in_specs=[VMEM],
-        out_specs=VMEM,
-        compiler_params=pltpu.CompilerParams(vmem_limit_bytes=8 * MIB),
-        cost_estimate=pl.CostEstimate(flops=10**9, bytes_accessed=MIB, transcendentals=0),
-        name="match",
-    )(jnp.concatenate(slot_lists, axis=0))
+    field_late, _ = lax.optimization_barrier((log_density, parcel[0]))
     parts = 8
     base = pl.pallas_call(
         prior_kernel,
@@ -636,6 +664,7 @@
             pltpu.VMEM((cells_x + 4, cells_y + 16, depth), f32),
             pltpu.VMEM((cells_x + 2, cells_y + 16, depth), f32),
             pltpu.VMEM(field_shape, f32),
+            pltpu.VMEM((2, 2, cells_x + 4, depth), f32),
             pltpu.SemaphoreType.DMA((parts,)),
             pltpu.SemaphoreType.DMA((parts,)),
         ],
@@ -654,6 +683,7 @@
         in_specs=[SMEM, ANY, ANY, ANY] + [VMEM] * exchanges,
         out_specs=ANY,
         scratch_shapes=[
+            pltpu.VMEM((blocks + capacity, 1, width), f32),
             pltpu.VMEM((blocks + capacity, 1, width), f32),
             pltpu.VMEM((all_slots, 1, width), f32),
             pltpu.VMEM((all_slots, LANES), bf16),

time: 97.5 us -> 102 us (1.046)
  blocking collectives: 0 us -> 12.8 us
  starting transfers between devices: 27.8 us -> 18.2 us
  waiting for transfers between devices: 11 us -> 17.9 us
  Pallas kernels: 51.2 us -> 48.9 us
  local copies, waits for them, and re-layouts: 3.81 us -> 1.59 us
  other arithmetic: 1.54 us -> 0.09 us
    all_to_all x0 -> x1, blocking collectives: none -> 12.8 us  [exchange(): return lax.all_to_all(x, mesh_axes, split_axis=0, concat_axis=0, tiled=True)]
    all_to_all x3 -> x2, starting transfers between devices: 16.6 us -> 7 us  [exchange(): return lax.all_to_all(x, mesh_axes, split_axis=0, concat_axis=0, tiled=True)]
    all_to_all x3 -> x2, waiting for transfers between devices: 5.66 us -> 11.8 us  [exchange(): return lax.all_to_all(x, mesh_axes, split_axis=0, concat_axis=0, tiled=True)]
    convert_element_type x4 -> x0, other arithmetic: 1.39 us -> none  [the longest x2 1.36 us: halo(): return (xlo, xhi, ylo.astype(jnp.float32), yhi.astype(jnp.float32))]
    ppermute x2 -> x0, local copies, waits for them, and re-layouts: 1.33 us -> none  [both_ways(): return (lax.ppermute(last, axis, up), lax.ppermute(first, axis, down))]
    pallas_call x1, Pallas kernels: 14.5 us -> 13.1 us  [on_device(): pl.pallas_call(prior_kernel, out_shape=shape(field_shape, f32), in_specs=...]
  transfers between devices with their start and end apart: 7 -> 6, of which waited for: 6 -> 3; matrix products, arithmetic and copies ran while one was open for 5% -> 2% of each run, Pallas kernels for 19% -> 15%
where the time goes in v12:
time: 102 us; the launch traced here: 101 us
  Pallas kernels  48.9 us (48%)
  starting transfers between devices  18.2 us (18%)
  waiting for transfers between devices  17.9 us (18%)
  blocking collectives  12.8 us (13%)
  local copies, waits for them, and re-layouts  1.59 us (2%)
  between operations  1.55 us (2%)
    pallas_call x1, Pallas kernels, on_device(): pl.pallas_call(prior_kernel, out_shape=shape(field_shape, f32), in_specs=...  13.1 us
    all_to_all x1, blocking collectives, exchange(): return lax.all_to_all(x, mesh_axes, split_axis=0, concat_axis=0, tiled=True)  12.8 us
    pallas_call x1, Pallas kernels, on_device(): pl.pallas_call(functools.partial(star_kernel, exchanges=exchanges), out_s...  12.4 us
    all_to_all x2, waiting for transfers between devices, exchange(): return lax.all_to_all(x, mesh_axes, split_axis=0, concat_axis=0, tiled=True)  11.8 us
    ppermute x4, starting transfers between devices, both_ways(): return (lax.ppermute(last, axis, up), lax.ppermute(first, axis, down))  11.2 us
    pallas_call x1, Pallas kernels, on_device(): pl.pallas_call(functools.partial(finish_kernel, exchanges=exchanges, capa...  8.98 us
    pallas_call x1, Pallas kernels, on_device(): pl.pallas_call(functools.partial(serve_kernel, capacity=capacity, first_s...  7.14 us
    all_to_all x2, starting transfers between devices, exchange(): return lax.all_to_all(x, mesh_axes, split_axis=0, concat_axis=0, tiled=True)  7 us
  transfers between devices with their start and end apart: 6, of which 3 were waited for; matrix products, arithmetic and copies ran while one was open for 2% of the time, Pallas kernels for 15%

profile of v12, /device:TPU:1, one launch (start us, length us, event | category | flops | bytes accessed | tf_op | source)
XLA Modules:
  0.0 101.0 jit_solution(1027486320413255541)
XLA Ops:
  0.6 3.1 %route.1 = (s32[32,128]{1,0:T(8,128)}, s32[16,128]{1,0:T(8,128)}) custom-call(s32[32,64]{1,0:T(8,128)} %bitcast.37), custom_call_target="tpu_custom_call" | custom-call | tf_op jit(solution)/shard_map/route/pallas_call | solution.py:538
  3.7 2.3 %edges.1 = (bf16[2,64,512]{2,1,0:T(8,128)(2,1)}, bf16[2,64,512]{2,1,0:T(8,128)(2,1)}, f32[2,36,512]{2,1,0:T(8,128)}, f32[2,36,512]{2,1,0:T(8,128)}) custom-call(f32[32,64,512]{2,1,0:T(8,128)} %field_hbm.3), custom_call_target="tpu_custom_call" | custom-call | bytes 2097152 | tf_op jit(solution)/shard_map/edges/pallas_call | solution.py:555
  6.0 0.0 copy-start.8
  6.0 0.0 copy-start.11
  6.0 0.0 copy-start.7
  6.1 4.6 %collective-permute-start = (bf16[2,64,512]{2,1,0:T(8,128)(2,1)}, bf16[2,64,512]{2,1,0:T(8,128)(2,1)S(1)}, u32[]{:S(2)}, u32[]{:S(2)}) collective-permute-start(bf16[2,64,512]{2,1,0:T(8,128)(2,1)} %get-tuple-element.57), channel_id=1, source_target_pairs={{0,4},{4,8},{8,12},{12,16},{16,20},{20,24},{24,28},{1,5},{5,9},{9,... | collective-permute-start | bytes 393224 | tf_op jit(solution)/shard_map/ppermute | solution.py:497
  10.7 1.9 %collective-permute-start.1 = (bf16[2,64,512]{2,1,0:T(8,128)(2,1)}, bf16[2,64,512]{2,1,0:T(8,128)(2,1)S(1)}, u32[]{:S(2)}, u32[]{:S(2)}) collective-permute-start(bf16[2,64,512]{2,1,0:T(8,128)(2,1)} %get-tuple-element.58), channel_id=1, source_target_pairs={{4,0},{8,4},{12,8},{16,12},{20,16},{24,20},{28,24},{5,1},{9,5},{13... | collective-permute-start | bytes 393224 | tf_op jit(solution)/shard_map/ppermute | solution.py:497
  12.6 12.8 %all_to_all.32 = s32[32,1,128]{2,1,0:T(1,128)} all-to-all(s32[32,1,128]{2,1,0:T(1,128)S(1)} %bitcast.38), channel_id=1, replica_groups=mesh['gx'=8,'gy'=4] {'gx','gy'}, dimensions={0} | all-to-all | bytes 32768 | tf_op jit(solution)/shard_map/all_to_all | solution.py:528
  25.5 7.1 %serve.1 = (bf16[2816,128]{1,0:T(8,128)(2,1)}, bf16[1280,128]{1,0:T(8,128)(2,1)S(1)}, s32[1]{0:T(128)}) custom-call(s32[4096]{0:T(1024)} %bitcast.24, f32[8192,1,128]{2,1,0:T(1,128)} %bitcast.28), custom_call_target="tpu_custom_call" | custom-call | flops 1048576 | bytes 6291456 | tf_op jit(solution)/shard_map/serve/pallas_call | solution.py:578
  33.3 2.9 %all-to-all-start.3 = ((bf16[32,88,128]{2,1,0:T(8,128)(2,1)}), bf16[32,88,128]{2,1,0:T(8,128)(2,1)S(1)}, u32[]{:S(2)}, u32[]{:S(2)}) async-start(bf16[32,88,128]{2,1,0:T(8,128)(2,1)} %bitcast.35), calls=%async_computation.3 | async-start | bytes 1441792 | tf_op jit(solution)/shard_map/all_to_all | solution.py:528
  36.3 0.1 reshape.92
  36.3 0.1 copy.16
  36.4 0.1 reshape.93.position_ref
  36.6 0.1 copy.18
  36.7 0.1 reshape.95.inverse_ref
  36.7 0.1 copy.17
  36.8 0.1 reshape.94.observed_ref
  37.0 3.4 %collective-permute-start.2 = (bf16[2,36,512]{2,1,0:T(8,128)(2,1)S(1)}, bf16[2,36,512]{2,1,0:T(8,128)(2,1)S(1)}, u32[]{:S(2)}, u32[]{:S(2)}) collective-permute-start(bf16[2,36,512]{2,1,0:T(8,128)(2,1)S(1)} %get-tuple-element.74), channel_id=1, source_target_pairs={{0,1},{1,2},{2,3},{4,5},{5,6},{6,7},{8,9},{9,10},{10,11},{12,13},{... | collective-permute-start | bytes 221192 | tf_op jit(solution)/shard_map/ppermute | solution.py:497
  40.3 1.3 %collective-permute-start.3 = (bf16[2,36,512]{2,1,0:T(8,128)(2,1)S(1)}, bf16[2,36,512]{2,1,0:T(8,128)(2,1)S(1)}, u32[]{:S(2)}, u32[]{:S(2)}) collective-permute-start(bf16[2,36,512]{2,1,0:T(8,128)(2,1)S(1)} %get-tuple-element.75), channel_id=1, source_target_pairs={{1,0},{2,1},{3,2},{5,4},{6,5},{7,6},{9,8},{10,9},{11,10},{13,12},{... | collective-permute-start | bytes 221192 | tf_op jit(solution)/shard_map/ppermute | solution.py:497
  41.6 0.1 slice_and_fusion
  41.7 0.1 reshape.91
  41.8 0.1 reshape.90
  41.9 1.8 %match.1.match_hbm = bf16[4096,128]{1,0:T(8,128)(2,1)S(1)} custom-call(s32[32,128]{1,0:T(8,128)S(1)} %pad_add_fusion.incoming_ref), custom_call_target="tpu_custom_call" | custom-call | flops 1000000000 | bytes 1048576 | tf_op jit(solution)/shard_map/match/pallas_call | solution.py:614
  43.7 6.1 %collective-permute-done.2.ylo_ref = bf16[2,36,512]{2,1,0:T(8,128)(2,1)S(1)} collective-permute-done((bf16[2,36,512]{2,1,0:T(8,128)(2,1)S(1)}, bf16[2,36,512]{2,1,0:T(8,128)(2,1)S(1)}, u32[]{:S(2)}, u32[]{:S(2)}) %collective-permute-start.2) | collective-permute-done | bytes 73760 | tf_op jit(solution)/shard_map/ppermute | solution.py:497
  49.8 6.2 %all-to-all-done.3 = bf16[32,88,128]{2,1,0:T(8,128)(2,1)S(1)} async-done(((bf16[32,88,128]{2,1,0:T(8,128)(2,1)}), bf16[32,88,128]{2,1,0:T(8,128)(2,1)S(1)}, u32[]{:S(2)}, u32[]{:S(2)}) %all-to-all-start.3) | async-done | bytes 720928 | tf_op jit(solution)/shard_map/all_to_all | solution.py:528
  56.1 12.4 %stars.1 = (f32[16,128]{1,0:T(8,128)S(1)}, bf16[2816,128]{1,0:T(8,128)(2,1)}, bf16[1280,128]{1,0:T(8,128)(2,1)S(1)}) custom-call(s32[2048]{0:T(1024)S(1)} %reshape.93.position_ref, f32[16,128]{1,0:T(8,128)S(1)} %reshape.94.observed_ref, f32[16,128]{1,0:T(8,128)S(1)} %reshape.95.inverse_ref, bf16[64,32,32,128]{3,2,1,0:T(8,128)(2,1)} %weights_hbm.1, ...), custom_call_target="tpu_custom_call" | custom-call | flops 33554432 | bytes 16777216 | tf_op jit(solution)/shard_map/stars/pallas_call | solution.py:629
  68.5 4.1 %all-to-all-start.4 = ((bf16[32,88,128]{2,1,0:T(8,128)(2,1)}), bf16[32,88,128]{2,1,0:T(8,128)(2,1)S(1)}, u32[]{:S(2)}, u32[]{:S(2)}) async-start(bf16[32,88,128]{2,1,0:T(8,128)(2,1)} %bitcast.14), calls=%async_computation.4 | async-start | bytes 1441792 | tf_op jit(solution)/shard_map/all_to_all | solution.py:528
  72.6 0.1 reshape.100
  72.7 0.7 copy.19
  73.4 13.1 %prior.1.base_hbm = f32[32,64,512]{2,1,0:T(8,128)} custom-call(f32[32,64,512]{2,1,0:T(8,128)} %field_hbm.3, bf16[2,64,512]{2,1,0:T(8,128)(2,1)} %copy-done, bf16[2,64,512]{2,1,0:T(8,128)(2,1)} %copy-done.1, bf16[2,36,512]{2,1,0:T(8,128)(2,1)} %copy-done.5, bf16[2,36,512]{2,1,0:T(8,128)(2,1)} %copy-done.6), custom_call_target="tpu_custom_call" | custom-call | flops 31457280 | bytes 8388608 | tf_op jit(solution)/shard_map/prior/pallas_call | solution.py:658
  86.5 5.5 %all-to-all-done.4 = bf16[32,88,128]{2,1,0:T(8,128)(2,1)S(1)} async-done(((bf16[32,88,128]{2,1,0:T(8,128)(2,1)}), bf16[32,88,128]{2,1,0:T(8,128)(2,1)S(1)}, u32[]{:S(2)}, u32[]{:S(2)}) %all-to-all-start.4) | async-done | bytes 720928 | tf_op jit(solution)/shard_map/all_to_all | solution.py:528
  92.0 9.0 %finish.1 = f32[32,64,512]{2,1,0:T(8,128)} custom-call(s32[4096]{0:T(1024)S(1)} %bitcast.27, bf16[4096,128]{1,0:T(8,128)(2,1)S(1)} %match.1.match_hbm, f32[32,64,512]{2,1,0:T(8,128)} %field_hbm.3, f32[32,64,512]{2,1,0:T(8,128)} %prior.1.base_hbm, bf16[2816,128]{1,0:T(8,128)(2,1)S(1)} %bitcast.23, bf16[1280,128]{1,0:T(8,128)(2,1)S(1)} %bitcast.31), custom_call_target="tpu_custom_call" | custom-call | flops 4194304 | bytes 12582912 | tf_op jit(solution)/shard_map/finish/pallas_call | solution.py:678
  (29 shorter events, 0.1 us)
Async XLA Ops:
  3.7 8.9 %copy-start.9 = (s32[32,128]{1,0:T(8,128)S(1)}, s32[32,128]{1,0:T(8,128)}, u32[]{:S(2)}) copy-start(s32[32,128]{1,0:T(8,128)} %get-tuple-element.55) | copy-start | bytes 49156
  6.0 30.3 %copy-start.10 = (s32[16,128]{1,0:T(8,128)S(1)}, s32[16,128]{1,0:T(8,128)}, u32[]{:S(2)}) copy-start(s32[16,128]{1,0:T(8,128)} %get-tuple-element.77) | copy-start | bytes 24580
  6.0 30.6 %copy-start.8 = (f32[64,32]{0,1:T(8,128)S(1)}, f32[64,32]{0,1:T(8,128)}, u32[]{:S(2)}) copy-start(f32[64,32]{0,1:T(8,128)} %param.13) | copy-start | bytes 24580
  6.0 30.6 %copy-start.11 = (s32[64]{0:T(128)S(1)}, s32[64]{0:T(128)}, u32[]{:S(2)}) copy-start(s32[64]{0:T(128)} %param.14) | copy-start | bytes 772
  6.0 30.7 %copy-start.7 = (f32[64,32]{0,1:T(8,128)S(1)}, f32[64,32]{0,1:T(8,128)}, u32[]{:S(2)}) copy-start(f32[64,32]{0,1:T(8,128)} %param.12) | copy-start | bytes 24580
  6.0 30.9 %copy-start.3 = (f32[2,36,512]{2,1,0:T(8,128)S(1)}, f32[2,36,512]{2,1,0:T(8,128)}, u32[]{:S(2)}) copy-start(f32[2,36,512]{2,1,0:T(8,128)} %get-tuple-element.72.yfirst_ref) | copy-start | bytes 442372
  6.0 30.9 %copy-start.4 = (f32[2,36,512]{2,1,0:T(8,128)S(1)}, f32[2,36,512]{2,1,0:T(8,128)}, u32[]{:S(2)}) copy-start(f32[2,36,512]{2,1,0:T(8,128)} %get-tuple-element.73.ylast_ref) | copy-start | bytes 442372
  6.1 19.4 %collective-permute-start = (bf16[2,64,512]{2,1,0:T(8,128)(2,1)}, bf16[2,64,512]{2,1,0:T(8,128)(2,1)S(1)}, u32[]{:S(2)}, u32[]{:S(2)}) collective-permute-start(bf16[2,64,512]{2,1,0:T(8,128)(2,1)} %get-tuple-element.57), channel_id=1, source_target_pairs={{0,4},{4,8},{8,12},{12,16},{16,20},{20,24},{24,28},{1,5},{5,9},{9,... | collective-permute-start | bytes 393224 | tf_op jit(solution)/shard_map/ppermute | solution.py:497
  10.7 14.8 %collective-permute-start.1 = (bf16[2,64,512]{2,1,0:T(8,128)(2,1)}, bf16[2,64,512]{2,1,0:T(8,128)(2,1)S(1)}, u32[]{:S(2)}, u32[]{:S(2)}) collective-permute-start(bf16[2,64,512]{2,1,0:T(8,128)(2,1)} %get-tuple-element.58), channel_id=1, source_target_pairs={{4,0},{8,4},{12,8},{16,12},{20,16},{24,20},{28,24},{5,1},{9,5},{13... | collective-permute-start | bytes 393224 | tf_op jit(solution)/shard_map/ppermute | solution.py:497
  25.5 16.2 %copy-start.2 = (s32[32,1,128]{2,1,0:T(1,128)S(1)}, s32[32,1,128]{2,1,0:T(1,128)}, u32[]{:S(2)}) copy-start(s32[32,1,128]{2,1,0:T(1,128)} %all_to_all.32) | copy-start | bytes 49156
  25.5 18.2 %copy-start = (bf16[2,64,512]{2,1,0:T(8,128)(2,1)}, bf16[2,64,512]{2,1,0:T(8,128)(2,1)S(1)}, u32[]{:S(2)}) copy-start(bf16[2,64,512]{2,1,0:T(8,128)(2,1)S(1)} %collective-permute-done.xlo_ref) | copy-start | bytes 393220
  25.5 18.2 %copy-start.1 = (bf16[2,64,512]{2,1,0:T(8,128)(2,1)}, bf16[2,64,512]{2,1,0:T(8,128)(2,1)S(1)}, u32[]{:S(2)}) copy-start(bf16[2,64,512]{2,1,0:T(8,128)(2,1)S(1)} %collective-permute-done.1.xhi_ref) | copy-start | bytes 393220
  33.3 22.7 %all-to-all-start.3 = ((bf16[32,88,128]{2,1,0:T(8,128)(2,1)}), bf16[32,88,128]{2,1,0:T(8,128)(2,1)S(1)}, u32[]{:S(2)}, u32[]{:S(2)}) async-start(bf16[32,88,128]{2,1,0:T(8,128)(2,1)} %bitcast.35), calls=%async_computation.3 | async-start | bytes 1441792 | tf_op jit(solution)/shard_map/all_to_all | solution.py:528
  37.0 12.9 %collective-permute-start.2 = (bf16[2,36,512]{2,1,0:T(8,128)(2,1)S(1)}, bf16[2,36,512]{2,1,0:T(8,128)(2,1)S(1)}, u32[]{:S(2)}, u32[]{:S(2)}) collective-permute-start(bf16[2,36,512]{2,1,0:T(8,128)(2,1)S(1)} %get-tuple-element.74), channel_id=1, source_target_pairs={{0,1},{1,2},{2,3},{4,5},{5,6},{6,7},{8,9},{9,10},{10,11},{12,13},{... | collective-permute-start | bytes 221192 | tf_op jit(solution)/shard_map/ppermute | solution.py:497
  40.3 9.5 %collective-permute-start.3 = (bf16[2,36,512]{2,1,0:T(8,128)(2,1)S(1)}, bf16[2,36,512]{2,1,0:T(8,128)(2,1)S(1)}, u32[]{:S(2)}, u32[]{:S(2)}) collective-permute-start(bf16[2,36,512]{2,1,0:T(8,128)(2,1)S(1)} %get-tuple-element.75), channel_id=1, source_target_pairs={{1,0},{2,1},{3,2},{5,4},{6,5},{7,6},{9,8},{10,9},{11,10},{13,12},{... | collective-permute-start | bytes 221192 | tf_op jit(solution)/shard_map/ppermute | solution.py:497
  49.8 18.7 %copy-start.5 = (bf16[2,36,512]{2,1,0:T(8,128)(2,1)}, bf16[2,36,512]{2,1,0:T(8,128)(2,1)S(1)}, u32[]{:S(2)}) copy-start(bf16[2,36,512]{2,1,0:T(8,128)(2,1)S(1)} %collective-permute-done.2.ylo_ref) | copy-start | bytes 221188
  49.8 18.7 %copy-start.6 = (bf16[2,36,512]{2,1,0:T(8,128)(2,1)}, bf16[2,36,512]{2,1,0:T(8,128)(2,1)S(1)}, u32[]{:S(2)}) copy-start(bf16[2,36,512]{2,1,0:T(8,128)(2,1)S(1)} %collective-permute-done.3.yhi_ref) | copy-start | bytes 221188
  68.5 23.5 %all-to-all-start.4 = ((bf16[32,88,128]{2,1,0:T(8,128)(2,1)}), bf16[32,88,128]{2,1,0:T(8,128)(2,1)S(1)}, u32[]{:S(2)}, u32[]{:S(2)}) async-start(bf16[32,88,128]{2,1,0:T(8,128)(2,1)} %bitcast.14), calls=%async_computation.4 | async-start | bytes 1441792 | tf_op jit(solution)/shard_map/all_to_all | solution.py:528

commit v13 on v12

--- a/solution.py
+++ b/solution.py
@@ -571,8 +571,7 @@
         cost_estimate=pl.CostEstimate(flops=0, bytes_accessed=2 * MIB, transcendentals=0),
         name="edges",
     )(field)
-    xlo, xhi = both_ways(xfirst, xlast, "gx")
-    incoming, *edges = lax.optimization_barrier((incoming, xlo, xhi, yfirst, ylast))
+    incoming, *edges = lax.optimization_barrier((incoming, xfirst, xlast, yfirst, ylast))
     wanted = incoming.reshape(-1)
 
     *served, crowded = pl.pallas_call(
@@ -595,6 +594,7 @@
 
     returned = exchange_rows(served, crowded)
     *edges, incoming_late, _ = lax.optimization_barrier((*edges, incoming, served[0]))
+    xlo, xhi = both_ways(*edges[:2], "gx")
     slabs = pl.pallas_call(
         ends_kernel,
         out_shape=[shape((2, cells_x + 4, depth), bf16)] * 2,
@@ -604,9 +604,8 @@
         compiler_params=pltpu.CompilerParams(vmem_limit_bytes=8 * MIB),
         cost_estimate=pl.CostEstimate(flops=0, bytes_accessed=MIB, transcendentals=0),
         name="ends",
-    )(*edges)
+    )(xlo, xhi, *edges[2:])
     ylo, yhi = both_ways(*slabs, "gy")
-    xlo, xhi, *_ = edges
     slot_lists = [
         incoming_late[:, :first_slots].reshape(-1, LANES),
         (incoming_late[:, first_slots:] & (MARK - 1)).reshape(-1, LANES),

time: 102 us -> 95.7 us (0.938)
  blocking collectives: 12.8 us -> 0 us
  starting transfers between devices: 18.2 us -> 25.5 us
  waiting for transfers between devices: 17.9 us -> 15.3 us
  local copies, waits for them, and re-layouts: 1.59 us -> 2.91 us
    all_to_all x1 -> x0, blocking collectives: 12.8 us -> none  [exchange(): return lax.all_to_all(x, mesh_axes, split_axis=0, concat_axis=0, tiled=True)]
    all_to_all x2 -> x3, starting transfers between devices: 7 us -> 15 us  [exchange(): return lax.all_to_all(x, mesh_axes, split_axis=0, concat_axis=0, tiled=True)]
    all_to_all x2 -> x3, waiting for transfers between devices: 11.8 us -> 9.77 us  [exchange(): return lax.all_to_all(x, mesh_axes, split_axis=0, concat_axis=0, tiled=True)]
  transfers between devices with their start and end apart: 6 -> 7, of which waited for: 3 -> 4; matrix products, arithmetic and copies ran while one was open for 2% -> 3% of each run, Pallas kernels for 15% -> 18%
where the time goes in v13:
time: 95.7 us; the launch traced here: 94.9 us
  Pallas kernels  48.8 us (51%)
  starting transfers between devices  25.5 us (27%)
  waiting for transfers between devices  15.3 us (16%)
  local copies, waits for them, and re-layouts  2.91 us (3%)
  between operations  1.58 us (2%)
    all_to_all x3, starting transfers between devices, exchange(): return lax.all_to_all(x, mesh_axes, split_axis=0, concat_axis=0, tiled=True)  15 us
    pallas_call x1, Pallas kernels, on_device(): pl.pallas_call(prior_kernel, out_shape=shape(field_shape, f32), in_specs=...  13.2 us
    pallas_call x1, Pallas kernels, on_device(): pl.pallas_call(functools.partial(star_kernel, exchanges=exchanges), out_s...  12.4 us
    ppermute x4, starting transfers between devices, both_ways(): return (lax.ppermute(last, axis, up), lax.ppermute(first, axis, down))  10.4 us
    all_to_all x3, waiting for transfers between devices, exchange(): return lax.all_to_all(x, mesh_axes, split_axis=0, concat_axis=0, tiled=True)  9.77 us
    pallas_call x1, Pallas kernels, on_device(): pl.pallas_call(functools.partial(finish_kernel, exchanges=exchanges, capa...  8.98 us
    pallas_call x1, Pallas kernels, on_device(): pl.pallas_call(functools.partial(serve_kernel, capacity=capacity, first_s...  7.09 us
    ppermute x4, waiting for transfers between devices, both_ways(): return (lax.ppermute(last, axis, up), lax.ppermute(first, axis, down))  5.52 us
  transfers between devices with their start and end apart: 7, of which 4 were waited for; matrix products, arithmetic and copies ran while one was open for 3% of the time, Pallas kernels for 18%

profile of v13, /device:TPU:1, one launch (start us, length us, event | category | flops | bytes accessed | tf_op | source)
XLA Modules:
  0.0 94.9 jit_solution(10070013422541034357)
XLA Ops:
  0.6 3.1 %route.1 = (s32[32,128]{1,0:T(8,128)}, s32[16,128]{1,0:T(8,128)}) custom-call(s32[32,64]{1,0:T(8,128)} %bitcast.37), custom_call_target="tpu_custom_call" | custom-call | tf_op jit(solution)/shard_map/route/pallas_call | solution.py:538
  3.7 7.1 %all-to-all-start.2 = ((s32[32,1,128]{2,1,0:T(1,128)}), s32[32,1,128]{2,1,0:T(1,128)S(1)}, u32[]{:S(2)}, u32[]{:S(2)}) async-start(s32[32,1,128]{2,1,0:T(1,128)} %bitcast.38), calls=%async_computation.2 | async-start | bytes 32768 | tf_op jit(solution)/shard_map/all_to_all | solution.py:528
  10.8 2.3 %edges.1 = (bf16[2,64,512]{2,1,0:T(8,128)(2,1)}, bf16[2,64,512]{2,1,0:T(8,128)(2,1)}, f32[2,36,512]{2,1,0:T(8,128)}, f32[2,36,512]{2,1,0:T(8,128)}) custom-call(f32[32,64,512]{2,1,0:T(8,128)} %field_hbm.3), custom_call_target="tpu_custom_call" | custom-call | bytes 2097152 | tf_op jit(solution)/shard_map/edges/pallas_call | solution.py:555
  13.1 0.0 copy-start.9
  13.2 4.2 %all-to-all-done.2 = s32[32,1,128]{2,1,0:T(1,128)S(1)} async-done(((s32[32,1,128]{2,1,0:T(1,128)}), s32[32,1,128]{2,1,0:T(1,128)S(1)}, u32[]{:S(2)}, u32[]{:S(2)}) %all-to-all-start.2) | async-done | bytes 16416 | tf_op jit(solution)/shard_map/all_to_all | solution.py:528
  17.4 0.6 copy-done.2
  18.0 7.1 %serve.1 = (bf16[2816,128]{1,0:T(8,128)(2,1)}, bf16[1280,128]{1,0:T(8,128)(2,1)S(1)}, s32[1]{0:T(128)}) custom-call(s32[4096]{0:T(1024)} %bitcast.24, f32[8192,1,128]{2,1,0:T(1,128)} %bitcast.28), custom_call_target="tpu_custom_call" | custom-call | flops 1048576 | bytes 6291456 | tf_op jit(solution)/shard_map/serve/pallas_call | solution.py:577
  25.8 3.0 %all-to-all-start.3 = ((bf16[32,88,128]{2,1,0:T(8,128)(2,1)}), bf16[32,88,128]{2,1,0:T(8,128)(2,1)S(1)}, u32[]{:S(2)}, u32[]{:S(2)}) async-start(bf16[32,88,128]{2,1,0:T(8,128)(2,1)} %bitcast.35), calls=%async_computation.3 | async-start | bytes 1441792 | tf_op jit(solution)/shard_map/all_to_all | solution.py:528
  28.8 0.1 reshape.92
  28.9 0.1 copy.16
  29.0 0.1 reshape.93.position_ref
  29.1 0.1 copy.18
  29.2 0.1 reshape.95.inverse_ref
  29.3 0.1 copy.17
  29.4 0.1 reshape.94.observed_ref
  29.4 3.5 %collective-permute-start = (bf16[2,64,512]{2,1,0:T(8,128)(2,1)S(1)}, bf16[2,64,512]{2,1,0:T(8,128)(2,1)S(1)}, u32[]{:S(2)}, u32[]{:S(2)}) collective-permute-start(bf16[2,64,512]{2,1,0:T(8,128)(2,1)S(1)} %copy-done.13), channel_id=1, source_target_pairs={{0,4},{4,8},{8,12},{12,16},{16,20},{20,24},{24,28},{1,5},{5,9},{9,... | collective-permute-start | bytes 393224 | tf_op jit(solution)/shard_map/ppermute | solution.py:497
  33.0 1.9 %collective-permute-start.1 = (bf16[2,64,512]{2,1,0:T(8,128)(2,1)S(1)}, bf16[2,64,512]{2,1,0:T(8,128)(2,1)S(1)}, u32[]{:S(2)}, u32[]{:S(2)}) collective-permute-start(bf16[2,64,512]{2,1,0:T(8,128)(2,1)S(1)} %copy-done.12), channel_id=1, source_target_pairs={{4,0},{8,4},{12,8},{16,12},{20,16},{24,20},{28,24},{5,1},{9,5},{13... | collective-permute-start | bytes 393224 | tf_op jit(solution)/shard_map/ppermute | solution.py:497
  34.9 0.8 slice_and_fusion
  35.7 0.1 reshape.91
  35.8 0.8 reshape.90
  36.7 3.3 %collective-permute-done.1.xhi_ref = bf16[2,64,512]{2,1,0:T(8,128)(2,1)S(1)} collective-permute-done((bf16[2,64,512]{2,1,0:T(8,128)(2,1)S(1)}, bf16[2,64,512]{2,1,0:T(8,128)(2,1)S(1)}, u32[]{:S(2)}, u32[]{:S(2)}) %collective-permute-start.1) | collective-permute-done | bytes 131104 | tf_op jit(solution)/shard_map/ppermute | solution.py:497
  40.0 3.7 %collective-permute-start.2 = (bf16[2,36,512]{2,1,0:T(8,128)(2,1)S(1)}, bf16[2,36,512]{2,1,0:T(8,128)(2,1)S(1)}, u32[]{:S(2)}, u32[]{:S(2)}) collective-permute-start(bf16[2,36,512]{2,1,0:T(8,128)(2,1)S(1)} %get-tuple-element.74), channel_id=1, source_target_pairs={{0,1},{1,2},{2,3},{4,5},{5,6},{6,7},{8,9},{9,10},{10,11},{12,13},{... | collective-permute-start | bytes 221192 | tf_op jit(solution)/shard_map/ppermute | solution.py:497
  43.7 1.3 %collective-permute-start.3 = (bf16[2,36,512]{2,1,0:T(8,128)(2,1)S(1)}, bf16[2,36,512]{2,1,0:T(8,128)(2,1)S(1)}, u32[]{:S(2)}, u32[]{:S(2)}) collective-permute-start(bf16[2,36,512]{2,1,0:T(8,128)(2,1)S(1)} %get-tuple-element.75), channel_id=1, source_target_pairs={{1,0},{2,1},{3,2},{5,4},{6,5},{7,6},{9,8},{10,9},{11,10},{13,12},{... | collective-permute-start | bytes 221192 | tf_op jit(solution)/shard_map/ppermute | solution.py:497
  45.0 1.8 %match.1.match_hbm = bf16[4096,128]{1,0:T(8,128)(2,1)S(1)} custom-call(s32[32,128]{1,0:T(8,128)S(1)} %pad_add_fusion.incoming_ref), custom_call_target="tpu_custom_call" | custom-call | flops 1000000000 | bytes 1048576 | tf_op jit(solution)/shard_map/match/pallas_call | solution.py:613
  46.8 2.2 %collective-permute-done.3.yhi_ref = bf16[2,36,512]{2,1,0:T(8,128)(2,1)S(1)} collective-permute-done((bf16[2,36,512]{2,1,0:T(8,128)(2,1)S(1)}, bf16[2,36,512]{2,1,0:T(8,128)(2,1)S(1)}, u32[]{:S(2)}, u32[]{:S(2)}) %collective-permute-start.3) | collective-permute-done | bytes 73760 | tf_op jit(solution)/shard_map/ppermute | solution.py:497
  49.0 12.4 %stars.1 = (f32[16,128]{1,0:T(8,128)S(1)}, bf16[2816,128]{1,0:T(8,128)(2,1)}, bf16[1280,128]{1,0:T(8,128)(2,1)S(1)}) custom-call(s32[2048]{0:T(1024)S(1)} %reshape.93.position_ref, f32[16,128]{1,0:T(8,128)S(1)} %reshape.94.observed_ref, f32[16,128]{1,0:T(8,128)S(1)} %reshape.95.inverse_ref, bf16[64,32,32,128]{3,2,1,0:T(8,128)(2,1)} %weights_hbm.1, ...), custom_call_target="tpu_custom_call" | custom-call | flops 33554432 | bytes 16777216 | tf_op jit(solution)/shard_map/stars/pallas_call | solution.py:628
  61.5 4.9 %all-to-all-start.4 = ((bf16[32,88,128]{2,1,0:T(8,128)(2,1)}), bf16[32,88,128]{2,1,0:T(8,128)(2,1)S(1)}, u32[]{:S(2)}, u32[]{:S(2)}) async-start(bf16[32,88,128]{2,1,0:T(8,128)(2,1)} %bitcast.14), calls=%async_computation.4 | async-start | bytes 1441792 | tf_op jit(solution)/shard_map/all_to_all | solution.py:528
  66.5 0.1 reshape.100
  66.5 0.7 copy.19
  67.2 13.2 %prior.1.base_hbm = f32[32,64,512]{2,1,0:T(8,128)} custom-call(f32[32,64,512]{2,1,0:T(8,128)} %field_hbm.3, bf16[2,64,512]{2,1,0:T(8,128)(2,1)} %copy-done, bf16[2,64,512]{2,1,0:T(8,128)(2,1)} %copy-done.1, bf16[2,36,512]{2,1,0:T(8,128)(2,1)} %copy-done.6, bf16[2,36,512]{2,1,0:T(8,128)(2,1)} %copy-done.7), custom_call_target="tpu_custom_call" | custom-call | flops 31457280 | bytes 8388608 | tf_op jit(solution)/shard_map/prior/pallas_call | solution.py:657
  80.4 5.5 %all-to-all-done.4 = bf16[32,88,128]{2,1,0:T(8,128)(2,1)S(1)} async-done(((bf16[32,88,128]{2,1,0:T(8,128)(2,1)}), bf16[32,88,128]{2,1,0:T(8,128)(2,1)S(1)}, u32[]{:S(2)}, u32[]{:S(2)}) %all-to-all-start.4) | async-done | bytes 720928 | tf_op jit(solution)/shard_map/all_to_all | solution.py:528
  85.9 9.0 %finish.1 = f32[32,64,512]{2,1,0:T(8,128)} custom-call(s32[4096]{0:T(1024)S(1)} %bitcast.27, bf16[4096,128]{1,0:T(8,128)(2,1)S(1)} %match.1.match_hbm, f32[32,64,512]{2,1,0:T(8,128)} %field_hbm.3, f32[32,64,512]{2,1,0:T(8,128)} %prior.1.base_hbm, bf16[2816,128]{1,0:T(8,128)(2,1)S(1)} %bitcast.23, bf16[1280,128]{1,0:T(8,128)(2,1)S(1)} %bitcast.31), custom_call_target="tpu_custom_call" | custom-call | flops 4194304 | bytes 12582912 | tf_op jit(solution)/shard_map/finish/pallas_call | solution.py:677
  (34 shorter events, 0.1 us)
Async XLA Ops:
  3.7 13.7 %all-to-all-start.2 = ((s32[32,1,128]{2,1,0:T(1,128)}), s32[32,1,128]{2,1,0:T(1,128)S(1)}, u32[]{:S(2)}, u32[]{:S(2)}) async-start(s32[32,1,128]{2,1,0:T(1,128)} %bitcast.38), calls=%async_computation.2 | async-start | bytes 32768 | tf_op jit(solution)/shard_map/all_to_all | solution.py:528
  13.1 15.7 %copy-start.10 = (s32[16,128]{1,0:T(8,128)S(1)}, s32[16,128]{1,0:T(8,128)}, u32[]{:S(2)}) copy-start(s32[16,128]{1,0:T(8,128)} %get-tuple-element.77) | copy-start | bytes 24580
  13.1 16.0 %copy-start.9 = (f32[64,32]{0,1:T(8,128)S(1)}, f32[64,32]{0,1:T(8,128)}, u32[]{:S(2)}) copy-start(f32[64,32]{0,1:T(8,128)} %param.13) | copy-start | bytes 24580
  13.1 16.0 %copy-start.11 = (s32[64]{0:T(128)S(1)}, s32[64]{0:T(128)}, u32[]{:S(2)}) copy-start(s32[64]{0:T(128)} %param.14) | copy-start | bytes 772
  13.1 16.2 %copy-start.8 = (f32[64,32]{0,1:T(8,128)S(1)}, f32[64,32]{0,1:T(8,128)}, u32[]{:S(2)}) copy-start(f32[64,32]{0,1:T(8,128)} %param.12) | copy-start | bytes 24580
  13.1 16.3 %copy-start.13 = (bf16[2,64,512]{2,1,0:T(8,128)(2,1)S(1)}, bf16[2,64,512]{2,1,0:T(8,128)(2,1)}, u32[]{:S(2)}) copy-start(bf16[2,64,512]{2,1,0:T(8,128)(2,1)} %get-tuple-element.70) | copy-start | bytes 393220
  13.2 19.9 %copy-start.12 = (bf16[2,64,512]{2,1,0:T(8,128)(2,1)S(1)}, bf16[2,64,512]{2,1,0:T(8,128)(2,1)}, u32[]{:S(2)}) copy-start(bf16[2,64,512]{2,1,0:T(8,128)(2,1)} %get-tuple-element.71) | copy-start | bytes 393220
  13.2 26.8 %copy-start.4 = (f32[2,36,512]{2,1,0:T(8,128)S(1)}, f32[2,36,512]{2,1,0:T(8,128)}, u32[]{:S(2)}) copy-start(f32[2,36,512]{2,1,0:T(8,128)} %get-tuple-element.72.yfirst_ref) | copy-start | bytes 442372
  13.2 26.8 %copy-start.5 = (f32[2,36,512]{2,1,0:T(8,128)S(1)}, f32[2,36,512]{2,1,0:T(8,128)}, u32[]{:S(2)}) copy-start(f32[2,36,512]{2,1,0:T(8,128)} %get-tuple-element.73.ylast_ref) | copy-start | bytes 442372
  17.4 0.6 copy-start.2
  25.8 23.2 %all-to-all-start.3 = ((bf16[32,88,128]{2,1,0:T(8,128)(2,1)}), bf16[32,88,128]{2,1,0:T(8,128)(2,1)S(1)}, u32[]{:S(2)}, u32[]{:S(2)}) async-start(bf16[32,88,128]{2,1,0:T(8,128)(2,1)} %bitcast.35), calls=%async_computation.3 | async-start | bytes 1441792 | tf_op jit(solution)/shard_map/all_to_all | solution.py:528
  29.4 7.2 %collective-permute-start = (bf16[2,64,512]{2,1,0:T(8,128)(2,1)S(1)}, bf16[2,64,512]{2,1,0:T(8,128)(2,1)S(1)}, u32[]{:S(2)}, u32[]{:S(2)}) collective-permute-start(bf16[2,64,512]{2,1,0:T(8,128)(2,1)S(1)} %copy-done.13), channel_id=1, source_target_pairs={{0,4},{4,8},{8,12},{12,16},{16,20},{20,24},{24,28},{1,5},{5,9},{9,... | collective-permute-start | bytes 393224 | tf_op jit(solution)/shard_map/ppermute | solution.py:497
  33.0 7.0 %collective-permute-start.1 = (bf16[2,64,512]{2,1,0:T(8,128)(2,1)S(1)}, bf16[2,64,512]{2,1,0:T(8,128)(2,1)S(1)}, u32[]{:S(2)}, u32[]{:S(2)}) collective-permute-start(bf16[2,64,512]{2,1,0:T(8,128)(2,1)S(1)} %copy-done.12), channel_id=1, source_target_pairs={{4,0},{8,4},{12,8},{16,12},{20,16},{24,20},{28,24},{5,1},{9,5},{13... | collective-permute-start | bytes 393224 | tf_op jit(solution)/shard_map/ppermute | solution.py:497
  36.6 24.8 %copy-start = (bf16[2,64,512]{2,1,0:T(8,128)(2,1)}, bf16[2,64,512]{2,1,0:T(8,128)(2,1)S(1)}, u32[]{:S(2)}) copy-start(bf16[2,64,512]{2,1,0:T(8,128)(2,1)S(1)} %collective-permute-done.xlo_ref) | copy-start | bytes 393220
  40.0 21.5 %copy-start.1 = (bf16[2,64,512]{2,1,0:T(8,128)(2,1)}, bf16[2,64,512]{2,1,0:T(8,128)(2,1)S(1)}, u32[]{:S(2)}) copy-start(bf16[2,64,512]{2,1,0:T(8,128)(2,1)S(1)} %collective-permute-done.1.xhi_ref) | copy-start | bytes 393220
  40.0 6.8 %collective-permute-start.2 = (bf16[2,36,512]{2,1,0:T(8,128)(2,1)S(1)}, bf16[2,36,512]{2,1,0:T(8,128)(2,1)S(1)}, u32[]{:S(2)}, u32[]{:S(2)}) collective-permute-start(bf16[2,36,512]{2,1,0:T(8,128)(2,1)S(1)} %get-tuple-element.74), channel_id=1, source_target_pairs={{0,1},{1,2},{2,3},{4,5},{5,6},{6,7},{8,9},{9,10},{10,11},{12,13},{... | collective-permute-start | bytes 221192 | tf_op jit(solution)/shard_map/ppermute | solution.py:497
  43.7 5.3 %collective-permute-start.3 = (bf16[2,36,512]{2,1,0:T(8,128)(2,1)S(1)}, bf16[2,36,512]{2,1,0:T(8,128)(2,1)S(1)}, u32[]{:S(2)}, u32[]{:S(2)}) collective-permute-start(bf16[2,36,512]{2,1,0:T(8,128)(2,1)S(1)} %get-tuple-element.75), channel_id=1, source_target_pairs={{1,0},{2,1},{3,2},{5,4},{6,5},{7,6},{9,8},{10,9},{11,10},{13,12},{... | collective-permute-start | bytes 221192 | tf_op jit(solution)/shard_map/ppermute | solution.py:497
  46.8 14.7 %copy-start.6 = (bf16[2,36,512]{2,1,0:T(8,128)(2,1)}, bf16[2,36,512]{2,1,0:T(8,128)(2,1)S(1)}, u32[]{:S(2)}) copy-start(bf16[2,36,512]{2,1,0:T(8,128)(2,1)S(1)} %collective-permute-done.2.ylo_ref) | copy-start | bytes 221188
  49.0 12.5 %copy-start.7 = (bf16[2,36,512]{2,1,0:T(8,128)(2,1)}, bf16[2,36,512]{2,1,0:T(8,128)(2,1)S(1)}, u32[]{:S(2)}) copy-start(bf16[2,36,512]{2,1,0:T(8,128)(2,1)S(1)} %collective-permute-done.3.yhi_ref) | copy-start | bytes 221188
  61.5 24.4 %all-to-all-start.4 = ((bf16[32,88,128]{2,1,0:T(8,128)(2,1)}), bf16[32,88,128]{2,1,0:T(8,128)(2,1)S(1)}, u32[]{:S(2)}, u32[]{:S(2)}) async-start(bf16[32,88,128]{2,1,0:T(8,128)(2,1)} %bitcast.14), calls=%async_computation.4 | async-start | bytes 1441792 | tf_op jit(solution)/shard_map/all_to_all | solution.py:528
  67.2 18.7 %copy-start.3 = (s32[32,1,128]{2,1,0:T(1,128)S(1)}, s32[32,1,128]{2,1,0:T(1,128)}, u32[]{:S(2)}) copy-start(s32[32,1,128]{2,1,0:T(1,128)} %copy-done.2) | copy-start | bytes 49156

commit v14 on v13

--- a/solution.py
+++ b/solution.py
@@ -437,13 +437,15 @@
     matches = copies_in_parts(match_hbm, match_ref, in_sems.at[2])
     loads = copies_in_parts(field_hbm, field_ref, in_sems.at[0])
     loads += copies_in_parts(base_hbm, base_ref, in_sems.at[1])
-    for load in matches + loads:
+    for load in matches:
         load.start()
     collected_rows = [ref.reshape(ref.shape[0], LANES) for ref in collected]
     for ref in collected_rows:
         ref[...] = jnp.zeros_like(ref)
     for load in matches:
         load.wait()
+    for load in loads:
+        load.start()
     merged = rows_ref.reshape(rows_ref.shape[0], LANES)
     start = 0
     for arrived_ref in arrived_refs:
@@ -549,7 +551,9 @@
         out_specs=[VMEM, VMEM],
         name="route",
     )(block_ids.T)
-    incoming = exchange(outgoing)
+    gathered = lax.all_gather(outgoing, mesh_axes, axis=0, tiled=False)
+    me = lax.axis_index("gx") * lax.axis_size("gy") + lax.axis_index("gy")
+    incoming = lax.dynamic_index_in_dim(gathered, me, axis=1, keepdims=False)
 
     field, _ = lax.optimization_barrier((log_density, outgoing))
     xfirst, xlast, yfirst, ylast = pl.pallas_call(

time: 95.7 us -> 157 us (1.64)
  blocking collectives: 0 us -> 68.6 us
  waiting for transfers between devices: 15.3 us -> 12 us
  starting transfers between devices: 25.5 us -> 23.3 us
    all_gather x0 -> x1, blocking collectives: none -> 68.6 us  [on_device(): gathered = lax.all_gather(outgoing, mesh_axes, axis=0, tiled=False)]
    all_to_all x3 -> x2, waiting for transfers between devices: 9.77 us -> 5.54 us  [exchange(): return lax.all_to_all(x, mesh_axes, split_axis=0, concat_axis=0, tiled=True)]
    all_to_all x3 -> x2, starting transfers between devices: 15 us -> 12.6 us  [exchange(): return lax.all_to_all(x, mesh_axes, split_axis=0, concat_axis=0, tiled=True)]
  transfers between devices with their start and end apart: 7 -> 6, of which waited for: 4 -> 4; matrix products, arithmetic and copies ran while one was open for 3% -> 1% of each run, Pallas kernels for 18% -> 10%
where the time goes in v14:
time: 157 us
  blocking collectives  68.6 us (44%)
  Pallas kernels  49.2 us (31%)
  starting transfers between devices  23.3 us (15%)
  waiting for transfers between devices  12 us (8%)
  local copies, waits for them, and re-layouts  2.24 us (1%)
    all_gather x1, blocking collectives, on_device(): gathered = lax.all_gather(outgoing, mesh_axes, axis=0, tiled=False)  68.6 us
    pallas_call x1, Pallas kernels, on_device(): pl.pallas_call(prior_kernel, out_shape=shape(field_shape, f32), in_specs=...  13.1 us
    all_to_all x2, starting transfers between devices, exchange(): return lax.all_to_all(x, mesh_axes, split_axis=0, concat_axis=0, tiled=True)  12.6 us
    pallas_call x1, Pallas kernels, on_device(): pl.pallas_call(functools.partial(star_kernel, exchanges=exchanges), out_s...  12.4 us
    ppermute x4, starting transfers between devices, both_ways(): return (lax.ppermute(last, axis, up), lax.ppermute(first, axis, down))  10.7 us
    pallas_call x1, Pallas kernels, on_device(): pl.pallas_call(functools.partial(finish_kernel, exchanges=exchanges, capa...  9.1 us
    pallas_call x1, Pallas kernels, on_device(): pl.pallas_call(functools.partial(serve_kernel, capacity=capacity, first_s...  7.32 us
    ppermute x4, waiting for transfers between devices, both_ways(): return (lax.ppermute(last, axis, up), lax.ppermute(first, axis, down))  6.45 us
  transfers between devices with their start and end apart: 6, of which 4 were waited for; matrix products, arithmetic and copies ran while one was open for 1% of the time, Pallas kernels for 10%

profile of v14, /device:TPU:1, one launch (start us, length us, event | category | flops | bytes accessed | tf_op | source)
XLA Modules:
  0.0 156.9 jit_solution(5660648137493593092)
XLA Ops:
  0.6 3.1 %route.1 = (s32[32,128]{1,0:T(8,128)}, s32[16,128]{1,0:T(8,128)}) custom-call(s32[32,64]{1,0:T(8,128)} %bitcast.36), custom_call_target="tpu_custom_call" | custom-call | tf_op jit(solution)/shard_map/route/pallas_call | solution.py:540
  3.7 68.6 %all-gather = s32[1024,128]{1,0:T(8,128)S(1)} all-gather(s32[32,128]{1,0:T(8,128)} %get-tuple-element.55), channel_id=2, replica_groups=mesh['gx'=8,'gy'=4] {'gx','gy'}, dimensions={0}, use_global_device_ids=true | all-gather | bytes 540672 | tf_op jit(solution)/shard_map/all_gather | solution.py:554
  72.3 2.3 %edges.1 = (bf16[2,64,512]{2,1,0:T(8,128)(2,1)}, bf16[2,64,512]{2,1,0:T(8,128)(2,1)}, f32[2,36,512]{2,1,0:T(8,128)}, f32[2,36,512]{2,1,0:T(8,128)}) custom-call(f32[32,64,512]{2,1,0:T(8,128)} %field_hbm.3), custom_call_target="tpu_custom_call" | custom-call | bytes 2097152 | tf_op jit(solution)/shard_map/edges/pallas_call | solution.py:559
  74.6 0.0 copy-start.8
  74.7 0.6 constant_dynamic-slice_fusion
  75.3 7.3 %serve.1 = (bf16[2816,128]{1,0:T(8,128)(2,1)}, bf16[1280,128]{1,0:T(8,128)(2,1)S(1)}, s32[1]{0:T(128)}) custom-call(s32[4096]{0:T(1024)} %bitcast.22, f32[8192,1,128]{2,1,0:T(1,128)} %bitcast.26), custom_call_target="tpu_custom_call" | custom-call | flops 1048576 | bytes 6291456 | tf_op jit(solution)/shard_map/serve/pallas_call | solution.py:581
  83.2 7.8 %all-to-all-start.2 = ((bf16[32,88,128]{2,1,0:T(8,128)(2,1)}), bf16[32,88,128]{2,1,0:T(8,128)(2,1)S(1)}, u32[]{:S(2)}, u32[]{:S(2)}) async-start(bf16[32,88,128]{2,1,0:T(8,128)(2,1)} %bitcast.33), calls=%async_computation.2 | async-start | bytes 1441792 | tf_op jit(solution)/shard_map/all_to_all | solution.py:530
  91.0 3.5 %collective-permute-start = (bf16[2,64,512]{2,1,0:T(8,128)(2,1)S(1)}, bf16[2,64,512]{2,1,0:T(8,128)(2,1)S(1)}, u32[]{:S(2)}, u32[]{:S(2)}) collective-permute-start(bf16[2,64,512]{2,1,0:T(8,128)(2,1)S(1)} %copy-done.12), channel_id=1, source_target_pairs={{0,4},{4,8},{8,12},{12,16},{16,20},{20,24},{24,28},{1,5},{5,9},{9,... | collective-permute-start | bytes 393224 | tf_op jit(solution)/shard_map/ppermute | solution.py:499
  94.6 1.9 %collective-permute-start.1 = (bf16[2,64,512]{2,1,0:T(8,128)(2,1)S(1)}, bf16[2,64,512]{2,1,0:T(8,128)(2,1)S(1)}, u32[]{:S(2)}, u32[]{:S(2)}) collective-permute-start(bf16[2,64,512]{2,1,0:T(8,128)(2,1)S(1)} %copy-done.11), channel_id=1, source_target_pairs={{4,0},{8,4},{12,8},{16,12},{20,16},{24,20},{28,24},{5,1},{9,5},{13... | collective-permute-start | bytes 393224 | tf_op jit(solution)/shard_map/ppermute | solution.py:499
  96.5 0.1 slice_and_fusion
  96.6 0.1 reshape.89
  96.7 0.1 reshape.88
  96.8 0.1 reshape.90
  96.9 0.1 copy.11
  97.0 0.1 reshape.91.position_ref
  97.1 0.1 copy.13
  97.2 0.1 reshape.93.inverse_ref
  97.3 0.1 copy.12
  97.4 0.1 reshape.92.observed_ref
  97.5 0.1 collective-permute-done.xlo_ref
  97.6 4.3 %collective-permute-done.1.xhi_ref = bf16[2,64,512]{2,1,0:T(8,128)(2,1)S(1)} collective-permute-done((bf16[2,64,512]{2,1,0:T(8,128)(2,1)S(1)}, bf16[2,64,512]{2,1,0:T(8,128)(2,1)S(1)}, u32[]{:S(2)}, u32[]{:S(2)}) %collective-permute-start.1) | collective-permute-done | bytes 131104 | tf_op jit(solution)/shard_map/ppermute | solution.py:499
  101.9 3.9 %collective-permute-start.2 = (bf16[2,36,512]{2,1,0:T(8,128)(2,1)S(1)}, bf16[2,36,512]{2,1,0:T(8,128)(2,1)S(1)}, u32[]{:S(2)}, u32[]{:S(2)}) collective-permute-start(bf16[2,36,512]{2,1,0:T(8,128)(2,1)S(1)} %get-tuple-element.74), channel_id=1, source_target_pairs={{0,1},{1,2},{2,3},{4,5},{5,6},{6,7},{8,9},{9,10},{10,11},{12,13},{... | collective-permute-start | bytes 221192 | tf_op jit(solution)/shard_map/ppermute | solution.py:499
  105.8 1.3 collective-permute-start.3
  107.1 1.8 %match.1.match_hbm = bf16[4096,128]{1,0:T(8,128)(2,1)S(1)} custom-call(s32[32,128]{1,0:T(8,128)S(1)} %pad_add_fusion.incoming_ref), custom_call_target="tpu_custom_call" | custom-call | flops 1000000000 | bytes 1048576 | tf_op jit(solution)/shard_map/match/pallas_call | solution.py:617
  108.9 2.1 %collective-permute-done.3.yhi_ref = bf16[2,36,512]{2,1,0:T(8,128)(2,1)S(1)} collective-permute-done((bf16[2,36,512]{2,1,0:T(8,128)(2,1)S(1)}, bf16[2,36,512]{2,1,0:T(8,128)(2,1)S(1)}, u32[]{:S(2)}, u32[]{:S(2)}) %collective-permute-start.3) | collective-permute-done | bytes 73760 | tf_op jit(solution)/shard_map/ppermute | solution.py:499
  111.0 12.4 %stars.1 = (f32[16,128]{1,0:T(8,128)S(1)}, bf16[2816,128]{1,0:T(8,128)(2,1)}, bf16[1280,128]{1,0:T(8,128)(2,1)S(1)}) custom-call(s32[2048]{0:T(1024)S(1)} %reshape.91.position_ref, f32[16,128]{1,0:T(8,128)S(1)} %reshape.92.observed_ref, f32[16,128]{1,0:T(8,128)S(1)} %reshape.93.inverse_ref, bf16[64,32,32,128]{3,2,1,0:T(8,128)(2,1)} %weights_hbm.1, ...), custom_call_target="tpu_custom_call" | custom-call | flops 33554432 | bytes 16777216 | tf_op jit(solution)/shard_map/stars/pallas_call | solution.py:632
  123.5 4.9 %all-to-all-start.3 = ((bf16[32,88,128]{2,1,0:T(8,128)(2,1)}), bf16[32,88,128]{2,1,0:T(8,128)(2,1)S(1)}, u32[]{:S(2)}, u32[]{:S(2)}) async-start(bf16[32,88,128]{2,1,0:T(8,128)(2,1)} %bitcast.13), calls=%async_computation.3 | async-start | bytes 1441792 | tf_op jit(solution)/shard_map/all_to_all | solution.py:530
  128.3 0.1 reshape.98
  128.4 0.7 copy.14
  129.1 13.1 %prior.1.base_hbm = f32[32,64,512]{2,1,0:T(8,128)} custom-call(f32[32,64,512]{2,1,0:T(8,128)} %field_hbm.3, bf16[2,64,512]{2,1,0:T(8,128)(2,1)} %copy-done, bf16[2,64,512]{2,1,0:T(8,128)(2,1)} %copy-done.1, bf16[2,36,512]{2,1,0:T(8,128)(2,1)} %copy-done.5, bf16[2,36,512]{2,1,0:T(8,128)(2,1)} %copy-done.6), custom_call_target="tpu_custom_call" | custom-call | flops 31457280 | bytes 8388608 | tf_op jit(solution)/shard_map/prior/pallas_call | solution.py:661
  142.2 5.5 %all-to-all-done.3 = bf16[32,88,128]{2,1,0:T(8,128)(2,1)S(1)} async-done(((bf16[32,88,128]{2,1,0:T(8,128)(2,1)}), bf16[32,88,128]{2,1,0:T(8,128)(2,1)S(1)}, u32[]{:S(2)}, u32[]{:S(2)}) %all-to-all-start.3) | async-done | bytes 720928 | tf_op jit(solution)/shard_map/all_to_all | solution.py:530
  147.8 9.1 %finish.1 = f32[32,64,512]{2,1,0:T(8,128)} custom-call(s32[4096]{0:T(1024)S(1)} %bitcast.25, bf16[4096,128]{1,0:T(8,128)(2,1)S(1)} %match.1.match_hbm, f32[32,64,512]{2,1,0:T(8,128)} %field_hbm.3, f32[32,64,512]{2,1,0:T(8,128)} %prior.1.base_hbm, bf16[2816,128]{1,0:T(8,128)(2,1)S(1)} %bitcast.21, bf16[1280,128]{1,0:T(8,128)(2,1)S(1)} %bitcast.29), custom_call_target="tpu_custom_call" | custom-call | flops 4194304 | bytes 12582912 | tf_op jit(solution)/shard_map/finish/pallas_call | solution.py:681
  (32 shorter events, 0.1 us)
Async XLA Ops:
  74.6 16.4 %copy-start.12 = (bf16[2,64,512]{2,1,0:T(8,128)(2,1)S(1)}, bf16[2,64,512]{2,1,0:T(8,128)(2,1)}, u32[]{:S(2)}) copy-start(bf16[2,64,512]{2,1,0:T(8,128)(2,1)} %get-tuple-element.70) | copy-start | bytes 393220
  74.6 20.0 %copy-start.11 = (bf16[2,64,512]{2,1,0:T(8,128)(2,1)S(1)}, bf16[2,64,512]{2,1,0:T(8,128)(2,1)}, u32[]{:S(2)}) copy-start(bf16[2,64,512]{2,1,0:T(8,128)(2,1)} %get-tuple-element.71) | copy-start | bytes 393220
  74.6 21.9 %copy-start.8 = (f32[64,32]{0,1:T(8,128)S(1)}, f32[64,32]{0,1:T(8,128)}, u32[]{:S(2)}) copy-start(f32[64,32]{0,1:T(8,128)} %param.13) | copy-start | bytes 24580
  74.6 21.9 %copy-start.10 = (s32[64]{0:T(128)S(1)}, s32[64]{0:T(128)}, u32[]{:S(2)}) copy-start(s32[64]{0:T(128)} %param.14) | copy-start | bytes 772
  74.6 22.2 %copy-start.9 = (s32[16,128]{1,0:T(8,128)S(1)}, s32[16,128]{1,0:T(8,128)}, u32[]{:S(2)}) copy-start(s32[16,128]{1,0:T(8,128)} %get-tuple-element.77) | copy-start | bytes 24580
  74.6 22.6 %copy-start.7 = (f32[64,32]{0,1:T(8,128)S(1)}, f32[64,32]{0,1:T(8,128)}, u32[]{:S(2)}) copy-start(f32[64,32]{0,1:T(8,128)} %param.12) | copy-start | bytes 24580
  74.6 27.2 %copy-start.3 = (f32[2,36,512]{2,1,0:T(8,128)S(1)}, f32[2,36,512]{2,1,0:T(8,128)}, u32[]{:S(2)}) copy-start(f32[2,36,512]{2,1,0:T(8,128)} %get-tuple-element.72.yfirst_ref) | copy-start | bytes 442372
  74.7 27.2 %copy-start.4 = (f32[2,36,512]{2,1,0:T(8,128)S(1)}, f32[2,36,512]{2,1,0:T(8,128)}, u32[]{:S(2)}) copy-start(f32[2,36,512]{2,1,0:T(8,128)} %get-tuple-element.73.ylast_ref) | copy-start | bytes 442372
  75.3 21.2 %copy-start.2 = (s32[32,1,128]{2,1,0:T(1,128)S(1)}, s32[32,1,128]{2,1,0:T(1,128)}, u32[]{:S(2)}) copy-start(s32[32,1,128]{2,1,0:T(1,128)} %constant_dynamic-slice_fusion) | copy-start | bytes 49156
  83.2 27.8 %all-to-all-start.2 = ((bf16[32,88,128]{2,1,0:T(8,128)(2,1)}), bf16[32,88,128]{2,1,0:T(8,128)(2,1)S(1)}, u32[]{:S(2)}, u32[]{:S(2)}) async-start(bf16[32,88,128]{2,1,0:T(8,128)(2,1)} %bitcast.33), calls=%async_computation.2 | async-start | bytes 1441792 | tf_op jit(solution)/shard_map/all_to_all | solution.py:530
  91.0 6.6 %collective-permute-start = (bf16[2,64,512]{2,1,0:T(8,128)(2,1)S(1)}, bf16[2,64,512]{2,1,0:T(8,128)(2,1)S(1)}, u32[]{:S(2)}, u32[]{:S(2)}) collective-permute-start(bf16[2,64,512]{2,1,0:T(8,128)(2,1)S(1)} %copy-done.12), channel_id=1, source_target_pairs={{0,4},{4,8},{8,12},{12,16},{16,20},{20,24},{24,28},{1,5},{5,9},{9,... | collective-permute-start | bytes 393224 | tf_op jit(solution)/shard_map/ppermute | solution.py:499
  94.6 7.3 %collective-permute-start.1 = (bf16[2,64,512]{2,1,0:T(8,128)(2,1)S(1)}, bf16[2,64,512]{2,1,0:T(8,128)(2,1)S(1)}, u32[]{:S(2)}, u32[]{:S(2)}) collective-permute-start(bf16[2,64,512]{2,1,0:T(8,128)(2,1)S(1)} %copy-done.11), channel_id=1, source_target_pairs={{4,0},{8,4},{12,8},{16,12},{20,16},{24,20},{28,24},{5,1},{9,5},{13... | collective-permute-start | bytes 393224 | tf_op jit(solution)/shard_map/ppermute | solution.py:499
  97.6 25.8 %copy-start = (bf16[2,64,512]{2,1,0:T(8,128)(2,1)}, bf16[2,64,512]{2,1,0:T(8,128)(2,1)S(1)}, u32[]{:S(2)}) copy-start(bf16[2,64,512]{2,1,0:T(8,128)(2,1)S(1)} %collective-permute-done.xlo_ref) | copy-start | bytes 393220
  101.8 21.6 %copy-start.1 = (bf16[2,64,512]{2,1,0:T(8,128)(2,1)}, bf16[2,64,512]{2,1,0:T(8,128)(2,1)S(1)}, u32[]{:S(2)}) copy-start(bf16[2,64,512]{2,1,0:T(8,128)(2,1)S(1)} %collective-permute-done.1.xhi_ref) | copy-start | bytes 393220
  101.9 7.0 %collective-permute-start.2 = (bf16[2,36,512]{2,1,0:T(8,128)(2,1)S(1)}, bf16[2,36,512]{2,1,0:T(8,128)(2,1)S(1)}, u32[]{:S(2)}, u32[]{:S(2)}) collective-permute-start(bf16[2,36,512]{2,1,0:T(8,128)(2,1)S(1)} %get-tuple-element.74), channel_id=1, source_target_pairs={{0,1},{1,2},{2,3},{4,5},{5,6},{6,7},{8,9},{9,10},{10,11},{12,13},{... | collective-permute-start | bytes 221192 | tf_op jit(solution)/shard_map/ppermute | solution.py:499
  105.8 5.2 %collective-permute-start.3 = (bf16[2,36,512]{2,1,0:T(8,128)(2,1)S(1)}, bf16[2,36,512]{2,1,0:T(8,128)(2,1)S(1)}, u32[]{:S(2)}, u32[]{:S(2)}) collective-permute-start(bf16[2,36,512]{2,1,0:T(8,128)(2,1)S(1)} %get-tuple-element.75), channel_id=1, source_target_pairs={{1,0},{2,1},{3,2},{5,4},{6,5},{7,6},{9,8},{10,9},{11,10},{13,12},{... | collective-permute-start | bytes 221192 | tf_op jit(solution)/shard_map/ppermute | solution.py:499
  108.9 14.5 %copy-start.5 = (bf16[2,36,512]{2,1,0:T(8,128)(2,1)}, bf16[2,36,512]{2,1,0:T(8,128)(2,1)S(1)}, u32[]{:S(2)}) copy-start(bf16[2,36,512]{2,1,0:T(8,128)(2,1)S(1)} %collective-permute-done.2.ylo_ref) | copy-start | bytes 221188
  111.0 12.5 %copy-start.6 = (bf16[2,36,512]{2,1,0:T(8,128)(2,1)}, bf16[2,36,512]{2,1,0:T(8,128)(2,1)S(1)}, u32[]{:S(2)}) copy-start(bf16[2,36,512]{2,1,0:T(8,128)(2,1)S(1)} %collective-permute-done.3.yhi_ref) | copy-start | bytes 221188
  123.5 24.3 %all-to-all-start.3 = ((bf16[32,88,128]{2,1,0:T(8,128)(2,1)}), bf16[32,88,128]{2,1,0:T(8,128)(2,1)S(1)}, u32[]{:S(2)}, u32[]{:S(2)}) async-start(bf16[32,88,128]{2,1,0:T(8,128)(2,1)} %bitcast.13), calls=%async_computation.3 | async-start | bytes 1441792 | tf_op jit(solution)/shard_map/all_to_all | solution.py:530

commit v15 on v13

--- a/solution.py
+++ b/solution.py
@@ -79,28 +79,31 @@
     outgoing_ref[...] = listed
 
 
-def edges_kernel(
-    field_hbm, xfirst_ref, xlast_ref, yfirst_ref, ylast_ref, planes_ref, strips_ref, sems
-):
-    cells_x, cells_y, _ = field_hbm.shape
-    copies = [
-        pltpu.make_async_copy(field_hbm.at[pl.ds(0, 2)], planes_ref.at[0], sems.at[0]),
-        pltpu.make_async_copy(field_hbm.at[pl.ds(cells_x - 2, 2)], planes_ref.at[1], sems.at[1]),
-        pltpu.make_async_copy(field_hbm.at[:, pl.ds(0, 8)], strips_ref.at[0], sems.at[2]),
-        pltpu.make_async_copy(
-            field_hbm.at[:, pl.ds(cells_y - 8, 8)], strips_ref.at[1], sems.at[3]
-        ),
-    ]
-    for copy in copies:
-        copy.start()
-    for copy in copies:
-        copy.wait()
-    xfirst_ref[...] = planes_ref[0].astype(xfirst_ref.dtype)
-    xlast_ref[...] = planes_ref[1].astype(xlast_ref.dtype)
-    for h in range(2):
-        for x in range(cells_x):
-            yfirst_ref[h, x + 2 : x + 3, :] = strips_ref[0, x, h : h + 1, :]
-            ylast_ref[h, x + 2 : x + 3, :] = strips_ref[1, x, 6 + h : 7 + h, :]
+def table_kernel(field_ref, table_ref, xfirst_ref, xlast_ref, yfirst_ref, ylast_ref):
+    cells_x, cells_y, depth = field_ref.shape
+    per_column = depth // LANES
+    blocks = cells_x * cells_y * per_column
+    xfirst_ref[...] = field_ref[:2].astype(xfirst_ref.dtype)
+    xlast_ref[...] = field_ref[cells_x - 2 :].astype(xlast_ref.dtype)
+
+    def one_plane(x, carry):
+        for yb in range(cells_y // 8):
+            for part in range(0, per_column, 2):
+                at = pl.multiple_of(((x * (cells_y // 8) + yb) * per_column + part) * 8, 16)
+                both = [
+                    field_ref[x, 8 * yb : 8 * yb + 8, p * LANES : (p + 1) * LANES]
+                    for p in (part, part + 1)
+                ]
+                rows = jnp.exp(jnp.concatenate(both, axis=0))
+                table_ref[pl.ds(at, 16), :] = rows.astype(table_ref.dtype)
+        for h in range(2):
+            yfirst_ref[h, pl.ds(x + 2, 1), :] = field_ref[x, h : h + 1, :]
+            ylast_ref[h, pl.ds(x + 2, 1), :] = field_ref[x, cells_y - 2 + h : cells_y - 1 + h, :]
+        return carry
+
+    lax.fori_loop(0, cells_x, one_plane, 0)
+    pad = table_ref.shape[0] - blocks
+    table_ref[blocks:, :] = jnp.zeros((pad, LANES), table_ref.dtype)
 
 
 def ends_kernel(
@@ -172,22 +175,15 @@
     lax.fori_loop(0, sources, one_source, 0)
 
 
-def serve_kernel(incoming_ref, field_hbm, *refs, capacity, first_slots):
-    *served_refs, crowded_ref, rows_ref, found_ref, sems = refs
-    blocks = field_hbm.shape[0]
-    loads = copies_in_parts(field_hbm, rows_ref, sems)
-    for load in loads:
-        load.start()
+def serve_kernel(incoming_ref, table_ref, *refs, capacity, first_slots, blocks):
+    *served_refs, crowded_ref, rows_ref, found_ref = refs
 
     def mark_of(source, most):
         return jnp.maximum(most, incoming_ref[source * capacity + capacity - 1] >> 16)
 
     fullest = lax.fori_loop(0, incoming_ref.shape[0] // capacity, mark_of, jnp.int32(0))
     crowded_ref[0] = jnp.where(fullest > first_slots, 1, 0)
-    rows_ref[blocks:] = jnp.zeros((rows_ref.shape[0] - blocks, 1, LANES), jnp.float32)
-    for load in loads:
-        load.wait()
-
+    rows_ref.reshape(rows_ref.shape[0], LANES)[...] = table_ref[...].astype(jnp.float32)
     part_starts = [0, served_refs[0].shape[0]]
 
     def visit(wanted, row, list_part, which):
@@ -200,7 +196,7 @@
     found = found_ref.reshape(found_ref.shape[0], LANES)
     for start, served_ref in zip(part_starts, served_refs):
         span = slice(start, start + served_ref.shape[0])
-        served_ref[...] = jnp.exp(found[span, :]).astype(jnp.bfloat16)
+        served_ref[...] = found[span, :].astype(jnp.bfloat16)
 
 
 def match_kernel(incoming_ref, match_ref):
@@ -520,10 +516,6 @@
     f32, bf16, i32 = jnp.float32, jnp.bfloat16, jnp.int32
     shape = jax.ShapeDtypeStruct
 
-    def to_rows(x):
-        x = x.reshape(cells_x, cells_y // 8, 8, per_column, width)
-        return x.transpose(0, 1, 3, 2, 4).reshape(blocks, 1, width)
-
     def exchange(x):
         return lax.all_to_all(x, mesh_axes, split_axis=0, concat_axis=0, tiled=True)
 
@@ -552,44 +544,43 @@
     incoming = exchange(outgoing)
 
     field, _ = lax.optimization_barrier((log_density, outgoing))
-    xfirst, xlast, yfirst, ylast = pl.pallas_call(
-        edges_kernel,
+    table, xfirst, xlast, yfirst, ylast = pl.pallas_call(
+        table_kernel,
         out_shape=[
+            shape((blocks + capacity, width), bf16),
             shape((2, cells_y, depth), bf16),
             shape((2, cells_y, depth), bf16),
             shape((2, cells_x + 4, depth), f32),
             shape((2, cells_x + 4, depth), f32),
         ],
-        in_specs=[ANY],
-        out_specs=[VMEM] * 4,
-        scratch_shapes=[
-            pltpu.VMEM((2, 2, cells_y, depth), f32),
-            pltpu.VMEM((2, cells_x, 8, depth), f32),
-            pltpu.SemaphoreType.DMA((4,)),
-        ],
-        compiler_params=pltpu.CompilerParams(vmem_limit_bytes=56 * MIB),
-        cost_estimate=pl.CostEstimate(flops=0, bytes_accessed=2 * MIB, transcendentals=0),
-        name="edges",
+        in_specs=[VMEM],
+        out_specs=[VMEM] * 5,
+        compiler_params=pltpu.CompilerParams(vmem_limit_bytes=16 * MIB),
+        cost_estimate=pl.CostEstimate(
+            flops=8 * cells, bytes_accessed=8 * cells, transcendentals=cells
+        ),
+        name="table",
     )(field)
     incoming, *edges = lax.optimization_barrier((incoming, xfirst, xlast, yfirst, ylast))
     wanted = incoming.reshape(-1)
 
     *served, crowded = pl.pallas_call(
-        functools.partial(serve_kernel, capacity=capacity, first_slots=first_slots),
+        functools.partial(
+            serve_kernel, capacity=capacity, first_slots=first_slots, blocks=blocks
+        ),
         out_shape=[shape((devices * n, width), bf16) for n in slots_of] + [shape((1,), i32)],
-        in_specs=[SMEM, ANY],
+        in_specs=[SMEM, VMEM],
         out_specs=[VMEM] * exchanges + [SMEM],
         scratch_shapes=[
             pltpu.VMEM((blocks + capacity, 1, width), f32),
             pltpu.VMEM((all_slots, 1, width), f32),
-            pltpu.SemaphoreType.DMA((16,)),
         ],
-        compiler_params=pltpu.CompilerParams(vmem_limit_bytes=56 * MIB),
+        compiler_params=pltpu.CompilerParams(vmem_limit_bytes=24 * MIB),
         cost_estimate=pl.CostEstimate(
             flops=cells, bytes_accessed=6 * MIB, transcendentals=cells
         ),
         name="serve",
-    )(wanted, to_rows(log_density))
+    )(wanted, table)
     crowded = crowded[0] != 0
 
     returned = exchange_rows(served, crowded)

time: 95.7 us -> 93 us (0.972)
  Pallas kernels: 48.8 us -> 45.5 us
    pallas_call x1, Pallas kernels: 7.09 us -> 5.15 us  [on_device(): pl.pallas_call(functools.partial(serve_kernel, capacity=capacity, first_s...]
    unnamed x30 -> x20, local copies, waits for them, and re-layouts: 1.42 us -> 2.98 us
    ppermute x4, waiting for transfers between devices: 5.52 us -> 6.99 us  [both_ways(): return (lax.ppermute(last, axis, up), lax.ppermute(first, axis, down))]
    pallas_call x1, Pallas kernels: 2.27 us -> 0.88 us  [on_device(): pl.pallas_call(table_kernel, out_shape=[shape((blocks + capacity, width),...]
  transfers between devices with their start and end apart: 7 -> 7, of which waited for: 4 -> 5; matrix products, arithmetic and copies ran while one was open for 3% -> 2% of each run, Pallas kernels for 18% -> 17%
where the time goes in v15:
time: 93 us; the launch traced here: 92.5 us
  Pallas kernels  45.5 us (49%)
  starting transfers between devices  25.6 us (28%)
  waiting for transfers between devices  16.1 us (17%)
  local copies, waits for them, and re-layouts  3.75 us (4%)
  between operations  1.5 us (2%)
    all_to_all x3, starting transfers between devices, exchange(): return lax.all_to_all(x, mesh_axes, split_axis=0, concat_axis=0, tiled=True)  15.1 us
    pallas_call x1, Pallas kernels, on_device(): pl.pallas_call(prior_kernel, out_shape=shape(field_shape, f32), in_specs=...  13.1 us
    pallas_call x1, Pallas kernels, on_device(): pl.pallas_call(functools.partial(star_kernel, exchanges=exchanges), out_s...  12.4 us
    ppermute x4, starting transfers between devices, both_ways(): return (lax.ppermute(last, axis, up), lax.ppermute(first, axis, down))  10.4 us
    all_to_all x3, waiting for transfers between devices, exchange(): return lax.all_to_all(x, mesh_axes, split_axis=0, concat_axis=0, tiled=True)  9.06 us
    pallas_call x1, Pallas kernels, on_device(): pl.pallas_call(functools.partial(finish_kernel, exchanges=exchanges, capa...  8.99 us
    ppermute x4, waiting for transfers between devices, both_ways(): return (lax.ppermute(last, axis, up), lax.ppermute(first, axis, down))  6.99 us
    pallas_call x1, Pallas kernels, on_device(): pl.pallas_call(functools.partial(serve_kernel, capacity=capacity, first_s...  5.15 us
  transfers between devices with their start and end apart: 7, of which 5 were waited for; matrix products, arithmetic and copies ran while one was open for 2% of the time, Pallas kernels for 17%

profile of v15, /device:TPU:1, one launch (start us, length us, event | category | flops | bytes accessed | tf_op | source)
XLA Modules:
  0.0 92.5 jit_solution(16050641442650676519)
XLA Ops:
  0.6 3.1 %route.1 = (s32[32,128]{1,0:T(8,128)}, s32[16,128]{1,0:T(8,128)}) custom-call(s32[32,64]{1,0:T(8,128)} %bitcast.30), custom_call_target="tpu_custom_call" | custom-call | tf_op jit(solution)/shard_map/route/pallas_call | solution.py:530
  3.7 7.1 %all-to-all-start.2 = ((s32[32,1,128]{2,1,0:T(1,128)}), s32[32,1,128]{2,1,0:T(1,128)S(1)}, u32[]{:S(2)}, u32[]{:S(2)}) async-start(s32[32,1,128]{2,1,0:T(1,128)} %bitcast.31), calls=%async_computation.2 | async-start | bytes 32768 | tf_op jit(solution)/shard_map/all_to_all | solution.py:520
  10.8 2.2 %copy-done = f32[32,64,512]{2,1,0:T(8,128)S(1)} copy-done((f32[32,64,512]{2,1,0:T(8,128)S(1)}, f32[32,64,512]{2,1,0:T(8,128)}, u32[]{:S(2)}) %copy-start) | copy-done | bytes 4194328
  13.0 0.9 table.1
  13.9 3.5 %all-to-all-done.2 = s32[32,1,128]{2,1,0:T(1,128)S(1)} async-done(((s32[32,1,128]{2,1,0:T(1,128)}), s32[32,1,128]{2,1,0:T(1,128)S(1)}, u32[]{:S(2)}, u32[]{:S(2)}) %all-to-all-start.2) | async-done | bytes 16416 | tf_op jit(solution)/shard_map/all_to_all | solution.py:520
  17.4 5.2 %serve.1 = (bf16[2816,128]{1,0:T(8,128)(2,1)}, bf16[1280,128]{1,0:T(8,128)(2,1)S(1)}, s32[1]{0:T(128)}) custom-call(s32[4096]{0:T(1024)S(1)} %bitcast.19, bf16[8320,128]{1,0:T(8,128)(2,1)S(1)} %get-tuple-element.63.table_ref), custom_call_target="tpu_custom_call" | custom-call | flops 1048576 | bytes 6291456 | tf_op jit(solution)/shard_map/serve/pallas_call | solution.py:567
  23.3 3.1 %all-to-all-start.3 = ((bf16[32,88,128]{2,1,0:T(8,128)(2,1)}), bf16[32,88,128]{2,1,0:T(8,128)(2,1)S(1)}, u32[]{:S(2)}, u32[]{:S(2)}) async-start(bf16[32,88,128]{2,1,0:T(8,128)(2,1)} %bitcast.5), calls=%async_computation.3 | async-start | bytes 1441792 | tf_op jit(solution)/shard_map/all_to_all | solution.py:520
  26.4 0.1 reshape.84
  26.4 0.1 copy.16
  26.5 0.1 reshape.85.position_ref
  26.7 0.1 copy.18
  26.8 0.1 reshape.87.inverse_ref
  26.8 0.1 copy.17
  26.9 0.1 reshape.86.observed_ref
  27.0 3.5 %collective-permute-start = (bf16[2,64,512]{2,1,0:T(8,128)(2,1)S(1)}, bf16[2,64,512]{2,1,0:T(8,128)(2,1)S(1)}, u32[]{:S(2)}, u32[]{:S(2)}) collective-permute-start(bf16[2,64,512]{2,1,0:T(8,128)(2,1)S(1)} %get-tuple-element.72), channel_id=1, source_target_pairs={{0,4},{4,8},{8,12},{12,16},{16,20},{20,24},{24,28},{1,5},{5,9},{9,... | collective-permute-start | bytes 393224 | tf_op jit(solution)/shard_map/ppermute | solution.py:493
  30.6 1.9 %collective-permute-start.1 = (bf16[2,64,512]{2,1,0:T(8,128)(2,1)S(1)}, bf16[2,64,512]{2,1,0:T(8,128)(2,1)S(1)}, u32[]{:S(2)}, u32[]{:S(2)}) collective-permute-start(bf16[2,64,512]{2,1,0:T(8,128)(2,1)S(1)} %get-tuple-element.73), channel_id=1, source_target_pairs={{4,0},{8,4},{12,8},{16,12},{20,16},{24,20},{28,24},{5,1},{9,5},{13... | collective-permute-start | bytes 393224 | tf_op jit(solution)/shard_map/ppermute | solution.py:493
  32.5 0.1 slice_and_fusion
  32.6 0.1 reshape.83
  32.6 0.1 reshape.82
  32.8 1.0 %collective-permute-done.xlo_ref = bf16[2,64,512]{2,1,0:T(8,128)(2,1)S(1)} collective-permute-done((bf16[2,64,512]{2,1,0:T(8,128)(2,1)S(1)}, bf16[2,64,512]{2,1,0:T(8,128)(2,1)S(1)}, u32[]{:S(2)}, u32[]{:S(2)}) %collective-permute-start) | collective-permute-done | bytes 131104 | tf_op jit(solution)/shard_map/ppermute | solution.py:493
  33.7 3.8 %collective-permute-done.1.xhi_ref = bf16[2,64,512]{2,1,0:T(8,128)(2,1)S(1)} collective-permute-done((bf16[2,64,512]{2,1,0:T(8,128)(2,1)S(1)}, bf16[2,64,512]{2,1,0:T(8,128)(2,1)S(1)}, u32[]{:S(2)}, u32[]{:S(2)}) %collective-permute-start.1) | collective-permute-done | bytes 131104 | tf_op jit(solution)/shard_map/ppermute | solution.py:493
  37.6 3.7 %collective-permute-start.2 = (bf16[2,36,512]{2,1,0:T(8,128)(2,1)S(1)}, bf16[2,36,512]{2,1,0:T(8,128)(2,1)S(1)}, u32[]{:S(2)}, u32[]{:S(2)}) collective-permute-start(bf16[2,36,512]{2,1,0:T(8,128)(2,1)S(1)} %get-tuple-element.76), channel_id=1, source_target_pairs={{0,1},{1,2},{2,3},{4,5},{5,6},{6,7},{8,9},{9,10},{10,11},{12,13},{... | collective-permute-start | bytes 221192 | tf_op jit(solution)/shard_map/ppermute | solution.py:493
  41.3 1.3 %collective-permute-start.3 = (bf16[2,36,512]{2,1,0:T(8,128)(2,1)S(1)}, bf16[2,36,512]{2,1,0:T(8,128)(2,1)S(1)}, u32[]{:S(2)}, u32[]{:S(2)}) collective-permute-start(bf16[2,36,512]{2,1,0:T(8,128)(2,1)S(1)} %get-tuple-element.77), channel_id=1, source_target_pairs={{1,0},{2,1},{3,2},{5,4},{6,5},{7,6},{9,8},{10,9},{11,10},{13,12},{... | collective-permute-start | bytes 221192 | tf_op jit(solution)/shard_map/ppermute | solution.py:493
  42.6 1.8 %match.1.match_hbm = bf16[4096,128]{1,0:T(8,128)(2,1)S(1)} custom-call(s32[32,128]{1,0:T(8,128)S(1)} %pad_add_fusion.incoming_ref), custom_call_target="tpu_custom_call" | custom-call | flops 1000000000 | bytes 1048576 | tf_op jit(solution)/shard_map/match/pallas_call | solution.py:604
  44.4 2.2 %collective-permute-done.3.yhi_ref = bf16[2,36,512]{2,1,0:T(8,128)(2,1)S(1)} collective-permute-done((bf16[2,36,512]{2,1,0:T(8,128)(2,1)S(1)}, bf16[2,36,512]{2,1,0:T(8,128)(2,1)S(1)}, u32[]{:S(2)}, u32[]{:S(2)}) %collective-permute-start.3) | collective-permute-done | bytes 73760 | tf_op jit(solution)/shard_map/ppermute | solution.py:493
  46.6 12.4 %stars.1 = (f32[16,128]{1,0:T(8,128)S(1)}, bf16[2816,128]{1,0:T(8,128)(2,1)}, bf16[1280,128]{1,0:T(8,128)(2,1)S(1)}) custom-call(s32[2048]{0:T(1024)S(1)} %reshape.85.position_ref, f32[16,128]{1,0:T(8,128)S(1)} %reshape.86.observed_ref, f32[16,128]{1,0:T(8,128)S(1)} %reshape.87.inverse_ref, bf16[64,32,32,128]{3,2,1,0:T(8,128)(2,1)} %weights_hbm.1, ...), custom_call_target="tpu_custom_call" | custom-call | flops 33554432 | bytes 16777216 | tf_op jit(solution)/shard_map/stars/pallas_call | solution.py:619
  59.1 4.9 %all-to-all-start.4 = ((bf16[32,88,128]{2,1,0:T(8,128)(2,1)}), bf16[32,88,128]{2,1,0:T(8,128)(2,1)S(1)}, u32[]{:S(2)}, u32[]{:S(2)}) async-start(bf16[32,88,128]{2,1,0:T(8,128)(2,1)} %bitcast.11), calls=%async_computation.4 | async-start | bytes 1441792 | tf_op jit(solution)/shard_map/all_to_all | solution.py:520
  64.0 0.1 reshape.92
  64.1 0.7 copy.19
  64.8 13.1 %prior.1.base_hbm = f32[32,64,512]{2,1,0:T(8,128)} custom-call(f32[32,64,512]{2,1,0:T(8,128)} %field_hbm.2, bf16[2,64,512]{2,1,0:T(8,128)(2,1)} %copy-done.1, bf16[2,64,512]{2,1,0:T(8,128)(2,1)} %copy-done.2, bf16[2,36,512]{2,1,0:T(8,128)(2,1)} %copy-done.3, bf16[2,36,512]{2,1,0:T(8,128)(2,1)} %copy-done.4), custom_call_target="tpu_custom_call" | custom-call | flops 31457280 | bytes 8388608 | tf_op jit(solution)/shard_map/prior/pallas_call | solution.py:648
  77.9 5.5 %all-to-all-done.4 = bf16[32,88,128]{2,1,0:T(8,128)(2,1)S(1)} async-done(((bf16[32,88,128]{2,1,0:T(8,128)(2,1)}), bf16[32,88,128]{2,1,0:T(8,128)(2,1)S(1)}, u32[]{:S(2)}, u32[]{:S(2)}) %all-to-all-start.4) | async-done | bytes 720928 | tf_op jit(solution)/shard_map/all_to_all | solution.py:520
  83.5 9.0 %finish.1 = f32[32,64,512]{2,1,0:T(8,128)} custom-call(s32[4096]{0:T(1024)S(1)} %bitcast.22, bf16[4096,128]{1,0:T(8,128)(2,1)S(1)} %match.1.match_hbm, f32[32,64,512]{2,1,0:T(8,128)} %field_hbm.2, f32[32,64,512]{2,1,0:T(8,128)} %prior.1.base_hbm, bf16[2816,128]{1,0:T(8,128)(2,1)S(1)} %bitcast.18, bf16[1280,128]{1,0:T(8,128)(2,1)S(1)} %bitcast.28), custom_call_target="tpu_custom_call" | custom-call | flops 4194304 | bytes 12582912 | tf_op jit(solution)/shard_map/finish/pallas_call | solution.py:668
  (24 shorter events, 0.1 us)
Async XLA Ops:
  3.7 13.7 %all-to-all-start.2 = ((s32[32,1,128]{2,1,0:T(1,128)}), s32[32,1,128]{2,1,0:T(1,128)S(1)}, u32[]{:S(2)}, u32[]{:S(2)}) async-start(s32[32,1,128]{2,1,0:T(1,128)} %bitcast.31), calls=%async_computation.2 | async-start | bytes 32768 | tf_op jit(solution)/shard_map/all_to_all | solution.py:520
  10.8 2.2 %copy-start = (f32[32,64,512]{2,1,0:T(8,128)S(1)}, f32[32,64,512]{2,1,0:T(8,128)}, u32[]{:S(2)}) copy-start(f32[32,64,512]{2,1,0:T(8,128)} %field_hbm.2) | copy-start | bytes 12582916
  13.0 13.3 %copy-start.7 = (s32[16,128]{1,0:T(8,128)S(1)}, s32[16,128]{1,0:T(8,128)}, u32[]{:S(2)}) copy-start(s32[16,128]{1,0:T(8,128)} %get-tuple-element.79) | copy-start | bytes 24580
  13.0 13.7 %copy-start.6 = (f32[64,32]{0,1:T(8,128)S(1)}, f32[64,32]{0,1:T(8,128)}, u32[]{:S(2)}) copy-start(f32[64,32]{0,1:T(8,128)} %param.13) | copy-start | bytes 24580
  13.0 13.7 %copy-start.8 = (s32[64]{0:T(128)S(1)}, s32[64]{0:T(128)}, u32[]{:S(2)}) copy-start(s32[64]{0:T(128)} %param.14) | copy-start | bytes 772
  13.0 13.8 %copy-start.5 = (f32[64,32]{0,1:T(8,128)S(1)}, f32[64,32]{0,1:T(8,128)}, u32[]{:S(2)}) copy-start(f32[64,32]{0,1:T(8,128)} %param.12) | copy-start | bytes 24580
  23.3 23.3 %all-to-all-start.3 = ((bf16[32,88,128]{2,1,0:T(8,128)(2,1)}), bf16[32,88,128]{2,1,0:T(8,128)(2,1)S(1)}, u32[]{:S(2)}, u32[]{:S(2)}) async-start(bf16[32,88,128]{2,1,0:T(8,128)(2,1)} %bitcast.5), calls=%async_computation.3 | async-start | bytes 1441792 | tf_op jit(solution)/shard_map/all_to_all | solution.py:520
  27.0 6.7 %collective-permute-start = (bf16[2,64,512]{2,1,0:T(8,128)(2,1)S(1)}, bf16[2,64,512]{2,1,0:T(8,128)(2,1)S(1)}, u32[]{:S(2)}, u32[]{:S(2)}) collective-permute-start(bf16[2,64,512]{2,1,0:T(8,128)(2,1)S(1)} %get-tuple-element.72), channel_id=1, source_target_pairs={{0,4},{4,8},{8,12},{12,16},{16,20},{20,24},{24,28},{1,5},{5,9},{9,... | collective-permute-start | bytes 393224 | tf_op jit(solution)/shard_map/ppermute | solution.py:493
  30.6 7.0 %collective-permute-start.1 = (bf16[2,64,512]{2,1,0:T(8,128)(2,1)S(1)}, bf16[2,64,512]{2,1,0:T(8,128)(2,1)S(1)}, u32[]{:S(2)}, u32[]{:S(2)}) collective-permute-start(bf16[2,64,512]{2,1,0:T(8,128)(2,1)S(1)} %get-tuple-element.73), channel_id=1, source_target_pairs={{4,0},{8,4},{12,8},{16,12},{20,16},{24,20},{28,24},{5,1},{9,5},{13... | collective-permute-start | bytes 393224 | tf_op jit(solution)/shard_map/ppermute | solution.py:493
  33.7 25.3 %copy-start.1 = (bf16[2,64,512]{2,1,0:T(8,128)(2,1)}, bf16[2,64,512]{2,1,0:T(8,128)(2,1)S(1)}, u32[]{:S(2)}) copy-start(bf16[2,64,512]{2,1,0:T(8,128)(2,1)S(1)} %collective-permute-done.xlo_ref) | copy-start | bytes 393220
  37.6 21.5 %copy-start.2 = (bf16[2,64,512]{2,1,0:T(8,128)(2,1)}, bf16[2,64,512]{2,1,0:T(8,128)(2,1)S(1)}, u32[]{:S(2)}) copy-start(bf16[2,64,512]{2,1,0:T(8,128)(2,1)S(1)} %collective-permute-done.1.xhi_ref) | copy-start | bytes 393220
  37.6 6.8 %collective-permute-start.2 = (bf16[2,36,512]{2,1,0:T(8,128)(2,1)S(1)}, bf16[2,36,512]{2,1,0:T(8,128)(2,1)S(1)}, u32[]{:S(2)}, u32[]{:S(2)}) collective-permute-start(bf16[2,36,512]{2,1,0:T(8,128)(2,1)S(1)} %get-tuple-element.76), channel_id=1, source_target_pairs={{0,1},{1,2},{2,3},{4,5},{5,6},{6,7},{8,9},{9,10},{10,11},{12,13},{... | collective-permute-start | bytes 221192 | tf_op jit(solution)/shard_map/ppermute | solution.py:493
  41.3 5.3 %collective-permute-start.3 = (bf16[2,36,512]{2,1,0:T(8,128)(2,1)S(1)}, bf16[2,36,512]{2,1,0:T(8,128)(2,1)S(1)}, u32[]{:S(2)}, u32[]{:S(2)}) collective-permute-start(bf16[2,36,512]{2,1,0:T(8,128)(2,1)S(1)} %get-tuple-element.77), channel_id=1, source_target_pairs={{1,0},{2,1},{3,2},{5,4},{6,5},{7,6},{9,8},{10,9},{11,10},{13,12},{... | collective-permute-start | bytes 221192 | tf_op jit(solution)/shard_map/ppermute | solution.py:493
  44.4 14.7 %copy-start.3 = (bf16[2,36,512]{2,1,0:T(8,128)(2,1)}, bf16[2,36,512]{2,1,0:T(8,128)(2,1)S(1)}, u32[]{:S(2)}) copy-start(bf16[2,36,512]{2,1,0:T(8,128)(2,1)S(1)} %collective-permute-done.2.ylo_ref) | copy-start | bytes 221188
  46.6 12.5 %copy-start.4 = (bf16[2,36,512]{2,1,0:T(8,128)(2,1)}, bf16[2,36,512]{2,1,0:T(8,128)(2,1)S(1)}, u32[]{:S(2)}) copy-start(bf16[2,36,512]{2,1,0:T(8,128)(2,1)S(1)} %collective-permute-done.3.yhi_ref) | copy-start | bytes 221188
  59.1 24.4 %all-to-all-start.4 = ((bf16[32,88,128]{2,1,0:T(8,128)(2,1)}), bf16[32,88,128]{2,1,0:T(8,128)(2,1)S(1)}, u32[]{:S(2)}, u32[]{:S(2)}) async-start(bf16[32,88,128]{2,1,0:T(8,128)(2,1)} %bitcast.11), calls=%async_computation.4 | async-start | bytes 1441792 | tf_op jit(solution)/shard_map/all_to_all | solution.py:520

commit v16 on v15

--- a/solution.py
+++ b/solution.py
@@ -32,40 +32,52 @@
 ):
     half = ids_ref.shape[0] // 2
     ids = jnp.concatenate([ids_ref[:half, :], ids_ref[half:, :]], axis=1)
+    target, local = split_by(ids, blocks)
+    column, part = split_by(local, per_column)
+    local = ((column >> 3) * per_column + part) * 8 + (column & 7)
+    high = ((local >> 7) + 1).astype(jnp.float32)
+    low = (local & 127).astype(jnp.float32)
     lane = lax.broadcasted_iota(jnp.int32, (LANES, LANES), 1)
     row = lax.broadcasted_iota(jnp.int32, (LANES, LANES), 0)
-    upper = jnp.where(row <= lane, 1.0, 0.0).astype(jnp.bfloat16)
+    upper = jnp.where(row <= lane, 1.0, 0.0)
+    sums = jnp.concatenate([upper, jnp.ones_like(upper)], axis=1).astype(jnp.bfloat16)
     tile_no = lax.broadcasted_iota(jnp.int32, (devices, LANES), 0)
     slot_no = lax.broadcasted_iota(jnp.int32, (capacity, LANES), 0)
-    before = jnp.zeros((devices, 1), jnp.float32)
-    lists = jnp.zeros((2 * devices, capacity), jnp.float32)
-    for chunk in range(half):
-        target, local = split_by(ids[chunk : chunk + 1, :], blocks)
-        column, part = split_by(local, per_column)
-        local = ((column >> 3) * per_column + part) * 8 + (column & 7)
-        hit = tile_no == target
-        onehot = jnp.where(hit, 1.0, 0.0)
-        upto = before + jnp.dot(
-            onehot.astype(jnp.bfloat16), upper, preferred_element_type=jnp.float32
+    hits = [tile_no == target[c : c + 1, :] for c in range(half)]
+    onehots = [jnp.where(hit, 1.0, 0.0) for hit in hits]
+    counts = jnp.dot(
+        jnp.concatenate(onehots, axis=0).astype(jnp.bfloat16),
+        sums,
+        preferred_element_type=jnp.float32,
+    )
+    before = jnp.zeros((devices, LANES), jnp.float32)
+    ranks, digits, in_slots = [], [], []
+    for c in range(half):
+        here = slice(c * devices, (c + 1) * devices)
+        upto = before + counts[here, :LANES]
+        before = before + counts[here, LANES:]
+        rank = jnp.sum(onehots[c] * upto, axis=0, keepdims=True).astype(jnp.int32) - 1
+        ranks.append(rank)
+        in_slots.append(jnp.where(slot_no == rank, 1.0, 0.0))
+        digits.append(
+            jnp.concatenate(
+                [jnp.where(hits[c], x[c : c + 1, :], 0.0) for x in (high, low)], axis=0
+            )
         )
-        before = upto[:, LANES - 1 :]
-        rank = jnp.sum(onehot * upto, axis=0, keepdims=True).astype(jnp.int32) - 1
-        in_slot = jnp.where(slot_no == rank, 1.0, 0.0).astype(jnp.bfloat16)
-        high = ((local >> 7) + 1).astype(jnp.float32)
-        low = (local & 127).astype(jnp.float32)
-        digits = jnp.concatenate([jnp.where(hit, high, 0.0), jnp.where(hit, low, 0.0)], axis=0)
-        lists = lists + lax.dot_general(
-            digits.astype(jnp.bfloat16),
-            in_slot,
-            CONTRACT_LANES,
-            preferred_element_type=jnp.float32,
-        )
-        last_slots = capacity - first_slots
-        position_ref[chunk : chunk + 1, :] = jnp.where(
-            rank < first_slots,
-            target * first_slots + rank,
-            devices * first_slots + target * last_slots + rank - first_slots,
-        )
+    lists = lax.dot_general(
+        jnp.concatenate(digits, axis=1).astype(jnp.bfloat16),
+        jnp.concatenate(in_slots, axis=1).astype(jnp.bfloat16),
+        CONTRACT_LANES,
+        preferred_element_type=jnp.float32,
+    )
+    rank = jnp.concatenate(ranks, axis=0)
+    last_slots = capacity - first_slots
+    position_ref[...] = jnp.where(
+        rank < first_slots,
+        target * first_slots + rank,
+        devices * first_slots + target * last_slots + rank - first_slots,
+    )
+    before = before[:, :1]
     high, low = lists[:devices], lists[devices:]
     wanted = ((high - 1.0) * 128.0 + low).astype(jnp.int32)
     filled = before.astype(jnp.int32)

time: 93 us -> 91.8 us (0.987)
  Pallas kernels: 45.5 us -> 44.3 us
    pallas_call x1, Pallas kernels: 3.09 us -> 1.94 us  [on_device(): pl.pallas_call(functools.partial(route_kernel, devices=devices, capacity=...]
where the time goes in v16:
time: 91.8 us; the launch traced here: 91.2 us
  Pallas kernels  44.3 us (48%)
  starting transfers between devices  25.5 us (28%)
  waiting for transfers between devices  16.1 us (18%)
  local copies, waits for them, and re-layouts  3.75 us (4%)
  between operations  1.5 us (2%)
    all_to_all x3, starting transfers between devices, exchange(): return lax.all_to_all(x, mesh_axes, split_axis=0, concat_axis=0, tiled=True)  15 us
    pallas_call x1, Pallas kernels, on_device(): pl.pallas_call(prior_kernel, out_shape=shape(field_shape, f32), in_specs=...  13.1 us
    pallas_call x1, Pallas kernels, on_device(): pl.pallas_call(functools.partial(star_kernel, exchanges=exchanges), out_s...  12.4 us
    ppermute x4, starting transfers between devices, both_ways(): return (lax.ppermute(last, axis, up), lax.ppermute(first, axis, down))  10.4 us
    all_to_all x3, waiting for transfers between devices, exchange(): return lax.all_to_all(x, mesh_axes, split_axis=0, concat_axis=0, tiled=True)  9.06 us
    pallas_call x1, Pallas kernels, on_device(): pl.pallas_call(functools.partial(finish_kernel, exchanges=exchanges, capa...  8.99 us
    ppermute x4, waiting for transfers between devices, both_ways(): return (lax.ppermute(last, axis, up), lax.ppermute(first, axis, down))  6.99 us
    pallas_call x1, Pallas kernels, on_device(): pl.pallas_call(functools.partial(serve_kernel, capacity=capacity, first_s...  5.15 us
  transfers between devices with their start and end apart: 7, of which 5 were waited for; matrix products, arithmetic and copies ran while one was open for 2% of the time, Pallas kernels for 17%

profile of v16, /device:TPU:1, one launch (start us, length us, event | category | flops | bytes accessed | tf_op | source)
XLA Modules:
  0.0 91.2 jit_solution(3417564991296314462)
XLA Ops:
  0.6 1.9 %route.1 = (s32[32,128]{1,0:T(8,128)}, s32[16,128]{1,0:T(8,128)}) custom-call(s32[32,64]{1,0:T(8,128)} %bitcast.30), custom_call_target="tpu_custom_call" | custom-call | tf_op jit(solution)/shard_map/route/pallas_call | solution.py:542
  2.6 7.1 %all-to-all-start.2 = ((s32[32,1,128]{2,1,0:T(1,128)}), s32[32,1,128]{2,1,0:T(1,128)S(1)}, u32[]{:S(2)}, u32[]{:S(2)}) async-start(s32[32,1,128]{2,1,0:T(1,128)} %bitcast.31), calls=%async_computation.2 | async-start | bytes 32768 | tf_op jit(solution)/shard_map/all_to_all | solution.py:532
  9.7 2.2 %copy-done = f32[32,64,512]{2,1,0:T(8,128)S(1)} copy-done((f32[32,64,512]{2,1,0:T(8,128)S(1)}, f32[32,64,512]{2,1,0:T(8,128)}, u32[]{:S(2)}) %copy-start) | copy-done | bytes 4194328
  11.9 0.9 table.1
  12.8 3.5 %all-to-all-done.2 = s32[32,1,128]{2,1,0:T(1,128)S(1)} async-done(((s32[32,1,128]{2,1,0:T(1,128)}), s32[32,1,128]{2,1,0:T(1,128)S(1)}, u32[]{:S(2)}, u32[]{:S(2)}) %all-to-all-start.2) | async-done | bytes 16416 | tf_op jit(solution)/shard_map/all_to_all | solution.py:532
  16.3 5.2 %serve.1 = (bf16[2816,128]{1,0:T(8,128)(2,1)}, bf16[1280,128]{1,0:T(8,128)(2,1)S(1)}, s32[1]{0:T(128)}) custom-call(s32[4096]{0:T(1024)S(1)} %bitcast.19, bf16[8320,128]{1,0:T(8,128)(2,1)S(1)} %get-tuple-element.63.table_ref), custom_call_target="tpu_custom_call" | custom-call | flops 1048576 | bytes 6291456 | tf_op jit(solution)/shard_map/serve/pallas_call | solution.py:579
  22.1 3.0 %all-to-all-start.3 = ((bf16[32,88,128]{2,1,0:T(8,128)(2,1)}), bf16[32,88,128]{2,1,0:T(8,128)(2,1)S(1)}, u32[]{:S(2)}, u32[]{:S(2)}) async-start(bf16[32,88,128]{2,1,0:T(8,128)(2,1)} %bitcast.5), calls=%async_computation.3 | async-start | bytes 1441792 | tf_op jit(solution)/shard_map/all_to_all | solution.py:532
  25.1 0.1 reshape.84
  25.2 0.1 copy.16
  25.3 0.1 reshape.85.position_ref
  25.4 0.1 copy.18
  25.5 0.1 reshape.87.inverse_ref
  25.6 0.1 copy.17
  25.7 0.1 reshape.86.observed_ref
  25.8 3.5 %collective-permute-start = (bf16[2,64,512]{2,1,0:T(8,128)(2,1)S(1)}, bf16[2,64,512]{2,1,0:T(8,128)(2,1)S(1)}, u32[]{:S(2)}, u32[]{:S(2)}) collective-permute-start(bf16[2,64,512]{2,1,0:T(8,128)(2,1)S(1)} %get-tuple-element.72), channel_id=1, source_target_pairs={{0,4},{4,8},{8,12},{12,16},{16,20},{20,24},{24,28},{1,5},{5,9},{9,... | collective-permute-start | bytes 393224 | tf_op jit(solution)/shard_map/ppermute | solution.py:505
  29.3 1.9 %collective-permute-start.1 = (bf16[2,64,512]{2,1,0:T(8,128)(2,1)S(1)}, bf16[2,64,512]{2,1,0:T(8,128)(2,1)S(1)}, u32[]{:S(2)}, u32[]{:S(2)}) collective-permute-start(bf16[2,64,512]{2,1,0:T(8,128)(2,1)S(1)} %get-tuple-element.73), channel_id=1, source_target_pairs={{4,0},{8,4},{12,8},{16,12},{20,16},{24,20},{28,24},{5,1},{9,5},{13... | collective-permute-start | bytes 393224 | tf_op jit(solution)/shard_map/ppermute | solution.py:505
  31.2 0.1 slice_and_fusion
  31.3 0.1 reshape.83
  31.4 0.1 reshape.82
  31.5 1.0 %collective-permute-done.xlo_ref = bf16[2,64,512]{2,1,0:T(8,128)(2,1)S(1)} collective-permute-done((bf16[2,64,512]{2,1,0:T(8,128)(2,1)S(1)}, bf16[2,64,512]{2,1,0:T(8,128)(2,1)S(1)}, u32[]{:S(2)}, u32[]{:S(2)}) %collective-permute-start) | collective-permute-done | bytes 131104 | tf_op jit(solution)/shard_map/ppermute | solution.py:505
  32.5 3.8 %collective-permute-done.1.xhi_ref = bf16[2,64,512]{2,1,0:T(8,128)(2,1)S(1)} collective-permute-done((bf16[2,64,512]{2,1,0:T(8,128)(2,1)S(1)}, bf16[2,64,512]{2,1,0:T(8,128)(2,1)S(1)}, u32[]{:S(2)}, u32[]{:S(2)}) %collective-permute-start.1) | collective-permute-done | bytes 131104 | tf_op jit(solution)/shard_map/ppermute | solution.py:505
  36.4 3.7 %collective-permute-start.2 = (bf16[2,36,512]{2,1,0:T(8,128)(2,1)S(1)}, bf16[2,36,512]{2,1,0:T(8,128)(2,1)S(1)}, u32[]{:S(2)}, u32[]{:S(2)}) collective-permute-start(bf16[2,36,512]{2,1,0:T(8,128)(2,1)S(1)} %get-tuple-element.76), channel_id=1, source_target_pairs={{0,1},{1,2},{2,3},{4,5},{5,6},{6,7},{8,9},{9,10},{10,11},{12,13},{... | collective-permute-start | bytes 221192 | tf_op jit(solution)/shard_map/ppermute | solution.py:505
  40.0 1.3 %collective-permute-start.3 = (bf16[2,36,512]{2,1,0:T(8,128)(2,1)S(1)}, bf16[2,36,512]{2,1,0:T(8,128)(2,1)S(1)}, u32[]{:S(2)}, u32[]{:S(2)}) collective-permute-start(bf16[2,36,512]{2,1,0:T(8,128)(2,1)S(1)} %get-tuple-element.77), channel_id=1, source_target_pairs={{1,0},{2,1},{3,2},{5,4},{6,5},{7,6},{9,8},{10,9},{11,10},{13,12},{... | collective-permute-start | bytes 221192 | tf_op jit(solution)/shard_map/ppermute | solution.py:505
  41.3 1.8 %match.1.match_hbm = bf16[4096,128]{1,0:T(8,128)(2,1)S(1)} custom-call(s32[32,128]{1,0:T(8,128)S(1)} %pad_add_fusion.incoming_ref), custom_call_target="tpu_custom_call" | custom-call | flops 1000000000 | bytes 1048576 | tf_op jit(solution)/shard_map/match/pallas_call | solution.py:616
  43.2 2.2 %collective-permute-done.3.yhi_ref = bf16[2,36,512]{2,1,0:T(8,128)(2,1)S(1)} collective-permute-done((bf16[2,36,512]{2,1,0:T(8,128)(2,1)S(1)}, bf16[2,36,512]{2,1,0:T(8,128)(2,1)S(1)}, u32[]{:S(2)}, u32[]{:S(2)}) %collective-permute-start.3) | collective-permute-done | bytes 73760 | tf_op jit(solution)/shard_map/ppermute | solution.py:505
  45.3 12.4 %stars.1 = (f32[16,128]{1,0:T(8,128)S(1)}, bf16[2816,128]{1,0:T(8,128)(2,1)}, bf16[1280,128]{1,0:T(8,128)(2,1)S(1)}) custom-call(s32[2048]{0:T(1024)S(1)} %reshape.85.position_ref, f32[16,128]{1,0:T(8,128)S(1)} %reshape.86.observed_ref, f32[16,128]{1,0:T(8,128)S(1)} %reshape.87.inverse_ref, bf16[64,32,32,128]{3,2,1,0:T(8,128)(2,1)} %weights_hbm.1, ...), custom_call_target="tpu_custom_call" | custom-call | flops 33554432 | bytes 16777216 | tf_op jit(solution)/shard_map/stars/pallas_call | solution.py:631
  57.8 4.9 %all-to-all-start.4 = ((bf16[32,88,128]{2,1,0:T(8,128)(2,1)}), bf16[32,88,128]{2,1,0:T(8,128)(2,1)S(1)}, u32[]{:S(2)}, u32[]{:S(2)}) async-start(bf16[32,88,128]{2,1,0:T(8,128)(2,1)} %bitcast.11), calls=%async_computation.4 | async-start | bytes 1441792 | tf_op jit(solution)/shard_map/all_to_all | solution.py:532
  62.8 0.1 reshape.92
  62.9 0.7 copy.19
  63.5 13.1 %prior.1.base_hbm = f32[32,64,512]{2,1,0:T(8,128)} custom-call(f32[32,64,512]{2,1,0:T(8,128)} %field_hbm.2, bf16[2,64,512]{2,1,0:T(8,128)(2,1)} %copy-done.1, bf16[2,64,512]{2,1,0:T(8,128)(2,1)} %copy-done.2, bf16[2,36,512]{2,1,0:T(8,128)(2,1)} %copy-done.3, bf16[2,36,512]{2,1,0:T(8,128)(2,1)} %copy-done.4), custom_call_target="tpu_custom_call" | custom-call | flops 31457280 | bytes 8388608 | tf_op jit(solution)/shard_map/prior/pallas_call | solution.py:660
  76.7 5.5 %all-to-all-done.4 = bf16[32,88,128]{2,1,0:T(8,128)(2,1)S(1)} async-done(((bf16[32,88,128]{2,1,0:T(8,128)(2,1)}), bf16[32,88,128]{2,1,0:T(8,128)(2,1)S(1)}, u32[]{:S(2)}, u32[]{:S(2)}) %all-to-all-start.4) | async-done | bytes 720928 | tf_op jit(solution)/shard_map/all_to_all | solution.py:532
  82.2 9.0 %finish.1 = f32[32,64,512]{2,1,0:T(8,128)} custom-call(s32[4096]{0:T(1024)S(1)} %bitcast.22, bf16[4096,128]{1,0:T(8,128)(2,1)S(1)} %match.1.match_hbm, f32[32,64,512]{2,1,0:T(8,128)} %field_hbm.2, f32[32,64,512]{2,1,0:T(8,128)} %prior.1.base_hbm, bf16[2816,128]{1,0:T(8,128)(2,1)S(1)} %bitcast.18, bf16[1280,128]{1,0:T(8,128)(2,1)S(1)} %bitcast.28), custom_call_target="tpu_custom_call" | custom-call | flops 4194304 | bytes 12582912 | tf_op jit(solution)/shard_map/finish/pallas_call | solution.py:680
  (24 shorter events, 0.1 us)
Async XLA Ops:
  2.6 13.7 %all-to-all-start.2 = ((s32[32,1,128]{2,1,0:T(1,128)}), s32[32,1,128]{2,1,0:T(1,128)S(1)}, u32[]{:S(2)}, u32[]{:S(2)}) async-start(s32[32,1,128]{2,1,0:T(1,128)} %bitcast.31), calls=%async_computation.2 | async-start | bytes 32768 | tf_op jit(solution)/shard_map/all_to_all | solution.py:532
  9.7 2.2 %copy-start = (f32[32,64,512]{2,1,0:T(8,128)S(1)}, f32[32,64,512]{2,1,0:T(8,128)}, u32[]{:S(2)}) copy-start(f32[32,64,512]{2,1,0:T(8,128)} %field_hbm.2) | copy-start | bytes 12582916
  11.9 13.2 %copy-start.7 = (s32[16,128]{1,0:T(8,128)S(1)}, s32[16,128]{1,0:T(8,128)}, u32[]{:S(2)}) copy-start(s32[16,128]{1,0:T(8,128)} %get-tuple-element.79) | copy-start | bytes 24580
  11.9 13.6 %copy-start.6 = (f32[64,32]{0,1:T(8,128)S(1)}, f32[64,32]{0,1:T(8,128)}, u32[]{:S(2)}) copy-start(f32[64,32]{0,1:T(8,128)} %param.13) | copy-start | bytes 24580
  11.9 13.6 %copy-start.8 = (s32[64]{0:T(128)S(1)}, s32[64]{0:T(128)}, u32[]{:S(2)}) copy-start(s32[64]{0:T(128)} %param.14) | copy-start | bytes 772
  11.9 13.7 %copy-start.5 = (f32[64,32]{0,1:T(8,128)S(1)}, f32[64,32]{0,1:T(8,128)}, u32[]{:S(2)}) copy-start(f32[64,32]{0,1:T(8,128)} %param.12) | copy-start | bytes 24580
  22.1 23.2 %all-to-all-start.3 = ((bf16[32,88,128]{2,1,0:T(8,128)(2,1)}), bf16[32,88,128]{2,1,0:T(8,128)(2,1)S(1)}, u32[]{:S(2)}, u32[]{:S(2)}) async-start(bf16[32,88,128]{2,1,0:T(8,128)(2,1)} %bitcast.5), calls=%async_computation.3 | async-start | bytes 1441792 | tf_op jit(solution)/shard_map/all_to_all | solution.py:532
  25.8 6.7 %collective-permute-start = (bf16[2,64,512]{2,1,0:T(8,128)(2,1)S(1)}, bf16[2,64,512]{2,1,0:T(8,128)(2,1)S(1)}, u32[]{:S(2)}, u32[]{:S(2)}) collective-permute-start(bf16[2,64,512]{2,1,0:T(8,128)(2,1)S(1)} %get-tuple-element.72), channel_id=1, source_target_pairs={{0,4},{4,8},{8,12},{12,16},{16,20},{20,24},{24,28},{1,5},{5,9},{9,... | collective-permute-start | bytes 393224 | tf_op jit(solution)/shard_map/ppermute | solution.py:505
  29.3 7.0 %collective-permute-start.1 = (bf16[2,64,512]{2,1,0:T(8,128)(2,1)S(1)}, bf16[2,64,512]{2,1,0:T(8,128)(2,1)S(1)}, u32[]{:S(2)}, u32[]{:S(2)}) collective-permute-start(bf16[2,64,512]{2,1,0:T(8,128)(2,1)S(1)} %get-tuple-element.73), channel_id=1, source_target_pairs={{4,0},{8,4},{12,8},{16,12},{20,16},{24,20},{28,24},{5,1},{9,5},{13... | collective-permute-start | bytes 393224 | tf_op jit(solution)/shard_map/ppermute | solution.py:505
  32.5 25.3 %copy-start.1 = (bf16[2,64,512]{2,1,0:T(8,128)(2,1)}, bf16[2,64,512]{2,1,0:T(8,128)(2,1)S(1)}, u32[]{:S(2)}) copy-start(bf16[2,64,512]{2,1,0:T(8,128)(2,1)S(1)} %collective-permute-done.xlo_ref) | copy-start | bytes 393220
  36.3 21.5 %copy-start.2 = (bf16[2,64,512]{2,1,0:T(8,128)(2,1)}, bf16[2,64,512]{2,1,0:T(8,128)(2,1)S(1)}, u32[]{:S(2)}) copy-start(bf16[2,64,512]{2,1,0:T(8,128)(2,1)S(1)} %collective-permute-done.1.xhi_ref) | copy-start | bytes 393220
  36.4 6.8 %collective-permute-start.2 = (bf16[2,36,512]{2,1,0:T(8,128)(2,1)S(1)}, bf16[2,36,512]{2,1,0:T(8,128)(2,1)S(1)}, u32[]{:S(2)}, u32[]{:S(2)}) collective-permute-start(bf16[2,36,512]{2,1,0:T(8,128)(2,1)S(1)} %get-tuple-element.76), channel_id=1, source_target_pairs={{0,1},{1,2},{2,3},{4,5},{5,6},{6,7},{8,9},{9,10},{10,11},{12,13},{... | collective-permute-start | bytes 221192 | tf_op jit(solution)/shard_map/ppermute | solution.py:505
  40.0 5.3 %collective-permute-start.3 = (bf16[2,36,512]{2,1,0:T(8,128)(2,1)S(1)}, bf16[2,36,512]{2,1,0:T(8,128)(2,1)S(1)}, u32[]{:S(2)}, u32[]{:S(2)}) collective-permute-start(bf16[2,36,512]{2,1,0:T(8,128)(2,1)S(1)} %get-tuple-element.77), channel_id=1, source_target_pairs={{1,0},{2,1},{3,2},{5,4},{6,5},{7,6},{9,8},{10,9},{11,10},{13,12},{... | collective-permute-start | bytes 221192 | tf_op jit(solution)/shard_map/ppermute | solution.py:505
  43.1 14.7 %copy-start.3 = (bf16[2,36,512]{2,1,0:T(8,128)(2,1)}, bf16[2,36,512]{2,1,0:T(8,128)(2,1)S(1)}, u32[]{:S(2)}) copy-start(bf16[2,36,512]{2,1,0:T(8,128)(2,1)S(1)} %collective-permute-done.2.ylo_ref) | copy-start | bytes 221188
  45.3 12.5 %copy-start.4 = (bf16[2,36,512]{2,1,0:T(8,128)(2,1)}, bf16[2,36,512]{2,1,0:T(8,128)(2,1)S(1)}, u32[]{:S(2)}) copy-start(bf16[2,36,512]{2,1,0:T(8,128)(2,1)S(1)} %collective-permute-done.3.yhi_ref) | copy-start | bytes 221188
  57.8 24.4 %all-to-all-start.4 = ((bf16[32,88,128]{2,1,0:T(8,128)(2,1)}), bf16[32,88,128]{2,1,0:T(8,128)(2,1)S(1)}, u32[]{:S(2)}, u32[]{:S(2)}) async-start(bf16[32,88,128]{2,1,0:T(8,128)(2,1)} %bitcast.11), calls=%async_computation.4 | async-start | bytes 1441792 | tf_op jit(solution)/shard_map/all_to_all | solution.py:532

commit v17 on v16

--- a/solution.py
+++ b/solution.py
@@ -241,10 +241,11 @@
     extinction_ref, refs = refs[0], refs[1:]
     parcel_refs, refs = refs[:exchanges], refs[exchanges:]
     weights_ref, returned_rows, sens_ref, parcel_rows, sems = refs
-    sets, in_set, per, slots, stars, width = weights_ref.shape
-    chunks = extinction_ref.shape[0]
-    rounds = chunks // (sets * in_set)
+    chunks, per, slots, stars, width = weights_ref.shape
+    quarter = chunks // 4
+    bounds = [0, quarter // 2, quarter, 2 * quarter, 3 * quarter, chunks]
     per_chunk = per * slots
+    held = sens_ref.shape[0] // per_chunk
     fold = LANES // stars
     all_slots = parcel_rows.shape[0]
     sens_blocks = sens_ref.reshape(sens_ref.shape[0], width)
@@ -253,24 +254,24 @@
     star_group = lane // stars
     own_slot = [row == star_group + fold * h for h in range(8 // fold)]
 
-    def load(one_round, one_set):
-        return [
+    loads = [
+        [
             pltpu.make_async_copy(
-                weights_hbm.at[pl.ds(((one_round * sets + one_set) * in_set + u) * per, per)],
-                weights_ref.at[one_set, u],
-                sems.at[one_set, u],
+                weights_hbm.at[pl.ds(c * per, per)], weights_ref.at[c], sems.at[c]
             )
-            for u in range(in_set)
+            for c in range(first, last)
         ]
-
-    def extinctions(one_set, u, chunk, places):
+        for first, last in zip(bounds[:-1], bounds[1:])
+    ]
+
+    def extinctions(chunk):
         sums = []
         for b in range(per):
             total = jnp.zeros((stars // 8, 8, width), jnp.float32)
             for k in range(slots):
-                at = places[u * per_chunk + b * slots + k]
+                at = position_ref[chunk * per_chunk + b * slots + k]
                 fetched = returned_rows[pl.ds(at, 8, stride=0), :]
-                block = weights_ref[one_set, u, b, k].astype(jnp.float32)
+                block = weights_ref[chunk, b, k].astype(jnp.float32)
                 total = total + block.reshape(stars // 8, 8, width) * fetched
             sums.append(total.reshape(stars, width))
         extinction = lax.dot_general(
@@ -280,11 +281,11 @@
             precision=lax.Precision.HIGHEST,
             preferred_element_type=jnp.float32,
         )
-        here = pl.ds(chunk, 1)
+        here = slice(chunk, chunk + 1)
         extinction_ref[here, :] = extinction[:1]
         return inverse_ref[here, :] * (extinction - observed_ref[here, :])
 
-    def sensitivities(one_set, u, weighted):
+    def sensitivities(chunk, weighted):
         for b in range(per):
             spread = jnp.where(star_group == b, weighted, 0.0)
             shift = stars
@@ -294,32 +295,21 @@
             left = jnp.concatenate(
                 [jnp.where(own, spread, 0.0) for own in own_slot], axis=1
             ).astype(jnp.bfloat16)
-            eights = [weights_ref[one_set, u, b, 8 * j : 8 * j + 8] for j in range(slots // 8)]
+            eights = [weights_ref[chunk, b, 8 * j : 8 * j + 8] for j in range(slots // 8)]
             right = jnp.concatenate([x.reshape(8 * stars, width) for x in eights], axis=1)
             sens = jnp.dot(left, right, preferred_element_type=jnp.float32)
             for j in range(slots // 8):
-                first = u * per_chunk + b * slots + 8 * j
+                first = chunk % held * per_chunk + b * slots + 8 * j
                 sens_blocks[first : first + 8, :] = sens[:, j * width : (j + 1) * width]
 
-    def scatter(u, places):
-        for i in range(u * per_chunk, (u + 1) * per_chunk):
-            parcel_rows[places[i]] = sens_ref[i]
-
-    def work(one_round, one_set):
-        first = (one_round * sets + one_set) * in_set
-        size = in_set * per_chunk
-        places = position_ref.at[pl.ds(pl.multiple_of(first * per_chunk, size), size)]
-        weighted = {}
-        for u in range(in_set + 2):
-            if u < in_set:
-                weighted[u] = extinctions(one_set, u, first + u, places)
-            if 1 <= u <= in_set:
-                sensitivities(one_set, u - 1, weighted[u - 1])
-            if u >= 2:
-                scatter(u - 2, places)
-
-    for copy in load(0, 0):
-        copy.start()
+    def scatter(chunk):
+        for i in range(per_chunk):
+            at = position_ref[chunk * per_chunk + i]
+            parcel_rows[at] = sens_ref[chunk % held * per_chunk + i]
+
+    for one_set in loads[:2]:
+        for copy in one_set:
+            copy.start()
     start = 0
     for returned_ref in returned_refs:
         span = slice(start, start + returned_ref.shape[0])
@@ -327,24 +317,20 @@
         start = span.stop
     parcel_rows.reshape(all_slots, width)[...] = jnp.zeros((all_slots, width), jnp.float32)
 
-    def one_round(i, carry):
-        for one_set in range(sets):
-            for copy in load(i, one_set):
+    weighted = {}
+    for chunk in range(chunks + 2):
+        if chunk in bounds[:-1]:
+            which = bounds.index(chunk)
+            for copy in loads[which]:
                 copy.wait()
-            if one_set + 1 < sets:
-                for copy in load(i, one_set + 1):
-                    copy.start()
-            else:
-
-                @pl.when(i + 1 < rounds)
-                def _():
-                    for copy in load(i + 1, 0):
-                        copy.start()
-
-            work(i, one_set)
-        return carry
-
-    lax.fori_loop(0, rounds, one_round, 0)
+            for copy in loads[which + 2] if which + 2 < len(loads) else []:
+                copy.start()
+        if chunk < chunks:
+            weighted[chunk] = extinctions(chunk)
+        if 1 <= chunk <= chunks:
+            sensitivities(chunk - 1, weighted[chunk - 1])
+        if chunk >= 2:
+            scatter(chunk - 2)
     start = 0
     for parcel_ref in parcel_refs:
         span = slice(start, start + parcel_ref.shape[0])
@@ -625,7 +611,6 @@
     *returned, match, ylo, yhi = lax.optimization_barrier((*returned, match, ylo, yhi))
 
     chunks = blocks_dev * stars // LANES
-    in_set = chunks // 4
     live = jnp.arange(stars)[None, :] < star_counts[:, None]
     live_inverse = jnp.where(live, inverse_var, 0.0)
     extinction, *parcel = pl.pallas_call(
@@ -635,11 +620,11 @@
         in_specs=[SMEM, VMEM, VMEM, ANY] + [VMEM] * exchanges,
         out_specs=[VMEM] * (1 + exchanges),
         scratch_shapes=[
-            pltpu.VMEM((2, in_set, blocks_dev // chunks, slots, stars, width), bf16),
+            pltpu.VMEM((chunks, blocks_dev // chunks, slots, stars, width), bf16),
             pltpu.VMEM((all_slots + 8, width), f32),
-            pltpu.VMEM((in_set * (blocks_dev // chunks) * slots, 1, width), f32),
+            pltpu.VMEM((4 * (blocks_dev // chunks) * slots, 1, width), f32),
             pltpu.VMEM((all_slots, 1, width), f32),
-            pltpu.SemaphoreType.DMA((2, in_set)),
+            pltpu.SemaphoreType.DMA((chunks,)),
         ],
         compiler_params=pltpu.CompilerParams(vmem_limit_bytes=50 * MIB),
         cost_estimate=pl.CostEstimate(

time: 91.8 us -> 90.8 us (0.989)
  Pallas kernels: 44.3 us -> 43.1 us
    pallas_call x1, Pallas kernels: 12.4 us -> 11.3 us  [on_device(): pl.pallas_call(functools.partial(star_kernel, exchanges=exchanges), out_s...]
  transfers between devices with their start and end apart: 7 -> 7, of which waited for: 5 -> 5; matrix products, arithmetic and copies ran while one was open for 2% -> 2% of each run, Pallas kernels for 17% -> 18%
where the time goes in v17:
time: 90.8 us; the launch traced here: 90.2 us
  Pallas kernels  43.1 us (47%)
  starting transfers between devices  25.5 us (28%)
  waiting for transfers between devices  16 us (18%)
  local copies, waits for them, and re-layouts  3.75 us (4%)
  between operations  1.66 us (2%)
    all_to_all x3, starting transfers between devices, exchange(): return lax.all_to_all(x, mesh_axes, split_axis=0, concat_axis=0, tiled=True)  15 us
    pallas_call x1, Pallas kernels, on_device(): pl.pallas_call(prior_kernel, out_shape=shape(field_shape, f32), in_specs=...  13.1 us
    pallas_call x1, Pallas kernels, on_device(): pl.pallas_call(functools.partial(star_kernel, exchanges=exchanges), out_s...  11.3 us
    ppermute x4, starting transfers between devices, both_ways(): return (lax.ppermute(last, axis, up), lax.ppermute(first, axis, down))  10.4 us
    all_to_all x3, waiting for transfers between devices, exchange(): return lax.all_to_all(x, mesh_axes, split_axis=0, concat_axis=0, tiled=True)  9.05 us
    pallas_call x1, Pallas kernels, on_device(): pl.pallas_call(functools.partial(finish_kernel, exchanges=exchanges, capa...  8.93 us
    ppermute x4, waiting for transfers between devices, both_ways(): return (lax.ppermute(last, axis, up), lax.ppermute(first, axis, down))  6.99 us
    pallas_call x1, Pallas kernels, on_device(): pl.pallas_call(functools.partial(serve_kernel, capacity=capacity, first_s...  5.11 us
  transfers between devices with their start and end apart: 7, of which 5 were waited for; matrix products, arithmetic and copies ran while one was open for 2% of the time, Pallas kernels for 18%

profile of v17, /device:TPU:1, one launch (start us, length us, event | category | flops | bytes accessed | tf_op | source)
XLA Modules:
  0.0 90.2 jit_solution(7915137854599641699)
XLA Ops:
  0.6 1.9 %route.1 = (s32[32,128]{1,0:T(8,128)}, s32[16,128]{1,0:T(8,128)}) custom-call(s32[32,64]{1,0:T(8,128)} %bitcast.30), custom_call_target="tpu_custom_call" | custom-call | tf_op jit(solution)/shard_map/route/pallas_call | solution.py:528
  2.6 7.1 %all-to-all-start.2 = ((s32[32,1,128]{2,1,0:T(1,128)}), s32[32,1,128]{2,1,0:T(1,128)S(1)}, u32[]{:S(2)}, u32[]{:S(2)}) async-start(s32[32,1,128]{2,1,0:T(1,128)} %bitcast.31), calls=%async_computation.2 | async-start | bytes 32768 | tf_op jit(solution)/shard_map/all_to_all | solution.py:518
  9.7 2.2 %copy-done = f32[32,64,512]{2,1,0:T(8,128)S(1)} copy-done((f32[32,64,512]{2,1,0:T(8,128)S(1)}, f32[32,64,512]{2,1,0:T(8,128)}, u32[]{:S(2)}) %copy-start) | copy-done | bytes 4194328
  11.9 0.9 table.1
  12.8 3.5 %all-to-all-done.2 = s32[32,1,128]{2,1,0:T(1,128)S(1)} async-done(((s32[32,1,128]{2,1,0:T(1,128)}), s32[32,1,128]{2,1,0:T(1,128)S(1)}, u32[]{:S(2)}, u32[]{:S(2)}) %all-to-all-start.2) | async-done | bytes 16416 | tf_op jit(solution)/shard_map/all_to_all | solution.py:518
  16.3 5.1 %serve.1 = (bf16[2816,128]{1,0:T(8,128)(2,1)}, bf16[1280,128]{1,0:T(8,128)(2,1)S(1)}, s32[1]{0:T(128)}) custom-call(s32[4096]{0:T(1024)S(1)} %bitcast.19, bf16[8320,128]{1,0:T(8,128)(2,1)S(1)} %get-tuple-element.63.table_ref), custom_call_target="tpu_custom_call" | custom-call | flops 1048576 | bytes 6291456 | tf_op jit(solution)/shard_map/serve/pallas_call | solution.py:565
  22.1 3.0 %all-to-all-start.3 = ((bf16[32,88,128]{2,1,0:T(8,128)(2,1)}), bf16[32,88,128]{2,1,0:T(8,128)(2,1)S(1)}, u32[]{:S(2)}, u32[]{:S(2)}) async-start(bf16[32,88,128]{2,1,0:T(8,128)(2,1)} %bitcast.5), calls=%async_computation.3 | async-start | bytes 1441792 | tf_op jit(solution)/shard_map/all_to_all | solution.py:518
  25.1 0.1 reshape.84
  25.1 0.1 copy.16
  25.2 0.1 reshape.85.position_ref
  25.4 0.1 copy.18
  25.5 0.1 reshape.87.inverse_ref
  25.6 0.1 copy.17
  25.6 0.1 reshape.86.observed_ref
  25.7 3.5 %collective-permute-start = (bf16[2,64,512]{2,1,0:T(8,128)(2,1)S(1)}, bf16[2,64,512]{2,1,0:T(8,128)(2,1)S(1)}, u32[]{:S(2)}, u32[]{:S(2)}) collective-permute-start(bf16[2,64,512]{2,1,0:T(8,128)(2,1)S(1)} %get-tuple-element.72), channel_id=1, source_target_pairs={{0,4},{4,8},{8,12},{12,16},{16,20},{20,24},{24,28},{1,5},{5,9},{9,... | collective-permute-start | bytes 393224 | tf_op jit(solution)/shard_map/ppermute | solution.py:491
  29.3 1.9 %collective-permute-start.1 = (bf16[2,64,512]{2,1,0:T(8,128)(2,1)S(1)}, bf16[2,64,512]{2,1,0:T(8,128)(2,1)S(1)}, u32[]{:S(2)}, u32[]{:S(2)}) collective-permute-start(bf16[2,64,512]{2,1,0:T(8,128)(2,1)S(1)} %get-tuple-element.73), channel_id=1, source_target_pairs={{4,0},{8,4},{12,8},{16,12},{20,16},{24,20},{28,24},{5,1},{9,5},{13... | collective-permute-start | bytes 393224 | tf_op jit(solution)/shard_map/ppermute | solution.py:491
  31.2 0.1 slice_and_fusion
  31.3 0.1 reshape.83
  31.4 0.1 reshape.82
  31.5 1.0 %collective-permute-done.xlo_ref = bf16[2,64,512]{2,1,0:T(8,128)(2,1)S(1)} collective-permute-done((bf16[2,64,512]{2,1,0:T(8,128)(2,1)S(1)}, bf16[2,64,512]{2,1,0:T(8,128)(2,1)S(1)}, u32[]{:S(2)}, u32[]{:S(2)}) %collective-permute-start) | collective-permute-done | bytes 131104 | tf_op jit(solution)/shard_map/ppermute | solution.py:491
  32.4 3.8 %collective-permute-done.1.xhi_ref = bf16[2,64,512]{2,1,0:T(8,128)(2,1)S(1)} collective-permute-done((bf16[2,64,512]{2,1,0:T(8,128)(2,1)S(1)}, bf16[2,64,512]{2,1,0:T(8,128)(2,1)S(1)}, u32[]{:S(2)}, u32[]{:S(2)}) %collective-permute-start.1) | collective-permute-done | bytes 131104 | tf_op jit(solution)/shard_map/ppermute | solution.py:491
  36.3 3.7 %collective-permute-start.2 = (bf16[2,36,512]{2,1,0:T(8,128)(2,1)S(1)}, bf16[2,36,512]{2,1,0:T(8,128)(2,1)S(1)}, u32[]{:S(2)}, u32[]{:S(2)}) collective-permute-start(bf16[2,36,512]{2,1,0:T(8,128)(2,1)S(1)} %get-tuple-element.76), channel_id=1, source_target_pairs={{0,1},{1,2},{2,3},{4,5},{5,6},{6,7},{8,9},{9,10},{10,11},{12,13},{... | collective-permute-start | bytes 221192 | tf_op jit(solution)/shard_map/ppermute | solution.py:491
  40.0 1.3 %collective-permute-start.3 = (bf16[2,36,512]{2,1,0:T(8,128)(2,1)S(1)}, bf16[2,36,512]{2,1,0:T(8,128)(2,1)S(1)}, u32[]{:S(2)}, u32[]{:S(2)}) collective-permute-start(bf16[2,36,512]{2,1,0:T(8,128)(2,1)S(1)} %get-tuple-element.77), channel_id=1, source_target_pairs={{1,0},{2,1},{3,2},{5,4},{6,5},{7,6},{9,8},{10,9},{11,10},{13,12},{... | collective-permute-start | bytes 221192 | tf_op jit(solution)/shard_map/ppermute | solution.py:491
  41.3 1.8 %match.1.match_hbm = bf16[4096,128]{1,0:T(8,128)(2,1)S(1)} custom-call(s32[32,128]{1,0:T(8,128)S(1)} %pad_add_fusion.incoming_ref), custom_call_target="tpu_custom_call" | custom-call | flops 1000000000 | bytes 1048576 | tf_op jit(solution)/shard_map/match/pallas_call | solution.py:602
  43.1 2.2 %collective-permute-done.3.yhi_ref = bf16[2,36,512]{2,1,0:T(8,128)(2,1)S(1)} collective-permute-done((bf16[2,36,512]{2,1,0:T(8,128)(2,1)S(1)}, bf16[2,36,512]{2,1,0:T(8,128)(2,1)S(1)}, u32[]{:S(2)}, u32[]{:S(2)}) %collective-permute-start.3) | collective-permute-done | bytes 73760 | tf_op jit(solution)/shard_map/ppermute | solution.py:491
  45.3 11.3 %stars.1 = (f32[16,128]{1,0:T(8,128)S(1)}, bf16[2816,128]{1,0:T(8,128)(2,1)}, bf16[1280,128]{1,0:T(8,128)(2,1)S(1)}) custom-call(s32[2048]{0:T(1024)S(1)} %reshape.85.position_ref, f32[16,128]{1,0:T(8,128)S(1)} %reshape.86.observed_ref, f32[16,128]{1,0:T(8,128)S(1)} %reshape.87.inverse_ref, bf16[64,32,32,128]{3,2,1,0:T(8,128)(2,1)} %weights_hbm.1, ...), custom_call_target="tpu_custom_call" | custom-call | flops 33554432 | bytes 16777216 | tf_op jit(solution)/shard_map/stars/pallas_call | solution.py:616
  56.7 5.0 %all-to-all-start.4 = ((bf16[32,88,128]{2,1,0:T(8,128)(2,1)}), bf16[32,88,128]{2,1,0:T(8,128)(2,1)S(1)}, u32[]{:S(2)}, u32[]{:S(2)}) async-start(bf16[32,88,128]{2,1,0:T(8,128)(2,1)} %bitcast.11), calls=%async_computation.4 | async-start | bytes 1441792 | tf_op jit(solution)/shard_map/all_to_all | solution.py:518
  61.7 0.1 reshape.92
  61.7 0.7 copy.19
  62.4 13.1 %prior.1.base_hbm = f32[32,64,512]{2,1,0:T(8,128)} custom-call(f32[32,64,512]{2,1,0:T(8,128)} %field_hbm.2, bf16[2,64,512]{2,1,0:T(8,128)(2,1)} %copy-done.1, bf16[2,64,512]{2,1,0:T(8,128)(2,1)} %copy-done.2, bf16[2,36,512]{2,1,0:T(8,128)(2,1)} %copy-done.3, bf16[2,36,512]{2,1,0:T(8,128)(2,1)} %copy-done.4), custom_call_target="tpu_custom_call" | custom-call | flops 31457280 | bytes 8388608 | tf_op jit(solution)/shard_map/prior/pallas_call | solution.py:645
  75.6 5.5 %all-to-all-done.4 = bf16[32,88,128]{2,1,0:T(8,128)(2,1)S(1)} async-done(((bf16[32,88,128]{2,1,0:T(8,128)(2,1)}), bf16[32,88,128]{2,1,0:T(8,128)(2,1)S(1)}, u32[]{:S(2)}, u32[]{:S(2)}) %all-to-all-start.4) | async-done | bytes 720928 | tf_op jit(solution)/shard_map/all_to_all | solution.py:518
  81.1 8.9 %finish.1 = f32[32,64,512]{2,1,0:T(8,128)} custom-call(s32[4096]{0:T(1024)S(1)} %bitcast.22, bf16[4096,128]{1,0:T(8,128)(2,1)S(1)} %match.1.match_hbm, f32[32,64,512]{2,1,0:T(8,128)} %field_hbm.2, f32[32,64,512]{2,1,0:T(8,128)} %prior.1.base_hbm, bf16[2816,128]{1,0:T(8,128)(2,1)S(1)} %bitcast.18, bf16[1280,128]{1,0:T(8,128)(2,1)S(1)} %bitcast.28), custom_call_target="tpu_custom_call" | custom-call | flops 4194304 | bytes 12582912 | tf_op jit(solution)/shard_map/finish/pallas_call | solution.py:665
  (24 shorter events, 0.1 us)
Async XLA Ops:
  2.6 13.7 %all-to-all-start.2 = ((s32[32,1,128]{2,1,0:T(1,128)}), s32[32,1,128]{2,1,0:T(1,128)S(1)}, u32[]{:S(2)}, u32[]{:S(2)}) async-start(s32[32,1,128]{2,1,0:T(1,128)} %bitcast.31), calls=%async_computation.2 | async-start | bytes 32768 | tf_op jit(solution)/shard_map/all_to_all | solution.py:518
  9.7 2.2 %copy-start = (f32[32,64,512]{2,1,0:T(8,128)S(1)}, f32[32,64,512]{2,1,0:T(8,128)}, u32[]{:S(2)}) copy-start(f32[32,64,512]{2,1,0:T(8,128)} %field_hbm.2) | copy-start | bytes 12582916
  11.9 13.2 %copy-start.7 = (s32[16,128]{1,0:T(8,128)S(1)}, s32[16,128]{1,0:T(8,128)}, u32[]{:S(2)}) copy-start(s32[16,128]{1,0:T(8,128)} %get-tuple-element.79) | copy-start | bytes 24580
  11.9 13.5 %copy-start.6 = (f32[64,32]{0,1:T(8,128)S(1)}, f32[64,32]{0,1:T(8,128)}, u32[]{:S(2)}) copy-start(f32[64,32]{0,1:T(8,128)} %param.13) | copy-start | bytes 24580
  11.9 13.5 %copy-start.8 = (s32[64]{0:T(128)S(1)}, s32[64]{0:T(128)}, u32[]{:S(2)}) copy-start(s32[64]{0:T(128)} %param.14) | copy-start | bytes 772
  11.9 13.7 %copy-start.5 = (f32[64,32]{0,1:T(8,128)S(1)}, f32[64,32]{0,1:T(8,128)}, u32[]{:S(2)}) copy-start(f32[64,32]{0,1:T(8,128)} %param.12) | copy-start | bytes 24580
  22.1 23.2 %all-to-all-start.3 = ((bf16[32,88,128]{2,1,0:T(8,128)(2,1)}), bf16[32,88,128]{2,1,0:T(8,128)(2,1)S(1)}, u32[]{:S(2)}, u32[]{:S(2)}) async-start(bf16[32,88,128]{2,1,0:T(8,128)(2,1)} %bitcast.5), calls=%async_computation.3 | async-start | bytes 1441792 | tf_op jit(solution)/shard_map/all_to_all | solution.py:518
  25.7 6.7 %collective-permute-start = (bf16[2,64,512]{2,1,0:T(8,128)(2,1)S(1)}, bf16[2,64,512]{2,1,0:T(8,128)(2,1)S(1)}, u32[]{:S(2)}, u32[]{:S(2)}) collective-permute-start(bf16[2,64,512]{2,1,0:T(8,128)(2,1)S(1)} %get-tuple-element.72), channel_id=1, source_target_pairs={{0,4},{4,8},{8,12},{12,16},{16,20},{20,24},{24,28},{1,5},{5,9},{9,... | collective-permute-start | bytes 393224 | tf_op jit(solution)/shard_map/ppermute | solution.py:491
  29.3 7.0 %collective-permute-start.1 = (bf16[2,64,512]{2,1,0:T(8,128)(2,1)S(1)}, bf16[2,64,512]{2,1,0:T(8,128)(2,1)S(1)}, u32[]{:S(2)}, u32[]{:S(2)}) collective-permute-start(bf16[2,64,512]{2,1,0:T(8,128)(2,1)S(1)} %get-tuple-element.73), channel_id=1, source_target_pairs={{4,0},{8,4},{12,8},{16,12},{20,16},{24,20},{28,24},{5,1},{9,5},{13... | collective-permute-start | bytes 393224 | tf_op jit(solution)/shard_map/ppermute | solution.py:491
  32.4 24.2 %copy-start.1 = (bf16[2,64,512]{2,1,0:T(8,128)(2,1)}, bf16[2,64,512]{2,1,0:T(8,128)(2,1)S(1)}, u32[]{:S(2)}) copy-start(bf16[2,64,512]{2,1,0:T(8,128)(2,1)S(1)} %collective-permute-done.xlo_ref) | copy-start | bytes 393220
  36.3 20.4 %copy-start.2 = (bf16[2,64,512]{2,1,0:T(8,128)(2,1)}, bf16[2,64,512]{2,1,0:T(8,128)(2,1)S(1)}, u32[]{:S(2)}) copy-start(bf16[2,64,512]{2,1,0:T(8,128)(2,1)S(1)} %collective-permute-done.1.xhi_ref) | copy-start | bytes 393220
  36.3 6.8 %collective-permute-start.2 = (bf16[2,36,512]{2,1,0:T(8,128)(2,1)S(1)}, bf16[2,36,512]{2,1,0:T(8,128)(2,1)S(1)}, u32[]{:S(2)}, u32[]{:S(2)}) collective-permute-start(bf16[2,36,512]{2,1,0:T(8,128)(2,1)S(1)} %get-tuple-element.76), channel_id=1, source_target_pairs={{0,1},{1,2},{2,3},{4,5},{5,6},{6,7},{8,9},{9,10},{10,11},{12,13},{... | collective-permute-start | bytes 221192 | tf_op jit(solution)/shard_map/ppermute | solution.py:491
  40.0 5.3 %collective-permute-start.3 = (bf16[2,36,512]{2,1,0:T(8,128)(2,1)S(1)}, bf16[2,36,512]{2,1,0:T(8,128)(2,1)S(1)}, u32[]{:S(2)}, u32[]{:S(2)}) collective-permute-start(bf16[2,36,512]{2,1,0:T(8,128)(2,1)S(1)} %get-tuple-element.77), channel_id=1, source_target_pairs={{1,0},{2,1},{3,2},{5,4},{6,5},{7,6},{9,8},{10,9},{11,10},{13,12},{... | collective-permute-start | bytes 221192 | tf_op jit(solution)/shard_map/ppermute | solution.py:491
  43.1 13.6 %copy-start.3 = (bf16[2,36,512]{2,1,0:T(8,128)(2,1)}, bf16[2,36,512]{2,1,0:T(8,128)(2,1)S(1)}, u32[]{:S(2)}) copy-start(bf16[2,36,512]{2,1,0:T(8,128)(2,1)S(1)} %collective-permute-done.2.ylo_ref) | copy-start | bytes 221188
  45.3 11.4 %copy-start.4 = (bf16[2,36,512]{2,1,0:T(8,128)(2,1)}, bf16[2,36,512]{2,1,0:T(8,128)(2,1)S(1)}, u32[]{:S(2)}) copy-start(bf16[2,36,512]{2,1,0:T(8,128)(2,1)S(1)} %collective-permute-done.3.yhi_ref) | copy-start | bytes 221188
  56.7 24.4 %all-to-all-start.4 = ((bf16[32,88,128]{2,1,0:T(8,128)(2,1)}), bf16[32,88,128]{2,1,0:T(8,128)(2,1)S(1)}, u32[]{:S(2)}, u32[]{:S(2)}) async-start(bf16[32,88,128]{2,1,0:T(8,128)(2,1)} %bitcast.11), calls=%async_computation.4 | async-start | bytes 1441792 | tf_op jit(solution)/shard_map/all_to_all | solution.py:518

commit v18 on v17

--- a/solution.py
+++ b/solution.py
@@ -599,16 +599,9 @@
         incoming_late[:, :first_slots].reshape(-1, LANES),
         (incoming_late[:, first_slots:] & (MARK - 1)).reshape(-1, LANES),
     ][:exchanges]
-    match = pl.pallas_call(
-        match_kernel,
-        out_shape=shape((all_slots, LANES), bf16),
-        in_specs=[VMEM],
-        out_specs=VMEM,
-        compiler_params=pltpu.CompilerParams(vmem_limit_bytes=8 * MIB),
-        cost_estimate=pl.CostEstimate(flops=10**9, bytes_accessed=MIB, transcendentals=0),
-        name="match",
-    )(jnp.concatenate(slot_lists, axis=0))
-    *returned, match, ylo, yhi = lax.optimization_barrier((*returned, match, ylo, yhi))
+    *returned, slot_rows, ylo, yhi = lax.optimization_barrier(
+        (*returned, jnp.concatenate(slot_lists, axis=0), ylo, yhi)
+    )
 
     chunks = blocks_dev * stars // LANES
     live = jnp.arange(stars)[None, :] < star_counts[:, None]
@@ -640,7 +633,16 @@
     )
     arrived = exchange_rows(parcel, crowded)
 
-    field_late, _ = lax.optimization_barrier((log_density, parcel[0]))
+    field_late, slot_rows, _ = lax.optimization_barrier((log_density, slot_rows, parcel[0]))
+    match = pl.pallas_call(
+        match_kernel,
+        out_shape=shape((all_slots, LANES), bf16),
+        in_specs=[VMEM],
+        out_specs=VMEM,
+        compiler_params=pltpu.CompilerParams(vmem_limit_bytes=8 * MIB),
+        cost_estimate=pl.CostEstimate(flops=10**9, bytes_accessed=MIB, transcendentals=0),
+        name="match",
+    )(slot_rows)
     parts = 8
     base = pl.pallas_call(
         prior_kernel,

time: 90.8 us -> 90.9 us (level)
    ppermute x4, waiting for transfers between devices: 6.99 us -> 8.79 us  [both_ways(): return (lax.ppermute(last, axis, up), lax.ppermute(first, axis, down))]
    all_to_all x3, waiting for transfers between devices: 9.05 us -> 7.27 us  [exchange(): return lax.all_to_all(x, mesh_axes, split_axis=0, concat_axis=0, tiled=True)]
  transfers between devices with their start and end apart: 7 -> 7, of which waited for: 5 -> 6; matrix products, arithmetic and copies ran while one was open for 2% -> 2% of each run, Pallas kernels for 18% -> 18%
where the time goes in v18:
time: 90.9 us; the launch traced here: 90.4 us
  Pallas kernels  43.5 us (48%)
  starting transfers between devices  25.4 us (28%)
  waiting for transfers between devices  16.1 us (18%)
  local copies, waits for them, and re-layouts  3.75 us (4%)
  between operations  1.65 us (2%)
    all_to_all x3, starting transfers between devices, exchange(): return lax.all_to_all(x, mesh_axes, split_axis=0, concat_axis=0, tiled=True)  15 us
    pallas_call x1, Pallas kernels, on_device(): pl.pallas_call(prior_kernel, out_shape=shape(field_shape, f32), in_specs=...  13.1 us
    pallas_call x1, Pallas kernels, on_device(): pl.pallas_call(functools.partial(star_kernel, exchanges=exchanges), out_s...  11.3 us
    ppermute x4, starting transfers between devices, both_ways(): return (lax.ppermute(last, axis, up), lax.ppermute(first, axis, down))  10.4 us
    pallas_call x1, Pallas kernels, on_device(): pl.pallas_call(functools.partial(finish_kernel, exchanges=exchanges, capa...  9.12 us
    ppermute x4, waiting for transfers between devices, both_ways(): return (lax.ppermute(last, axis, up), lax.ppermute(first, axis, down))  8.79 us
    all_to_all x3, waiting for transfers between devices, exchange(): return lax.all_to_all(x, mesh_axes, split_axis=0, concat_axis=0, tiled=True)  7.27 us
    pallas_call x1, Pallas kernels, on_device(): pl.pallas_call(functools.partial(serve_kernel, capacity=capacity, first_s...  5.25 us
  transfers between devices with their start and end apart: 7, of which 6 were waited for; matrix products, arithmetic and copies ran while one was open for 2% of the time, Pallas kernels for 18%

profile of v18, /device:TPU:1, one launch (start us, length us, event | category | flops | bytes accessed | tf_op | source)
XLA Modules:
  0.0 90.4 jit_solution(4949134264255988427)
XLA Ops:
  0.6 1.9 %route.1 = (s32[32,128]{1,0:T(8,128)}, s32[16,128]{1,0:T(8,128)}) custom-call(s32[32,64]{1,0:T(8,128)} %bitcast.30), custom_call_target="tpu_custom_call" | custom-call | tf_op jit(solution)/shard_map/route/pallas_call | solution.py:528
  2.6 7.1 %all-to-all-start.2 = ((s32[32,1,128]{2,1,0:T(1,128)}), s32[32,1,128]{2,1,0:T(1,128)S(1)}, u32[]{:S(2)}, u32[]{:S(2)}) async-start(s32[32,1,128]{2,1,0:T(1,128)} %bitcast.31), calls=%async_computation.2 | async-start | bytes 32768 | tf_op jit(solution)/shard_map/all_to_all | solution.py:518
  9.7 2.2 %copy-done = f32[32,64,512]{2,1,0:T(8,128)S(1)} copy-done((f32[32,64,512]{2,1,0:T(8,128)S(1)}, f32[32,64,512]{2,1,0:T(8,128)}, u32[]{:S(2)}) %copy-start) | copy-done | bytes 4194328
  11.9 0.9 table.1
  12.8 3.5 %all-to-all-done.2 = s32[32,1,128]{2,1,0:T(1,128)S(1)} async-done(((s32[32,1,128]{2,1,0:T(1,128)}), s32[32,1,128]{2,1,0:T(1,128)S(1)}, u32[]{:S(2)}, u32[]{:S(2)}) %all-to-all-start.2) | async-done | bytes 16416 | tf_op jit(solution)/shard_map/all_to_all | solution.py:518
  16.3 5.2 %serve.1 = (bf16[2816,128]{1,0:T(8,128)(2,1)}, bf16[1280,128]{1,0:T(8,128)(2,1)S(1)}, s32[1]{0:T(128)}) custom-call(s32[4096]{0:T(1024)S(1)} %bitcast.19, bf16[8320,128]{1,0:T(8,128)(2,1)S(1)} %get-tuple-element.64.table_ref), custom_call_target="tpu_custom_call" | custom-call | flops 1048576 | bytes 6291456 | tf_op jit(solution)/shard_map/serve/pallas_call | solution.py:565
  22.2 2.9 %all-to-all-start.3 = ((bf16[32,88,128]{2,1,0:T(8,128)(2,1)}), bf16[32,88,128]{2,1,0:T(8,128)(2,1)S(1)}, u32[]{:S(2)}, u32[]{:S(2)}) async-start(bf16[32,88,128]{2,1,0:T(8,128)(2,1)} %bitcast.5), calls=%async_computation.3 | async-start | bytes 1441792 | tf_op jit(solution)/shard_map/all_to_all | solution.py:518
  25.1 0.1 reshape.84
  25.2 0.1 copy.16
  25.3 0.1 reshape.85.position_ref
  25.4 0.1 copy.18
  25.5 0.1 reshape.87.inverse_ref
  25.6 0.1 copy.17
  25.7 0.1 reshape.86.observed_ref
  25.8 3.5 %collective-permute-start = (bf16[2,64,512]{2,1,0:T(8,128)(2,1)S(1)}, bf16[2,64,512]{2,1,0:T(8,128)(2,1)S(1)}, u32[]{:S(2)}, u32[]{:S(2)}) collective-permute-start(bf16[2,64,512]{2,1,0:T(8,128)(2,1)S(1)} %get-tuple-element.73), channel_id=1, source_target_pairs={{0,4},{4,8},{8,12},{12,16},{16,20},{20,24},{24,28},{1,5},{5,9},{9,... | collective-permute-start | bytes 393224 | tf_op jit(solution)/shard_map/ppermute | solution.py:491
  29.3 1.9 %collective-permute-start.1 = (bf16[2,64,512]{2,1,0:T(8,128)(2,1)S(1)}, bf16[2,64,512]{2,1,0:T(8,128)(2,1)S(1)}, u32[]{:S(2)}, u32[]{:S(2)}) collective-permute-start(bf16[2,64,512]{2,1,0:T(8,128)(2,1)S(1)} %get-tuple-element.74), channel_id=1, source_target_pairs={{4,0},{8,4},{12,8},{16,12},{20,16},{24,20},{28,24},{5,1},{9,5},{13... | collective-permute-start | bytes 393224 | tf_op jit(solution)/shard_map/ppermute | solution.py:491
  31.2 0.1 slice_and_fusion
  31.3 0.1 reshape.83
  31.4 0.1 reshape.82
  31.5 1.0 %collective-permute-done.xlo_ref = bf16[2,64,512]{2,1,0:T(8,128)(2,1)S(1)} collective-permute-done((bf16[2,64,512]{2,1,0:T(8,128)(2,1)S(1)}, bf16[2,64,512]{2,1,0:T(8,128)(2,1)S(1)}, u32[]{:S(2)}, u32[]{:S(2)}) %collective-permute-start) | collective-permute-done | bytes 131104 | tf_op jit(solution)/shard_map/ppermute | solution.py:491
  32.5 3.8 %collective-permute-done.1.xhi_ref = bf16[2,64,512]{2,1,0:T(8,128)(2,1)S(1)} collective-permute-done((bf16[2,64,512]{2,1,0:T(8,128)(2,1)S(1)}, bf16[2,64,512]{2,1,0:T(8,128)(2,1)S(1)}, u32[]{:S(2)}, u32[]{:S(2)}) %collective-permute-start.1) | collective-permute-done | bytes 131104 | tf_op jit(solution)/shard_map/ppermute | solution.py:491
  36.4 3.7 %collective-permute-start.2 = (bf16[2,36,512]{2,1,0:T(8,128)(2,1)S(1)}, bf16[2,36,512]{2,1,0:T(8,128)(2,1)S(1)}, u32[]{:S(2)}, u32[]{:S(2)}) collective-permute-start(bf16[2,36,512]{2,1,0:T(8,128)(2,1)S(1)} %get-tuple-element.77), channel_id=1, source_target_pairs={{0,1},{1,2},{2,3},{4,5},{5,6},{6,7},{8,9},{9,10},{10,11},{12,13},{... | collective-permute-start | bytes 221192 | tf_op jit(solution)/shard_map/ppermute | solution.py:491
  40.0 1.3 %collective-permute-start.3 = (bf16[2,36,512]{2,1,0:T(8,128)(2,1)S(1)}, bf16[2,36,512]{2,1,0:T(8,128)(2,1)S(1)}, u32[]{:S(2)}, u32[]{:S(2)}) collective-permute-start(bf16[2,36,512]{2,1,0:T(8,128)(2,1)S(1)} %get-tuple-element.78), channel_id=1, source_target_pairs={{1,0},{2,1},{3,2},{5,4},{6,5},{7,6},{9,8},{10,9},{11,10},{13,12},{... | collective-permute-start | bytes 221192 | tf_op jit(solution)/shard_map/ppermute | solution.py:491
  41.4 0.1 collective-permute-done.2.ylo_ref
  41.5 3.8 %collective-permute-done.3.yhi_ref = bf16[2,36,512]{2,1,0:T(8,128)(2,1)S(1)} collective-permute-done((bf16[2,36,512]{2,1,0:T(8,128)(2,1)S(1)}, bf16[2,36,512]{2,1,0:T(8,128)(2,1)S(1)}, u32[]{:S(2)}, u32[]{:S(2)}) %collective-permute-start.3) | collective-permute-done | bytes 73760 | tf_op jit(solution)/shard_map/ppermute | solution.py:491
  45.3 11.3 %stars.1 = (f32[16,128]{1,0:T(8,128)S(1)}, bf16[2816,128]{1,0:T(8,128)(2,1)}, bf16[1280,128]{1,0:T(8,128)(2,1)S(1)}) custom-call(s32[2048]{0:T(1024)S(1)} %reshape.85.position_ref, f32[16,128]{1,0:T(8,128)S(1)} %reshape.86.observed_ref, f32[16,128]{1,0:T(8,128)S(1)} %reshape.87.inverse_ref, bf16[64,32,32,128]{3,2,1,0:T(8,128)(2,1)} %weights_hbm.1, ...), custom_call_target="tpu_custom_call" | custom-call | flops 33554432 | bytes 16777216 | tf_op jit(solution)/shard_map/stars/pallas_call | solution.py:609
  56.7 5.0 %all-to-all-start.4 = ((bf16[32,88,128]{2,1,0:T(8,128)(2,1)}), bf16[32,88,128]{2,1,0:T(8,128)(2,1)S(1)}, u32[]{:S(2)}, u32[]{:S(2)}) async-start(bf16[32,88,128]{2,1,0:T(8,128)(2,1)} %bitcast.11), calls=%async_computation.4 | async-start | bytes 1441792 | tf_op jit(solution)/shard_map/all_to_all | solution.py:518
  61.8 0.7 copy.19
  62.5 13.1 %prior.1.base_hbm = f32[32,64,512]{2,1,0:T(8,128)} custom-call(f32[32,64,512]{2,1,0:T(8,128)} %field_hbm.2, bf16[2,64,512]{2,1,0:T(8,128)(2,1)} %copy-done.1, bf16[2,64,512]{2,1,0:T(8,128)(2,1)} %copy-done.2, bf16[2,36,512]{2,1,0:T(8,128)(2,1)} %copy-done.3, bf16[2,36,512]{2,1,0:T(8,128)(2,1)} %copy-done.4), custom_call_target="tpu_custom_call" | custom-call | flops 31457280 | bytes 8388608 | tf_op jit(solution)/shard_map/prior/pallas_call | solution.py:647
  75.6 1.8 %match.1.match_hbm = bf16[4096,128]{1,0:T(8,128)(2,1)S(1)} custom-call(s32[32,128]{1,0:T(8,128)S(1)} %pad_add_fusion.incoming_ref), custom_call_target="tpu_custom_call" | custom-call | flops 1000000000 | bytes 1048576 | tf_op jit(solution)/shard_map/match/pallas_call | solution.py:637
  77.4 3.7 %all-to-all-done.4 = bf16[32,88,128]{2,1,0:T(8,128)(2,1)S(1)} async-done(((bf16[32,88,128]{2,1,0:T(8,128)(2,1)}), bf16[32,88,128]{2,1,0:T(8,128)(2,1)S(1)}, u32[]{:S(2)}, u32[]{:S(2)}) %all-to-all-start.4) | async-done | bytes 720928 | tf_op jit(solution)/shard_map/all_to_all | solution.py:518
  81.2 9.1 %finish.1 = f32[32,64,512]{2,1,0:T(8,128)} custom-call(s32[4096]{0:T(1024)S(1)} %bitcast.22, bf16[4096,128]{1,0:T(8,128)(2,1)S(1)} %match.1.match_hbm, f32[32,64,512]{2,1,0:T(8,128)} %field_hbm.2, f32[32,64,512]{2,1,0:T(8,128)} %prior.1.base_hbm, bf16[2816,128]{1,0:T(8,128)(2,1)S(1)} %bitcast.18, bf16[1280,128]{1,0:T(8,128)(2,1)S(1)} %bitcast.28), custom_call_target="tpu_custom_call" | custom-call | flops 4194304 | bytes 12582912 | tf_op jit(solution)/shard_map/finish/pallas_call | solution.py:667
  (24 shorter events, 0.2 us)
Async XLA Ops:
  2.6 13.7 %all-to-all-start.2 = ((s32[32,1,128]{2,1,0:T(1,128)}), s32[32,1,128]{2,1,0:T(1,128)S(1)}, u32[]{:S(2)}, u32[]{:S(2)}) async-start(s32[32,1,128]{2,1,0:T(1,128)} %bitcast.31), calls=%async_computation.2 | async-start | bytes 32768 | tf_op jit(solution)/shard_map/all_to_all | solution.py:518
  9.7 2.2 %copy-start = (f32[32,64,512]{2,1,0:T(8,128)S(1)}, f32[32,64,512]{2,1,0:T(8,128)}, u32[]{:S(2)}) copy-start(f32[32,64,512]{2,1,0:T(8,128)} %field_hbm.2) | copy-start | bytes 12582916
  11.9 13.2 %copy-start.7 = (s32[16,128]{1,0:T(8,128)S(1)}, s32[16,128]{1,0:T(8,128)}, u32[]{:S(2)}) copy-start(s32[16,128]{1,0:T(8,128)} %get-tuple-element.80) | copy-start | bytes 24580
  11.9 13.6 %copy-start.6 = (f32[64,32]{0,1:T(8,128)S(1)}, f32[64,32]{0,1:T(8,128)}, u32[]{:S(2)}) copy-start(f32[64,32]{0,1:T(8,128)} %param.13) | copy-start | bytes 24580
  11.9 13.6 %copy-start.8 = (s32[64]{0:T(128)S(1)}, s32[64]{0:T(128)}, u32[]{:S(2)}) copy-start(s32[64]{0:T(128)} %param.14) | copy-start | bytes 772
  11.9 13.7 %copy-start.5 = (f32[64,32]{0,1:T(8,128)S(1)}, f32[64,32]{0,1:T(8,128)}, u32[]{:S(2)}) copy-start(f32[64,32]{0,1:T(8,128)} %param.12) | copy-start | bytes 24580
  22.2 23.1 %all-to-all-start.3 = ((bf16[32,88,128]{2,1,0:T(8,128)(2,1)}), bf16[32,88,128]{2,1,0:T(8,128)(2,1)S(1)}, u32[]{:S(2)}, u32[]{:S(2)}) async-start(bf16[32,88,128]{2,1,0:T(8,128)(2,1)} %bitcast.5), calls=%async_computation.3 | async-start | bytes 1441792 | tf_op jit(solution)/shard_map/all_to_all | solution.py:518
  25.8 6.7 %collective-permute-start = (bf16[2,64,512]{2,1,0:T(8,128)(2,1)S(1)}, bf16[2,64,512]{2,1,0:T(8,128)(2,1)S(1)}, u32[]{:S(2)}, u32[]{:S(2)}) collective-permute-start(bf16[2,64,512]{2,1,0:T(8,128)(2,1)S(1)} %get-tuple-element.73), channel_id=1, source_target_pairs={{0,4},{4,8},{8,12},{12,16},{16,20},{20,24},{24,28},{1,5},{5,9},{9,... | collective-permute-start | bytes 393224 | tf_op jit(solution)/shard_map/ppermute | solution.py:491
  29.3 7.0 %collective-permute-start.1 = (bf16[2,64,512]{2,1,0:T(8,128)(2,1)S(1)}, bf16[2,64,512]{2,1,0:T(8,128)(2,1)S(1)}, u32[]{:S(2)}, u32[]{:S(2)}) collective-permute-start(bf16[2,64,512]{2,1,0:T(8,128)(2,1)S(1)} %get-tuple-element.74), channel_id=1, source_target_pairs={{4,0},{8,4},{12,8},{16,12},{20,16},{24,20},{28,24},{5,1},{9,5},{13... | collective-permute-start | bytes 393224 | tf_op jit(solution)/shard_map/ppermute | solution.py:491
  32.5 24.2 %copy-start.1 = (bf16[2,64,512]{2,1,0:T(8,128)(2,1)}, bf16[2,64,512]{2,1,0:T(8,128)(2,1)S(1)}, u32[]{:S(2)}) copy-start(bf16[2,64,512]{2,1,0:T(8,128)(2,1)S(1)} %collective-permute-done.xlo_ref) | copy-start | bytes 393220
  36.3 20.4 %copy-start.2 = (bf16[2,64,512]{2,1,0:T(8,128)(2,1)}, bf16[2,64,512]{2,1,0:T(8,128)(2,1)S(1)}, u32[]{:S(2)}) copy-start(bf16[2,64,512]{2,1,0:T(8,128)(2,1)S(1)} %collective-permute-done.1.xhi_ref) | copy-start | bytes 393220
  36.4 5.2 %collective-permute-start.2 = (bf16[2,36,512]{2,1,0:T(8,128)(2,1)S(1)}, bf16[2,36,512]{2,1,0:T(8,128)(2,1)S(1)}, u32[]{:S(2)}, u32[]{:S(2)}) collective-permute-start(bf16[2,36,512]{2,1,0:T(8,128)(2,1)S(1)} %get-tuple-element.77), channel_id=1, source_target_pairs={{0,1},{1,2},{2,3},{4,5},{5,6},{6,7},{8,9},{9,10},{10,11},{12,13},{... | collective-permute-start | bytes 221192 | tf_op jit(solution)/shard_map/ppermute | solution.py:491
  40.0 5.3 %collective-permute-start.3 = (bf16[2,36,512]{2,1,0:T(8,128)(2,1)S(1)}, bf16[2,36,512]{2,1,0:T(8,128)(2,1)S(1)}, u32[]{:S(2)}, u32[]{:S(2)}) collective-permute-start(bf16[2,36,512]{2,1,0:T(8,128)(2,1)S(1)} %get-tuple-element.78), channel_id=1, source_target_pairs={{1,0},{2,1},{3,2},{5,4},{6,5},{7,6},{9,8},{10,9},{11,10},{13,12},{... | collective-permute-start | bytes 221192 | tf_op jit(solution)/shard_map/ppermute | solution.py:491
  41.5 15.2 %copy-start.3 = (bf16[2,36,512]{2,1,0:T(8,128)(2,1)}, bf16[2,36,512]{2,1,0:T(8,128)(2,1)S(1)}, u32[]{:S(2)}) copy-start(bf16[2,36,512]{2,1,0:T(8,128)(2,1)S(1)} %collective-permute-done.2.ylo_ref) | copy-start | bytes 221188
  45.3 11.4 %copy-start.4 = (bf16[2,36,512]{2,1,0:T(8,128)(2,1)}, bf16[2,36,512]{2,1,0:T(8,128)(2,1)S(1)}, u32[]{:S(2)}) copy-start(bf16[2,36,512]{2,1,0:T(8,128)(2,1)S(1)} %collective-permute-done.3.yhi_ref) | copy-start | bytes 221188
  56.7 24.4 %all-to-all-start.4 = ((bf16[32,88,128]{2,1,0:T(8,128)(2,1)}), bf16[32,88,128]{2,1,0:T(8,128)(2,1)S(1)}, u32[]{:S(2)}, u32[]{:S(2)}) async-start(bf16[32,88,128]{2,1,0:T(8,128)(2,1)} %bitcast.11), calls=%async_computation.4 | async-start | bytes 1441792 | tf_op jit(solution)/shard_map/all_to_all | solution.py:518
